TPU v7x, 32 devices: a whole 2x2x4 slice. The times are simulated.
32 devices in a mesh: dp: 4 (over y, core), expert: 8 (over z, x).
Axes of the slice: x: 2, y: 2, z: 4, core: 2. Of those that a mesh axis runs over, the one named last changes fastest.
Arguments:
- tokens: bfloat16 [4, 1024, 3584], P('dp', 'expert'), may hold values from -6 to 6
- cotangent: bfloat16 [4, 1024, 1024], P('dp', 'expert'), may hold values from -12 to 12
- gate_weights: float32 [4, 1024], replicated, may hold values from 0.1 to 1
- tile_expert: int32 [4, 8], replicated, may hold values from 0 to 7, as said below
- w_gate: bfloat16 [8, 3584, 1024], P('expert', None, 'dp'), may hold values from -0.09375 to 0.09375
- w_up: bfloat16 [8, 3584, 1024], P('expert', None, 'dp'), may hold values from -0.09375 to 0.09375
Outputs:
- d_tokens: bfloat16 [4, 1024, 3584], P('dp', 'expert')
- hidden: bfloat16 [4, 1024, 1024], P(None, 'expert', 'dp')
- grad_gate: bfloat16 [8, 3584, 1024], P('expert', None, 'dp')
- grad_up: bfloat16 [8, 3584, 1024], P('expert', None, 'dp')
Inputs may be any that keep to these rules, and one draw needn't show every extreme that they name: tile_expert[g, j] is either j or (j + 1) mod 8: the expert of the tile's own index of the expert axis or of the next index round the closed cycle.
All inputs are finite; a program needn't handle non-finite values.
Results may differ from a plain program's by a relative error of at most 0.009.
Values may be sent and summed in bfloat16 or wider, within the bound.
No kernel may reach another device: no remote copies, remote signals or barrier semaphores. Data moves between devices by JAX's collectives and lax.ppermute only.
A program may use at most 128 MiB of HBM per device.

v0:
```python
import jax
import jax.numpy as jnp
from jax import lax
from jax.sharding import PartitionSpec as P

TILE = 128


def shifted(value, axis, steps):
    count = lax.axis_size(axis)
    pairs = [(source, (source + steps) % count) for source in range(count)]
    return lax.ppermute(value, axis, pairs)


def contract(left, right, left_axis, right_axis):
    return lax.dot_general(
        left, right, (((left_axis,), (right_axis,)), ((), ())), preferred_element_type=jnp.float32
    )


def route_scale(tile_expert, gate_weights, source, expert, row_count):
    tile_count = row_count // TILE
    owners = lax.dynamic_slice_in_dim(tile_expert, source * tile_count, tile_count, 1)
    weights = lax.dynamic_slice_in_dim(gate_weights, source * row_count, row_count, 1)
    routed = jnp.repeat(owners == expert, TILE, axis=1, total_repeat_length=row_count)
    return jnp.where(routed, weights, jnp.zeros_like(weights))


def expert_pass(cand_rows, cand_grads, row_scale, gate_panel, up_panel):
    groups, row_total, model_width = cand_rows.shape
    quarter = gate_panel.shape[1]
    flat_rows = cand_rows.reshape(groups * row_total, model_width)
    gate_val = jnp.dot(flat_rows, gate_panel, preferred_element_type=jnp.float32)
    up_val = jnp.dot(flat_rows, up_panel, preferred_element_type=jnp.float32)
    sigmoid_val = jax.nn.sigmoid(gate_val)
    activation = gate_val * sigmoid_val
    factor = row_scale.reshape(groups * row_total, 1)
    hidden_part = (factor * activation * up_val).astype(jnp.bfloat16)
    act_grad = factor * cand_grads.reshape(groups * row_total, quarter).astype(jnp.float32)
    up_grad = (act_grad * activation).astype(jnp.bfloat16)
    gate_grad = (act_grad * up_val * sigmoid_val * (1.0 + gate_val * (1.0 - sigmoid_val))).astype(
        jnp.bfloat16
    )
    partial_value = (
        contract(gate_grad, gate_panel, 1, 1) + contract(up_grad, up_panel, 1, 1)
    ).astype(jnp.bfloat16)
    partial_value = lax.optimization_barrier(partial_value)
    grad_gate = contract(flat_rows, gate_grad, 0, 0)
    grad_up = contract(flat_rows, up_grad, 0, 0)
    return (
        partial_value.reshape(groups, row_total, model_width),
        hidden_part.reshape(groups, row_total, quarter),
        grad_gate,
        grad_up,
    )


def to_groups(tile_rows, tile_grads):
    gathered = lax.all_gather(tile_rows, "dp", axis=0, tiled=True)
    quarters = lax.all_to_all(tile_grads, "dp", split_axis=2, concat_axis=0, tiled=True)
    return (gathered, quarters)


def quarter_total(terms):
    return lax.psum_scatter(
        terms.astype(jnp.bfloat16), "dp", scatter_dimension=0, tiled=True
    ).astype(jnp.float32)


def per_device(tokens, cotangent, gate_weights, tile_expert, w_gate, w_up):
    row_count = tokens.shape[1]
    cycle_size = lax.axis_size("expert")
    position = lax.axis_index("expert")
    next_place = (position + 1) % cycle_size
    gate_panel = w_gate[0]
    up_panel = w_up[0]
    own_scale = route_scale(tile_expert, gate_weights, position, position, row_count)
    home_rows, home_grads = to_groups(tokens, cotangent)
    next_gate, next_up = shifted((w_gate, w_up), "expert", -1)
    next_scale = route_scale(tile_expert, gate_weights, position, next_place, row_count)
    part_own, hidden_own, grad_gate, grad_up = expert_pass(
        home_rows, home_grads, own_scale, gate_panel, up_panel
    )
    part_next, hidden_next, lent_gate, lent_up = expert_pass(
        home_rows, home_grads, next_scale, next_gate[0], next_up[0]
    )
    back_gate, back_up = (
        shifted(lent_gate.astype(jnp.bfloat16), "expert", 1).astype(lent_gate.dtype),
        shifted(lent_up.astype(jnp.bfloat16), "expert", 1).astype(lent_up.dtype),
    )
    grad_gate = grad_gate + back_gate
    grad_up = grad_up + back_up
    home_sum = part_own.astype(jnp.float32) + part_next.astype(jnp.float32)
    d_tokens = quarter_total(home_sum).astype(jnp.bfloat16)
    hidden = (hidden_own.astype(jnp.float32) + hidden_next.astype(jnp.float32)).astype(jnp.bfloat16)
    grad_gate = (grad_gate / TILE).astype(jnp.bfloat16)[None]
    grad_up = (grad_up / TILE).astype(jnp.bfloat16)[None]
    return (d_tokens, hidden, grad_gate, grad_up)


def solution(mesh):
    in_specs = (
        P("dp", "expert", None),
        P("dp", "expert", None),
        P(),
        P(),
        P("expert", None, "dp"),
        P("expert", None, "dp"),
    )
    out_specs = (
        P("dp", "expert", None),
        P(None, "expert", "dp"),
        P("expert", None, "dp"),
        P("expert", None, "dp"),
    )
    return jax.shard_map(
        per_device, mesh=mesh, in_specs=in_specs, out_specs=out_specs, check_vma=False
    )
```

profile of v0, /device:TPU:0, one launch (start us, length us, event | category | flops | bytes accessed | tf_op | source)
XLA Modules:
  0.0 207.0 jit_solution(18124887622528972965)
XLA Ops:
  7.2 0.0 copy-start.2
  7.2 0.0 all-gather.2.cloned.1.call-start
  7.2 0.7 all-gather.2.cloned.1.call-update
  7.9 6.0 %collective-permute-start.1 = (bf16[1,3584,256]{2,1,0:T(8,128)(2,1)}, bf16[1,3584,256]{2,1,0:T(8,128)(2,1)}, u32[]{:S(2)}, u32[]{:S(2)}) collective-permute-start(bf16[1,3584,256]{2,1,0:T(8,128)(2,1)} %param.20), channel_id=1, source_target_pairs={{0,7},{1,0},{2,1},{3,2},{4,3},{5,4},{6,5},{7,6},{8,15},{9,8},{10,9... | collective-permute-start | bytes 5505032 | tf_op jit(solution)/shard_map/ppermute | solution.py:12
  13.9 0.5 collective-permute-start
  14.5 1.3 copy.13
  15.7 0.5 broadcast.95
  16.3 2.2 %reduce.10 = bf16[1024,128]{1,0:T(8,128)(2,1)S(1)} reduce(bf16[1024,1,128]{2,1,0:T(2,128)(2,1)S(1)} %bitcast.87, bf16[]{:T(256)} %broadcast.95), dimensions={1}, to_apply=%bitcast.53.reduce_sub_computation | reduce | bytes 524290
  18.5 0.8 reshape.126
  19.2 3.4 %all-to-all-start = ((bf16[4,2,16384]{2,1,0:T(2,128)(2,1)}), bf16[4,2,16384]{2,1,0:T(2,128)(2,1)S(1)}, u32[]{:S(2)}, u32[]{:S(2)}) async-start(bf16[4,2,16384]{2,1,0:T(2,128)(2,1)} %reshape.126), calls=%async_computation | async-start | bytes 524288 | tf_op jit(solution)/shard_map/all_to_all | solution.py:60
  22.7 0.2 reduce-scatter.2.cloned.1.call-start
  22.9 0.9 compare_reduce_fusion.1
  23.8 0.8 select_bitcast_fusion.1
  24.6 7.2 %all-to-all-done = bf16[4,2,16384]{2,1,0:T(2,128)(2,1)S(1)} async-done(((bf16[4,2,16384]{2,1,0:T(2,128)(2,1)}), bf16[4,2,16384]{2,1,0:T(2,128)(2,1)S(1)}, u32[]{:S(2)}, u32[]{:S(2)}) %all-to-all-start) | async-done | bytes 262176 | tf_op jit(solution)/shard_map/all_to_all | solution.py:60
  31.8 0.3 reshape.127
  32.1 0.5 bitcast_convert_fusion
  32.6 0.2 copy.14
  32.8 13.8 %all-gather.2.cloned.1.call-done = bf16[4,128,3584]{2,1,0:T(8,128)(2,1)} async-done(((bf16[1,128,3584]{2,1,0:T(8,128)(2,1)}), bf16[4,128,3584]{2,1,0:T(8,128)(2,1)}) %all-gather.2.cloned.1.call-update) | async-done | bytes 3670032 | tf_op jit(solution)/shard_map/all_gather | solution.py:59
  46.6 0.0 copy-start
  46.6 0.0 copy-start.3
  46.6 0.0 copy-done.2
  46.6 3.3 %fusion.13 = f32[512,256]{1,0:T(8,128)S(1)} fusion(bf16[512,3584]{1,0:T(8,128)(2,1)} %bitcast.78, bf16[1,3584,256]{2,1,0:T(8,128)(2,1)S(1)} %copy-done.2), kind=kOutput, calls=%fused_computation.22 | convolution fusion | flops 939524096 | bytes 6029312 | tf_op jit(solution)/shard_map/dot_general | solution.py:33
  49.9 0.0 copy-done
  49.9 0.4 copy-done.3
  50.3 1.1 fusion.16
  51.5 3.2 %collective-permute-done.1 = bf16[1,3584,256]{2,1,0:T(8,128)(2,1)} collective-permute-done((bf16[1,3584,256]{2,1,0:T(8,128)(2,1)}, bf16[1,3584,256]{2,1,0:T(8,128)(2,1)}, u32[]{:S(2)}, u32[]{:S(2)}) %collective-permute-start.1) | collective-permute-done | bytes 1835040 | tf_op jit(solution)/shard_map/ppermute | solution.py:12
  54.7 2.6 %fusion.5 = f32[512,256]{1,0:T(8,128)S(1)} fusion(bf16[512,3584]{1,0:T(8,128)(2,1)S(1)} %bitcast.82, bf16[1,3584,256]{2,1,0:T(8,128)(2,1)} %collective-permute-done.1), kind=kOutput, calls=%fused_computation.14 | convolution fusion | flops 939524096 | bytes 6029312 | tf_op jit(solution)/shard_map/dot_general | solution.py:33
  57.3 35.6 %collective-permute-done = bf16[1,3584,256]{2,1,0:T(8,128)(2,1)} collective-permute-done((bf16[1,3584,256]{2,1,0:T(8,128)(2,1)}, bf16[1,3584,256]{2,1,0:T(8,128)(2,1)}, u32[]{:S(2)}, u32[]{:S(2)}) %collective-permute-start) | collective-permute-done | bytes 1835040 | tf_op jit(solution)/shard_map/ppermute | solution.py:12
  92.8 3.8 %add_convert_fusion.3 = (bf16[512,256]{1,0:T(8,128)(2,1)}, bf16[512,256]{1,0:T(8,128)(2,1)S(1)}, bf16[512,256]{1,0:T(8,128)(2,1)S(1)}, bf16[512,256]{1,0:T(8,128)(2,1)S(1)}, bf16[512,256]{1,0:T(8,128)(2,1)S(1)}) fusion(f32[512,256]{1,0:T(8,128)S(1)} %fusion.16, f32[512]{0:T(512)S(1)} %get-tuple-element.61, f32[512]{0:T(512)S(1)} %get-tuple-element.60, ...), kind=kOutput, calls=%fused_computation.29 | convolution fusion | flops 944504832 | bytes 8916992 | tf_op jit(solution)/shard_map/dot_general | solution.py:34
  96.6 2.6 %fusion.7 = f32[512,3584]{1,0:T(8,128)S(1)} fusion(bf16[512,256]{1,0:T(8,128)(2,1)S(1)} %get-tuple-element.59, bf16[1,3584,256]{2,1,0:T(8,128)(2,1)} %collective-permute-done), kind=kOutput, calls=%fused_computation.16 | convolution fusion | flops 939524096 | bytes 9437184 | tf_op jit(solution)/shard_map/dot_general | solution.py:16
  99.3 2.7 %add_convert_fusion.1 = bf16[512,3584]{1,0:T(8,128)(2,1)S(1)} fusion(f32[512,3584]{1,0:T(8,128)S(1)} %fusion.7, bf16[512,256]{1,0:T(8,128)(2,1)S(1)} %get-tuple-element.56, bf16[1,3584,256]{2,1,0:T(8,128)(2,1)} %collective-permute-done.1), kind=kOutput, calls=%fused_computation.1 | convolution fusion | flops 943194112 | bytes 13107200 | tf_op jit(solution)/shard_map/dot_general | solution.py:16
  101.9 1.2 fusion.11
  103.1 1.2 add_convert_fusion.2
  104.3 2.7 %add_convert_fusion = bf16[512,3584]{1,0:T(8,128)(2,1)} fusion(bf16[512,3584]{1,0:T(8,128)(2,1)S(1)} %add_convert_fusion.1, bf16[512,3584]{1,0:T(8,128)(2,1)S(1)} %add_convert_fusion.2), kind=kLoop, calls=%fused_computation | loop fusion | flops 7340032 | bytes 11010048 | tf_op jit(solution)/shard_map/convert_element_type | solution.py:66
  107.0 0.0 reduce-scatter.2.cloned.1.call-update
  107.0 0.0 copy-start.1
  107.0 3.3 %fusion.1 = bf16[3584,256]{0,1:T(8,128)(2,1)S(1)} fusion(bf16[512,256]{1,0:T(8,128)(2,1)S(1)} %get-tuple-element.59, bf16[512,3584]{1,0:T(8,128)(2,1)} %bitcast.79), kind=kOutput, calls=%fused_computation.8 | convolution fusion | flops 940441600 | bytes 5767168 | tf_op jit(solution)/shard_map/dot_general | solution.py:16
  110.3 0.4 collective-permute-start.3
  110.7 0.0 copy-done.1
  110.7 2.4 %fusion = bf16[3584,256]{0,1:T(8,128)(2,1)} fusion(bf16[512,256]{1,0:T(8,128)(2,1)S(1)} %get-tuple-element.56, bf16[512,3584]{1,0:T(8,128)(2,1)S(1)} %bitcast.84), kind=kOutput, calls=%fused_computation.7 | convolution fusion | flops 940441600 | bytes 5767168 | tf_op jit(solution)/shard_map/dot_general | solution.py:16
  113.1 0.7 collective-permute-start.2
  113.8 42.7 %collective-permute-done.3 = bf16[3584,256]{0,1:T(8,128)(2,1)S(1)} collective-permute-done((bf16[3584,256]{0,1:T(8,128)(2,1)S(1)}, bf16[3584,256]{0,1:T(8,128)(2,1)S(1)}, u32[]{:S(2)}, u32[]{:S(2)}) %collective-permute-start.3) | collective-permute-done | bytes 1835040 | tf_op jit(solution)/shard_map/ppermute | solution.py:12
  156.5 1.2 fusion.3
  157.7 2.3 %copy.16 = bf16[1,3584,256]{2,1,0:T(8,128)(2,1)} copy(bf16[1,3584,256]{1,2,0:T(8,128)(2,1)S(1)} %fusion.3) | data formatting | bytes 3670016
  160.0 34.1 %collective-permute-done.2 = bf16[3584,256]{0,1:T(8,128)(2,1)} collective-permute-done((bf16[3584,256]{0,1:T(8,128)(2,1)}, bf16[3584,256]{0,1:T(8,128)(2,1)}, u32[]{:S(2)}, u32[]{:S(2)}) %collective-permute-start.2) | collective-permute-done | bytes 1835040 | tf_op jit(solution)/shard_map/ppermute | solution.py:12
  194.1 3.8 %fusion.2 = bf16[1,3584,256]{1,2,0:T(8,128)(2,1)S(1)} fusion(bf16[3584,256]{0,1:T(8,128)(2,1)} %collective-permute-done.2, bf16[512,256]{1,0:T(8,128)(2,1)S(1)} %get-tuple-element.57, bf16[512,3584]{1,0:T(8,128)(2,1)} %bitcast.80), kind=kOutput, calls=%fused_computation.11 | convolution fusion | flops 943194112 | bytes 7602176 | tf_op jit(solution)/shard_map/dot_general | solution.py:16
  197.9 2.3 %copy.15 = bf16[1,3584,256]{2,1,0:T(8,128)(2,1)} copy(bf16[1,3584,256]{1,2,0:T(8,128)(2,1)S(1)} %fusion.2) | data formatting | bytes 3670016
  200.2 0.0 reduce-scatter.2.cloned.1.call-done
Async XLA Ops:
  7.2 39.5 %copy-start.2 = (bf16[1,3584,256]{2,1,0:T(8,128)(2,1)S(1)}, bf16[1,3584,256]{2,1,0:T(8,128)(2,1)}, u32[]{:S(2)}) copy-start(bf16[1,3584,256]{2,1,0:T(8,128)(2,1)} %param.20) | copy-start | bytes 5505028
  7.2 39.4 %all-gather.2.cloned.1.call-start = ((), (), s32[]{:S(2)}) async-start(), calls=%async_computation.2 | async-start | bytes 4587520 | tf_op jit(solution)/shard_map/all_gather | solution.py:59
  7.9 46.8 %collective-permute-start.1 = (bf16[1,3584,256]{2,1,0:T(8,128)(2,1)}, bf16[1,3584,256]{2,1,0:T(8,128)(2,1)}, u32[]{:S(2)}, u32[]{:S(2)}) collective-permute-start(bf16[1,3584,256]{2,1,0:T(8,128)(2,1)} %param.20), channel_id=1, source_target_pairs={{0,7},{1,0},{2,1},{3,2},{4,3},{5,4},{6,5},{7,6},{8,15},{9,8},{10,9... | collective-permute-start | bytes 5505032 | tf_op jit(solution)/shard_map/ppermute | solution.py:12
  13.9 78.9 %collective-permute-start = (bf16[1,3584,256]{2,1,0:T(8,128)(2,1)}, bf16[1,3584,256]{2,1,0:T(8,128)(2,1)}, u32[]{:S(2)}, u32[]{:S(2)}) collective-permute-start(bf16[1,3584,256]{2,1,0:T(8,128)(2,1)} %param.21), channel_id=1, source_target_pairs={{0,7},{1,0},{2,1},{3,2},{4,3},{5,4},{6,5},{7,6},{8,15},{9,8},{10,9... | collective-permute-start | bytes 5505032 | tf_op jit(solution)/shard_map/ppermute | solution.py:12
  19.2 12.6 %all-to-all-start = ((bf16[4,2,16384]{2,1,0:T(2,128)(2,1)}), bf16[4,2,16384]{2,1,0:T(2,128)(2,1)S(1)}, u32[]{:S(2)}, u32[]{:S(2)}) async-start(bf16[4,2,16384]{2,1,0:T(2,128)(2,1)} %reshape.126), calls=%async_computation | async-start | bytes 524288 | tf_op jit(solution)/shard_map/all_to_all | solution.py:60
  22.7 177.5 %reduce-scatter.2.cloned.1.call-start = ((), (), s32[]{:S(2)}) async-start(), calls=%async_computation.3 | async-start | bytes 4587520 | tf_op jit(solution)/shard_map/reduce_scatter | solution.py:65
  46.6 3.3 %copy-start = (bf16[4,128,3584]{2,1,0:T(8,128)(2,1)S(1)}, bf16[4,128,3584]{2,1,0:T(8,128)(2,1)}, u32[]{:S(2)}) copy-start(bf16[4,128,3584]{2,1,0:T(8,128)(2,1)} %all-gather.2.cloned.1.call-done) | copy-start | bytes 11010052
  46.6 3.7 %copy-start.3 = (bf16[1,3584,256]{2,1,0:T(8,128)(2,1)S(1)}, bf16[1,3584,256]{2,1,0:T(8,128)(2,1)}, u32[]{:S(2)}) copy-start(bf16[1,3584,256]{2,1,0:T(8,128)(2,1)} %param.21) | copy-start | bytes 5505028
  107.0 3.7 %copy-start.1 = (bf16[4,128,3584]{2,1,0:T(8,128)(2,1)S(1)}, bf16[4,128,3584]{2,1,0:T(8,128)(2,1)}, u32[]{:S(2)}) copy-start(bf16[4,128,3584]{2,1,0:T(8,128)(2,1)} %all-gather.2.cloned.1.call-done) | copy-start | bytes 11010052
  110.3 46.2 %collective-permute-start.3 = (bf16[3584,256]{0,1:T(8,128)(2,1)S(1)}, bf16[3584,256]{0,1:T(8,128)(2,1)S(1)}, u32[]{:S(2)}, u32[]{:S(2)}) collective-permute-start(bf16[3584,256]{0,1:T(8,128)(2,1)S(1)} %fusion.1), channel_id=1, source_target_pairs={{0,1},{1,2},{2,3},{3,4},{4,5},{5,6},{6,7},{7,0},{8,9},{9,10},{10,1... | collective-permute-start | bytes 5505032 | tf_op jit(solution)/shard_map/ppermute | solution.py:12
  113.1 81.0 %collective-permute-start.2 = (bf16[3584,256]{0,1:T(8,128)(2,1)}, bf16[3584,256]{0,1:T(8,128)(2,1)}, u32[]{:S(2)}, u32[]{:S(2)}) collective-permute-start(bf16[3584,256]{0,1:T(8,128)(2,1)} %fusion), channel_id=1, source_target_pairs={{0,1},{1,2},{2,3},{3,4},{4,5},{5,6},{6,7},{7,0},{8,9},{9,10},{10,1... | collective-permute-start | bytes 5505032 | tf_op jit(solution)/shard_map/ppermute | solution.py:12
Sparse Core Ops, SparseCore 0:
  9.6 37.0 all-gather.1
  107.1 43.1 reduce-scatter.1
where the time goes:
time: 207 us
  waiting for transfers between devices  137 us (66%)
  matrix products  29.1 us (14%)
  between operations  14.2 us (7%)
  starting transfers between devices  11.3 us (5%)
  local copies, waits for them, and re-layouts  7.95 us (4%)
  other arithmetic  7.13 us (3%)
    ppermute x4, waiting for transfers between devices, shifted(): return lax.ppermute(value, axis, pairs)  116 us
    dot_general x8, matrix products, contract(): lax.dot_general(left, right, (((left_axis,), (right_axis,)), ((), ())), p...  18.3 us
    all_gather x1, waiting for transfers between devices, to_groups(): gathered = lax.all_gather(tile_rows, 'dp', axis=0, tiled=True)  13.8 us
    unnamed x14, local copies, waits for them, and re-layouts  7.75 us
    ppermute x4, starting transfers between devices, shifted(): return lax.ppermute(value, axis, pairs)  7.61 us
    all_to_all x1, waiting for transfers between devices, to_groups(): lax.all_to_all(tile_grads, 'dp', split_axis=2, concat_axis=0, tiled=True)  7.22 us
    dot_general x2, matrix products, expert_pass(): jnp.dot(flat_rows, gate_panel, preferred_element_type=jnp.float32)  5.9 us
    dot_general x2, matrix products, expert_pass(): up_val = jnp.dot(flat_rows, up_panel, preferred_element_type=jnp.float32)  4.86 us
  transfers between devices with their start and end apart: 7, of which 6 were waited for; matrix products, arithmetic and copies ran while one was open for 14% of the time, Pallas kernels for 0%

commit v1 on v0

v1 whole, which is shorter than its diff:
```python
import functools

import jax
import jax.numpy as jnp
from jax import lax
from jax.experimental import pallas as pl
from jax.experimental.pallas import tpu as pltpu
from jax.sharding import PartitionSpec as P

TILE = 128
HEAD = 80


def shifted(value, steps):
    count = lax.axis_size("expert")
    pairs = [(source, (source + steps) % count) for source in range(count)]
    return lax.ppermute(value, "expert", pairs)


def across(value):
    count = lax.axis_size("dp")
    pairs = [(source, (source + count // 2) % count) for source in range(count)]
    return lax.ppermute(value, "dp", pairs)


def within(value):
    count = lax.axis_size("dp")
    pairs = [(source, source + 1 - 2 * (source % 2)) for source in range(count)]
    return lax.ppermute(value, "dp", pairs)


def column_step(width):
    for step in (512, 256, 128):
        if width % step == 0:
            return step
    return width


def contract(left, right, left_axis, right_axis):
    return lax.dot_general(
        left, right, (((left_axis,), (right_axis,)), ((), ())), preferred_element_type=jnp.float32
    )


def joined(refs, columns):
    return jnp.concatenate([ref[:, columns] for ref in refs], axis=0)


def block_body(piece_count, step, *refs):
    pieces = refs[:piece_count]
    scale_ref, grads_ref, gate_ref, up_ref, hidden_ref, value_grads_ref, part_ref = refs[piece_count:]
    width, quarter = gate_ref.shape
    rows = hidden_ref.shape[0]
    gate_val = jnp.zeros((rows, quarter), jnp.float32)
    up_val = jnp.zeros((rows, quarter), jnp.float32)
    for start in range(0, width, step):
        columns = pl.ds(start, step)
        values = joined(pieces, columns)
        gate_val += contract(values, gate_ref[columns, :], 1, 0)
        up_val += contract(values, up_ref[columns, :], 1, 0)
    factor = scale_ref[...]
    sigmoid_val = jax.nn.sigmoid(gate_val)
    activation = gate_val * sigmoid_val
    hidden_ref[...] = (factor * activation * up_val).astype(hidden_ref.dtype)
    act_grad = factor * grads_ref[...].astype(jnp.float32)
    up_grad = (act_grad * activation).astype(jnp.bfloat16)
    gate_grad = (act_grad * up_val * sigmoid_val * (1.0 + gate_val * (1.0 - sigmoid_val))).astype(
        jnp.bfloat16
    )
    value_grads_ref[:, :quarter] = gate_grad
    value_grads_ref[:, quarter:] = up_grad
    for start in range(0, width, step):
        columns = pl.ds(start, step)
        part_ref[:, columns] = (
            contract(gate_grad, gate_ref[columns, :], 1, 1)
            + contract(up_grad, up_ref[columns, :], 1, 1)
        ).astype(part_ref.dtype)


def block_pass(pieces, scale, grads, gate_panel, up_panel):
    rows = sum(piece.shape[0] for piece in pieces)
    width, quarter = gate_panel.shape
    return pl.pallas_call(
        functools.partial(block_body, len(pieces), column_step(width)),
        out_shape=(
            jax.ShapeDtypeStruct((rows, quarter), jnp.bfloat16),
            jax.ShapeDtypeStruct((rows, 2 * quarter), jnp.bfloat16),
            jax.ShapeDtypeStruct((rows, width), jnp.bfloat16),
        ),
        compiler_params=pltpu.CompilerParams(vmem_limit_bytes=40 * 2**20),
        cost_estimate=pl.CostEstimate(
            flops=8 * rows * width * quarter,
            bytes_accessed=4 * (rows + quarter) * width,
            transcendentals=rows * quarter,
        ),
        name="block_pass",
    )(*pieces, scale, grads, gate_panel, up_panel)


def weight_body(piece_count, grad_count, *refs):
    pieces = refs[:piece_count]
    grads = refs[piece_count : piece_count + grad_count]
    gate_out, up_out = refs[piece_count + grad_count :]
    quarter = gate_out.shape[1]
    values = joined(pieces, slice(None))
    value_grads = joined(grads, slice(None))
    total = contract(values, value_grads, 0, 0) * (1.0 / TILE)
    gate_out[...] = total[:, :quarter].astype(gate_out.dtype)
    up_out[...] = total[:, quarter:].astype(up_out.dtype)


def weight_pass(pieces, grads):
    width = pieces[0].shape[1]
    quarter = grads[0].shape[1] // 2
    step = column_step(width)
    rows = sum(piece.shape[0] for piece in pieces)
    return pl.pallas_call(
        functools.partial(weight_body, len(pieces), len(grads)),
        grid=(width // step,),
        in_specs=[pl.BlockSpec((piece.shape[0], step), lambda i: (0, i)) for piece in pieces]
        + [pl.BlockSpec(grad.shape, lambda i: (0, 0)) for grad in grads],
        out_specs=[pl.BlockSpec((step, quarter), lambda i: (i, 0))] * 2,
        out_shape=[jax.ShapeDtypeStruct((width, quarter), jnp.bfloat16)] * 2,
        compiler_params=pltpu.CompilerParams(vmem_limit_bytes=40 * 2**20),
        cost_estimate=pl.CostEstimate(
            flops=4 * rows * width * quarter,
            bytes_accessed=2 * rows * width + 4 * quarter * width,
            transcendentals=0,
        ),
        name="weight_pass",
    )(*pieces, *grads)


def route_scale(tile_expert, gate_weights, source, expert, row_count):
    tile_count = row_count // TILE
    owners = lax.dynamic_slice_in_dim(tile_expert, source * tile_count, tile_count, 1)
    weights = lax.dynamic_slice_in_dim(gate_weights, source * row_count, row_count, 1)
    routed = jnp.repeat(owners == expert, TILE, axis=1, total_repeat_length=row_count)
    return jnp.where(routed, weights, jnp.zeros_like(weights))


def relative(value, side, core):
    flipped = jnp.where(core == 1, value[jnp.array([1, 0, 3, 2])], value)
    return jnp.where(side == 1, flipped[jnp.array([2, 3, 0, 1])], flipped)


def f32(value):
    return value.astype(jnp.float32)


def b16(value):
    return value.astype(jnp.bfloat16)


def per_device(tokens, cotangent, gate_weights, tile_expert, w_gate, w_up):
    row_count = tokens.shape[1]
    cycle_size = lax.axis_size("expert")
    position = lax.axis_index("expert")
    rank = lax.axis_index("dp")
    side, core = rank // 2, rank % 2
    gate_panel, up_panel = w_gate[0], w_up[0]
    quarter = gate_panel.shape[1]
    head = HEAD * row_count // TILE
    tile, tile_grad = tokens[0], cotangent[0]
    top, low = tile[:head], tile[head:]

    y_low = across(low)
    x_top = shifted(top, 1)
    grad_sent = lax.dynamic_slice_in_dim(tile_grad, (1 - side) * 2 * quarter, 2 * quarter, 1)
    grad_kept = lax.dynamic_slice_in_dim(tile_grad, side * 2 * quarter, 2 * quarter, 1)
    grad_got = across(grad_sent)
    y_top = across(top)
    x_low = shifted(low, 1)
    c_tile = within(tile)
    both = jnp.stack([grad_kept, grad_got])
    both_kept = lax.dynamic_slice_in_dim(both, core * quarter, quarter, 2)
    both_got = within(lax.dynamic_slice_in_dim(both, (1 - core) * quarter, quarter, 2))
    home_grads = jnp.stack([both_kept, both_got], axis=1).reshape(2, 2 * row_count, quarter)
    past_grads = shifted(home_grads, 1)
    xy_low = shifted(y_low, 1)
    xy_top = across(x_top)
    cy_low, cy_top = within(y_low), within(y_top)
    cx_top, cx_low = within(x_top), within(x_low)
    cxy_low, cxy_top = within(xy_low), within(xy_top)

    before = (position + cycle_size - 1) % cycle_size
    home_scale = relative(
        route_scale(tile_expert, gate_weights, position, position, row_count), side, core
    ).reshape(2, 2 * row_count, 1)
    past_scale = relative(
        route_scale(tile_expert, gate_weights, before, position, row_count), side, core
    ).reshape(2, 2 * row_count, 1)

    home_near = (tile, c_tile)
    home_far = (y_top, y_low, cy_top, cy_low)
    past_near = (x_top, x_low, cx_top, cx_low)
    past_far = (xy_top, xy_low, cxy_top, cxy_low)
    panels = (gate_panel, up_panel)
    hid_hn, vg_hn, part_hn = block_pass(home_near, home_scale[0], home_grads[0], *panels)
    hid_hf, vg_hf, part_hf = block_pass(home_far, home_scale[1], home_grads[1], *panels)
    hid_pn, vg_pn, part_pn = block_pass(past_near, past_scale[0], past_grads[0], *panels)
    hid_pf, vg_pf, part_pf = block_pass(past_far, past_scale[1], past_grads[1], *panels)

    def pair_sum(part):
        return b16(f32(part[:row_count]) + f32(within(part[row_count:])))

    pair_hn, pair_hf = pair_sum(part_hn), pair_sum(part_hf)
    pair_pn, pair_pf = pair_sum(part_pn), pair_sum(part_pf)
    hid_back = shifted(jnp.stack([hid_pn, hid_pf]), -1)
    low_near = shifted(pair_pn[head:], -1)
    low_far = shifted(pair_pf[head:], -1)
    top_home = across(pair_hf[:head])
    top_past = across(pair_pf[:head])
    top_back = shifted(b16(f32(pair_pn[:head]) + f32(top_past)), -1)
    low_home = across(b16(f32(pair_hf[head:]) + f32(low_far)))
    d_top = f32(pair_hn[:head]) + f32(top_home) + f32(top_back)
    d_low = f32(pair_hn[head:]) + f32(low_near) + f32(low_home)
    d_tokens = b16(jnp.concatenate([d_top, d_low], axis=0))[None]

    hidden = b16(f32(jnp.stack([hid_hn, hid_hf])) + f32(hid_back))
    hidden = relative(hidden.reshape(4, row_count, quarter), side, core)
    grad_gate, grad_up = weight_pass(
        home_near + home_far + past_near + past_far, (vg_hn, vg_hf, vg_pn, vg_pf)
    )
    return (d_tokens, hidden, grad_gate[None], grad_up[None])


def solution(mesh):
    in_specs = (
        P("dp", "expert", None),
        P("dp", "expert", None),
        P(),
        P(),
        P("expert", None, "dp"),
        P("expert", None, "dp"),
    )
    out_specs = (
        P("dp", "expert", None),
        P(None, "expert", "dp"),
        P("expert", None, "dp"),
        P("expert", None, "dp"),
    )
    return jax.shard_map(
        per_device, mesh=mesh, in_specs=in_specs, out_specs=out_specs, check_vma=False
    )
```

time: 207 us -> 138 us (0.67)
  waiting for transfers between devices: 137 us -> 64.7 us
  matrix products: 29.1 us -> 0 us
  Pallas kernels: 0 us -> 20.6 us
  between operations: 14.2 us -> 1.1 us
  starting transfers between devices: 11.3 us -> 23.5 us
  local copies, waits for them, and re-layouts: 7.95 us -> 18.5 us
    ppermute x4 -> x27, waiting for transfers between devices: 116 us -> 64.7 us  [the longest x7 35 us: across(): return lax.ppermute(value, 'dp', pairs)]
    dot_general x12 -> x0, matrix products: 29.1 us -> none  [the longest x8 18.3 us: contract(): lax.dot_general(left, right, (((left_axis,), (right_axis,)), ((), ())), p...]
    pallas_call x0 -> x5, Pallas kernels: none -> 20.6 us  [the longest x4 12.2 us: block_pass(): pl.pallas_call(functools.partial(block_body, len(pieces), column_step(wid...]
    ppermute x4 -> x27, starting transfers between devices: 7.61 us -> 23.5 us  [the longest x8 12.9 us: shifted(): return lax.ppermute(value, 'expert', pairs)]
    all_gather x1 -> x0, waiting for transfers between devices: 13.8 us -> none  [to_groups(): gathered = lax.all_gather(tile_rows, 'dp', axis=0, tiled=True)]
    all_to_all x1 -> x0, waiting for transfers between devices: 7.22 us -> none  [to_groups(): lax.all_to_all(tile_grads, 'dp', split_axis=2, concat_axis=0, tiled=True)]
    slice x0 -> x12, local copies, waits for them, and re-layouts: none -> 6.96 us  [the longest x2 3.73 us: per_device(): top, low = (tile[:head], tile[head:])]
    all_to_all x1 -> x0, starting transfers between devices: 3.42 us -> none  [to_groups(): lax.all_to_all(tile_grads, 'dp', split_axis=2, concat_axis=0, tiled=True)]
  transfers between devices with their start and end apart: 7 -> 27, of which waited for: 6 -> 7; matrix products, arithmetic and copies ran while one was open for 14% -> 13% of each run, Pallas kernels for 0% -> 15%
where the time goes in v1:
time: 138 us
  waiting for transfers between devices  64.7 us (47%)
  starting transfers between devices  23.5 us (17%)
  Pallas kernels  20.6 us (15%)
  local copies, waits for them, and re-layouts  18.5 us (13%)
  other arithmetic  9.14 us (7%)
    ppermute x7, waiting for transfers between devices, across(): return lax.ppermute(value, 'dp', pairs)  35 us
    ppermute x8, waiting for transfers between devices, shifted(): return lax.ppermute(value, 'expert', pairs)  28.4 us
    ppermute x8, starting transfers between devices, shifted(): return lax.ppermute(value, 'expert', pairs)  12.9 us
    pallas_call x4, Pallas kernels, block_pass(): pl.pallas_call(functools.partial(block_body, len(pieces), column_step(wid...  12.2 us
    pallas_call x1, Pallas kernels, weight_pass(): pl.pallas_call(functools.partial(weight_body, len(pieces), len(grads)), g...  8.4 us
    ppermute x7, starting transfers between devices, across(): return lax.ppermute(value, 'dp', pairs)  7.88 us
    unnamed x30, local copies, waits for them, and re-layouts  5.93 us
    convert_element_type x7, other arithmetic, b16(): return value.astype(jnp.bfloat16)  5.07 us
  transfers between devices with their start and end apart: 27, of which 7 were waited for; matrix products, arithmetic and copies ran while one was open for 13% of the time, Pallas kernels for 15%

profile of v1, /device:TPU:0, one launch (start us, length us, event | category | flops | bytes accessed | tf_op | source)
XLA Modules:
  0.0 137.6 jit_solution(12335768964130206399)
XLA Ops:
  0.7 2.0 %slice_bitcast_fusion = bf16[80,3584]{1,0:T(8,128)(2,1)} fusion(bf16[1,128,3584]{2,1,0:T(8,128)(2,1)} %param.22), kind=kLoop, calls=%fused_computation.16 | loop fusion | bytes 1146880 | tf_op jit(solution)/shard_map/slice | solution.py:165
  2.7 2.9 %collective-permute-start.10 = (bf16[80,3584]{1,0:T(8,128)(2,1)}, bf16[80,3584]{1,0:T(8,128)(2,1)}, u32[]{:S(2)}, u32[]{:S(2)}) collective-permute-start(bf16[80,3584]{1,0:T(8,128)(2,1)} %slice_bitcast_fusion), channel_id=1, source_target_pairs={{0,1},{1,2},{2,3},{3,4},{4,5},{5,6},{6,7},{7,0},{8,9},{9,10},{10,1... | collective-permute-start | bytes 1720328 | tf_op jit(solution)/shard_map/ppermute | solution.py:17
  5.6 1.5 %collective-permute-start.4 = (bf16[80,3584]{1,0:T(8,128)(2,1)}, bf16[80,3584]{1,0:T(8,128)(2,1)S(1)}, u32[]{:S(2)}, u32[]{:S(2)}) collective-permute-start(bf16[80,3584]{1,0:T(8,128)(2,1)} %slice_bitcast_fusion), channel_id=1, source_target_pairs={{0,16},{8,24},{16,0},{24,8},{1,17},{9,25},{17,1},{25,9},{2,18},{10... | collective-permute-start | bytes 1720328 | tf_op jit(solution)/shard_map/ppermute | solution.py:23
  7.1 1.7 %slice_bitcast_fusion.1 = bf16[48,3584]{1,0:T(8,128)(2,1)} fusion(bf16[1,128,3584]{2,1,0:T(8,128)(2,1)} %param.22), kind=kLoop, calls=%fused_computation.19 | loop fusion | bytes 688128 | tf_op jit(solution)/shard_map/slice | solution.py:165
  9.4 1.5 %collective-permute-start.11 = (bf16[48,3584]{1,0:T(8,128)(2,1)}, bf16[48,3584]{1,0:T(8,128)(2,1)}, u32[]{:S(2)}, u32[]{:S(2)}) collective-permute-start(bf16[48,3584]{1,0:T(8,128)(2,1)} %slice_bitcast_fusion.1), channel_id=1, source_target_pairs={{0,1},{1,2},{2,3},{3,4},{4,5},{5,6},{6,7},{7,0},{8,9},{9,10},{10,1... | collective-permute-start | bytes 1032200 | tf_op jit(solution)/shard_map/ppermute | solution.py:17
  11.0 1.6 %collective-permute-start.1 = (bf16[128,512]{1,0:T(8,128)(2,1)S(1)}, bf16[128,512]{1,0:T(8,128)(2,1)S(1)}, u32[]{:S(2)}, u32[]{:S(2)}) collective-permute-start(bf16[128,512]{1,0:T(8,128)(2,1)S(1)} %get-tuple-element.81), channel_id=1, source_target_pairs={{0,16},{8,24},{16,0},{24,8},{1,17},{9,25},{17,1},{25,9},{2,18},{10... | collective-permute-start | bytes 393224 | tf_op jit(solution)/shard_map/ppermute | solution.py:23
  12.8 0.8 fusion.8
  13.6 0.6 gather_fusion.2
  14.8 0.6 gather_fusion.3
  15.9 14.6 %collective-permute-done.1 = bf16[128,512]{1,0:T(8,128)(2,1)S(1)} collective-permute-done((bf16[128,512]{1,0:T(8,128)(2,1)S(1)}, bf16[128,512]{1,0:T(8,128)(2,1)S(1)}, u32[]{:S(2)}, u32[]{:S(2)}) %collective-permute-start.1) | collective-permute-done | bytes 131104 | tf_op jit(solution)/shard_map/ppermute | solution.py:23
  30.6 1.3 collective-permute-done.2
  32.0 1.5 %collective-permute-start.16 = (bf16[80,3584]{1,0:T(8,128)(2,1)}, bf16[80,3584]{1,0:T(8,128)(2,1)}, u32[]{:S(2)}, u32[]{:S(2)}) collective-permute-start(bf16[80,3584]{1,0:T(8,128)(2,1)} %collective-permute-done.10.refs_0_.refs_6_), channel_id=1, source_target_pairs={{0,16},{8,24},{16,0},{24,8},{1,17},{9,25},{17,1},{25,9},{2,18},{10... | collective-permute-start | bytes 1720328 | tf_op jit(solution)/shard_map/ppermute | solution.py:23
  33.6 1.5 %collective-permute-start.17 = (bf16[48,3584]{1,0:T(8,128)(2,1)S(1)}, bf16[48,3584]{1,0:T(8,128)(2,1)}, u32[]{:S(2)}, u32[]{:S(2)}) collective-permute-start(bf16[48,3584]{1,0:T(8,128)(2,1)S(1)} %collective-permute-done.5.refs_1_.refs_3_), channel_id=1, source_target_pairs={{0,1},{1,2},{2,3},{3,4},{4,5},{5,6},{6,7},{7,0},{8,9},{9,10},{10,1... | collective-permute-start | bytes 1032200 | tf_op jit(solution)/shard_map/ppermute | solution.py:17
  35.2 0.7 copy.19
  35.9 1.5 %collective-permute-start.14 = (bf16[2,256,256]{2,1,0:T(8,128)(2,1)}, bf16[2,256,256]{2,1,0:T(8,128)(2,1)}, u32[]{:S(2)}, u32[]{:S(2)}) collective-permute-start(bf16[2,256,256]{2,1,0:T(8,128)(2,1)} %bitcast.14), channel_id=1, source_target_pairs={{0,1},{1,2},{2,3},{3,4},{4,5},{5,6},{6,7},{7,0},{8,9},{9,10},{10,1... | collective-permute-start | bytes 786440 | tf_op jit(solution)/shard_map/ppermute | solution.py:17
  38.0 0.9 fusion.5
  38.9 13.1 %collective-permute-done.14 = bf16[2,256,256]{2,1,0:T(8,128)(2,1)} collective-permute-done((bf16[2,256,256]{2,1,0:T(8,128)(2,1)}, bf16[2,256,256]{2,1,0:T(8,128)(2,1)}, u32[]{:S(2)}, u32[]{:S(2)}) %collective-permute-start.14) | collective-permute-done | bytes 262176 | tf_op jit(solution)/shard_map/ppermute | solution.py:17
  52.6 1.0 slice_bitcast_fusion.3
  54.2 1.5 %copy-done.4 = bf16[1,3584,256]{2,1,0:T(8,128)(2,1)S(1)} copy-done((bf16[1,3584,256]{2,1,0:T(8,128)(2,1)S(1)}, bf16[1,3584,256]{2,1,0:T(8,128)(2,1)}, u32[]{:S(2)}) %copy-start.4) | copy-done | bytes 1835032
  55.7 1.5 %copy-done.5 = bf16[1,3584,256]{2,1,0:T(8,128)(2,1)S(1)} copy-done((bf16[1,3584,256]{2,1,0:T(8,128)(2,1)S(1)}, bf16[1,3584,256]{2,1,0:T(8,128)(2,1)}, u32[]{:S(2)}) %copy-start.5) | copy-done | bytes 1835032
  57.2 2.2 %block_pass.4 = (bf16[256,256]{1,0:T(8,128)(2,1)S(1)}, bf16[256,512]{1,0:T(8,128)(2,1)S(1)}, bf16[256,3584]{1,0:T(8,128)(2,1)S(1)}) custom-call(bf16[128,3584]{1,0:T(8,128)(2,1)S(1)} %bitcast.36, bf16[128,3584]{1,0:T(8,128)(2,1)S(1)} %collective-permute-done.refs_1_, f32[256,1]{1,0:T(8,128)S(1)} %copy.17.refs_2_, bf16[256,256]{1,0:T(8,128)(2,1)S(1)} %bitcast.41, ...), custom_call_target="tpu_custom_call" | custom-call | flops 1879048192 | bytes 7340032 | tf_op jit(solution)/shard_map/block_pass/pallas_call | solution.py:83
  60.5 3.3 %block_pass.5 = (bf16[256,256]{1,0:T(8,128)(2,1)S(1)}, bf16[256,512]{1,0:T(8,128)(2,1)S(1)}, bf16[256,3584]{1,0:T(8,128)(2,1)S(1)}) custom-call(bf16[80,3584]{1,0:T(8,128)(2,1)S(1)} %copy-done.9, bf16[48,3584]{1,0:T(8,128)(2,1)S(1)} %collective-permute-done.5.refs_1_.refs_3_, bf16[80,3584]{1,0:T(8,128)(2,1)} %collective-permute-done.6.refs_2_.refs_4_, ...), custom_call_target="tpu_custom_call" | custom-call | flops 1879048192 | bytes 7340032 | tf_op jit(solution)/shard_map/block_pass/pallas_call | solution.py:83
  63.7 1.0 slice.130
  65.0 3.4 %block_pass.6 = (bf16[256,256]{1,0:T(8,128)(2,1)S(1)}, bf16[256,512]{1,0:T(8,128)(2,1)S(1)}, bf16[256,3584]{1,0:T(8,128)(2,1)S(1)}) custom-call(bf16[80,3584]{1,0:T(8,128)(2,1)} %collective-permute-done.10.refs_0_.refs_6_, bf16[48,3584]{1,0:T(8,128)(2,1)} %collective-permute-done.11.refs_1_.refs_7_, ...), custom_call_target="tpu_custom_call" | custom-call | flops 1879048192 | bytes 7340032 | tf_op jit(solution)/shard_map/block_pass/pallas_call | solution.py:83
  68.4 1.3 copy-done
  69.7 1.1 slice.135
  71.0 3.4 %block_pass.7 = (bf16[256,256]{1,0:T(8,128)(2,1)S(1)}, bf16[256,512]{1,0:T(8,128)(2,1)S(1)}, bf16[256,3584]{1,0:T(8,128)(2,1)S(1)}) custom-call(bf16[80,3584]{1,0:T(8,128)(2,1)} %collective-permute-done.16.refs_0_.refs_10_, bf16[48,3584]{1,0:T(8,128)(2,1)} %collective-permute-done.17.refs_1_.refs_11_, ...), custom_call_target="tpu_custom_call" | custom-call | flops 1879048192 | bytes 7340032 | tf_op jit(solution)/shard_map/block_pass/pallas_call | solution.py:83
  74.4 1.2 copy-done.1
  75.6 1.0 slice.140
  76.9 0.7 collective-permute-start.26
  77.6 8.4 %weight_pass.1 = (bf16[3584,256]{1,0:T(8,128)(2,1)}, bf16[3584,256]{1,0:T(8,128)(2,1)}) custom-call(bf16[128,3584]{1,0:T(8,128)(2,1)S(1)} %bitcast.37, bf16[128,3584]{1,0:T(8,128)(2,1)S(1)} %copy-done.7, bf16[80,3584]{1,0:T(8,128)(2,1)S(1)} %copy-done.9, bf16[48,3584]{1,0:T(8,128)(2,1)S(1)} %collective-permute-done.5.refs_1_.refs_3_, ...), custom_call_target="tpu_custom_call" | custom-call | flops 3758096384 | bytes 11010048 | tf_op jit(solution)/shard_map/weight_pass/pallas_call | solution.py:117
  86.3 0.6 gather_fusion.4
  86.9 0.6 gather_fusion.5
  87.4 0.7 broadcast_select_fusion.1
  88.2 1.8 %add_convert_fusion.1 = bf16[128,3584]{1,0:T(8,128)(2,1)S(1)} fusion(bf16[128,3584]{1,0:T(8,128)(2,1)} %collective-permute-done.15, bf16[256,3584]{1,0:T(8,128)(2,1)} %copy-done), kind=kLoop, calls=%fused_computation.7 | loop fusion | flops 1835008 | bytes 2752512 | tf_op jit(solution)/shard_map/convert_element_type | solution.py:152
  90.0 2.7 %collective-permute-start.23 = (bf16[48,3584]{1,0:T(8,128)(2,1)S(1)}, bf16[48,3584]{1,0:T(8,128)(2,1)S(1)}, u32[]{:S(2)}, u32[]{:S(2)}) collective-permute-start(bf16[48,3584]{1,0:T(8,128)(2,1)S(1)} %slice.169), channel_id=1, source_target_pairs={{0,7},{1,0},{2,1},{3,2},{4,3},{5,4},{6,5},{7,6},{8,15},{9,8},{10,9... | collective-permute-start | bytes 1032200 | tf_op jit(solution)/shard_map/ppermute | solution.py:17
  92.7 1.4 %add_convert_fusion = bf16[128,3584]{1,0:T(8,128)(2,1)S(1)} fusion(bf16[128,3584]{1,0:T(8,128)(2,1)} %collective-permute-done.20, bf16[256,3584]{1,0:T(8,128)(2,1)S(1)} %copy-done.2), kind=kLoop, calls=%fused_computation.6 | loop fusion | flops 1835008 | bytes 2752512 | tf_op jit(solution)/shard_map/convert_element_type | solution.py:152
  94.1 0.6 collective-permute-start.24
  94.7 1.4 %add_convert_fusion.2 = bf16[128,3584]{1,0:T(8,128)(2,1)S(1)} fusion(bf16[128,3584]{1,0:T(8,128)(2,1)} %collective-permute-done.8, bf16[256,3584]{1,0:T(8,128)(2,1)S(1)} %get-tuple-element.60), kind=kLoop, calls=%fused_computation.8 | loop fusion | flops 1835008 | bytes 2752512 | tf_op jit(solution)/shard_map/convert_element_type | solution.py:152
  96.2 0.6 collective-permute-start.9
  96.8 1.6 %collective-permute-start.21 = (bf16[80,3584]{1,0:T(8,128)(2,1)S(1)}, bf16[80,3584]{1,0:T(8,128)(2,1)S(1)}, u32[]{:S(2)}, u32[]{:S(2)}) collective-permute-start(bf16[80,3584]{1,0:T(8,128)(2,1)S(1)} %slice.167), channel_id=1, source_target_pairs={{0,16},{8,24},{16,0},{24,8},{1,17},{9,25},{17,1},{25,9},{2,18},{10... | collective-permute-start | bytes 1720328 | tf_op jit(solution)/shard_map/ppermute | solution.py:23
  98.4 9.2 %collective-permute-done.24 = bf16[48,3584]{1,0:T(8,128)(2,1)S(1)} collective-permute-done((bf16[48,3584]{1,0:T(8,128)(2,1)S(1)}, bf16[48,3584]{1,0:T(8,128)(2,1)S(1)}, u32[]{:S(2)}, u32[]{:S(2)}) %collective-permute-start.24) | collective-permute-done | bytes 344096 | tf_op jit(solution)/shard_map/ppermute | solution.py:17
  107.6 0.6 collective-permute-start.25
  108.2 16.2 %collective-permute-done.21 = bf16[80,3584]{1,0:T(8,128)(2,1)S(1)} collective-permute-done((bf16[80,3584]{1,0:T(8,128)(2,1)S(1)}, bf16[80,3584]{1,0:T(8,128)(2,1)S(1)}, u32[]{:S(2)}, u32[]{:S(2)}) %collective-permute-start.21) | collective-permute-done | bytes 573472 | tf_op jit(solution)/shard_map/ppermute | solution.py:23
  124.6 1.4 %collective-permute-start.22 = (bf16[80,3584]{1,0:T(8,128)(2,1)S(1)}, bf16[80,3584]{1,0:T(8,128)(2,1)S(1)}, u32[]{:S(2)}, u32[]{:S(2)}) collective-permute-start(bf16[80,3584]{1,0:T(8,128)(2,1)S(1)} %add_convert_fusion.5), channel_id=1, source_target_pairs={{0,7},{1,0},{2,1},{3,2},{4,3},{5,4},{6,5},{7,6},{8,15},{9,8},{10,9... | collective-permute-start | bytes 1720328 | tf_op jit(solution)/shard_map/ppermute | solution.py:17
  126.0 4.2 %collective-permute-done.25 = bf16[48,3584]{1,0:T(8,128)(2,1)S(1)} collective-permute-done((bf16[48,3584]{1,0:T(8,128)(2,1)S(1)}, bf16[48,3584]{1,0:T(8,128)(2,1)S(1)}, u32[]{:S(2)}, u32[]{:S(2)}) %collective-permute-start.25) | collective-permute-done | bytes 344096 | tf_op jit(solution)/shard_map/ppermute | solution.py:23
  130.3 6.0 %collective-permute-done.22 = bf16[80,3584]{1,0:T(8,128)(2,1)S(1)} collective-permute-done((bf16[80,3584]{1,0:T(8,128)(2,1)S(1)}, bf16[80,3584]{1,0:T(8,128)(2,1)S(1)}, u32[]{:S(2)}, u32[]{:S(2)}) %collective-permute-start.22) | collective-permute-done | bytes 573472 | tf_op jit(solution)/shard_map/ppermute | solution.py:17
  136.6 1.0 pad_maximum_fusion
  (89 shorter events, 6.7 us)
Async XLA Ops:
  0.6 11.9 %copy-start.14 = (s32[4]{0:T(128)S(1)}, s32[4]{0:T(128)}, u32[]{:S(2)}) copy-start(s32[4]{0:T(128)} %constant.198) | copy-start | bytes 52
  0.6 14.1 %copy-start.13 = (s32[4]{0:T(128)S(1)}, s32[4]{0:T(128)}, u32[]{:S(2)}) copy-start(s32[4]{0:T(128)} %constant.199) | copy-start | bytes 52
  0.7 31.2 %copy-start.3 = (bf16[1,128,3584]{2,1,0:T(8,128)(2,1)S(1)}, bf16[1,128,3584]{2,1,0:T(8,128)(2,1)}, u32[]{:S(2)}) copy-start(bf16[1,128,3584]{2,1,0:T(8,128)(2,1)} %param.22) | copy-start | bytes 2752516
  0.7 10.3 %copy-start.11 = (bf16[1,128,1024]{2,1,0:T(8,128)(2,1)S(1)}, bf16[1,128,1024]{2,1,0:T(8,128)(2,1)}, u32[]{:S(2)}) copy-start(bf16[1,128,1024]{2,1,0:T(8,128)(2,1)} %param.23) | copy-start | bytes 786436
  0.7 11.9 %copy-start.12 = (s32[4,8]{1,0:T(4,128)S(1)}, s32[4,8]{1,0:T(4,128)}, u32[]{:S(2)}) copy-start(s32[4,8]{1,0:T(4,128)} %param.25) | copy-start | bytes 388
  2.7 29.4 %collective-permute-start.10 = (bf16[80,3584]{1,0:T(8,128)(2,1)}, bf16[80,3584]{1,0:T(8,128)(2,1)}, u32[]{:S(2)}, u32[]{:S(2)}) collective-permute-start(bf16[80,3584]{1,0:T(8,128)(2,1)} %slice_bitcast_fusion), channel_id=1, source_target_pairs={{0,1},{1,2},{2,3},{3,4},{4,5},{5,6},{6,7},{7,0},{8,9},{9,10},{10,1... | collective-permute-start | bytes 1720328 | tf_op jit(solution)/shard_map/ppermute | solution.py:17
  5.6 31.8 %collective-permute-start.4 = (bf16[80,3584]{1,0:T(8,128)(2,1)}, bf16[80,3584]{1,0:T(8,128)(2,1)S(1)}, u32[]{:S(2)}, u32[]{:S(2)}) collective-permute-start(bf16[80,3584]{1,0:T(8,128)(2,1)} %slice_bitcast_fusion), channel_id=1, source_target_pairs={{0,16},{8,24},{16,0},{24,8},{1,17},{9,25},{17,1},{25,9},{2,18},{10... | collective-permute-start | bytes 1720328 | tf_op jit(solution)/shard_map/ppermute | solution.py:23
  8.9 24.7 %collective-permute-start.5 = (bf16[48,3584]{1,0:T(8,128)(2,1)}, bf16[48,3584]{1,0:T(8,128)(2,1)S(1)}, u32[]{:S(2)}, u32[]{:S(2)}) collective-permute-start(bf16[48,3584]{1,0:T(8,128)(2,1)} %slice_bitcast_fusion.1), channel_id=1, source_target_pairs={{0,16},{8,24},{16,0},{24,8},{1,17},{9,25},{17,1},{25,9},{2,18},{10... | collective-permute-start | bytes 1032200 | tf_op jit(solution)/shard_map/ppermute | solution.py:23
  9.4 26.5 %collective-permute-start.11 = (bf16[48,3584]{1,0:T(8,128)(2,1)}, bf16[48,3584]{1,0:T(8,128)(2,1)}, u32[]{:S(2)}, u32[]{:S(2)}) collective-permute-start(bf16[48,3584]{1,0:T(8,128)(2,1)} %slice_bitcast_fusion.1), channel_id=1, source_target_pairs={{0,1},{1,2},{2,3},{3,4},{4,5},{5,6},{6,7},{7,0},{8,9},{9,10},{10,1... | collective-permute-start | bytes 1032200 | tf_op jit(solution)/shard_map/ppermute | solution.py:17
  11.0 19.5 %collective-permute-start.1 = (bf16[128,512]{1,0:T(8,128)(2,1)S(1)}, bf16[128,512]{1,0:T(8,128)(2,1)S(1)}, u32[]{:S(2)}, u32[]{:S(2)}) collective-permute-start(bf16[128,512]{1,0:T(8,128)(2,1)S(1)} %get-tuple-element.81), channel_id=1, source_target_pairs={{0,16},{8,24},{16,0},{24,8},{1,17},{9,25},{17,1},{25,9},{2,18},{10... | collective-permute-start | bytes 393224 | tf_op jit(solution)/shard_map/ppermute | solution.py:23
  30.5 1.4 %collective-permute-start.2 = (bf16[2,128,256]{2,1,0:T(8,128)(2,1)S(1)}, bf16[2,128,256]{2,1,0:T(8,128)(2,1)S(1)}, u32[]{:S(2)}, u32[]{:S(2)}) collective-permute-start(bf16[2,128,256]{2,1,0:T(8,128)(2,1)S(1)} %get-tuple-element.80), channel_id=1, source_target_pairs={{0,8},{8,0},{16,24},{24,16},{1,9},{9,1},{17,25},{25,17},{2,10},{10... | collective-permute-start | bytes 393224 | tf_op jit(solution)/shard_map/ppermute | solution.py:29
  31.9 5.7 %copy-start.10 = (bf16[2,128,256]{2,1,0:T(8,128)(2,1)}, bf16[2,128,256]{2,1,0:T(8,128)(2,1)S(1)}, u32[]{:S(2)}) copy-start(bf16[2,128,256]{2,1,0:T(8,128)(2,1)S(1)} %collective-permute-done.2) | copy-start | bytes 393220
  31.9 21.7 %collective-permute-start = (bf16[128,3584]{1,0:T(8,128)(2,1)S(1)}, bf16[128,3584]{1,0:T(8,128)(2,1)S(1)}, u32[]{:S(2)}, u32[]{:S(2)}) collective-permute-start(bf16[128,3584]{1,0:T(8,128)(2,1)S(1)} %bitcast.35), channel_id=1, source_target_pairs={{0,8},{8,0},{16,24},{24,16},{1,9},{9,1},{17,25},{25,17},{2,10},{10... | collective-permute-start | bytes 2752520 | tf_op jit(solution)/shard_map/ppermute | solution.py:29
  32.0 20.5 %collective-permute-start.16 = (bf16[80,3584]{1,0:T(8,128)(2,1)}, bf16[80,3584]{1,0:T(8,128)(2,1)}, u32[]{:S(2)}, u32[]{:S(2)}) collective-permute-start(bf16[80,3584]{1,0:T(8,128)(2,1)} %collective-permute-done.10.refs_0_.refs_6_), channel_id=1, source_target_pairs={{0,16},{8,24},{16,0},{24,8},{1,17},{9,25},{17,1},{25,9},{2,18},{10... | collective-permute-start | bytes 1720328 | tf_op jit(solution)/shard_map/ppermute | solution.py:23
  33.6 18.5 %collective-permute-start.17 = (bf16[48,3584]{1,0:T(8,128)(2,1)S(1)}, bf16[48,3584]{1,0:T(8,128)(2,1)}, u32[]{:S(2)}, u32[]{:S(2)}) collective-permute-start(bf16[48,3584]{1,0:T(8,128)(2,1)S(1)} %collective-permute-done.5.refs_1_.refs_3_), channel_id=1, source_target_pairs={{0,1},{1,2},{2,3},{3,4},{4,5},{5,6},{6,7},{7,0},{8,9},{9,10},{10,1... | collective-permute-start | bytes 1032200 | tf_op jit(solution)/shard_map/ppermute | solution.py:17
  35.9 16.2 %collective-permute-start.14 = (bf16[2,256,256]{2,1,0:T(8,128)(2,1)}, bf16[2,256,256]{2,1,0:T(8,128)(2,1)}, u32[]{:S(2)}, u32[]{:S(2)}) collective-permute-start(bf16[2,256,256]{2,1,0:T(8,128)(2,1)} %bitcast.14), channel_id=1, source_target_pairs={{0,1},{1,2},{2,3},{3,4},{4,5},{5,6},{6,7},{7,0},{8,9},{9,10},{10,1... | collective-permute-start | bytes 786440 | tf_op jit(solution)/shard_map/ppermute | solution.py:17
  37.4 22.0 %copy-start.8 = (bf16[80,3584]{1,0:T(8,128)(2,1)}, bf16[80,3584]{1,0:T(8,128)(2,1)S(1)}, u32[]{:S(2)}) copy-start(bf16[80,3584]{1,0:T(8,128)(2,1)S(1)} %collective-permute-done.4.refs_0_.refs_2_) | copy-start | bytes 1720324
  37.4 22.4 %collective-permute-start.6 = (bf16[80,3584]{1,0:T(8,128)(2,1)S(1)}, bf16[80,3584]{1,0:T(8,128)(2,1)}, u32[]{:S(2)}, u32[]{:S(2)}) collective-permute-start(bf16[80,3584]{1,0:T(8,128)(2,1)S(1)} %collective-permute-done.4.refs_0_.refs_2_), channel_id=1, source_target_pairs={{0,8},{8,0},{16,24},{24,16},{1,9},{9,1},{17,25},{25,17},{2,10},{10... | collective-permute-start | bytes 1720328 | tf_op jit(solution)/shard_map/ppermute | solution.py:29
  52.0 7.4 %collective-permute-start.7 = (bf16[48,3584]{1,0:T(8,128)(2,1)S(1)}, bf16[48,3584]{1,0:T(8,128)(2,1)S(1)}, u32[]{:S(2)}, u32[]{:S(2)}) collective-permute-start(bf16[48,3584]{1,0:T(8,128)(2,1)S(1)} %collective-permute-done.5.refs_1_.refs_3_), channel_id=1, source_target_pairs={{0,8},{8,0},{16,24},{24,16},{1,9},{9,1},{17,25},{25,17},{2,10},{10... | collective-permute-start | bytes 1032200 | tf_op jit(solution)/shard_map/ppermute | solution.py:29
  52.1 12.9 %collective-permute-start.12 = (bf16[80,3584]{1,0:T(8,128)(2,1)}, bf16[80,3584]{1,0:T(8,128)(2,1)S(1)}, u32[]{:S(2)}, u32[]{:S(2)}) collective-permute-start(bf16[80,3584]{1,0:T(8,128)(2,1)} %collective-permute-done.10.refs_0_.refs_6_), channel_id=1, source_target_pairs={{0,8},{8,0},{16,24},{24,16},{1,9},{9,1},{17,25},{25,17},{2,10},{10... | collective-permute-start | bytes 1720328 | tf_op jit(solution)/shard_map/ppermute | solution.py:29
  52.6 18.4 %collective-permute-start.18 = (bf16[80,3584]{1,0:T(8,128)(2,1)}, bf16[80,3584]{1,0:T(8,128)(2,1)S(1)}, u32[]{:S(2)}, u32[]{:S(2)}) collective-permute-start(bf16[80,3584]{1,0:T(8,128)(2,1)} %collective-permute-done.16.refs_0_.refs_10_), channel_id=1, source_target_pairs={{0,8},{8,0},{16,24},{24,16},{1,9},{9,1},{17,25},{25,17},{2,10},{10... | collective-permute-start | bytes 1720328 | tf_op jit(solution)/shard_map/ppermute | solution.py:29
  53.6 5.8 %copy-start.6 = (bf16[128,3584]{1,0:T(8,128)(2,1)}, bf16[128,3584]{1,0:T(8,128)(2,1)S(1)}, u32[]{:S(2)}) copy-start(bf16[128,3584]{1,0:T(8,128)(2,1)S(1)} %collective-permute-done.refs_1_) | copy-start | bytes 2752516
  53.6 11.1 %collective-permute-start.13 = (bf16[48,3584]{1,0:T(8,128)(2,1)}, bf16[48,3584]{1,0:T(8,128)(2,1)S(1)}, u32[]{:S(2)}, u32[]{:S(2)}) collective-permute-start(bf16[48,3584]{1,0:T(8,128)(2,1)} %collective-permute-done.11.refs_1_.refs_7_), channel_id=1, source_target_pairs={{0,8},{8,0},{16,24},{24,16},{1,9},{9,1},{17,25},{25,17},{2,10},{10... | collective-permute-start | bytes 1032200 | tf_op jit(solution)/shard_map/ppermute | solution.py:29
  54.2 1.5 %copy-start.4 = (bf16[1,3584,256]{2,1,0:T(8,128)(2,1)S(1)}, bf16[1,3584,256]{2,1,0:T(8,128)(2,1)}, u32[]{:S(2)}) copy-start(bf16[1,3584,256]{2,1,0:T(8,128)(2,1)} %param.26) | copy-start | bytes 5505028
  55.7 1.5 %copy-start.5 = (bf16[1,3584,256]{2,1,0:T(8,128)(2,1)S(1)}, bf16[1,3584,256]{2,1,0:T(8,128)(2,1)}, u32[]{:S(2)}) copy-start(bf16[1,3584,256]{2,1,0:T(8,128)(2,1)} %param.27) | copy-start | bytes 5505028
  59.4 1.1 copy-start.9
  59.5 11.5 %collective-permute-start.19 = (bf16[48,3584]{1,0:T(8,128)(2,1)}, bf16[48,3584]{1,0:T(8,128)(2,1)S(1)}, u32[]{:S(2)}, u32[]{:S(2)}) collective-permute-start(bf16[48,3584]{1,0:T(8,128)(2,1)} %collective-permute-done.17.refs_1_.refs_11_), channel_id=1, source_target_pairs={{0,8},{8,0},{16,24},{24,16},{1,9},{9,1},{17,25},{25,17},{2,10},{10... | collective-permute-start | bytes 1032200 | tf_op jit(solution)/shard_map/ppermute | solution.py:29
  59.8 26.1 %collective-permute-start.3 = (bf16[128,3584]{1,0:T(8,128)(2,1)S(1)}, bf16[128,3584]{1,0:T(8,128)(2,1)S(1)}, u32[]{:S(2)}, u32[]{:S(2)}) collective-permute-start(bf16[128,3584]{1,0:T(8,128)(2,1)S(1)} %slice.121), channel_id=1, source_target_pairs={{0,8},{8,0},{16,24},{24,16},{1,9},{9,1},{17,25},{25,17},{2,10},{10... | collective-permute-start | bytes 2752520 | tf_op jit(solution)/shard_map/ppermute | solution.py:29
  64.7 30.0 %collective-permute-start.8 = (bf16[128,3584]{1,0:T(8,128)(2,1)}, bf16[128,3584]{1,0:T(8,128)(2,1)}, u32[]{:S(2)}, u32[]{:S(2)}) collective-permute-start(bf16[128,3584]{1,0:T(8,128)(2,1)} %slice.130), channel_id=1, source_target_pairs={{0,8},{8,0},{16,24},{24,16},{1,9},{9,1},{17,25},{25,17},{2,10},{10... | collective-permute-start | bytes 2752520 | tf_op jit(solution)/shard_map/ppermute | solution.py:29
  68.4 1.3 copy-start
  70.7 17.4 %collective-permute-start.15 = (bf16[128,3584]{1,0:T(8,128)(2,1)}, bf16[128,3584]{1,0:T(8,128)(2,1)}, u32[]{:S(2)}, u32[]{:S(2)}) collective-permute-start(bf16[128,3584]{1,0:T(8,128)(2,1)} %slice.135), channel_id=1, source_target_pairs={{0,8},{8,0},{16,24},{24,16},{1,9},{9,1},{17,25},{25,17},{2,10},{10... | collective-permute-start | bytes 2752520 | tf_op jit(solution)/shard_map/ppermute | solution.py:29
  74.4 1.2 copy-start.1
  74.4 3.2 %copy-start.7 = (bf16[128,3584]{1,0:T(8,128)(2,1)S(1)}, bf16[128,3584]{1,0:T(8,128)(2,1)}, u32[]{:S(2)}) copy-start(bf16[128,3584]{1,0:T(8,128)(2,1)} %copy-done.6) | copy-start | bytes 2752516
  76.6 16.1 %collective-permute-start.20 = (bf16[128,3584]{1,0:T(8,128)(2,1)}, bf16[128,3584]{1,0:T(8,128)(2,1)}, u32[]{:S(2)}, u32[]{:S(2)}) collective-permute-start(bf16[128,3584]{1,0:T(8,128)(2,1)} %slice.140), channel_id=1, source_target_pairs={{0,8},{8,0},{16,24},{24,16},{1,9},{9,1},{17,25},{25,17},{2,10},{10... | collective-permute-start | bytes 2752520 | tf_op jit(solution)/shard_map/ppermute | solution.py:29
  76.9 9.3 %collective-permute-start.26 = (bf16[2,256,256]{2,1,0:T(8,128)(2,1)S(1)}, bf16[2,256,256]{2,1,0:T(8,128)(2,1)S(1)}, u32[]{:S(2)}, u32[]{:S(2)}) collective-permute-start(bf16[2,256,256]{2,1,0:T(8,128)(2,1)S(1)} %pad_maximum_fusion.2), channel_id=1, source_target_pairs={{0,7},{1,0},{2,1},{3,2},{4,3},{5,4},{6,5},{7,6},{8,15},{9,8},{10,9... | collective-permute-start | bytes 786440 | tf_op jit(solution)/shard_map/ppermute | solution.py:17
  88.2 4.5 %copy-start.2 = (bf16[256,3584]{1,0:T(8,128)(2,1)S(1)}, bf16[256,3584]{1,0:T(8,128)(2,1)}, u32[]{:S(2)}) copy-start(bf16[256,3584]{1,0:T(8,128)(2,1)} %copy-done.1) | copy-start | bytes 5505028
  90.0 36.0 %collective-permute-start.23 = (bf16[48,3584]{1,0:T(8,128)(2,1)S(1)}, bf16[48,3584]{1,0:T(8,128)(2,1)S(1)}, u32[]{:S(2)}, u32[]{:S(2)}) collective-permute-start(bf16[48,3584]{1,0:T(8,128)(2,1)S(1)} %slice.169), channel_id=1, source_target_pairs={{0,7},{1,0},{2,1},{3,2},{4,3},{5,4},{6,5},{7,6},{8,15},{9,8},{10,9... | collective-permute-start | bytes 1032200 | tf_op jit(solution)/shard_map/ppermute | solution.py:17
  94.1 13.4 %collective-permute-start.24 = (bf16[48,3584]{1,0:T(8,128)(2,1)S(1)}, bf16[48,3584]{1,0:T(8,128)(2,1)S(1)}, u32[]{:S(2)}, u32[]{:S(2)}) collective-permute-start(bf16[48,3584]{1,0:T(8,128)(2,1)S(1)} %slice.171), channel_id=1, source_target_pairs={{0,7},{1,0},{2,1},{3,2},{4,3},{5,4},{6,5},{7,6},{8,15},{9,8},{10,9... | collective-permute-start | bytes 1032200 | tf_op jit(solution)/shard_map/ppermute | solution.py:17
  96.2 34.2 %collective-permute-start.9 = (bf16[80,3584]{1,0:T(8,128)(2,1)S(1)}, bf16[80,3584]{1,0:T(8,128)(2,1)S(1)}, u32[]{:S(2)}, u32[]{:S(2)}) collective-permute-start(bf16[80,3584]{1,0:T(8,128)(2,1)S(1)} %slice.163), channel_id=1, source_target_pairs={{0,16},{8,24},{16,0},{24,8},{1,17},{9,25},{17,1},{25,9},{2,18},{10... | collective-permute-start | bytes 1720328 | tf_op jit(solution)/shard_map/ppermute | solution.py:23
  96.8 27.6 %collective-permute-start.21 = (bf16[80,3584]{1,0:T(8,128)(2,1)S(1)}, bf16[80,3584]{1,0:T(8,128)(2,1)S(1)}, u32[]{:S(2)}, u32[]{:S(2)}) collective-permute-start(bf16[80,3584]{1,0:T(8,128)(2,1)S(1)} %slice.167), channel_id=1, source_target_pairs={{0,16},{8,24},{16,0},{24,8},{1,17},{9,25},{17,1},{25,9},{2,18},{10... | collective-permute-start | bytes 1720328 | tf_op jit(solution)/shard_map/ppermute | solution.py:23
  107.6 22.6 %collective-permute-start.25 = (bf16[48,3584]{1,0:T(8,128)(2,1)S(1)}, bf16[48,3584]{1,0:T(8,128)(2,1)S(1)}, u32[]{:S(2)}, u32[]{:S(2)}) collective-permute-start(bf16[48,3584]{1,0:T(8,128)(2,1)S(1)} %add_convert_fusion.7), channel_id=1, source_target_pairs={{0,16},{8,24},{16,0},{24,8},{1,17},{9,25},{17,1},{25,9},{2,18},{10... | collective-permute-start | bytes 1032200 | tf_op jit(solution)/shard_map/ppermute | solution.py:23
  124.6 11.8 %collective-permute-start.22 = (bf16[80,3584]{1,0:T(8,128)(2,1)S(1)}, bf16[80,3584]{1,0:T(8,128)(2,1)S(1)}, u32[]{:S(2)}, u32[]{:S(2)}) collective-permute-start(bf16[80,3584]{1,0:T(8,128)(2,1)S(1)} %add_convert_fusion.5), channel_id=1, source_target_pairs={{0,7},{1,0},{2,1},{3,2},{4,3},{5,4},{6,5},{7,6},{8,15},{9,8},{10,9... | collective-permute-start | bytes 1720328 | tf_op jit(solution)/shard_map/ppermute | solution.py:17

commit v2 on v0

v2 whole, which is shorter than its diff:
```python
import functools

import jax
import jax.numpy as jnp
from jax import lax
from jax.experimental import pallas as pl
from jax.experimental.pallas import tpu as pltpu
from jax.sharding import PartitionSpec as P

TILE = 128
OUT_SHARE = 64
BACK_SHARE = (48, 80)
LIMIT = 28 * 2**20
COST = pl.CostEstimate(flops=10**12, bytes_accessed=10**9, transcendentals=0)


def shifted(value, steps):
    count = lax.axis_size("expert")
    pairs = [(source, (source + steps) % count) for source in range(count)]
    return lax.ppermute(value, "expert", pairs)


def across(value):
    count = lax.axis_size("dp")
    pairs = [(source, (source + count // 2) % count) for source in range(count)]
    return lax.ppermute(value, "dp", pairs)


def within(value):
    count = lax.axis_size("dp")
    pairs = [(source, source + 1 - 2 * (source % 2)) for source in range(count)]
    return lax.ppermute(value, "dp", pairs)


def after(values, *earlier):
    return lax.optimization_barrier((values, earlier))[0]


def f32(value):
    return value.astype(jnp.float32)


def b16(value):
    return value.astype(jnp.bfloat16)


def column_step(width):
    for step in (512, 256, 128):
        if width % step == 0:
            return step
    return width


def contract(left, right, left_axis, right_axis):
    return lax.dot_general(
        left, right, (((left_axis,), (right_axis,)), ((), ())), preferred_element_type=jnp.float32
    )


def joined(refs, columns):
    return jnp.concatenate([ref[:, columns] for ref in refs], axis=0)


def block_body(piece_count, grad_count, step, *refs):
    pieces, refs = refs[:piece_count], refs[piece_count:]
    grad_refs, refs = refs[:grad_count], refs[grad_count:]
    scale_ref, *panels = refs[:5]
    hidden_ref, own_ref, other_ref, *refs = refs[5:]
    *part_refs, values_ref, panels_ref, piece_sems, panel_sems = refs
    rows, width = values_ref.shape
    quarter = panels_ref.shape[2]
    chunks = width // step

    copies = []
    first = 0
    for index, piece in enumerate(pieces):
        target = values_ref.at[pl.ds(first, piece.shape[0]), :]
        copies.append(pltpu.make_async_copy(piece, target, piece_sems.at[index]))
        first += piece.shape[0]
    loads = []
    for chunk in range(chunks):
        columns = pl.ds(chunk * step, step)
        loads.append(
            [
                pltpu.make_async_copy(
                    panel.at[columns, :], panels_ref.at[which, columns, :], panel_sems.at[which, chunk]
                )
                for which, panel in enumerate(panels)
            ]
        )
    for copy in copies:
        copy.start()
    for load in loads:
        for copy in load:
            copy.start()
    for copy in copies:
        copy.wait()

    sums = [jnp.zeros((rows, quarter), jnp.float32) for _ in panels]
    for chunk in range(chunks):
        columns = pl.ds(chunk * step, step)
        for copy in loads[chunk]:
            copy.wait()
        values = values_ref[:, columns]
        sums = [
            total + contract(values, panels_ref[which, columns, :], 1, 0)
            for which, total in enumerate(sums)
        ]
    factor = scale_ref[...]
    grads = []
    for which, out_ref in enumerate((own_ref, other_ref)):
        gate_val, up_val = sums[2 * which : 2 * which + 2]
        columns = pl.ds(which * quarter, quarter)
        sigmoid_val = jax.nn.sigmoid(gate_val)
        activation = gate_val * sigmoid_val
        hidden_ref[:, columns] = b16(factor * activation * up_val)
        act_grad = factor * f32(joined(grad_refs, columns))
        up_grad = b16(act_grad * activation)
        gate_grad = b16(act_grad * up_val * sigmoid_val * (1.0 + gate_val * (1.0 - sigmoid_val)))
        out_ref[:, :quarter] = gate_grad
        out_ref[:, quarter:] = up_grad
        grads += [gate_grad, up_grad]
    for chunk in range(chunks):
        columns = pl.ds(chunk * step, step)
        part = b16(
            sum(
                contract(grad, panels_ref[which, columns, :], 1, 1)
                for which, grad in enumerate(grads)
            )
        )
        first = 0
        for part_ref in part_refs:
            part_ref[:, columns] = part[first : first + part_ref.shape[0]]
            first += part_ref.shape[0]


def block_pass(pieces, grads, scale, panels, part_rows):
    rows = sum(piece.shape[0] for piece in pieces)
    width, quarter = panels[0].shape
    step = column_step(width)
    wide = jax.ShapeDtypeStruct((rows, 2 * quarter), jnp.bfloat16)
    here, there = pl.BlockSpec(memory_space=pltpu.VMEM), pl.BlockSpec(memory_space=pl.ANY)
    hidden, own, other, *parts = pl.pallas_call(
        functools.partial(block_body, len(pieces), len(grads), step),
        out_shape=[wide] * 3
        + [jax.ShapeDtypeStruct((count, width), jnp.bfloat16) for count in part_rows],
        in_specs=[there] * len(pieces) + [here] * (len(grads) + 1) + [there] * 4,
        out_specs=[here] * (3 + len(part_rows)),
        scratch_shapes=[
            pltpu.VMEM((rows, width), jnp.bfloat16),
            pltpu.VMEM((4, width, quarter), jnp.bfloat16),
            pltpu.SemaphoreType.DMA((len(pieces),)),
            pltpu.SemaphoreType.DMA((4, width // step)),
        ],
        compiler_params=pltpu.CompilerParams(vmem_limit_bytes=LIMIT),
        cost_estimate=COST,
        name="block_pass",
    )(*pieces, *grads, scale, *panels)
    return hidden, own, other, parts


def weight_body(piece_count, grad_count, *refs):
    pieces = refs[:piece_count]
    grads = refs[piece_count : piece_count + grad_count]
    gate_ref, up_ref = refs[piece_count + grad_count :]
    quarter = gate_ref.shape[1]
    total = contract(joined(pieces, slice(None)), joined(grads, slice(None)), 0, 0)
    total = b16(total * (1.0 / TILE))
    gate_ref[...] = total[:, :quarter]
    up_ref[...] = total[:, quarter:]


def weight_pass(pieces, grads, width):
    quarter = grads[0].shape[1] // 2
    step = column_step(width)
    return pl.pallas_call(
        functools.partial(weight_body, len(pieces), len(grads)),
        grid=(width // step,),
        in_specs=[pl.BlockSpec((piece.shape[0], step), lambda i: (0, i)) for piece in pieces]
        + [pl.BlockSpec(grad.shape, lambda i: (0, 0)) for grad in grads],
        out_specs=[pl.BlockSpec((step, quarter), lambda i: (i, 0))] * 2,
        out_shape=[jax.ShapeDtypeStruct((width, quarter), jnp.bfloat16)] * 2,
        compiler_params=pltpu.CompilerParams(vmem_limit_bytes=LIMIT),
        cost_estimate=COST,
        name="weight_pass",
    )(*pieces, *grads)


def hidden_body(rank_ref, own_ref, got_ref, out_ref):
    for block in range(2):
        group = 2 * block
        out_ref[group ^ rank_ref[0]] = own_ref[block]
        out_ref[(group + 1) ^ rank_ref[0]] = got_ref[block]


def hidden_pass(rank, own, got):
    blocks, rows, quarter = own.shape
    return pl.pallas_call(
        hidden_body,
        out_shape=jax.ShapeDtypeStruct((2 * blocks, rows, quarter), own.dtype),
        in_specs=[pl.BlockSpec(memory_space=pltpu.SMEM)] + [pl.BlockSpec(memory_space=pltpu.VMEM)] * 2,
        cost_estimate=COST,
        name="hidden_pass",
    )(rank.reshape(1), own, got)


def total_body(*refs):
    base_ref, *part_refs, out_ref = refs
    first = 0
    for part_ref in part_refs:
        rows = pl.ds(first, part_ref.shape[0])
        out_ref[rows, :] = b16(f32(base_ref[rows, :]) + f32(part_ref[...]))
        first += part_ref.shape[0]


def total(base, *parts):
    return pl.pallas_call(
        total_body,
        out_shape=jax.ShapeDtypeStruct(base.shape, base.dtype),
        compiler_params=pltpu.CompilerParams(vmem_limit_bytes=LIMIT),
        cost_estimate=COST,
        name="total",
    )(base, *parts)


def per_device(tokens, cotangent, gate_weights, tile_expert, w_gate, w_up):
    row_count = tokens.shape[1]
    tile_count = row_count // TILE
    cycle_size = lax.axis_size("expert")
    position = lax.axis_index("expert")
    before = (position + cycle_size - 1) % cycle_size
    group_count = lax.axis_size("dp")
    rank = lax.axis_index("dp")
    side, core = rank // 2, rank % 2
    quarter = w_gate.shape[2]
    out_head = OUT_SHARE * tile_count
    mid, head = (share * tile_count for share in BACK_SHARE)
    tile, tile_grad = tokens[0], cotangent[0]

    def row_scale(group, place):
        owners = lax.dynamic_slice(tile_expert, (group, place * tile_count), (1, tile_count))
        weights = lax.dynamic_slice(gate_weights, (group, place * row_count), (1, row_count))
        routed = jnp.repeat(owners == position, TILE, axis=1, total_repeat_length=row_count)
        return jnp.where(routed, weights, jnp.zeros_like(weights)).reshape(row_count, 1)

    def side_grads(which):
        return jnp.concatenate(
            [
                lax.dynamic_slice_in_dim(tile_grad, (2 * which + first) * quarter, quarter, 1)
                for first in (core, 1 - core)
            ],
            axis=1,
        )

    far = (rank + group_count // 2) % group_count
    scale_hn = row_scale(rank, position)
    scale_hf = row_scale(far, position)
    scale_pn = row_scale(rank, before)
    scale_pf = row_scale(far, before)

    grads, grads_sent = side_grads(side), side_grads(1 - side)
    x_tile, x_grads = shifted(tile, 1), shifted(grads, 1)
    y_tile, y_grads = across(tile), across(grads_sent)
    panels = (w_gate[0], w_up[0], within(w_gate[0]), within(w_up[0]))
    hid_hn, own_hn, other_hn, (part_hn,) = block_pass(
        (tile,), (grads,), scale_hn, panels, (row_count,)
    )
    x_tile, y_tile, x_grads, y_grads = after((x_tile, y_tile, x_grads, y_grads), hid_hn)
    xy_top = across(x_tile[:out_head])
    xy_low = shifted(y_tile[out_head:], 1)
    xy_grads = shifted(y_grads, 1)

    upper, middle, lower = mid, head - mid, row_count - head
    hid_mid, own_mid, other_mid, mid_parts = block_pass(
        (y_tile, x_tile),
        (y_grads, x_grads),
        jnp.concatenate([scale_hf, scale_pn]),
        panels,
        (upper, middle, lower, upper, middle, lower),
    )
    upper_hf, middle_hf, lower_hf, upper_pn, middle_pn, lower_pn = mid_parts
    up_home = across(upper_hf)
    mid_home = across(middle_hf)
    low_near = shifted(lower_pn, -1)
    xy_low, xy_top, xy_grads = after((xy_low, xy_top, xy_grads), hid_mid)
    hid_pf, own_pf, other_pf, (upper_pf, middle_pf, lower_pf) = block_pass(
        (xy_top, xy_low), (xy_grads,), scale_pf, panels, (upper, middle, lower)
    )
    low_far = shifted(lower_pf, -1)
    up_past = across(upper_pf)
    mid_past = across(middle_pf)
    hid_back = shifted(jnp.stack([hid_mid[row_count:], hid_pf]), -1)

    pieces = (tile, y_tile, x_tile, xy_top, xy_low)
    far_pieces = tuple(within(piece) for piece in pieces)
    far_grads = tuple(within(grad) for grad in (other_hn, other_mid, other_pf))
    grad_gate, grad_up = weight_pass(
        pieces + far_pieces,
        after((own_hn, own_mid, own_pf) + far_grads, up_home, low_near),
        tile.shape[1],
    )

    up_past, mid_past, low_far, hid_back = after((up_past, mid_past, low_far, hid_back), grad_gate)
    up_back = shifted(b16(f32(upper_pn) + f32(up_past)), -1)
    mid_back = shifted(b16(f32(middle_pn) + f32(mid_past)), -1)
    low_home = across(b16(f32(lower_hf) + f32(low_far)))
    base = total(part_hn, up_home, mid_home, low_near)
    hidden = b16(f32(jnp.stack([hid_hn, hid_mid[:row_count]])) + f32(hid_back))
    hidden = hidden_pass(rank, hidden[:, :, :quarter], within(hidden[:, :, quarter:]))
    d_tokens = total(base, up_back, mid_back, low_home)
    return (d_tokens[None], hidden, grad_gate[None], grad_up[None])


def solution(mesh):
    in_specs = (
        P("dp", "expert", None),
        P("dp", "expert", None),
        P(),
        P(),
        P("expert", None, "dp"),
        P("expert", None, "dp"),
    )
    out_specs = (
        P("dp", "expert", None),
        P(None, "expert", "dp"),
        P("expert", None, "dp"),
        P("expert", None, "dp"),
    )
    return jax.shard_map(
        per_device, mesh=mesh, in_specs=in_specs, out_specs=out_specs, check_vma=False
    )
```

time: 207 us -> 110 us (0.53)
  waiting for transfers between devices: 137 us -> 17.6 us
  Pallas kernels: 0 us -> 36.6 us
  matrix products: 29.1 us -> 0 us
  starting transfers between devices: 11.3 us -> 28.9 us
  between operations: 14.2 us -> 3.37 us
  local copies, waits for them, and re-layouts: 7.95 us -> 13 us
    ppermute x4 -> x28, waiting for transfers between devices: 116 us -> 17.6 us  [the longest x9 13.6 us: shifted(): return lax.ppermute(value, 'expert', pairs)]
    pallas_call x0 -> x7, Pallas kernels: none -> 36.6 us  [the longest x3 21.5 us: block_pass(): pl.pallas_call(functools.partial(block_body, len(pieces), len(grads), ste...]
    dot_general x12 -> x0, matrix products: 29.1 us -> none  [the longest x8 18.3 us: contract(): lax.dot_general(left, right, (((left_axis,), (right_axis,)), ((), ())), p...]
    ppermute x4 -> x28, starting transfers between devices: 7.61 us -> 28.9 us  [the longest x9 17.8 us: shifted(): return lax.ppermute(value, 'expert', pairs)]
    all_gather x1 -> x0, waiting for transfers between devices: 13.8 us -> none  [to_groups(): gathered = lax.all_gather(tile_rows, 'dp', axis=0, tiled=True)]
    all_to_all x1 -> x0, waiting for transfers between devices: 7.22 us -> none  [to_groups(): lax.all_to_all(tile_grads, 'dp', split_axis=2, concat_axis=0, tiled=True)]
    slice x0 -> x3, local copies, waits for them, and re-layouts: none -> 4.3 us  [the longest x1 1.82 us: per_device(): xy_low = shifted(y_tile[out_head:], 1)]
    all_to_all x1 -> x0, starting transfers between devices: 3.42 us -> none  [to_groups(): lax.all_to_all(tile_grads, 'dp', split_axis=2, concat_axis=0, tiled=True)]
  transfers between devices with their start and end apart: 7 -> 28, of which waited for: 6 -> 5; matrix products, arithmetic and copies ran while one was open for 14% -> 12% of each run, Pallas kernels for 0% -> 32%
where the time goes in v2:
time: 110 us; the launch traced here: 109 us
  Pallas kernels  36.6 us (33%)
  starting transfers between devices  28.9 us (26%)
  waiting for transfers between devices  17.6 us (16%)
  local copies, waits for them, and re-layouts  13 us (12%)
  other arithmetic  9.2 us (8%)
  between operations  3.37 us (3%)
    pallas_call x3, Pallas kernels, block_pass(): pl.pallas_call(functools.partial(block_body, len(pieces), len(grads), ste...  21.5 us
    ppermute x9, starting transfers between devices, shifted(): return lax.ppermute(value, 'expert', pairs)  17.8 us
    ppermute x9, waiting for transfers between devices, shifted(): return lax.ppermute(value, 'expert', pairs)  13.6 us
    pallas_call x1, Pallas kernels, weight_pass(): pl.pallas_call(functools.partial(weight_body, len(pieces), len(grads)), g...  9.65 us
    ppermute x8, starting transfers between devices, across(): return lax.ppermute(value, 'dp', pairs)  8.36 us
    convert_element_type x4, other arithmetic, b16(): return value.astype(jnp.bfloat16)  6.29 us
    unnamed x14, local copies, waits for them, and re-layouts  5.16 us
    ppermute x8, waiting for transfers between devices, across(): return lax.ppermute(value, 'dp', pairs)  3.96 us
  transfers between devices with their start and end apart: 28, of which 5 were waited for; matrix products, arithmetic and copies ran while one was open for 12% of the time, Pallas kernels for 32%

profile of v2, /device:TPU:0, one launch (start us, length us, event | category | flops | bytes accessed | tf_op | source)
XLA Modules:
  0.0 108.6 jit_solution(8111420568039289444)
XLA Ops:
  0.6 0.5 collective-permute-start
  1.2 2.9 %collective-permute-start.2 = (bf16[128,3584]{1,0:T(8,128)(2,1)}, bf16[128,3584]{1,0:T(8,128)(2,1)}, u32[]{:S(2)}, u32[]{:S(2)}) collective-permute-start(bf16[128,3584]{1,0:T(8,128)(2,1)} %bitcast.refs_0_), channel_id=1, source_target_pairs={{0,1},{1,2},{2,3},{3,4},{4,5},{5,6},{6,7},{7,0},{8,9},{9,10},{10,1... | collective-permute-start | bytes 2752520 | tf_op jit(solution)/shard_map/ppermute | solution.py:20
  4.1 1.5 %collective-permute-start.3 = (bf16[128,3584]{1,0:T(8,128)(2,1)}, bf16[128,3584]{1,0:T(8,128)(2,1)}, u32[]{:S(2)}, u32[]{:S(2)}) collective-permute-start(bf16[128,3584]{1,0:T(8,128)(2,1)} %bitcast.refs_0_), channel_id=1, source_target_pairs={{0,16},{8,24},{16,0},{24,8},{1,17},{9,25},{17,1},{25,9},{2,18},{10... | collective-permute-start | bytes 2752520 | tf_op jit(solution)/shard_map/ppermute | solution.py:26
  5.7 1.0 dynamic-slice_bitcast_fusion.1
  6.6 0.7 pad_maximum_fusion.1.refs_1_
  7.3 1.5 %collective-permute-start.4 = (bf16[128,512]{1,0:T(8,128)(2,1)}, bf16[128,512]{1,0:T(8,128)(2,1)}, u32[]{:S(2)}, u32[]{:S(2)}) collective-permute-start(bf16[128,512]{1,0:T(8,128)(2,1)} %pad_maximum_fusion.1.refs_1_), channel_id=1, source_target_pairs={{0,1},{1,2},{2,3},{3,4},{4,5},{5,6},{6,7},{7,0},{8,9},{9,10},{10,1... | collective-permute-start | bytes 393224 | tf_op jit(solution)/shard_map/ppermute | solution.py:20
  8.8 1.5 %fusion.5 = (s32[1,1]{1,0:T(1,128)}, s32[1,1]{1,0:T(1,128)}, s32[1,1]{1,0:T(1,128)}, s32[1,1]{1,0:T(1,128)}) fusion(s32[4,8]{1,0:T(4,128)} %param.27, s32[]{:T(128)S(6)} %select_n.93, s32[]{:T(128)S(6)} %select_n.96, s32[]{:T(128)S(6)} %select_n.87, s32[]{:T(128)S(6)} %select_n.86), kind=kLoop, calls=%fused_computation.23 | loop fusion | bytes 48 | tf_op jit(solution)/shard_map/dynamic_slice | solution.py:241
  12.9 0.8 fusion.3
  14.2 0.7 pad_maximum_fusion.2
  14.8 0.5 collective-permute-start.5
  15.3 1.5 %copy-done = bf16[1,3584,256]{2,1,0:T(8,128)(2,1)S(1)} copy-done((bf16[1,3584,256]{2,1,0:T(8,128)(2,1)S(1)}, bf16[1,3584,256]{2,1,0:T(8,128)(2,1)}, u32[]{:S(2)}) %copy-start) | copy-done | bytes 1835032
  16.8 1.5 %copy-done.2 = bf16[1,3584,256]{2,1,0:T(8,128)(2,1)S(1)} copy-done((bf16[1,3584,256]{2,1,0:T(8,128)(2,1)S(1)}, bf16[1,3584,256]{2,1,0:T(8,128)(2,1)}, u32[]{:S(2)}) %copy-start.2) | copy-done | bytes 1835032
  18.3 6.3 %block_pass.3 = (bf16[128,512]{1,0:T(8,128)(2,1)S(1)}, bf16[128,512]{1,0:T(8,128)(2,1)S(1)}, bf16[128,512]{1,0:T(8,128)(2,1)}, bf16[128,3584]{1,0:T(8,128)(2,1)S(1)}) custom-call(bf16[128,3584]{1,0:T(8,128)(2,1)} %bitcast.refs_0_, bf16[128,512]{1,0:T(8,128)(2,1)} %pad_maximum_fusion.1.refs_1_, f32[128,1]{1,0:T(8,128)S(1)} %copy.14.refs_2_, ...), custom_call_target="tpu_custom_call" | custom-call | flops 999999995904 | bytes 1000000000 | tf_op jit(solution)/shard_map/block_pass/pallas_call | solution.py:143
  24.6 6.3 %collective-permute-done.4.refs_3_ = bf16[128,512]{1,0:T(8,128)(2,1)} collective-permute-done((bf16[128,512]{1,0:T(8,128)(2,1)}, bf16[128,512]{1,0:T(8,128)(2,1)}, u32[]{:S(2)}, u32[]{:S(2)}) %collective-permute-start.4) | collective-permute-done | bytes 131104 | tf_op jit(solution)/shard_map/ppermute | solution.py:20
  30.9 1.8 %slice.66 = bf16[64,3584]{1,0:T(8,128)(2,1)} slice(bf16[128,3584]{1,0:T(8,128)(2,1)} %collective-permute-done.3.refs_0_.refs_1_), slice={[64:128], [0:3584]} | slice | bytes 917504 | tf_op jit(solution)/shard_map/slice | solution.py:270
  32.7 1.8 %slice.67 = bf16[64,3584]{1,0:T(8,128)(2,1)} slice(bf16[128,3584]{1,0:T(8,128)(2,1)} %collective-permute-done.2.refs_1_.refs_2_), slice={[0:64], [0:3584]} | slice | bytes 917504 | tf_op jit(solution)/shard_map/slice | solution.py:269
  34.5 1.5 %collective-permute-start.10 = (bf16[64,3584]{1,0:T(8,128)(2,1)}, bf16[64,3584]{1,0:T(8,128)(2,1)}, u32[]{:S(2)}, u32[]{:S(2)}) collective-permute-start(bf16[64,3584]{1,0:T(8,128)(2,1)} %slice.67), channel_id=1, source_target_pairs={{0,16},{8,24},{16,0},{24,8},{1,17},{9,25},{17,1},{25,9},{2,18},{10... | collective-permute-start | bytes 1376264 | tf_op jit(solution)/shard_map/ppermute | solution.py:26
  36.1 1.5 %collective-permute-start.11 = (bf16[128,512]{1,0:T(8,128)(2,1)}, bf16[128,512]{1,0:T(8,128)(2,1)}, u32[]{:S(2)}, u32[]{:S(2)}) collective-permute-start(bf16[128,512]{1,0:T(8,128)(2,1)} %collective-permute-done.5.refs_2_), channel_id=1, source_target_pairs={{0,1},{1,2},{2,3},{3,4},{4,5},{5,6},{6,7},{7,0},{8,9},{9,10},{10,1... | collective-permute-start | bytes 393224 | tf_op jit(solution)/shard_map/ppermute | solution.py:20
  37.5 1.5 %copy-done.3 = bf16[1,3584,256]{2,1,0:T(8,128)(2,1)S(1)} copy-done((bf16[1,3584,256]{2,1,0:T(8,128)(2,1)S(1)}, bf16[1,3584,256]{2,1,0:T(8,128)(2,1)}, u32[]{:S(2)}) %copy-start.3) | copy-done | bytes 1835032
  39.0 8.0 %block_pass.4 = (bf16[256,512]{1,0:T(8,128)(2,1)S(1)}, bf16[256,512]{1,0:T(8,128)(2,1)S(1)}, bf16[256,512]{1,0:T(8,128)(2,1)}, bf16[48,3584]{1,0:T(8,128)(2,1)},...) custom-call(bf16[128,3584]{1,0:T(8,128)(2,1)} %collective-permute-do, ...), custom_call_target="tpu_custom_call" | custom-call | flops 999999995904 | bytes 1000000000 | tf_op jit(solution)/shard_map/block_pass/pallas_call | solution.py:143
  47.0 0.6 collective-permute-start.6
  47.6 1.5 %collective-permute-start.7 = (bf16[32,3584]{1,0:T(8,128)(2,1)}, bf16[32,3584]{1,0:T(8,128)(2,1)}, u32[]{:S(2)}, u32[]{:S(2)}) collective-permute-start(bf16[32,3584]{1,0:T(8,128)(2,1)} %get-tuple-element.122), channel_id=1, source_target_pairs={{0,16},{8,24},{16,0},{24,8},{1,17},{9,25},{17,1},{25,9},{2,18},{10... | collective-permute-start | bytes 688136 | tf_op jit(solution)/shard_map/ppermute | solution.py:26
  49.1 1.4 %collective-permute-done.11.refs_2_ = bf16[128,512]{1,0:T(8,128)(2,1)} collective-permute-done((bf16[128,512]{1,0:T(8,128)(2,1)}, bf16[128,512]{1,0:T(8,128)(2,1)}, u32[]{:S(2)}, u32[]{:S(2)}) %collective-permute-start.11) | collective-permute-done | bytes 131104 | tf_op jit(solution)/shard_map/ppermute | solution.py:20
  50.5 1.9 %collective-permute-start.8 = (bf16[48,3584]{1,0:T(8,128)(2,1)}, bf16[48,3584]{1,0:T(8,128)(2,1)}, u32[]{:S(2)}, u32[]{:S(2)}) collective-permute-start(bf16[48,3584]{1,0:T(8,128)(2,1)} %get-tuple-element.123), channel_id=1, source_target_pairs={{0,7},{1,0},{2,1},{3,2},{4,3},{5,4},{6,5},{7,6},{8,15},{9,8},{10,9... | collective-permute-start | bytes 1032200 | tf_op jit(solution)/shard_map/ppermute | solution.py:20
  52.4 0.5 collective-permute-start.22
  52.9 7.2 %block_pass.5 = (bf16[128,512]{1,0:T(8,128)(2,1)S(1)}, bf16[128,512]{1,0:T(8,128)(2,1)S(1)}, bf16[128,512]{1,0:T(8,128)(2,1)S(1)}, bf16[48,3584]{1,0:T(8,128)(2,...) custom-call(bf16[64,3584]{1,0:T(8,128)(2,1)} %collective-permute-done.10.refs_0_.refs_3_, ...), custom_call_target="tpu_custom_call" | custom-call | flops 999999995904 | bytes 1000000000 | tf_op jit(solution)/shard_map/block_pass/pallas_call | solution.py:143
  60.3 0.7 slice_bitcast_fusion
  61.0 0.4 collective-permute-start.16
  62.5 1.4 %total.2.refs_0_ = bf16[128,3584]{1,0:T(8,128)(2,1)S(1)} custom-call(bf16[128,3584]{1,0:T(8,128)(2,1)S(1)} %get-tuple-element.115.refs_0_, bf16[48,3584]{1,0:T(8,128)(2,1)} %collective-permute-done.6.refs_1_, bf16[32,3584]{1,0:T(8,128)(2,1)} %collective-permute-done.7.refs_2_, bf16[48,3584]{1,0:T(8,128)(2,1)} %collective-permute-done.8.refs_3_), custom_call_target="tpu_custom_call" | custom-call | flops 999999995904 | bytes 1000000000 | tf_op jit(solution)/shard_map/total/pallas_call | solution.py:217
  63.9 0.7 pad_maximum_fusion
  64.6 0.5 collective-permute-start.12
  65.2 1.5 %collective-permute-start.13 = (bf16[32,3584]{1,0:T(8,128)(2,1)}, bf16[32,3584]{1,0:T(8,128)(2,1)}, u32[]{:S(2)}, u32[]{:S(2)}) collective-permute-start(bf16[32,3584]{1,0:T(8,128)(2,1)} %get-tuple-element.130), channel_id=1, source_target_pairs={{0,16},{8,24},{16,0},{24,8},{1,17},{9,25},{17,1},{25,9},{2,18},{10... | collective-permute-start | bytes 688136 | tf_op jit(solution)/shard_map/ppermute | solution.py:26
  66.7 3.1 %collective-permute-start.14 = (bf16[48,3584]{1,0:T(8,128)(2,1)}, bf16[48,3584]{1,0:T(8,128)(2,1)}, u32[]{:S(2)}, u32[]{:S(2)}) collective-permute-start(bf16[48,3584]{1,0:T(8,128)(2,1)} %get-tuple-element.131), channel_id=1, source_target_pairs={{0,7},{1,0},{2,1},{3,2},{4,3},{5,4},{6,5},{7,6},{8,15},{9,8},{10,9... | collective-permute-start | bytes 1032200 | tf_op jit(solution)/shard_map/ppermute | solution.py:20
  69.8 1.7 %collective-permute-start.15 = (bf16[2,128,512]{2,1,0:T(8,128)(2,1)}, bf16[2,128,512]{2,1,0:T(8,128)(2,1)}, u32[]{:S(2)}, u32[]{:S(2)}) collective-permute-start(bf16[2,128,512]{2,1,0:T(8,128)(2,1)} %pad_maximum_fusion), channel_id=1, source_target_pairs={{0,7},{1,0},{2,1},{3,2},{4,3},{5,4},{6,5},{7,6},{8,15},{9,8},{10,9... | collective-permute-start | bytes 786440 | tf_op jit(solution)/shard_map/ppermute | solution.py:20
  71.6 9.6 %weight_pass.1 = (bf16[3584,256]{1,0:T(8,128)(2,1)}, bf16[3584,256]{1,0:T(8,128)(2,1)}) custom-call(bf16[128,3584]{1,0:T(8,128)(2,1)} %bitcast.refs_0_, bf16[128,3584]{1,0:T(8,128)(2,1)} %collective-permute-done.3.refs_0_.refs_1_, bf16[128,3584]{1,0:T(8,128)(2,1)} %collective-permute-done.2.refs_1_.refs_2_, ...), custom_call_target="tpu_custom_call" | custom-call | flops 999999995904 | bytes 1000000000 | tf_op jit(solution)/shard_map/weight_pass/pallas_call | solution.py:176
  81.2 2.1 %collective-permute-done.15 = bf16[2,128,512]{2,1,0:T(8,128)(2,1)} collective-permute-done((bf16[2,128,512]{2,1,0:T(8,128)(2,1)}, bf16[2,128,512]{2,1,0:T(8,128)(2,1)}, u32[]{:S(2)}, u32[]{:S(2)}) %collective-permute-start.15) | collective-permute-done | bytes 262176 | tf_op jit(solution)/shard_map/ppermute | solution.py:20
  83.4 1.8 %add_convert_fusion.1 = bf16[48,3584]{1,0:T(8,128)(2,1)} fusion(bf16[48,3584]{1,0:T(8,128)(2,1)} %collective-permute-done.12, bf16[48,3584]{1,0:T(8,128)(2,1)S(1)} %get-tuple-element.124), kind=kLoop, calls=%fused_computation.1 | loop fusion | flops 688128 | bytes 1032192 | tf_op jit(solution)/shard_map/convert_element_type | solution.py:44
  85.2 5.2 %collective-permute-start.24 = (bf16[48,3584]{1,0:T(8,128)(2,1)}, bf16[48,3584]{1,0:T(8,128)(2,1)}, u32[]{:S(2)}, u32[]{:S(2)}) collective-permute-start(bf16[48,3584]{1,0:T(8,128)(2,1)} %add_convert_fusion.1), channel_id=1, source_target_pairs={{0,7},{1,0},{2,1},{3,2},{4,3},{5,4},{6,5},{7,6},{8,15},{9,8},{10,9... | collective-permute-start | bytes 1032200 | tf_op jit(solution)/shard_map/ppermute | solution.py:20
  90.3 1.7 %add_convert_fusion.3 = bf16[32,3584]{1,0:T(8,128)(2,1)} fusion(bf16[32,3584]{1,0:T(8,128)(2,1)} %collective-permute-done.13, bf16[32,3584]{1,0:T(8,128)(2,1)S(1)} %get-tuple-element.147), kind=kLoop, calls=%fused_computation.3 | loop fusion | flops 458752 | bytes 688128 | tf_op jit(solution)/shard_map/convert_element_type | solution.py:44
  92.0 1.0 add_convert_fusion.2
  93.0 0.7 fusion.4
  93.7 1.8 %add_convert_fusion = bf16[48,3584]{1,0:T(8,128)(2,1)} fusion(bf16[48,3584]{1,0:T(8,128)(2,1)} %collective-permute-done.14, bf16[48,3584]{1,0:T(8,128)(2,1)S(1)} %get-tuple-element.149), kind=kLoop, calls=%fused_computation | loop fusion | flops 688128 | bytes 1032192 | tf_op jit(solution)/shard_map/convert_element_type | solution.py:44
  95.5 0.7 collective-permute-start.26
  96.2 0.6 copy-done.6
  96.9 1.7 %hidden_pass.1 = bf16[4,128,256]{2,1,0:T(8,128)(2,1)} custom-call(s32[1]{0:T(128)} %bitcast.19.rank_ref, bf16[2,128,256]{2,1,0:T(8,128)(2,1)} %get-tuple-element.154.own_ref, bf16[2,128,256]{2,1,0:T(8,128)(2,1)} %copy-done.6), custom_call_target="tpu_custom_call" | custom-call | flops 999999995904 | bytes 1000000000 | tf_op jit(solution)/shard_map/hidden_pass/pallas_call | solution.py:198
  98.6 3.8 %collective-permute-done.25.refs_2_ = bf16[32,3584]{1,0:T(8,128)(2,1)} collective-permute-done((bf16[32,3584]{1,0:T(8,128)(2,1)}, bf16[32,3584]{1,0:T(8,128)(2,1)}, u32[]{:S(2)}, u32[]{:S(2)}) %collective-permute-start.25) | collective-permute-done | bytes 229408 | tf_op jit(solution)/shard_map/ppermute | solution.py:20
  102.4 3.9 %collective-permute-done.26.refs_3_ = bf16[48,3584]{1,0:T(8,128)(2,1)} collective-permute-done((bf16[48,3584]{1,0:T(8,128)(2,1)}, bf16[48,3584]{1,0:T(8,128)(2,1)}, u32[]{:S(2)}, u32[]{:S(2)}) %collective-permute-start.26) | collective-permute-done | bytes 344096 | tf_op jit(solution)/shard_map/ppermute | solution.py:26
  106.3 2.3 %total.3 = bf16[128,3584]{1,0:T(8,128)(2,1)} custom-call(bf16[128,3584]{1,0:T(8,128)(2,1)S(1)} %total.2.refs_0_, bf16[48,3584]{1,0:T(8,128)(2,1)} %collective-permute-done.24.refs_1_, bf16[32,3584]{1,0:T(8,128)(2,1)} %collective-permute-done.25.refs_2_, bf16[48,3584]{1,0:T(8,128)(2,1)} %collective-permute-done.26.refs_3_), custom_call_target="tpu_custom_call" | custom-call | flops 999999995904 | bytes 1000000000 | tf_op jit(solution)/shard_map/total/pallas_call | solution.py:217
  (47 shorter events, 1.7 us)
Async XLA Ops:
  0.6 14.2 %collective-permute-start = (bf16[3584,256]{1,0:T(8,128)(2,1)}, bf16[3584,256]{1,0:T(8,128)(2,1)S(1)}, u32[]{:S(2)}, u32[]{:S(2)}) collective-permute-start(bf16[3584,256]{1,0:T(8,128)(2,1)} %bitcast.36), channel_id=1, source_target_pairs={{0,8},{8,0},{16,24},{24,16},{1,9},{9,1},{17,25},{25,17},{2,10},{10... | collective-permute-start | bytes 5505032 | tf_op jit(solution)/shard_map/ppermute | solution.py:32
  1.1 14.2 %collective-permute-start.1 = (bf16[3584,256]{1,0:T(8,128)(2,1)}, bf16[3584,256]{1,0:T(8,128)(2,1)}, u32[]{:S(2)}, u32[]{:S(2)}) collective-permute-start(bf16[3584,256]{1,0:T(8,128)(2,1)} %bitcast.40), channel_id=1, source_target_pairs={{0,8},{8,0},{16,24},{24,16},{1,9},{9,1},{17,25},{25,17},{2,10},{10... | collective-permute-start | bytes 5505032 | tf_op jit(solution)/shard_map/ppermute | solution.py:32
  1.2 29.7 %collective-permute-start.2 = (bf16[128,3584]{1,0:T(8,128)(2,1)}, bf16[128,3584]{1,0:T(8,128)(2,1)}, u32[]{:S(2)}, u32[]{:S(2)}) collective-permute-start(bf16[128,3584]{1,0:T(8,128)(2,1)} %bitcast.refs_0_), channel_id=1, source_target_pairs={{0,1},{1,2},{2,3},{3,4},{4,5},{5,6},{6,7},{7,0},{8,9},{9,10},{10,1... | collective-permute-start | bytes 2752520 | tf_op jit(solution)/shard_map/ppermute | solution.py:20
  4.1 26.8 %collective-permute-start.3 = (bf16[128,3584]{1,0:T(8,128)(2,1)}, bf16[128,3584]{1,0:T(8,128)(2,1)}, u32[]{:S(2)}, u32[]{:S(2)}) collective-permute-start(bf16[128,3584]{1,0:T(8,128)(2,1)} %bitcast.refs_0_), channel_id=1, source_target_pairs={{0,16},{8,24},{16,0},{24,8},{1,17},{9,25},{17,1},{25,9},{2,18},{10... | collective-permute-start | bytes 2752520 | tf_op jit(solution)/shard_map/ppermute | solution.py:26
  7.3 23.6 %collective-permute-start.4 = (bf16[128,512]{1,0:T(8,128)(2,1)}, bf16[128,512]{1,0:T(8,128)(2,1)}, u32[]{:S(2)}, u32[]{:S(2)}) collective-permute-start(bf16[128,512]{1,0:T(8,128)(2,1)} %pad_maximum_fusion.1.refs_1_), channel_id=1, source_target_pairs={{0,1},{1,2},{2,3},{3,4},{4,5},{5,6},{6,7},{7,0},{8,9},{9,10},{10,1... | collective-permute-start | bytes 393224 | tf_op jit(solution)/shard_map/ppermute | solution.py:20
  14.8 16.1 %collective-permute-start.5 = (bf16[128,512]{1,0:T(8,128)(2,1)}, bf16[128,512]{1,0:T(8,128)(2,1)}, u32[]{:S(2)}, u32[]{:S(2)}) collective-permute-start(bf16[128,512]{1,0:T(8,128)(2,1)} %pad_maximum_fusion.2), channel_id=1, source_target_pairs={{0,16},{8,24},{16,0},{24,8},{1,17},{9,25},{17,1},{25,9},{2,18},{10... | collective-permute-start | bytes 393224 | tf_op jit(solution)/shard_map/ppermute | solution.py:26
  15.3 1.5 %copy-start = (bf16[1,3584,256]{2,1,0:T(8,128)(2,1)S(1)}, bf16[1,3584,256]{2,1,0:T(8,128)(2,1)}, u32[]{:S(2)}) copy-start(bf16[1,3584,256]{2,1,0:T(8,128)(2,1)} %param.28) | copy-start | bytes 5505028
  16.8 1.5 %copy-start.2 = (bf16[1,3584,256]{2,1,0:T(8,128)(2,1)S(1)}, bf16[1,3584,256]{2,1,0:T(8,128)(2,1)}, u32[]{:S(2)}) copy-start(bf16[1,3584,256]{2,1,0:T(8,128)(2,1)} %param.29) | copy-start | bytes 5505028
  24.6 12.9 %copy-start.1 = (bf16[1,3584,256]{2,1,0:T(8,128)(2,1)S(1)}, bf16[1,3584,256]{2,1,0:T(8,128)(2,1)}, u32[]{:S(2)}) copy-start(bf16[1,3584,256]{2,1,0:T(8,128)(2,1)} %param.28) | copy-start | bytes 5505028
  32.7 19.7 %collective-permute-start.9 = (bf16[64,3584]{1,0:T(8,128)(2,1)}, bf16[64,3584]{1,0:T(8,128)(2,1)}, u32[]{:S(2)}, u32[]{:S(2)}) collective-permute-start(bf16[64,3584]{1,0:T(8,128)(2,1)} %slice.66), channel_id=1, source_target_pairs={{0,1},{1,2},{2,3},{3,4},{4,5},{5,6},{6,7},{7,0},{8,9},{9,10},{10,1... | collective-permute-start | bytes 1376264 | tf_op jit(solution)/shard_map/ppermute | solution.py:20
  34.5 17.9 %collective-permute-start.10 = (bf16[64,3584]{1,0:T(8,128)(2,1)}, bf16[64,3584]{1,0:T(8,128)(2,1)}, u32[]{:S(2)}, u32[]{:S(2)}) collective-permute-start(bf16[64,3584]{1,0:T(8,128)(2,1)} %slice.67), channel_id=1, source_target_pairs={{0,16},{8,24},{16,0},{24,8},{1,17},{9,25},{17,1},{25,9},{2,18},{10... | collective-permute-start | bytes 1376264 | tf_op jit(solution)/shard_map/ppermute | solution.py:26
  36.1 14.5 %collective-permute-start.11 = (bf16[128,512]{1,0:T(8,128)(2,1)}, bf16[128,512]{1,0:T(8,128)(2,1)}, u32[]{:S(2)}, u32[]{:S(2)}) collective-permute-start(bf16[128,512]{1,0:T(8,128)(2,1)} %collective-permute-done.5.refs_2_), channel_id=1, source_target_pairs={{0,1},{1,2},{2,3},{3,4},{4,5},{5,6},{6,7},{7,0},{8,9},{9,10},{10,1... | collective-permute-start | bytes 393224 | tf_op jit(solution)/shard_map/ppermute | solution.py:20
  37.5 1.5 %copy-start.3 = (bf16[1,3584,256]{2,1,0:T(8,128)(2,1)S(1)}, bf16[1,3584,256]{2,1,0:T(8,128)(2,1)}, u32[]{:S(2)}) copy-start(bf16[1,3584,256]{2,1,0:T(8,128)(2,1)} %param.29) | copy-start | bytes 5505028
  47.0 14.5 %collective-permute-start.6 = (bf16[48,3584]{1,0:T(8,128)(2,1)}, bf16[48,3584]{1,0:T(8,128)(2,1)}, u32[]{:S(2)}, u32[]{:S(2)}) collective-permute-start(bf16[48,3584]{1,0:T(8,128)(2,1)} %get-tuple-element.121), channel_id=1, source_target_pairs={{0,16},{8,24},{16,0},{24,8},{1,17},{9,25},{17,1},{25,9},{2,18},{10... | collective-permute-start | bytes 1032200 | tf_op jit(solution)/shard_map/ppermute | solution.py:26
  47.6 13.4 %collective-permute-start.7 = (bf16[32,3584]{1,0:T(8,128)(2,1)}, bf16[32,3584]{1,0:T(8,128)(2,1)}, u32[]{:S(2)}, u32[]{:S(2)}) collective-permute-start(bf16[32,3584]{1,0:T(8,128)(2,1)} %get-tuple-element.122), channel_id=1, source_target_pairs={{0,16},{8,24},{16,0},{24,8},{1,17},{9,25},{17,1},{25,9},{2,18},{10... | collective-permute-start | bytes 688136 | tf_op jit(solution)/shard_map/ppermute | solution.py:26
  50.5 11.4 %collective-permute-start.8 = (bf16[48,3584]{1,0:T(8,128)(2,1)}, bf16[48,3584]{1,0:T(8,128)(2,1)}, u32[]{:S(2)}, u32[]{:S(2)}) collective-permute-start(bf16[48,3584]{1,0:T(8,128)(2,1)} %get-tuple-element.123), channel_id=1, source_target_pairs={{0,7},{1,0},{2,1},{3,2},{4,3},{5,4},{6,5},{7,6},{8,15},{9,8},{10,9... | collective-permute-start | bytes 1032200 | tf_op jit(solution)/shard_map/ppermute | solution.py:20
  52.4 7.7 %collective-permute-start.21 = (bf16[128,512]{1,0:T(8,128)(2,1)}, bf16[128,512]{1,0:T(8,128)(2,1)}, u32[]{:S(2)}, u32[]{:S(2)}) collective-permute-start(bf16[128,512]{1,0:T(8,128)(2,1)} %get-tuple-element.136), channel_id=1, source_target_pairs={{0,8},{8,0},{16,24},{24,16},{1,9},{9,1},{17,25},{25,17},{2,10},{10... | collective-permute-start | bytes 393224 | tf_op jit(solution)/shard_map/ppermute | solution.py:32
  52.4 9.0 %collective-permute-start.22 = (bf16[256,512]{1,0:T(8,128)(2,1)}, bf16[256,512]{1,0:T(8,128)(2,1)}, u32[]{:S(2)}, u32[]{:S(2)}) collective-permute-start(bf16[256,512]{1,0:T(8,128)(2,1)} %get-tuple-element.137), channel_id=1, source_target_pairs={{0,8},{8,0},{16,24},{24,16},{1,9},{9,1},{17,25},{25,17},{2,10},{10... | collective-permute-start | bytes 786440 | tf_op jit(solution)/shard_map/ppermute | solution.py:32
  60.1 1.9 %collective-permute-start.23 = (bf16[128,512]{1,0:T(8,128)(2,1)S(1)}, bf16[128,512]{1,0:T(8,128)(2,1)S(1)}, u32[]{:S(2)}, u32[]{:S(2)}) collective-permute-start(bf16[128,512]{1,0:T(8,128)(2,1)S(1)} %get-tuple-element.138), channel_id=1, source_target_pairs={{0,8},{8,0},{16,24},{24,16},{1,9},{9,1},{17,25},{25,17},{2,10},{10... | collective-permute-start | bytes 393224 | tf_op jit(solution)/shard_map/ppermute | solution.py:32
  61.0 3.7 %collective-permute-start.16 = (bf16[128,3584]{1,0:T(8,128)(2,1)}, bf16[128,3584]{1,0:T(8,128)(2,1)}, u32[]{:S(2)}, u32[]{:S(2)}) collective-permute-start(bf16[128,3584]{1,0:T(8,128)(2,1)} %bitcast.refs_0_), channel_id=1, source_target_pairs={{0,8},{8,0},{16,24},{24,16},{1,9},{9,1},{17,25},{25,17},{2,10},{10... | collective-permute-start | bytes 2752520 | tf_op jit(solution)/shard_map/ppermute | solution.py:32
  61.4 3.8 %collective-permute-start.17 = (bf16[128,3584]{1,0:T(8,128)(2,1)}, bf16[128,3584]{1,0:T(8,128)(2,1)}, u32[]{:S(2)}, u32[]{:S(2)}) collective-permute-start(bf16[128,3584]{1,0:T(8,128)(2,1)} %collective-permute-done.3.refs_0_.refs_1_), channel_id=1, source_target_pairs={{0,8},{8,0},{16,24},{24,16},{1,9},{9,1},{17,25},{25,17},{2,10},{10... | collective-permute-start | bytes 2752520 | tf_op jit(solution)/shard_map/ppermute | solution.py:32
  61.5 5.2 %collective-permute-start.18 = (bf16[128,3584]{1,0:T(8,128)(2,1)}, bf16[128,3584]{1,0:T(8,128)(2,1)}, u32[]{:S(2)}, u32[]{:S(2)}) collective-permute-start(bf16[128,3584]{1,0:T(8,128)(2,1)} %collective-permute-done.2.refs_1_.refs_2_), channel_id=1, source_target_pairs={{0,8},{8,0},{16,24},{24,16},{1,9},{9,1},{17,25},{25,17},{2,10},{10... | collective-permute-start | bytes 2752520 | tf_op jit(solution)/shard_map/ppermute | solution.py:32
  61.9 7.9 %collective-permute-start.19 = (bf16[64,3584]{1,0:T(8,128)(2,1)}, bf16[64,3584]{1,0:T(8,128)(2,1)}, u32[]{:S(2)}, u32[]{:S(2)}) collective-permute-start(bf16[64,3584]{1,0:T(8,128)(2,1)} %collective-permute-done.10.refs_0_.refs_3_), channel_id=1, source_target_pairs={{0,8},{8,0},{16,24},{24,16},{1,9},{9,1},{17,25},{25,17},{2,10},{10... | collective-permute-start | bytes 1376264 | tf_op jit(solution)/shard_map/ppermute | solution.py:32
  62.0 9.5 %collective-permute-start.20 = (bf16[64,3584]{1,0:T(8,128)(2,1)}, bf16[64,3584]{1,0:T(8,128)(2,1)}, u32[]{:S(2)}, u32[]{:S(2)}) collective-permute-start(bf16[64,3584]{1,0:T(8,128)(2,1)} %collective-permute-done.9.refs_1_.refs_4_), channel_id=1, source_target_pairs={{0,8},{8,0},{16,24},{24,16},{1,9},{9,1},{17,25},{25,17},{2,10},{10... | collective-permute-start | bytes 1376264 | tf_op jit(solution)/shard_map/ppermute | solution.py:32
  62.5 1.4 %copy-start.5 = (bf16[1,128,512]{2,1,0:T(8,128)(2,1)S(1)}, bf16[1,128,512]{2,1,0:T(8,128)(2,1)}, u32[]{:S(2)}) copy-start(bf16[1,128,512]{2,1,0:T(8,128)(2,1)} %get-tuple-element.156) | copy-start | bytes 393220
  64.6 18.7 %collective-permute-start.12 = (bf16[48,3584]{1,0:T(8,128)(2,1)}, bf16[48,3584]{1,0:T(8,128)(2,1)}, u32[]{:S(2)}, u32[]{:S(2)}) collective-permute-start(bf16[48,3584]{1,0:T(8,128)(2,1)} %get-tuple-element.129), channel_id=1, source_target_pairs={{0,16},{8,24},{16,0},{24,8},{1,17},{9,25},{17,1},{25,9},{2,18},{10... | collective-permute-start | bytes 1032200 | tf_op jit(solution)/shard_map/ppermute | solution.py:26
  65.2 16.0 %collective-permute-start.13 = (bf16[32,3584]{1,0:T(8,128)(2,1)}, bf16[32,3584]{1,0:T(8,128)(2,1)}, u32[]{:S(2)}, u32[]{:S(2)}) collective-permute-start(bf16[32,3584]{1,0:T(8,128)(2,1)} %get-tuple-element.130), channel_id=1, source_target_pairs={{0,16},{8,24},{16,0},{24,8},{1,17},{9,25},{17,1},{25,9},{2,18},{10... | collective-permute-start | bytes 688136 | tf_op jit(solution)/shard_map/ppermute | solution.py:26
  66.7 16.7 %collective-permute-start.14 = (bf16[48,3584]{1,0:T(8,128)(2,1)}, bf16[48,3584]{1,0:T(8,128)(2,1)}, u32[]{:S(2)}, u32[]{:S(2)}) collective-permute-start(bf16[48,3584]{1,0:T(8,128)(2,1)} %get-tuple-element.131), channel_id=1, source_target_pairs={{0,7},{1,0},{2,1},{3,2},{4,3},{5,4},{6,5},{7,6},{8,15},{9,8},{10,9... | collective-permute-start | bytes 1032200 | tf_op jit(solution)/shard_map/ppermute | solution.py:20
  69.8 13.6 %collective-permute-start.15 = (bf16[2,128,512]{2,1,0:T(8,128)(2,1)}, bf16[2,128,512]{2,1,0:T(8,128)(2,1)}, u32[]{:S(2)}, u32[]{:S(2)}) collective-permute-start(bf16[2,128,512]{2,1,0:T(8,128)(2,1)} %pad_maximum_fusion), channel_id=1, source_target_pairs={{0,7},{1,0},{2,1},{3,2},{4,3},{5,4},{6,5},{7,6},{8,15},{9,8},{10,9... | collective-permute-start | bytes 786440 | tf_op jit(solution)/shard_map/ppermute | solution.py:20
  71.5 20.5 %copy-start.4 = (bf16[1,128,512]{2,1,0:T(8,128)(2,1)S(1)}, bf16[1,128,512]{2,1,0:T(8,128)(2,1)}, u32[]{:S(2)}) copy-start(bf16[1,128,512]{2,1,0:T(8,128)(2,1)} %get-tuple-element.155) | copy-start | bytes 393220
  85.2 17.2 %collective-permute-start.24 = (bf16[48,3584]{1,0:T(8,128)(2,1)}, bf16[48,3584]{1,0:T(8,128)(2,1)}, u32[]{:S(2)}, u32[]{:S(2)}) collective-permute-start(bf16[48,3584]{1,0:T(8,128)(2,1)} %add_convert_fusion.1), channel_id=1, source_target_pairs={{0,7},{1,0},{2,1},{3,2},{4,3},{5,4},{6,5},{7,6},{8,15},{9,8},{10,9... | collective-permute-start | bytes 1032200 | tf_op jit(solution)/shard_map/ppermute | solution.py:20
  92.0 10.3 %collective-permute-start.25 = (bf16[32,3584]{1,0:T(8,128)(2,1)}, bf16[32,3584]{1,0:T(8,128)(2,1)}, u32[]{:S(2)}, u32[]{:S(2)}) collective-permute-start(bf16[32,3584]{1,0:T(8,128)(2,1)} %add_convert_fusion.3), channel_id=1, source_target_pairs={{0,7},{1,0},{2,1},{3,2},{4,3},{5,4},{6,5},{7,6},{8,15},{9,8},{10,9... | collective-permute-start | bytes 688136 | tf_op jit(solution)/shard_map/ppermute | solution.py:20
  93.7 2.5 %collective-permute-start.27 = (bf16[2,128,256]{2,1,0:T(8,128)(2,1)S(1)}, bf16[2,128,256]{2,1,0:T(8,128)(2,1)S(1)}, u32[]{:S(2)}, u32[]{:S(2)}) collective-permute-start(bf16[2,128,256]{2,1,0:T(8,128)(2,1)S(1)} %get-tuple-element.153), channel_id=1, source_target_pairs={{0,8},{8,0},{16,24},{24,16},{1,9},{9,1},{17,25},{25,17},{2,10},{10... | collective-permute-start | bytes 393224 | tf_op jit(solution)/shard_map/ppermute | solution.py:32
  95.5 10.8 %collective-permute-start.26 = (bf16[48,3584]{1,0:T(8,128)(2,1)}, bf16[48,3584]{1,0:T(8,128)(2,1)}, u32[]{:S(2)}, u32[]{:S(2)}) collective-permute-start(bf16[48,3584]{1,0:T(8,128)(2,1)} %add_convert_fusion), channel_id=1, source_target_pairs={{0,16},{8,24},{16,0},{24,8},{1,17},{9,25},{17,1},{25,9},{2,18},{10... | collective-permute-start | bytes 1032200 | tf_op jit(solution)/shard_map/ppermute | solution.py:26
  96.2 0.6 copy-start.6

commit v3 on v2

v3 whole, which is shorter than its diff:
```python
import functools

import jax
import jax.numpy as jnp
from jax import lax
from jax.experimental import pallas as pl
from jax.experimental.pallas import tpu as pltpu
from jax.sharding import PartitionSpec as P

TILE = 128
OUT_SHARE = 80
BACK_SHARE = (32, 48, 80)
LIMIT = 20 * 2**20
LONG = pl.CostEstimate(flops=10**12, bytes_accessed=10**9, transcendentals=0)


def work(flops, moved):
    return pl.CostEstimate(flops=flops, bytes_accessed=moved, transcendentals=0)


def shifted(value, steps):
    count = lax.axis_size("expert")
    pairs = [(source, (source + steps) % count) for source in range(count)]
    return lax.ppermute(value, "expert", pairs)


def across(value):
    count = lax.axis_size("dp")
    pairs = [(source, (source + count // 2) % count) for source in range(count)]
    return lax.ppermute(value, "dp", pairs)


def within(value):
    count = lax.axis_size("dp")
    pairs = [(source, source + 1 - 2 * (source % 2)) for source in range(count)]
    return lax.ppermute(value, "dp", pairs)


def after(values, *earlier):
    return lax.optimization_barrier((values, earlier))[0]


def f32(value):
    return value.astype(jnp.float32)


def b16(value):
    return value.astype(jnp.bfloat16)


def column_step(width):
    for step in (512, 256, 128):
        if width % step == 0:
            return step
    return width


def contract(left, right, left_axis, right_axis):
    return lax.dot_general(
        left, right, (((left_axis,), (right_axis,)), ((), ())), preferred_element_type=jnp.float32
    )


def joined(refs, columns):
    return jnp.concatenate([ref[:, columns] for ref in refs], axis=0)


def pack_body(tile_ref, grads_ref, top_ref, low_ref, far_ref):
    rank = lax.axis_index("dp")
    side, core = rank // 2, rank % 2
    width = tile_ref.shape[1]
    quarter = grads_ref.shape[1] // 4
    head, both = top_ref.shape[0], 2 * quarter
    parts = [
        grads_ref[:, pl.ds(pl.multiple_of((2 * which + first) * quarter, quarter), quarter)]
        for which in (1 - side, side)
        for first in (core, 1 - core)
    ]
    sent, kept = jnp.concatenate(parts[:2], axis=1), jnp.concatenate(parts[2:], axis=1)
    tile = tile_ref[...]
    far_ref[:, :width] = tile
    far_ref[:, width:] = sent
    for out_ref, rows in ((top_ref, slice(0, head)), (low_ref, slice(head, tile.shape[0]))):
        out_ref[:, :width] = tile[rows]
        out_ref[:, width : width + both] = sent[rows]
        out_ref[:, width + both :] = kept[rows]


def pack(tile, grads, head):
    rows, width = tile.shape
    whole = grads.shape[1]
    return pl.pallas_call(
        pack_body,
        out_shape=[
            jax.ShapeDtypeStruct((head, width + whole), tile.dtype),
            jax.ShapeDtypeStruct((rows - head, width + whole), tile.dtype),
            jax.ShapeDtypeStruct((rows, width + whole // 2), tile.dtype),
        ],
        compiler_params=pltpu.CompilerParams(vmem_limit_bytes=LIMIT),
        cost_estimate=work(0, 4 * rows * (width + whole)),
        name="pack",
    )(
        pltpu.with_memory_space_constraint(tile, pltpu.HBM),
        pltpu.with_memory_space_constraint(grads, pltpu.HBM),
    )


def block_body(grad_starts, scale_start, step, *refs):
    pieces, refs = refs[: len(grad_starts)], refs[len(grad_starts) :]
    scale_ref, *panels = refs[:5]
    hidden_ref, own_ref, other_ref, *part_refs = refs[5:]
    width, quarter = panels[0].shape
    values = joined(pieces, pl.ds(0, width))
    factor = scale_ref[pl.ds(scale_start, hidden_ref.shape[0]), :]
    grads = []
    for which, out_ref in enumerate((own_ref, other_ref)):
        gate_val = contract(values, panels[2 * which][...], 1, 0)
        up_val = contract(values, panels[2 * which + 1][...], 1, 0)
        columns = pl.ds(which * quarter, quarter)
        sigmoid_val = jax.nn.sigmoid(gate_val)
        activation = gate_val * sigmoid_val
        hidden_ref[:, columns] = b16(factor * activation * up_val)
        received = jnp.concatenate(
            [
                piece[:, pl.ds(start + which * quarter, quarter)]
                for piece, start in zip(pieces, grad_starts)
            ]
        )
        act_grad = factor * f32(received)
        up_grad = b16(act_grad * activation)
        gate_grad = b16(act_grad * up_val * sigmoid_val * (1.0 + gate_val * (1.0 - sigmoid_val)))
        out_ref[:, :quarter] = gate_grad
        out_ref[:, quarter:] = up_grad
        grads += [gate_grad.T, up_grad.T]
    for start in range(0, width, step):
        columns = pl.ds(start, step)
        part = b16(
            sum(contract(panel[columns, :], grad, 1, 0) for panel, grad in zip(panels, grads))
        ).T
        first = 0
        for part_ref in part_refs:
            part_ref[:, columns] = part[first : first + part_ref.shape[0]]
            first += part_ref.shape[0]


def block_pass(pieces, grad_starts, scales, scale_start, panels, part_rows):
    rows = sum(piece.shape[0] for piece in pieces)
    width, quarter = panels[0].shape
    wide = jax.ShapeDtypeStruct((rows, 2 * quarter), jnp.bfloat16)
    hidden, own, other, *parts = pl.pallas_call(
        functools.partial(block_body, grad_starts, scale_start, column_step(width)),
        out_shape=[wide] * 3
        + [jax.ShapeDtypeStruct((count, width), jnp.bfloat16) for count in part_rows],
        compiler_params=pltpu.CompilerParams(vmem_limit_bytes=LIMIT),
        cost_estimate=work(16 * rows * width * quarter, 4 * rows * width),
        name="block_pass",
    )(*pieces, scales, *panels)
    return hidden, own, other, parts


def weight_body(piece_count, grad_count, *refs):
    pieces = refs[:piece_count]
    grads = refs[piece_count : piece_count + grad_count]
    others = refs[piece_count + grad_count :]
    total = contract(joined(pieces, slice(None)), joined(grads, slice(None)), 0, 0)
    if len(others) == 1:
        others[0][...] = b16(total)
    else:
        got_ref, gate_ref, up_ref = others
        quarter = gate_ref.shape[1]
        total = b16((total + f32(got_ref[...])) * (1.0 / TILE))
        gate_ref[...] = total[:, :quarter]
        up_ref[...] = total[:, quarter:]


def weight_pass(width, pieces, grads, got=None):
    both = grads[0].shape[1]
    rows = sum(piece.shape[0] for piece in pieces)
    step = column_step(width)
    widths = [both] if got is None else [both // 2] * 2
    return pl.pallas_call(
        functools.partial(weight_body, len(pieces), len(grads)),
        grid=(width // step,),
        in_specs=[pl.BlockSpec((piece.shape[0], step), lambda i: (0, i)) for piece in pieces]
        + [pl.BlockSpec(grad.shape, lambda i: (0, 0)) for grad in grads]
        + ([] if got is None else [pl.BlockSpec((step, both), lambda i: (i, 0))]),
        out_specs=[pl.BlockSpec((step, columns), lambda i: (i, 0)) for columns in widths],
        out_shape=[jax.ShapeDtypeStruct((width, columns), jnp.bfloat16) for columns in widths],
        compiler_params=pltpu.CompilerParams(vmem_limit_bytes=LIMIT),
        cost_estimate=work(2 * rows * width * both, 2 * width * (rows + 2 * both)),
        name="weight_pass",
    )(*pieces, *grads, *([] if got is None else [got]))


def hidden_body(rank_ref, own_ref, got_ref, out_ref):
    for block in range(2):
        group = 2 * block
        out_ref[group ^ rank_ref[0]] = own_ref[block]
        out_ref[(group + 1) ^ rank_ref[0]] = got_ref[block]


def hidden_pass(rank, own, got):
    blocks, rows, quarter = own.shape
    return pl.pallas_call(
        hidden_body,
        out_shape=jax.ShapeDtypeStruct((2 * blocks, rows, quarter), own.dtype),
        in_specs=[pl.BlockSpec(memory_space=pltpu.SMEM)] + [pl.BlockSpec(memory_space=pltpu.VMEM)] * 2,
        cost_estimate=LONG,
        name="hidden_pass",
    )(rank.reshape(1), own, got)


def total_body(*refs):
    base_ref, *part_refs, out_ref = refs
    first = 0
    for part_ref in part_refs:
        rows = pl.ds(first, part_ref.shape[0])
        out_ref[rows, :] = b16(f32(base_ref[rows, :]) + f32(part_ref[...]))
        first += part_ref.shape[0]


def total(base, *parts):
    return pl.pallas_call(
        total_body,
        out_shape=jax.ShapeDtypeStruct(base.shape, base.dtype),
        compiler_params=pltpu.CompilerParams(vmem_limit_bytes=LIMIT),
        cost_estimate=LONG,
        name="total",
    )(base, *parts)


def per_device(tokens, cotangent, gate_weights, tile_expert, w_gate, w_up):
    row_count = tokens.shape[1]
    tile_count = row_count // TILE
    cycle_size = lax.axis_size("expert")
    position = lax.axis_index("expert")
    before = (position + cycle_size - 1) % cycle_size
    group_count = lax.axis_size("dp")
    rank = lax.axis_index("dp")
    quarter = w_gate.shape[2]
    out_head = OUT_SHARE * tile_count
    first, mid, head = (share * tile_count for share in BACK_SHARE)
    tile, tile_grad = tokens[0], cotangent[0]

    def row_scale(group, place):
        owners = lax.dynamic_slice(tile_expert, (group, place * tile_count), (1, tile_count))
        weights = lax.dynamic_slice(gate_weights, (group, place * row_count), (1, row_count))
        routed = jnp.repeat(owners == position, TILE, axis=1, total_repeat_length=row_count)
        return jnp.where(routed, weights, jnp.zeros_like(weights)).reshape(row_count, 1)

    far = (rank + group_count // 2) % group_count
    scales = jnp.concatenate(
        [
            row_scale(group, place)
            for group, place in ((rank, position), (far, position), (rank, before), (far, before))
        ]
    )

    width = tile.shape[1]
    sent_at, kept_at = width, width + 2 * quarter
    near_top, near_low, far_message = pack(tile, tile_grad, out_head)
    x_top, x_low, y_tile = shifted(near_top, 1), shifted(near_low, 1), across(far_message)
    panels = (w_gate[0], w_up[0], within(w_gate[0]), within(w_up[0]))
    hid_hn, own_hn, other_hn, (part_hn,) = block_pass(
        (near_top, near_low), (kept_at, kept_at), scales, 0, panels, (row_count,)
    )
    x_top = after(x_top, hid_hn)
    x_sent = x_top[:, :kept_at]
    xy_top = across(x_sent)
    y_tile = after(y_tile, x_sent)
    y_sent = y_tile[out_head:]
    xy_low = shifted(y_sent, 1)
    x_low = after(x_low, y_sent)

    upper, middle, lower = mid, head - mid, row_count - head
    hid_mid, own_mid, other_mid, mid_parts = block_pass(
        (y_tile, x_top, x_low),
        (sent_at, kept_at, kept_at),
        scales,
        row_count,
        panels,
        (first, head - first, lower, upper, middle, lower),
    )
    first_hf, rest_hf, lower_hf, upper_pn, middle_pn, lower_pn = mid_parts
    first_home = across(first_hf)
    low_near = shifted(lower_pn, -1)
    xy_low, xy_top = after((xy_low, xy_top), hid_mid)
    hid_pf, own_pf, other_pf, (upper_pf, middle_pf, lower_pf) = block_pass(
        (xy_top, xy_low), (sent_at, sent_at), scales, 3 * row_count, panels, (upper, middle, lower)
    )
    low_far = shifted(lower_pf, -1)
    up_past, mid_past = across(upper_pf), across(middle_pf)
    hid_back = shifted(jnp.stack([hid_mid[row_count:], hid_pf]), -1)

    pieces = (near_top, near_low, y_tile, x_top, x_low, xy_top, xy_low)
    (sent,) = weight_pass(width, pieces, after((other_hn, other_mid, other_pf), first_home, low_near))
    got = within(sent)
    up_past, rest_hf = after((up_past, rest_hf), sent)
    rest_home = across(rest_hf)
    up_sum = b16(f32(upper_pn) + f32(up_past))
    up_back = shifted(up_sum, -1)
    mid_past, low_far, hid_back = after((mid_past, low_far, hid_back), up_sum)
    mid_sum = b16(f32(middle_pn) + f32(mid_past))
    mid_back = shifted(mid_sum, -1)
    low_sum = b16(f32(lower_hf) + f32(low_far))
    low_home = across(low_sum)
    hidden = b16(f32(jnp.stack([hid_hn, hid_mid[:row_count]])) + f32(hid_back))
    hidden = hidden_pass(rank, hidden[:, :, :quarter], within(hidden[:, :, quarter:]))
    got = after(got, hidden, mid_sum, low_sum)
    grad_gate, grad_up = weight_pass(width, pieces, (own_hn, own_mid, own_pf), got)
    base = total(after(part_hn, grad_gate), first_home, rest_home, low_near)
    d_tokens = total(base, up_back, mid_back, low_home)
    return (d_tokens[None], hidden, grad_gate[None], grad_up[None])


def solution(mesh):
    in_specs = (
        P("dp", "expert", None),
        P("dp", "expert", None),
        P(),
        P(),
        P("expert", None, "dp"),
        P("expert", None, "dp"),
    )
    out_specs = (
        P("dp", "expert", None),
        P(None, "expert", "dp"),
        P("expert", None, "dp"),
        P("expert", None, "dp"),
    )
    return jax.shard_map(
        per_device, mesh=mesh, in_specs=in_specs, out_specs=out_specs, check_vma=False
    )
```

time: 110 us -> 91.9 us (0.84)
  waiting for transfers between devices: 17.6 us -> 11.5 us
  other arithmetic: 9.2 us -> 3.36 us
  local copies, waits for them, and re-layouts: 13 us -> 8.09 us
  starting transfers between devices: 28.9 us -> 24.9 us
  Pallas kernels: 36.6 us -> 39.9 us
    pallas_call x1 -> x2, Pallas kernels: 9.65 us -> 15.1 us  [weight_pass(): pl.pallas_call(functools.partial(weight_body, len(pieces), len(grads)), g...]
    ppermute x9 -> x8, waiting for transfers between devices: 13.6 us -> 9.66 us  [shifted(): return lax.ppermute(value, 'expert', pairs)]
    convert_element_type x4, other arithmetic: 6.29 us -> 2.47 us  [b16(): return value.astype(jnp.bfloat16)]
    slice x2, local copies, waits for them, and re-layouts: 3.63 us -> 1.07 us  [the longest x1 1.02 us: per_device(): y_sent = y_tile[out_head:]]
    ppermute x8 -> x7, waiting for transfers between devices: 3.96 us -> 1.81 us  [across(): return lax.ppermute(value, 'dp', pairs)]
    ppermute x11 -> x4, starting transfers between devices: 2.71 us -> 0.67 us  [within(): return lax.ppermute(value, 'dp', pairs)]
    pallas_call x3 -> x4, Pallas kernels: 21.5 us -> 19.5 us  [the longest x3 17 us: block_pass(): pl.pallas_call(functools.partial(block_body, grad_starts, scale_start, co...]
    ppermute x9 -> x8, starting transfers between devices: 17.8 us -> 16.3 us  [shifted(): return lax.ppermute(value, 'expert', pairs)]
  transfers between devices with their start and end apart: 28 -> 19, of which waited for: 5 -> 4; matrix products, arithmetic and copies ran while one was open for 12% -> 8% of each run, Pallas kernels for 32% -> 41%
where the time goes in v3:
time: 91.9 us; the launch traced here: 91.1 us
  Pallas kernels  39.9 us (43%)
  starting transfers between devices  24.9 us (27%)
  waiting for transfers between devices  11.5 us (13%)
  local copies, waits for them, and re-layouts  8.09 us (9%)
  between operations  3.41 us (4%)
  other arithmetic  3.36 us (4%)
    pallas_call x3, Pallas kernels, block_pass(): pl.pallas_call(functools.partial(block_body, grad_starts, scale_start, co...  17 us
    ppermute x8, starting transfers between devices, shifted(): return lax.ppermute(value, 'expert', pairs)  16.3 us
    pallas_call x2, Pallas kernels, weight_pass(): pl.pallas_call(functools.partial(weight_body, len(pieces), len(grads)), g...  15.1 us
    ppermute x8, waiting for transfers between devices, shifted(): return lax.ppermute(value, 'expert', pairs)  9.66 us
    ppermute x7, starting transfers between devices, across(): return lax.ppermute(value, 'dp', pairs)  7.92 us
    unnamed x40, local copies, waits for them, and re-layouts  4.02 us
    pallas_call x2, Pallas kernels, total(): pl.pallas_call(total_body, out_shape=jax.ShapeDtypeStruct(base.shape, bas...  3.53 us
    pallas_call x1, Pallas kernels, pack(): pl.pallas_call(pack_body, out_shape=[jax.ShapeDtypeStruct((head, width +...  2.5 us
  transfers between devices with their start and end apart: 19, of which 4 were waited for; matrix products, arithmetic and copies ran while one was open for 8% of the time, Pallas kernels for 41%

profile of v3, /device:TPU:0, one launch (start us, length us, event | category | flops | bytes accessed | tf_op | source)
XLA Modules:
  0.0 91.1 jit_solution(12515864160554068305)
XLA Ops:
  0.6 0.5 collective-permute-start
  1.1 0.1 collective-permute-start.1
  1.2 2.5 %pack.1 = (bf16[80,4608]{1,0:T(8,128)(2,1)S(1)}, bf16[48,4608]{1,0:T(8,128)(2,1)}, bf16[128,4096]{1,0:T(8,128)(2,1)}) custom-call(bf16[128,3584]{1,0:T(8,128)(2,1)} %bitcast.37, bf16[128,1024]{1,0:T(8,128)(2,1)} %bitcast.38), custom_call_target="tpu_custom_call" | custom-call | bytes 2359296 | tf_op jit(solution)/shard_map/pack/pallas_call | solution.py:92
  3.7 2.9 %collective-permute-start.2 = (bf16[128,4096]{1,0:T(8,128)(2,1)}, bf16[128,4096]{1,0:T(8,128)(2,1)}, u32[]{:S(2)}, u32[]{:S(2)}) collective-permute-start(bf16[128,4096]{1,0:T(8,128)(2,1)} %get-tuple-element.119), channel_id=1, source_target_pairs={{0,16},{8,24},{16,0},{24,8},{1,17},{9,25},{17,1},{25,9},{2,18},{10... | collective-permute-start | bytes 3145736 | tf_op jit(solution)/shard_map/ppermute | solution.py:30
  6.7 1.5 %collective-permute-start.3 = (bf16[80,4608]{1,0:T(8,128)(2,1)S(1)}, bf16[80,4608]{1,0:T(8,128)(2,1)S(1)}, u32[]{:S(2)}, u32[]{:S(2)}) collective-permute-start(bf16[80,4608]{1,0:T(8,128)(2,1)S(1)} %get-tuple-element.116.refs_0_), channel_id=1, source_target_pairs={{0,1},{1,2},{2,3},{3,4},{4,5},{5,6},{6,7},{7,0},{8,9},{9,10},{10,1... | collective-permute-start | bytes 2211848 | tf_op jit(solution)/shard_map/ppermute | solution.py:24
  8.2 1.5 %collective-permute-start.4 = (bf16[48,4608]{1,0:T(8,128)(2,1)}, bf16[48,4608]{1,0:T(8,128)(2,1)}, u32[]{:S(2)}, u32[]{:S(2)}) collective-permute-start(bf16[48,4608]{1,0:T(8,128)(2,1)} %get-tuple-element.117.refs_1_), channel_id=1, source_target_pairs={{0,1},{1,2},{2,3},{3,4},{4,5},{5,6},{6,7},{7,0},{8,9},{9,10},{10,1... | collective-permute-start | bytes 1327112 | tf_op jit(solution)/shard_map/ppermute | solution.py:24
  9.7 1.4 %fusion.5 = (s32[1,1]{1,0:T(1,128)}, s32[1,1]{1,0:T(1,128)}, s32[1,1]{1,0:T(1,128)}, s32[1,1]{1,0:T(1,128)}) fusion(s32[4,8]{1,0:T(4,128)} %param.27, s32[]{:T(128)S(6)} %select_n.62, s32[]{:T(128)S(6)} %select_n.63, s32[]{:T(128)S(6)} %select_n.67, s32[]{:T(128)S(6)} %select_n.70), kind=kLoop, calls=%fused_computation.17 | loop fusion | bytes 48 | tf_op jit(solution)/shard_map/dynamic_slice | solution.py:246
  13.7 0.8 fusion
  14.5 0.9 copy.14.refs_2_.refs_3_
  15.4 0.0 collective-permute-done.refs_5_.refs_6_
  15.4 0.0 collective-permute-done.1.refs_6_.refs_7_
  15.4 1.5 %copy-done = bf16[1,3584,256]{2,1,0:T(8,128)(2,1)S(1)} copy-done((bf16[1,3584,256]{2,1,0:T(8,128)(2,1)S(1)}, bf16[1,3584,256]{2,1,0:T(8,128)(2,1)}, u32[]{:S(2)}) %copy-start) | copy-done | bytes 1835032
  16.9 1.5 %copy-done.2 = bf16[1,3584,256]{2,1,0:T(8,128)(2,1)S(1)} copy-done((bf16[1,3584,256]{2,1,0:T(8,128)(2,1)S(1)}, bf16[1,3584,256]{2,1,0:T(8,128)(2,1)}, u32[]{:S(2)}) %copy-start.2) | copy-done | bytes 1835032
  18.4 0.9 %copy-done.8 = f32[512,1]{1,0:T(8,128)S(1)} copy-done((f32[512,1]{1,0:T(8,128)S(1)}, f32[512,1]{1,0:T(8,128)}, u32[]{:S(2)}) %copy-start.8) | copy-done | bytes 2072
  19.3 5.0 %block_pass.3 = (bf16[128,512]{1,0:T(8,128)(2,1)S(1)}, bf16[128,512]{1,0:T(8,128)(2,1)S(1)}, bf16[128,512]{1,0:T(8,128)(2,1)S(1)}, bf16[128,3584]{1,0:T(8,128)(2,1)S(1)}) custom-call(bf16[80,4608]{1,0:T(8,128)(2,1)S(1)} %get-tuple-element.116.refs_0_, bf16[48,4608]{1,0:T(8,128)(2,1)} %get-tuple-element.117.refs_1_, f32[512,1]{1,0:T(8,128)S(1)} %copy-done.8, ...), custom_call_target="tpu_custom_call" | custom-call | flops 1879048192 | bytes 1835008 | tf_op jit(solution)/shard_map/block_pass/pallas_call | solution.py:150
  24.4 0.0 copy-start.13
  24.4 0.0 copy-start.1
  24.4 4.4 %collective-permute-done.3.refs_1_.refs_3_ = bf16[80,4608]{1,0:T(8,128)(2,1)S(1)} collective-permute-done((bf16[80,4608]{1,0:T(8,128)(2,1)S(1)}, bf16[80,4608]{1,0:T(8,128)(2,1)S(1)}, u32[]{:S(2)}, u32[]{:S(2)}) %collective-permute-start.3) | collective-permute-done | bytes 737312 | tf_op jit(solution)/shard_map/ppermute | solution.py:24
  28.8 0.4 collective-permute-start.6
  29.2 1.8 %collective-permute-done.2.refs_0_.refs_2_ = bf16[128,4096]{1,0:T(8,128)(2,1)} collective-permute-done((bf16[128,4096]{1,0:T(8,128)(2,1)}, bf16[128,4096]{1,0:T(8,128)(2,1)}, u32[]{:S(2)}, u32[]{:S(2)}) %collective-permute-start.2) | collective-permute-done | bytes 1048608 | tf_op jit(solution)/shard_map/ppermute | solution.py:30
  31.0 1.0 %slice.67 = bf16[48,4096]{1,0:T(8,128)(2,1)S(1)} slice(bf16[128,4096]{1,0:T(8,128)(2,1)} %collective-permute-done.2.refs_0_.refs_2_), slice={[80:128], [0:4096]} | slice | bytes 786432 | tf_op jit(solution)/shard_map/slice | solution.py:271
  32.0 2.1 %collective-permute-start.5 = (bf16[48,4096]{1,0:T(8,128)(2,1)S(1)}, bf16[48,4096]{1,0:T(8,128)(2,1)S(1)}, u32[]{:S(2)}, u32[]{:S(2)}) collective-permute-start(bf16[48,4096]{1,0:T(8,128)(2,1)S(1)} %slice.67), channel_id=1, source_target_pairs={{0,1},{1,2},{2,3},{3,4},{4,5},{5,6},{6,7},{7,0},{8,9},{9,10},{10,1... | collective-permute-start | bytes 1179656 | tf_op jit(solution)/shard_map/ppermute | solution.py:24
  34.1 3.9 %collective-permute-done.4.refs_2_.refs_4_ = bf16[48,4608]{1,0:T(8,128)(2,1)} collective-permute-done((bf16[48,4608]{1,0:T(8,128)(2,1)}, bf16[48,4608]{1,0:T(8,128)(2,1)}, u32[]{:S(2)}, u32[]{:S(2)}) %collective-permute-start.4) | collective-permute-done | bytes 442400 | tf_op jit(solution)/shard_map/ppermute | solution.py:24
  38.0 6.9 %block_pass.4 = (bf16[256,512]{1,0:T(8,128)(2,1)S(1)}, bf16[256,512]{1,0:T(8,128)(2,1)S(1)}, bf16[256,512]{1,0:T(8,128)(2,1)S(1)}, bf16[32,3584]{1,0:T(8,128)(2,...) custom-call(bf16[128,4096]{1,0:T(8,128)(2,1)} %collective-permute-do, ...), custom_call_target="tpu_custom_call" | custom-call | flops 3758096384 | bytes 3670016 | tf_op jit(solution)/shard_map/block_pass/pallas_call | solution.py:150
  44.9 1.7 %collective-permute-start.8 = (bf16[48,3584]{1,0:T(8,128)(2,1)S(1)}, bf16[48,3584]{1,0:T(8,128)(2,1)S(1)}, u32[]{:S(2)}, u32[]{:S(2)}) collective-permute-start(bf16[48,3584]{1,0:T(8,128)(2,1)S(1)} %get-tuple-element.134), channel_id=1, source_target_pairs={{0,7},{1,0},{2,1},{3,2},{4,3},{5,4},{6,5},{7,6},{8,15},{9,8},{10,9... | collective-permute-start | bytes 1032200 | tf_op jit(solution)/shard_map/ppermute | solution.py:24
  46.6 0.0 copy-start.4
  46.6 5.1 %block_pass.5 = (bf16[128,512]{1,0:T(8,128)(2,1)S(1)}, bf16[128,512]{1,0:T(8,128)(2,1)S(1)}, bf16[128,512]{1,0:T(8,128)(2,1)S(1)}, bf16[48,3584]{1,0:T(8,128)(2,...) custom-call(bf16[80,4096]{1,0:T(8,128)(2,1)S(1)} %collective-permute-done.6.refs_0_.refs_5_, ...), custom_call_target="tpu_custom_call" | custom-call | flops 1879048192 | bytes 1835008 | tf_op jit(solution)/shard_map/block_pass/pallas_call | solution.py:150
  51.8 2.1 %collective-permute-start.13 = (bf16[48,3584]{1,0:T(8,128)(2,1)S(1)}, bf16[48,3584]{1,0:T(8,128)(2,1)S(1)}, u32[]{:S(2)}, u32[]{:S(2)}) collective-permute-start(bf16[48,3584]{1,0:T(8,128)(2,1)S(1)} %get-tuple-element.142), channel_id=1, source_target_pairs={{0,16},{8,24},{16,0},{24,8},{1,17},{9,25},{17,1},{25,9},{2,18},{10... | collective-permute-start | bytes 1032200 | tf_op jit(solution)/shard_map/ppermute | solution.py:30
  54.0 3.6 %collective-permute-start.12 = (bf16[2,128,512]{2,1,0:T(8,128)(2,1)S(1)}, bf16[2,128,512]{2,1,0:T(8,128)(2,1)S(1)}, u32[]{:S(2)}, u32[]{:S(2)}) collective-permute-start(bf16[2,128,512]{2,1,0:T(8,128)(2,1)S(1)} %pad_maximum_fusion), channel_id=1, source_target_pairs={{0,7},{1,0},{2,1},{3,2},{4,3},{5,4},{6,5},{7,6},{8,15},{9,8},{10,9... | collective-permute-start | bytes 786440 | tf_op jit(solution)/shard_map/ppermute | solution.py:24
  57.5 0.1 collective-permute-start.11
  57.6 0.5 collective-permute-start.10
  58.1 7.1 %weight_pass.2 = bf16[3584,512]{1,0:T(8,128)(2,1)} custom-call(bf16[80,4608]{1,0:T(8,128)(2,1)S(1)} %get-tuple-element.116.refs_0_, bf16[48,4608]{1,0:T(8,128)(2,1)} %get-tuple-element.117.refs_1_, bf16[128,4096]{1,0:T(8,128)(2,1)} %collective-permute-done.2.refs_0_.refs_2_, bf16[80,4608]{1,0:T(8,128)(2,1)S(1)} %collective-permute-done.3.refs_1_.refs_3_, ...), custom_call_target="tpu_custom_call" | custom-call | flops 1879048192 | bytes 11010048 | tf_op jit(solution)/shard_map/weight_pass/pallas_call | solution.py:181
  65.2 0.1 collective-permute-start.9
  65.3 0.8 add_convert_fusion.1
  66.1 0.7 collective-permute-start.16
  66.8 1.4 %collective-permute-done.11 = bf16[48,3584]{1,0:T(8,128)(2,1)S(1)} collective-permute-done((bf16[48,3584]{1,0:T(8,128)(2,1)S(1)}, bf16[48,3584]{1,0:T(8,128)(2,1)S(1)}, u32[]{:S(2)}, u32[]{:S(2)}) %collective-permute-start.11) | collective-permute-done | bytes 344096 | tf_op jit(solution)/shard_map/ppermute | solution.py:24
  68.1 0.1 add_convert_fusion.2
  68.2 0.7 fusion.4
  68.9 1.0 %collective-permute-start.15 = (bf16[48,3584]{1,0:T(8,128)(2,1)}, bf16[48,3584]{1,0:T(8,128)(2,1)}, u32[]{:S(2)}, u32[]{:S(2)}) collective-permute-start(bf16[48,3584]{1,0:T(8,128)(2,1)} %get-tuple-element.153), channel_id=1, source_target_pairs={{0,16},{8,24},{16,0},{24,8},{1,17},{9,25},{17,1},{25,9},{2,18},{10... | collective-permute-start | bytes 1032200 | tf_op jit(solution)/shard_map/ppermute | solution.py:30
  69.9 0.8 add_convert_fusion
  70.7 1.0 %collective-permute-start.18 = (bf16[48,3584]{1,0:T(8,128)(2,1)}, bf16[48,3584]{1,0:T(8,128)(2,1)}, u32[]{:S(2)}, u32[]{:S(2)}) collective-permute-start(bf16[48,3584]{1,0:T(8,128)(2,1)} %add_convert_fusion), channel_id=1, source_target_pairs={{0,16},{8,24},{16,0},{24,8},{1,17},{9,25},{17,1},{25,9},{2,18},{10... | collective-permute-start | bytes 1032200 | tf_op jit(solution)/shard_map/ppermute | solution.py:30
  71.7 0.8 add_convert_fusion.3
  72.5 5.2 %collective-permute-start.17 = (bf16[32,3584]{1,0:T(8,128)(2,1)}, bf16[32,3584]{1,0:T(8,128)(2,1)}, u32[]{:S(2)}, u32[]{:S(2)}) collective-permute-start(bf16[32,3584]{1,0:T(8,128)(2,1)} %add_convert_fusion.3), channel_id=1, source_target_pairs={{0,7},{1,0},{2,1},{3,2},{4,3},{5,4},{6,5},{7,6},{8,15},{9,8},{10,9... | collective-permute-start | bytes 688136 | tf_op jit(solution)/shard_map/ppermute | solution.py:24
  77.7 1.8 %hidden_pass.1 = bf16[4,128,256]{2,1,0:T(8,128)(2,1)} custom-call(s32[1]{0:T(128)} %bitcast.13.rank_ref, bf16[2,128,256]{2,1,0:T(8,128)(2,1)} %get-tuple-element.156.own_ref, bf16[2,128,256]{2,1,0:T(8,128)(2,1)} %copy-done.19), custom_call_target="tpu_custom_call" | custom-call | flops 999999995904 | bytes 1000000000 | tf_op jit(solution)/shard_map/hidden_pass/pallas_call | solution.py:204
  79.5 0.0 copy-start.14
  79.5 8.0 %weight_pass.3 = (bf16[3584,256]{1,0:T(8,128)(2,1)}, bf16[3584,256]{1,0:T(8,128)(2,1)}) custom-call(bf16[80,4608]{1,0:T(8,128)(2,1)S(1)} %get-tuple-element.116.refs_0_, bf16[48,4608]{1,0:T(8,128)(2,1)} %get-tuple-element.117.refs_1_, bf16[128,4096]{1,0:T(8,128)(2,1)} %collective-permute-done.2.refs_0_.refs_2_, ...), custom_call_target="tpu_custom_call" | custom-call | flops 1879048192 | bytes 11010048 | tf_op jit(solution)/shard_map/weight_pass/pallas_call | solution.py:181
  87.6 1.2 %total.2.refs_0_ = bf16[128,3584]{1,0:T(8,128)(2,1)S(1)} custom-call(bf16[128,3584]{1,0:T(8,128)(2,1)S(1)} %copy-done.14, bf16[32,3584]{1,0:T(8,128)(2,1)S(1)} %copy-done.18, bf16[48,3584]{1,0:T(8,128)(2,1)} %collective-permute-done.15.refs_2_, bf16[48,3584]{1,0:T(8,128)(2,1)S(1)} %copy-done.16), custom_call_target="tpu_custom_call" | custom-call | flops 999999995904 | bytes 1000000000 | tf_op jit(solution)/shard_map/total/pallas_call | solution.py:223
  88.8 2.3 %total.3 = bf16[128,3584]{1,0:T(8,128)(2,1)} custom-call(bf16[128,3584]{1,0:T(8,128)(2,1)S(1)} %total.2.refs_0_, bf16[48,3584]{1,0:T(8,128)(2,1)} %collective-permute-done.16.refs_1_, bf16[32,3584]{1,0:T(8,128)(2,1)} %collective-permute-done.17.refs_2_, bf16[48,3584]{1,0:T(8,128)(2,1)} %collective-permute-done.18.refs_3_), custom_call_target="tpu_custom_call" | custom-call | flops 999999995904 | bytes 1000000000 | tf_op jit(solution)/shard_map/total/pallas_call | solution.py:223
  (52 shorter events, 0.2 us)
Async XLA Ops:
  0.6 14.8 %collective-permute-start = (bf16[3584,256]{1,0:T(8,128)(2,1)}, bf16[3584,256]{1,0:T(8,128)(2,1)S(1)}, u32[]{:S(2)}, u32[]{:S(2)}) collective-permute-start(bf16[3584,256]{1,0:T(8,128)(2,1)} %bitcast.27), channel_id=1, source_target_pairs={{0,8},{8,0},{16,24},{24,16},{1,9},{9,1},{17,25},{25,17},{2,10},{10... | collective-permute-start | bytes 5505032 | tf_op jit(solution)/shard_map/ppermute | solution.py:36
  1.1 14.2 %collective-permute-start.1 = (bf16[3584,256]{1,0:T(8,128)(2,1)}, bf16[3584,256]{1,0:T(8,128)(2,1)}, u32[]{:S(2)}, u32[]{:S(2)}) collective-permute-start(bf16[3584,256]{1,0:T(8,128)(2,1)} %bitcast.31), channel_id=1, source_target_pairs={{0,8},{8,0},{16,24},{24,16},{1,9},{9,1},{17,25},{25,17},{2,10},{10... | collective-permute-start | bytes 5505032 | tf_op jit(solution)/shard_map/ppermute | solution.py:36
  3.7 27.2 %collective-permute-start.2 = (bf16[128,4096]{1,0:T(8,128)(2,1)}, bf16[128,4096]{1,0:T(8,128)(2,1)}, u32[]{:S(2)}, u32[]{:S(2)}) collective-permute-start(bf16[128,4096]{1,0:T(8,128)(2,1)} %get-tuple-element.119), channel_id=1, source_target_pairs={{0,16},{8,24},{16,0},{24,8},{1,17},{9,25},{17,1},{25,9},{2,18},{10... | collective-permute-start | bytes 3145736 | tf_op jit(solution)/shard_map/ppermute | solution.py:30
  6.7 22.1 %collective-permute-start.3 = (bf16[80,4608]{1,0:T(8,128)(2,1)S(1)}, bf16[80,4608]{1,0:T(8,128)(2,1)S(1)}, u32[]{:S(2)}, u32[]{:S(2)}) collective-permute-start(bf16[80,4608]{1,0:T(8,128)(2,1)S(1)} %get-tuple-element.116.refs_0_), channel_id=1, source_target_pairs={{0,1},{1,2},{2,3},{3,4},{4,5},{5,6},{6,7},{7,0},{8,9},{9,10},{10,1... | collective-permute-start | bytes 2211848 | tf_op jit(solution)/shard_map/ppermute | solution.py:24
  8.2 29.8 %collective-permute-start.4 = (bf16[48,4608]{1,0:T(8,128)(2,1)}, bf16[48,4608]{1,0:T(8,128)(2,1)}, u32[]{:S(2)}, u32[]{:S(2)}) collective-permute-start(bf16[48,4608]{1,0:T(8,128)(2,1)} %get-tuple-element.117.refs_1_), channel_id=1, source_target_pairs={{0,1},{1,2},{2,3},{3,4},{4,5},{5,6},{6,7},{7,0},{8,9},{9,10},{10,1... | collective-permute-start | bytes 1327112 | tf_op jit(solution)/shard_map/ppermute | solution.py:24
  15.4 1.5 %copy-start = (bf16[1,3584,256]{2,1,0:T(8,128)(2,1)S(1)}, bf16[1,3584,256]{2,1,0:T(8,128)(2,1)}, u32[]{:S(2)}) copy-start(bf16[1,3584,256]{2,1,0:T(8,128)(2,1)} %param.28) | copy-start | bytes 5505028
  16.9 1.5 %copy-start.2 = (bf16[1,3584,256]{2,1,0:T(8,128)(2,1)S(1)}, bf16[1,3584,256]{2,1,0:T(8,128)(2,1)}, u32[]{:S(2)}) copy-start(bf16[1,3584,256]{2,1,0:T(8,128)(2,1)} %param.29) | copy-start | bytes 5505028
  18.4 0.9 %copy-start.8 = (f32[512,1]{1,0:T(8,128)S(1)}, f32[512,1]{1,0:T(8,128)}, u32[]{:S(2)}) copy-start(f32[512,1]{1,0:T(8,128)} %copy.14.refs_2_.refs_3_) | copy-start | bytes 6148
  19.3 18.7 %copy-start.3 = (bf16[1,3584,256]{2,1,0:T(8,128)(2,1)S(1)}, bf16[1,3584,256]{2,1,0:T(8,128)(2,1)}, u32[]{:S(2)}) copy-start(bf16[1,3584,256]{2,1,0:T(8,128)(2,1)} %param.29) | copy-start | bytes 5505028
  24.4 9.7 %copy-start.13 = (bf16[128,3584]{1,0:T(8,128)(2,1)}, bf16[128,3584]{1,0:T(8,128)(2,1)S(1)}, u32[]{:S(2)}) copy-start(bf16[128,3584]{1,0:T(8,128)(2,1)S(1)} %get-tuple-element.152.refs_0_) | copy-start | bytes 2752516
  24.4 13.6 %copy-start.1 = (bf16[1,3584,256]{2,1,0:T(8,128)(2,1)S(1)}, bf16[1,3584,256]{2,1,0:T(8,128)(2,1)}, u32[]{:S(2)}) copy-start(bf16[1,3584,256]{2,1,0:T(8,128)(2,1)} %param.28) | copy-start | bytes 5505028
  28.8 17.8 %collective-permute-start.6 = (bf16[80,4096]{1,0:T(8,128)(2,1)S(1)}, bf16[80,4096]{1,0:T(8,128)(2,1)S(1)}, u32[]{:S(2)}, u32[]{:S(2)}) collective-permute-start(bf16[80,4096]{1,0:T(8,128)(2,1)S(1)} %slice.66), channel_id=1, source_target_pairs={{0,16},{8,24},{16,0},{24,8},{1,17},{9,25},{17,1},{25,9},{2,18},{10... | collective-permute-start | bytes 1966088 | tf_op jit(solution)/shard_map/ppermute | solution.py:30
  32.0 14.6 %collective-permute-start.5 = (bf16[48,4096]{1,0:T(8,128)(2,1)S(1)}, bf16[48,4096]{1,0:T(8,128)(2,1)S(1)}, u32[]{:S(2)}, u32[]{:S(2)}) collective-permute-start(bf16[48,4096]{1,0:T(8,128)(2,1)S(1)} %slice.67), channel_id=1, source_target_pairs={{0,1},{1,2},{2,3},{3,4},{4,5},{5,6},{6,7},{7,0},{8,9},{9,10},{10,1... | collective-permute-start | bytes 1179656 | tf_op jit(solution)/shard_map/ppermute | solution.py:24
  44.9 6.9 %copy-start.9 = (bf16[256,512]{1,0:T(8,128)(2,1)}, bf16[256,512]{1,0:T(8,128)(2,1)S(1)}, u32[]{:S(2)}) copy-start(bf16[256,512]{1,0:T(8,128)(2,1)S(1)} %get-tuple-element.128.refs_8_) | copy-start | bytes 786436
  44.9 9.0 %collective-permute-start.8 = (bf16[48,3584]{1,0:T(8,128)(2,1)S(1)}, bf16[48,3584]{1,0:T(8,128)(2,1)S(1)}, u32[]{:S(2)}, u32[]{:S(2)}) collective-permute-start(bf16[48,3584]{1,0:T(8,128)(2,1)S(1)} %get-tuple-element.134), channel_id=1, source_target_pairs={{0,7},{1,0},{2,1},{3,2},{4,3},{5,4},{6,5},{7,6},{8,15},{9,8},{10,9... | collective-permute-start | bytes 1032200 | tf_op jit(solution)/shard_map/ppermute | solution.py:24
  46.6 7.3 %collective-permute-start.7 = (bf16[32,3584]{1,0:T(8,128)(2,1)S(1)}, bf16[32,3584]{1,0:T(8,128)(2,1)S(1)}, u32[]{:S(2)}, u32[]{:S(2)}) collective-permute-start(bf16[32,3584]{1,0:T(8,128)(2,1)S(1)} %get-tuple-element.133), channel_id=1, source_target_pairs={{0,16},{8,24},{16,0},{24,8},{1,17},{9,25},{17,1},{25,9},{2,18},{10... | collective-permute-start | bytes 688136 | tf_op jit(solution)/shard_map/ppermute | solution.py:30
  46.6 11.5 %copy-start.6 = (bf16[48,4096]{1,0:T(8,128)(2,1)}, bf16[48,4096]{1,0:T(8,128)(2,1)S(1)}, u32[]{:S(2)}) copy-start(bf16[48,4096]{1,0:T(8,128)(2,1)S(1)} %collective-permute-done.5.refs_1_.refs_6_) | copy-start | bytes 1179652
  46.6 11.5 %copy-start.4 = (bf16[80,4096]{1,0:T(8,128)(2,1)}, bf16[80,4096]{1,0:T(8,128)(2,1)S(1)}, u32[]{:S(2)}) copy-start(bf16[80,4096]{1,0:T(8,128)(2,1)S(1)} %collective-permute-done.6.refs_0_.refs_5_) | copy-start | bytes 1966084
  51.8 13.4 %copy-start.11 = (bf16[128,512]{1,0:T(8,128)(2,1)}, bf16[128,512]{1,0:T(8,128)(2,1)S(1)}, u32[]{:S(2)}) copy-start(bf16[128,512]{1,0:T(8,128)(2,1)S(1)} %get-tuple-element.129.refs_9_) | copy-start | bytes 393220
  51.8 13.5 %collective-permute-start.13 = (bf16[48,3584]{1,0:T(8,128)(2,1)S(1)}, bf16[48,3584]{1,0:T(8,128)(2,1)S(1)}, u32[]{:S(2)}, u32[]{:S(2)}) collective-permute-start(bf16[48,3584]{1,0:T(8,128)(2,1)S(1)} %get-tuple-element.142), channel_id=1, source_target_pairs={{0,16},{8,24},{16,0},{24,8},{1,17},{9,25},{17,1},{25,9},{2,18},{10... | collective-permute-start | bytes 1032200 | tf_op jit(solution)/shard_map/ppermute | solution.py:30
  53.9 11.3 %copy-start.17 = (bf16[32,3584]{1,0:T(8,128)(2,1)}, bf16[32,3584]{1,0:T(8,128)(2,1)S(1)}, u32[]{:S(2)}) copy-start(bf16[32,3584]{1,0:T(8,128)(2,1)S(1)} %collective-permute-done.7.refs_1_) | copy-start | bytes 688132
  53.9 11.3 %copy-start.15 = (bf16[48,3584]{1,0:T(8,128)(2,1)}, bf16[48,3584]{1,0:T(8,128)(2,1)S(1)}, u32[]{:S(2)}) copy-start(bf16[48,3584]{1,0:T(8,128)(2,1)S(1)} %collective-permute-done.8.refs_3_) | copy-start | bytes 1032196
  54.0 12.8 %collective-permute-start.12 = (bf16[2,128,512]{2,1,0:T(8,128)(2,1)S(1)}, bf16[2,128,512]{2,1,0:T(8,128)(2,1)S(1)}, u32[]{:S(2)}, u32[]{:S(2)}) collective-permute-start(bf16[2,128,512]{2,1,0:T(8,128)(2,1)S(1)} %pad_maximum_fusion), channel_id=1, source_target_pairs={{0,7},{1,0},{2,1},{3,2},{4,3},{5,4},{6,5},{7,6},{8,15},{9,8},{10,9... | collective-permute-start | bytes 786440 | tf_op jit(solution)/shard_map/ppermute | solution.py:24
  57.5 10.6 %collective-permute-start.11 = (bf16[48,3584]{1,0:T(8,128)(2,1)S(1)}, bf16[48,3584]{1,0:T(8,128)(2,1)S(1)}, u32[]{:S(2)}, u32[]{:S(2)}) collective-permute-start(bf16[48,3584]{1,0:T(8,128)(2,1)S(1)} %get-tuple-element.139), channel_id=1, source_target_pairs={{0,7},{1,0},{2,1},{3,2},{4,3},{5,4},{6,5},{7,6},{8,15},{9,8},{10,9... | collective-permute-start | bytes 1032200 | tf_op jit(solution)/shard_map/ppermute | solution.py:24
  57.6 9.2 %collective-permute-start.10 = (bf16[32,3584]{1,0:T(8,128)(2,1)S(1)}, bf16[32,3584]{1,0:T(8,128)(2,1)S(1)}, u32[]{:S(2)}, u32[]{:S(2)}) collective-permute-start(bf16[32,3584]{1,0:T(8,128)(2,1)S(1)} %get-tuple-element.138), channel_id=1, source_target_pairs={{0,16},{8,24},{16,0},{24,8},{1,17},{9,25},{17,1},{25,9},{2,18},{10... | collective-permute-start | bytes 688136 | tf_op jit(solution)/shard_map/ppermute | solution.py:30
  65.2 14.3 %collective-permute-start.9 = (bf16[3584,512]{1,0:T(8,128)(2,1)}, bf16[3584,512]{1,0:T(8,128)(2,1)}, u32[]{:S(2)}, u32[]{:S(2)}) collective-permute-start(bf16[3584,512]{1,0:T(8,128)(2,1)} %weight_pass.2), channel_id=1, source_target_pairs={{0,8},{8,0},{16,24},{24,16},{1,9},{9,1},{17,25},{25,17},{2,10},{10... | collective-permute-start | bytes 11010056 | tf_op jit(solution)/shard_map/ppermute | solution.py:36
  66.1 22.7 %collective-permute-start.16 = (bf16[48,3584]{1,0:T(8,128)(2,1)}, bf16[48,3584]{1,0:T(8,128)(2,1)}, u32[]{:S(2)}, u32[]{:S(2)}) collective-permute-start(bf16[48,3584]{1,0:T(8,128)(2,1)} %add_convert_fusion.1), channel_id=1, source_target_pairs={{0,7},{1,0},{2,1},{3,2},{4,3},{5,4},{6,5},{7,6},{8,15},{9,8},{10,9... | collective-permute-start | bytes 1032200 | tf_op jit(solution)/shard_map/ppermute | solution.py:24
  68.9 3.6 %collective-permute-start.14 = (bf16[2,128,256]{2,1,0:T(8,128)(2,1)S(1)}, bf16[2,128,256]{2,1,0:T(8,128)(2,1)S(1)}, u32[]{:S(2)}, u32[]{:S(2)}) collective-permute-start(bf16[2,128,256]{2,1,0:T(8,128)(2,1)S(1)} %get-tuple-element.155), channel_id=1, source_target_pairs={{0,8},{8,0},{16,24},{24,16},{1,9},{9,1},{17,25},{25,17},{2,10},{10... | collective-permute-start | bytes 393224 | tf_op jit(solution)/shard_map/ppermute | solution.py:36
  68.9 18.7 %collective-permute-start.15 = (bf16[48,3584]{1,0:T(8,128)(2,1)}, bf16[48,3584]{1,0:T(8,128)(2,1)}, u32[]{:S(2)}, u32[]{:S(2)}) collective-permute-start(bf16[48,3584]{1,0:T(8,128)(2,1)} %get-tuple-element.153), channel_id=1, source_target_pairs={{0,16},{8,24},{16,0},{24,8},{1,17},{9,25},{17,1},{25,9},{2,18},{10... | collective-permute-start | bytes 1032200 | tf_op jit(solution)/shard_map/ppermute | solution.py:30
  70.7 18.1 %collective-permute-start.18 = (bf16[48,3584]{1,0:T(8,128)(2,1)}, bf16[48,3584]{1,0:T(8,128)(2,1)}, u32[]{:S(2)}, u32[]{:S(2)}) collective-permute-start(bf16[48,3584]{1,0:T(8,128)(2,1)} %add_convert_fusion), channel_id=1, source_target_pairs={{0,16},{8,24},{16,0},{24,8},{1,17},{9,25},{17,1},{25,9},{2,18},{10... | collective-permute-start | bytes 1032200 | tf_op jit(solution)/shard_map/ppermute | solution.py:30
  72.5 5.2 %copy-start.19 = (bf16[2,128,256]{2,1,0:T(8,128)(2,1)}, bf16[2,128,256]{2,1,0:T(8,128)(2,1)S(1)}, u32[]{:S(2)}) copy-start(bf16[2,128,256]{2,1,0:T(8,128)(2,1)S(1)} %collective-permute-done.14.got_ref) | copy-start | bytes 393220
  72.5 16.3 %collective-permute-start.17 = (bf16[32,3584]{1,0:T(8,128)(2,1)}, bf16[32,3584]{1,0:T(8,128)(2,1)}, u32[]{:S(2)}, u32[]{:S(2)}) collective-permute-start(bf16[32,3584]{1,0:T(8,128)(2,1)} %add_convert_fusion.3), channel_id=1, source_target_pairs={{0,7},{1,0},{2,1},{3,2},{4,3},{5,4},{6,5},{7,6},{8,15},{9,8},{10,9... | collective-permute-start | bytes 688136 | tf_op jit(solution)/shard_map/ppermute | solution.py:24
  77.7 1.8 %copy-start.5 = (bf16[80,4096]{1,0:T(8,128)(2,1)S(1)}, bf16[80,4096]{1,0:T(8,128)(2,1)}, u32[]{:S(2)}) copy-start(bf16[80,4096]{1,0:T(8,128)(2,1)} %copy-done.4) | copy-start | bytes 1966084
  77.7 1.8 %copy-start.7 = (bf16[48,4096]{1,0:T(8,128)(2,1)S(1)}, bf16[48,4096]{1,0:T(8,128)(2,1)}, u32[]{:S(2)}) copy-start(bf16[48,4096]{1,0:T(8,128)(2,1)} %copy-done.6) | copy-start | bytes 1179652
  77.7 1.8 %copy-start.10 = (bf16[256,512]{1,0:T(8,128)(2,1)S(1)}, bf16[256,512]{1,0:T(8,128)(2,1)}, u32[]{:S(2)}) copy-start(bf16[256,512]{1,0:T(8,128)(2,1)} %copy-done.9) | copy-start | bytes 786436
  77.7 1.8 %copy-start.12 = (bf16[128,512]{1,0:T(8,128)(2,1)S(1)}, bf16[128,512]{1,0:T(8,128)(2,1)}, u32[]{:S(2)}) copy-start(bf16[128,512]{1,0:T(8,128)(2,1)} %copy-done.11) | copy-start | bytes 393220
  79.5 8.1 %copy-start.14 = (bf16[128,3584]{1,0:T(8,128)(2,1)S(1)}, bf16[128,3584]{1,0:T(8,128)(2,1)}, u32[]{:S(2)}) copy-start(bf16[128,3584]{1,0:T(8,128)(2,1)} %copy-done.13) | copy-start | bytes 2752516
  79.5 8.1 %copy-start.16 = (bf16[48,3584]{1,0:T(8,128)(2,1)S(1)}, bf16[48,3584]{1,0:T(8,128)(2,1)}, u32[]{:S(2)}) copy-start(bf16[48,3584]{1,0:T(8,128)(2,1)} %copy-done.15) | copy-start | bytes 1032196
  79.5 8.1 %copy-start.18 = (bf16[32,3584]{1,0:T(8,128)(2,1)S(1)}, bf16[32,3584]{1,0:T(8,128)(2,1)}, u32[]{:S(2)}) copy-start(bf16[32,3584]{1,0:T(8,128)(2,1)} %copy-done.17) | copy-start | bytes 688132

commit v4 on v3

v4 whole, which is shorter than its diff:
```python
import functools

import jax
import jax.numpy as jnp
from jax import lax
from jax.experimental import pallas as pl
from jax.experimental.pallas import tpu as pltpu
from jax.sharding import PartitionSpec as P

TILE = 128
OUT_SHARE = 80
BACK_SHARE = (48, 64)
LIMIT = 20 * 2**20
LONG = pl.CostEstimate(flops=10**12, bytes_accessed=10**9, transcendentals=0)


def work(flops, moved):
    return pl.CostEstimate(flops=flops, bytes_accessed=moved, transcendentals=0)


def shifted(value, steps):
    count = lax.axis_size("expert")
    pairs = [(source, (source + steps) % count) for source in range(count)]
    return lax.ppermute(value, "expert", pairs)


def across(value):
    count = lax.axis_size("dp")
    pairs = [(source, (source + count // 2) % count) for source in range(count)]
    return lax.ppermute(value, "dp", pairs)


def within(value):
    count = lax.axis_size("dp")
    pairs = [(source, source + 1 - 2 * (source % 2)) for source in range(count)]
    return lax.ppermute(value, "dp", pairs)


def after(values, *earlier):
    return lax.optimization_barrier((values, earlier))[0]


def f32(value):
    return value.astype(jnp.float32)


def b16(value):
    return value.astype(jnp.bfloat16)


def column_step(width):
    for step in (512, 256, 128):
        if width % step == 0:
            return step
    return width


def contract(left, right, left_axis, right_axis):
    return lax.dot_general(
        left, right, (((left_axis,), (right_axis,)), ((), ())), preferred_element_type=jnp.float32
    )


def joined(refs, columns):
    return jnp.concatenate([ref[:, columns] for ref in refs], axis=0)


def pack_body(tile_ref, grads_ref, top_ref, low_ref, far_ref):
    rank = lax.axis_index("dp")
    side, core = rank // 2, rank % 2
    width = tile_ref.shape[1]
    quarter = grads_ref.shape[1] // 4
    head, both = top_ref.shape[0], 2 * quarter
    top, low = slice(0, head), slice(head, tile_ref.shape[0])
    parts = [
        grads_ref[:, pl.ds(pl.multiple_of((2 * which + first) * quarter, quarter), quarter)]
        for which in (1 - side, side)
        for first in (core, 1 - core)
    ]
    sent, kept = jnp.concatenate(parts[:2], axis=1), jnp.concatenate(parts[2:], axis=1)
    tile = tile_ref[...]
    far_ref[:, :width] = tile
    far_ref[:, width:] = sent
    top_ref[:, :width] = tile[top]
    top_ref[:, width : width + both] = sent[top]
    top_ref[:, width + both :] = kept[top]
    low_ref[:, :width] = tile[low]
    low_ref[:, width:] = kept[low]


def pack(tile, grads, head):
    rows, width = tile.shape
    whole = grads.shape[1]
    return pl.pallas_call(
        pack_body,
        out_shape=[
            jax.ShapeDtypeStruct((head, width + whole), tile.dtype),
            jax.ShapeDtypeStruct((rows - head, width + whole // 2), tile.dtype),
            jax.ShapeDtypeStruct((rows, width + whole // 2), tile.dtype),
        ],
        compiler_params=pltpu.CompilerParams(vmem_limit_bytes=LIMIT),
        cost_estimate=work(0, 4 * rows * (width + whole)),
        name="pack",
    )(
        pltpu.with_memory_space_constraint(tile, pltpu.HBM),
        pltpu.with_memory_space_constraint(grads, pltpu.HBM),
    )


def block_body(grad_starts, scale_start, step, carried, *refs):
    pieces, refs = refs[: len(grad_starts)], refs[len(grad_starts) :]
    scale_ref, *panels = refs[:5]
    carry_refs, refs = refs[5 : 5 + carried], refs[5 + carried :]
    hidden_ref, own_ref, other_ref, *part_refs = refs
    width, quarter = panels[0].shape
    rows = own_ref.shape[0]
    kept = hidden_ref.shape[0] - rows
    for carry_ref in carry_refs:
        hidden_ref[:kept, :] = carry_ref[pl.ds(carry_ref.shape[0] - kept, kept), :]
    values = joined(pieces, pl.ds(0, width))
    factor = scale_ref[pl.ds(scale_start, rows), :]
    grads = []
    for which, out_ref in enumerate((own_ref, other_ref)):
        gate_val = contract(values, panels[2 * which][...], 1, 0)
        up_val = contract(values, panels[2 * which + 1][...], 1, 0)
        columns = pl.ds(which * quarter, quarter)
        sigmoid_val = jax.nn.sigmoid(gate_val)
        activation = gate_val * sigmoid_val
        hidden_ref[kept:, columns] = b16(factor * activation * up_val)
        received = jnp.concatenate(
            [
                piece[:, pl.ds(start + which * quarter, quarter)]
                for piece, start in zip(pieces, grad_starts)
            ]
        )
        act_grad = factor * f32(received)
        up_grad = b16(act_grad * activation)
        gate_grad = b16(act_grad * up_val * sigmoid_val * (1.0 + gate_val * (1.0 - sigmoid_val)))
        out_ref[:, :quarter] = gate_grad
        out_ref[:, quarter:] = up_grad
        grads += [gate_grad.T, up_grad.T]
    for start in range(0, width, step):
        columns = pl.ds(start, step)
        part = b16(
            sum(contract(panel[columns, :], grad, 1, 0) for panel, grad in zip(panels, grads))
        ).T
        first = 0
        for part_ref in part_refs:
            part_ref[:, columns] = part[first : first + part_ref.shape[0]]
            first += part_ref.shape[0]


def block_pass(pieces, grad_starts, scales, scale_start, panels, part_rows, carry=()):
    rows = sum(piece.shape[0] for piece in pieces)
    width, quarter = panels[0].shape

    def wide(count):
        return jax.ShapeDtypeStruct((count, 2 * quarter), jnp.bfloat16)

    hidden, own, other, *parts = pl.pallas_call(
        functools.partial(block_body, grad_starts, scale_start, column_step(width), len(carry)),
        out_shape=[wide(rows + len(carry) * rows), wide(rows), wide(rows)]
        + [jax.ShapeDtypeStruct((count, width), jnp.bfloat16) for count in part_rows],
        compiler_params=pltpu.CompilerParams(vmem_limit_bytes=LIMIT),
        cost_estimate=work(16 * rows * width * quarter, 4 * rows * width),
        name="block_pass",
    )(*pieces, scales, *panels, *carry)
    return hidden, own, other, parts


def weight_body(piece_count, grad_count, step, *refs):
    pieces, refs = refs[:piece_count], refs[piece_count:]
    grad_refs, refs = refs[:grad_count], refs[grad_count:]
    *outs, held_ref, out_sems = refs
    got_ref, outs = (None, outs) if len(outs) == 1 else (outs[0], outs[1:])
    width, columns = outs[0].shape
    chunks = width // step
    grads = joined(grad_refs, slice(None))

    def store(chunk):
        slot = chunk % 2
        return [
            pltpu.make_async_copy(
                held_ref.at[slot, :, pl.ds(index * columns, columns)],
                out_ref.at[pl.ds(chunk * step, step), :],
                out_sems.at[slot, index],
            )
            for index, out_ref in enumerate(outs)
        ]

    for chunk in range(chunks):
        slot = chunk % 2
        total = contract(joined(pieces, pl.ds(chunk * step, step)), grads, 0, 0)
        if got_ref is not None:
            total = (total + f32(got_ref[pl.ds(chunk * step, step), :])) * (1.0 / TILE)
        if chunk >= 2:
            for copy in store(chunk - 2):
                copy.wait()
        held_ref[slot] = b16(total)
        for copy in store(chunk):
            copy.start()
    for chunk in range(max(chunks - 2, 0), chunks):
        for copy in store(chunk):
            copy.wait()


def weight_pass(width, pieces, grads, got=None):
    both = grads[0].shape[1]
    rows = sum(piece.shape[0] for piece in pieces)
    step = column_step(width)
    widths = [both] if got is None else [both // 2] * 2
    here, there = pl.BlockSpec(memory_space=pltpu.VMEM), pl.BlockSpec(memory_space=pl.ANY)
    return pl.pallas_call(
        functools.partial(weight_body, len(pieces), len(grads), step),
        in_specs=[here] * (len(pieces) + len(grads) + (got is not None)),
        out_specs=[there] * len(widths),
        out_shape=[jax.ShapeDtypeStruct((width, columns), jnp.bfloat16) for columns in widths],
        scratch_shapes=[
            pltpu.VMEM((2, step, both), jnp.bfloat16),
            pltpu.SemaphoreType.DMA((2, 2)),
        ],
        compiler_params=pltpu.CompilerParams(vmem_limit_bytes=LIMIT),
        cost_estimate=work(2 * rows * width * both, 2 * width * (rows + 2 * both)),
        name="weight_pass",
    )(
        *(
            pltpu.with_memory_space_constraint(part, pltpu.VMEM)
            for part in (*pieces, *grads, *([] if got is None else [got]))
        )
    )


def join_body(home_ref, far_ref, out_ref):
    kept = out_ref.shape[0] - far_ref.shape[0]
    out_ref[:kept, :] = home_ref[:kept, :]
    out_ref[kept:, :] = b16(f32(home_ref[kept:, :]) + f32(far_ref[...]))


def join(home, far):
    return pl.pallas_call(
        join_body,
        out_shape=jax.ShapeDtypeStruct(home.shape, home.dtype),
        compiler_params=pltpu.CompilerParams(vmem_limit_bytes=LIMIT),
        cost_estimate=LONG,
        name="join",
    )(home, far)


def final_body(
    near_ref,
    first_ref,
    low_near_ref,
    head_ref,
    low_ref,
    hidden_near_ref,
    hidden_far_ref,
    hidden_back_ref,
    hidden_got_ref,
    tokens_ref,
    hidden_ref,
):
    rows = tokens_ref.shape[0]
    first, head = first_ref.shape[0], head_ref.shape[0]
    rest = head - first
    tokens_ref[:first, :] = b16(
        f32(near_ref[:first, :]) + f32(first_ref[...]) + f32(head_ref[:first, :])
    )
    tokens_ref[first:head, :] = b16(
        f32(near_ref[first:head, :]) + f32(low_ref[:rest, :]) + f32(head_ref[first:, :])
    )
    tokens_ref[head:, :] = b16(
        f32(near_ref[head:, :]) + f32(low_near_ref[...]) + f32(low_ref[rest:, :])
    )
    rank = lax.axis_index("dp")
    quarter = hidden_ref.shape[2]
    for block, home_ref in enumerate((hidden_near_ref, hidden_far_ref)):
        back = hidden_back_ref[pl.ds(block * rows, rows), :quarter]
        hidden_ref[(2 * block) ^ rank] = b16(f32(home_ref[:rows, :quarter]) + f32(back))
        hidden_ref[(2 * block + 1) ^ rank] = hidden_got_ref[pl.ds(block * rows, rows), :]


def final(near, *others):
    rows = near.shape[0]
    quarter = others[-1].shape[1]
    return pl.pallas_call(
        final_body,
        out_shape=[
            jax.ShapeDtypeStruct(near.shape, near.dtype),
            jax.ShapeDtypeStruct((4, rows, quarter), near.dtype),
        ],
        compiler_params=pltpu.CompilerParams(vmem_limit_bytes=LIMIT),
        cost_estimate=LONG,
        name="final",
    )(*(pltpu.with_memory_space_constraint(part, pltpu.VMEM) for part in (near, *others)))


def per_device(tokens, cotangent, gate_weights, tile_expert, w_gate, w_up):
    row_count = tokens.shape[1]
    tile_count = row_count // TILE
    cycle_size = lax.axis_size("expert")
    position = lax.axis_index("expert")
    before = (position + cycle_size - 1) % cycle_size
    group_count = lax.axis_size("dp")
    rank = lax.axis_index("dp")
    quarter = w_gate.shape[2]
    out_head = OUT_SHARE * tile_count
    first, head = (share * tile_count for share in BACK_SHARE)
    tile, tile_grad = tokens[0], cotangent[0]

    def row_scale(group, place):
        owners = lax.dynamic_slice(tile_expert, (group, place * tile_count), (1, tile_count))
        weights = lax.dynamic_slice(gate_weights, (group, place * row_count), (1, row_count))
        routed = jnp.repeat(owners == position, TILE, axis=1, total_repeat_length=row_count)
        return jnp.where(routed, weights, jnp.zeros_like(weights)).reshape(row_count, 1)

    far = (rank + group_count // 2) % group_count
    scales = jnp.concatenate(
        [
            row_scale(group, place)
            for group, place in ((rank, position), (far, position), (rank, before), (far, before))
        ]
    )

    width = tile.shape[1]
    sent_at, kept_at = width, width + 2 * quarter
    near_top, near_low, far_message = pack(tile, tile_grad, out_head)
    x_top, x_low, y_tile = shifted(near_top, 1), shifted(near_low, 1), across(far_message)
    panels = (w_gate[0], w_up[0], within(w_gate[0]), within(w_up[0]))
    hid_hn, own_hn, other_hn, (part_hn,) = block_pass(
        (near_top, near_low), (kept_at, sent_at), scales, 0, panels, (row_count,)
    )
    x_top = after(x_top, hid_hn)
    x_sent = x_top[:, :kept_at]
    xy_top = across(x_sent)
    y_tile = after(y_tile, x_sent)
    y_sent = y_tile[out_head:]
    xy_low = shifted(y_sent, 1)
    x_low = after(x_low, y_sent)

    lower = row_count - head
    hid_mid, own_mid, other_mid, (first_hf, rest_hf, head_pn, lower_pn) = block_pass(
        (y_tile, x_top, x_low),
        (sent_at, kept_at, sent_at),
        scales,
        row_count,
        panels,
        (first, row_count - first, head, lower),
    )
    first_home = across(first_hf)
    low_near = shifted(lower_pn, -1)
    xy_low, xy_top = after((xy_low, xy_top), hid_mid)
    hid_past, own_pf, other_pf, (head_pf, lower_pf) = block_pass(
        (xy_top, xy_low), (sent_at, sent_at), scales, 3 * row_count, panels, (head, lower), (hid_mid,)
    )
    head_past = across(head_pf)
    low_far = shifted(lower_pf, -1)

    pieces = (near_top, near_low, y_tile, x_top, x_low, xy_top, xy_low)
    (sent,) = weight_pass(width, pieces, after((other_hn, other_mid, other_pf), first_home, low_near))
    got = within(sent)
    hid_back = shifted(after(hid_past, sent), -1)
    head_sum = b16(f32(head_pn) + f32(after(head_past, sent)))
    head_back = shifted(head_sum, -1)
    low_sum = join(rest_hf, after(low_far, head_sum))
    hid_back = after(hid_back, low_sum)
    low_home = across(low_sum)
    hid_other = jnp.concatenate([hid_hn[:, quarter:], hid_mid[:row_count, quarter:]])
    hid_other = b16(f32(hid_other) + f32(hid_back[:, quarter:]))
    hid_got = within(hid_other)
    got = after(got, hid_other, low_sum)
    grad_gate, grad_up = weight_pass(width, pieces, (own_hn, own_mid, own_pf), got)
    d_tokens, hidden = final(
        part_hn,
        *(first_home, low_near, head_back, low_home),
        *(hid_hn, hid_mid, hid_back, after(hid_got, grad_gate)),
    )
    return (d_tokens[None], hidden, grad_gate[None], grad_up[None])


def solution(mesh):
    in_specs = (
        P("dp", "expert", None),
        P("dp", "expert", None),
        P(),
        P(),
        P("expert", None, "dp"),
        P("expert", None, "dp"),
    )
    out_specs = (
        P("dp", "expert", None),
        P(None, "expert", "dp"),
        P("expert", None, "dp"),
        P("expert", None, "dp"),
    )
    return jax.shard_map(
        per_device, mesh=mesh, in_specs=in_specs, out_specs=out_specs, check_vma=False
    )
```

time: 91.9 us -> 85.3 us (0.928)
  Pallas kernels: 39.9 us -> 34.9 us
    pallas_call x5 -> x4, Pallas kernels: 20.4 us -> 15.7 us  [the longest x2 13.4 us: weight_pass(): pl.pallas_call(functools.partial(weight_body, len(pieces), len(grads), st...]
    ppermute x7 -> x5, starting transfers between devices: 7.92 us -> 6.14 us  [across(): return lax.ppermute(value, 'dp', pairs)]
    ppermute x8 -> x7, starting transfers between devices: 16.3 us -> 17.3 us  [shifted(): return lax.ppermute(value, 'expert', pairs)]
    unnamed x40 -> x24, local copies, waits for them, and re-layouts: 4.02 us -> 4.94 us
    convert_element_type x4 -> x2, other arithmetic: 2.47 us -> 1.81 us  [b16(): return value.astype(jnp.bfloat16)]
    ppermute x8 -> x7, waiting for transfers between devices: 9.66 us -> 9.53 us  [shifted(): return lax.ppermute(value, 'expert', pairs)]
  transfers between devices with their start and end apart: 19 -> 16, of which waited for: 4 -> 5; matrix products, arithmetic and copies ran while one was open for 8% -> 7% of each run, Pallas kernels for 41% -> 39%
where the time goes in v4:
time: 85.3 us; the launch traced here: 84.8 us
  Pallas kernels  34.9 us (41%)
  starting transfers between devices  24.2 us (28%)
  waiting for transfers between devices  11.3 us (13%)
  local copies, waits for them, and re-layouts  8.36 us (10%)
  between operations  3.3 us (4%)
  other arithmetic  2.67 us (3%)
    ppermute x7, starting transfers between devices, shifted(): return lax.ppermute(value, 'expert', pairs)  17.3 us
    pallas_call x3, Pallas kernels, block_pass(): pl.pallas_call(functools.partial(block_body, grad_starts, scale_start, co...  16.7 us
    pallas_call x2, Pallas kernels, weight_pass(): pl.pallas_call(functools.partial(weight_body, len(pieces), len(grads), st...  13.4 us
    ppermute x7, waiting for transfers between devices, shifted(): return lax.ppermute(value, 'expert', pairs)  9.53 us
    ppermute x5, starting transfers between devices, across(): return lax.ppermute(value, 'dp', pairs)  6.14 us
    unnamed x24, local copies, waits for them, and re-layouts  4.94 us
    pallas_call x1, Pallas kernels, pack(): pl.pallas_call(pack_body, out_shape=[jax.ShapeDtypeStruct((head, width +...  2.5 us
    pallas_call x1, Pallas kernels, final(): pl.pallas_call(final_body, out_shape=[jax.ShapeDtypeStruct(near.shape, ne...  2.25 us
  transfers between devices with their start and end apart: 16, of which 5 were waited for; matrix products, arithmetic and copies ran while one was open for 7% of the time, Pallas kernels for 39%

profile of v4, /device:TPU:0, one launch (start us, length us, event | category | flops | bytes accessed | tf_op | source)
XLA Modules:
  0.0 84.8 jit_solution(14490551858398328220)
XLA Ops:
  0.6 0.5 collective-permute-start
  1.1 0.1 collective-permute-start.1
  1.2 2.5 %pack.1 = (bf16[80,4608]{1,0:T(8,128)(2,1)S(1)}, bf16[48,4096]{1,0:T(8,128)(2,1)}, bf16[128,4096]{1,0:T(8,128)(2,1)}) custom-call(bf16[128,3584]{1,0:T(8,128)(2,1)} %bitcast.28, bf16[128,1024]{1,0:T(8,128)(2,1)} %bitcast.29), custom_call_target="tpu_custom_call" | custom-call | bytes 2359296 | tf_op jit(solution)/shard_map/pack/pallas_call | solution.py:94
  3.7 2.9 %collective-permute-start.2 = (bf16[128,4096]{1,0:T(8,128)(2,1)}, bf16[128,4096]{1,0:T(8,128)(2,1)}, u32[]{:S(2)}, u32[]{:S(2)}) collective-permute-start(bf16[128,4096]{1,0:T(8,128)(2,1)} %get-tuple-element.117), channel_id=1, source_target_pairs={{0,16},{8,24},{16,0},{24,8},{1,17},{9,25},{17,1},{25,9},{2,18},{10... | collective-permute-start | bytes 3145736 | tf_op jit(solution)/shard_map/ppermute | solution.py:30
  6.7 1.5 %collective-permute-start.3 = (bf16[80,4608]{1,0:T(8,128)(2,1)S(1)}, bf16[80,4608]{1,0:T(8,128)(2,1)S(1)}, u32[]{:S(2)}, u32[]{:S(2)}) collective-permute-start(bf16[80,4608]{1,0:T(8,128)(2,1)S(1)} %get-tuple-element.114.refs_0_), channel_id=1, source_target_pairs={{0,1},{1,2},{2,3},{3,4},{4,5},{5,6},{6,7},{7,0},{8,9},{9,10},{10,1... | collective-permute-start | bytes 2211848 | tf_op jit(solution)/shard_map/ppermute | solution.py:24
  8.2 1.5 %collective-permute-start.4 = (bf16[48,4096]{1,0:T(8,128)(2,1)}, bf16[48,4096]{1,0:T(8,128)(2,1)}, u32[]{:S(2)}, u32[]{:S(2)}) collective-permute-start(bf16[48,4096]{1,0:T(8,128)(2,1)} %get-tuple-element.115.refs_1_), channel_id=1, source_target_pairs={{0,1},{1,2},{2,3},{3,4},{4,5},{5,6},{6,7},{7,0},{8,9},{9,10},{10,1... | collective-permute-start | bytes 1179656 | tf_op jit(solution)/shard_map/ppermute | solution.py:24
  9.7 1.5 %fusion.4 = (s32[1,1]{1,0:T(1,128)}, s32[1,1]{1,0:T(1,128)}, s32[1,1]{1,0:T(1,128)}, s32[1,1]{1,0:T(1,128)}) fusion(s32[4,8]{1,0:T(4,128)} %param.27, s32[]{:T(128)S(6)} %select_n.62, s32[]{:T(128)S(6)} %select_n.63, s32[]{:T(128)S(6)} %select_n.67, s32[]{:T(128)S(6)} %select_n.70), kind=kLoop, calls=%fused_computation.11 | loop fusion | bytes 48 | tf_op jit(solution)/shard_map/dynamic_slice | solution.py:311
  13.7 0.8 %fusion = (f32[128,1]{0,1:T(1,128)S(1)}, f32[128,1]{0,1:T(1,128)S(1)}, f32[128,1]{0,1:T(1,128)S(1)}, f32[128,1]{0,1:T(1,128)S(1)}) fusion(pred[]{:T(512)} %bitcast.3, f32[4,1024]{1,0:T(4,128)} %param.26, s32[]{:T(128)S(6)} %select_n.62, s32[]{:T(128)S(6)} %select_n.64, s32[]{:T(128)S(6)} %select_n.67, pred[]{:T(512)} %bitcast.5, s32[]{:T(128)S(6)} %select_n.71, ...), kind=kLoop, calls=%fused_computation.7 | loop fusion | flops 512 | bytes 4116 | tf_op jit(solution)/shard_map/reshape | solution.py:314
  14.6 0.9 %copy.14.refs_2_.refs_3_ = f32[512,1]{1,0:T(8,128)} copy(f32[512,1]{0,1:T(1,128)S(1)} %pad_maximum_fusion) | data formatting | bytes 4096 | tf_op jit(solution)/shard_map/concatenate | solution.py:317
  15.4 0.0 collective-permute-done.refs_5_.refs_6_
  15.4 0.0 collective-permute-done.1.refs_6_.refs_7_
  15.4 1.5 %copy-done = bf16[1,3584,256]{2,1,0:T(8,128)(2,1)S(1)} copy-done((bf16[1,3584,256]{2,1,0:T(8,128)(2,1)S(1)}, bf16[1,3584,256]{2,1,0:T(8,128)(2,1)}, u32[]{:S(2)}) %copy-start) | copy-done | bytes 1835032
  16.9 1.5 %copy-done.2 = bf16[1,3584,256]{2,1,0:T(8,128)(2,1)S(1)} copy-done((bf16[1,3584,256]{2,1,0:T(8,128)(2,1)S(1)}, bf16[1,3584,256]{2,1,0:T(8,128)(2,1)}, u32[]{:S(2)}) %copy-start.2) | copy-done | bytes 1835032
  18.4 0.9 %copy-done.6 = f32[512,1]{1,0:T(8,128)S(1)} copy-done((f32[512,1]{1,0:T(8,128)S(1)}, f32[512,1]{1,0:T(8,128)}, u32[]{:S(2)}) %copy-start.6) | copy-done | bytes 2072
  19.4 5.0 %block_pass.3 = (bf16[128,512]{1,0:T(8,128)(2,1)S(1)}, bf16[128,512]{1,0:T(8,128)(2,1)S(1)}, bf16[128,512]{1,0:T(8,128)(2,1)S(1)}, bf16[128,3584]{1,0:T(8,128)(2,1)S(1)}) custom-call(bf16[80,4608]{1,0:T(8,128)(2,1)S(1)} %get-tuple-element.114.refs_0_, bf16[48,4096]{1,0:T(8,128)(2,1)} %get-tuple-element.115.refs_1_, f32[512,1]{1,0:T(8,128)S(1)} %copy-done.6, ...), custom_call_target="tpu_custom_call" | custom-call | flops 1879048192 | bytes 1835008 | tf_op jit(solution)/shard_map/block_pass/pallas_call | solution.py:160
  24.4 0.0 copy-start.1
  24.4 4.4 %collective-permute-done.3.refs_1_.refs_3_ = bf16[80,4608]{1,0:T(8,128)(2,1)S(1)} collective-permute-done((bf16[80,4608]{1,0:T(8,128)(2,1)S(1)}, bf16[80,4608]{1,0:T(8,128)(2,1)S(1)}, u32[]{:S(2)}, u32[]{:S(2)}) %collective-permute-start.3) | collective-permute-done | bytes 737312 | tf_op jit(solution)/shard_map/ppermute | solution.py:24
  28.8 0.4 collective-permute-start.8
  29.1 1.8 %collective-permute-done.2.refs_0_.refs_2_ = bf16[128,4096]{1,0:T(8,128)(2,1)} collective-permute-done((bf16[128,4096]{1,0:T(8,128)(2,1)}, bf16[128,4096]{1,0:T(8,128)(2,1)}, u32[]{:S(2)}, u32[]{:S(2)}) %collective-permute-start.2) | collective-permute-done | bytes 1048608 | tf_op jit(solution)/shard_map/ppermute | solution.py:30
  30.9 1.0 %slice.64 = bf16[48,4096]{1,0:T(8,128)(2,1)S(1)} slice(bf16[128,4096]{1,0:T(8,128)(2,1)} %collective-permute-done.2.refs_0_.refs_2_), slice={[80:128], [0:4096]} | slice | bytes 786432 | tf_op jit(solution)/shard_map/slice | solution.py:336
  32.0 2.1 %collective-permute-start.7 = (bf16[48,4096]{1,0:T(8,128)(2,1)S(1)}, bf16[48,4096]{1,0:T(8,128)(2,1)S(1)}, u32[]{:S(2)}, u32[]{:S(2)}) collective-permute-start(bf16[48,4096]{1,0:T(8,128)(2,1)S(1)} %slice.64), channel_id=1, source_target_pairs={{0,1},{1,2},{2,3},{3,4},{4,5},{5,6},{6,7},{7,0},{8,9},{9,10},{10,1... | collective-permute-start | bytes 1179656 | tf_op jit(solution)/shard_map/ppermute | solution.py:24
  34.1 2.1 %collective-permute-done.4.refs_2_.refs_4_ = bf16[48,4096]{1,0:T(8,128)(2,1)} collective-permute-done((bf16[48,4096]{1,0:T(8,128)(2,1)}, bf16[48,4096]{1,0:T(8,128)(2,1)}, u32[]{:S(2)}, u32[]{:S(2)}) %collective-permute-start.4) | collective-permute-done | bytes 393248 | tf_op jit(solution)/shard_map/ppermute | solution.py:24
  36.2 6.2 %block_pass.4 = (bf16[256,512]{1,0:T(8,128)(2,1)S(1)}, bf16[256,512]{1,0:T(8,128)(2,1)S(1)}, bf16[256,512]{1,0:T(8,128)(2,1)S(1)}, bf16[48,3584]{1,0:T(8,128)(2,...) custom-call(bf16[128,4096]{1,0:T(8,128)(2,1)} %collective-permute-done.2.refs_0_.re, ...), custom_call_target="tpu_custom_call" | custom-call | flops 3758096384 | bytes 3670016 | tf_op jit(solution)/shard_map/block_pass/pallas_call | solution.py:160
  42.4 0.0 copy-start.7
  42.4 1.8 %collective-permute-start.6 = (bf16[64,3584]{1,0:T(8,128)(2,1)S(1)}, bf16[64,3584]{1,0:T(8,128)(2,1)S(1)}, u32[]{:S(2)}, u32[]{:S(2)}) collective-permute-start(bf16[64,3584]{1,0:T(8,128)(2,1)S(1)} %get-tuple-element.123), channel_id=1, source_target_pairs={{0,7},{1,0},{2,1},{3,2},{4,3},{5,4},{6,5},{7,6},{8,15},{9,8},{10,9... | collective-permute-start | bytes 1376264 | tf_op jit(solution)/shard_map/ppermute | solution.py:24
  44.2 0.9 %collective-permute-start.5 = (bf16[48,3584]{1,0:T(8,128)(2,1)S(1)}, bf16[48,3584]{1,0:T(8,128)(2,1)S(1)}, u32[]{:S(2)}, u32[]{:S(2)}) collective-permute-start(bf16[48,3584]{1,0:T(8,128)(2,1)S(1)} %get-tuple-element.122), channel_id=1, source_target_pairs={{0,16},{8,24},{16,0},{24,8},{1,17},{9,25},{17,1},{25,9},{2,18},{10... | collective-permute-start | bytes 1032200 | tf_op jit(solution)/shard_map/ppermute | solution.py:30
  45.1 5.5 %block_pass.5 = (bf16[256,512]{1,0:T(8,128)(2,1)}, bf16[128,512]{1,0:T(8,128)(2,1)S(1)}, bf16[128,512]{1,0:T(8,128)(2,1)S(1)}, bf16[64,3584]{1,0:T(8,128)(2,1)S(1)}, bf16[64,3584]{1,0:T(8,128)(2,1)S(1)}) custom-call(bf16[80,4096]{1,0:T(8,128)(2,1)S(1)} %collective-permute-done.8.refs_0_.refs_5_, bf16[48,4096]{1,0:T(8,128)(2,1)S(1)} %collective-permute-done.7.refs_1_.refs_6_, ...), custom_call_target="tpu_custom_call" | custom-call | flops 1879048192 | bytes 1835008 | tf_op jit(solution)/shard_map/block_pass/pallas_call | solution.py:160
  50.6 1.3 %collective-permute-start.9 = (bf16[64,3584]{1,0:T(8,128)(2,1)S(1)}, bf16[64,3584]{1,0:T(8,128)(2,1)S(1)}, u32[]{:S(2)}, u32[]{:S(2)}) collective-permute-start(bf16[64,3584]{1,0:T(8,128)(2,1)S(1)} %get-tuple-element.128), channel_id=1, source_target_pairs={{0,16},{8,24},{16,0},{24,8},{1,17},{9,25},{17,1},{25,9},{2,18},{10... | collective-permute-start | bytes 1376264 | tf_op jit(solution)/shard_map/ppermute | solution.py:30
  51.9 5.0 %collective-permute-start.11 = (bf16[64,3584]{1,0:T(8,128)(2,1)S(1)}, bf16[64,3584]{1,0:T(8,128)(2,1)S(1)}, u32[]{:S(2)}, u32[]{:S(2)}) collective-permute-start(bf16[64,3584]{1,0:T(8,128)(2,1)S(1)} %get-tuple-element.137), channel_id=1, source_target_pairs={{0,7},{1,0},{2,1},{3,2},{4,3},{5,4},{6,5},{7,6},{8,15},{9,8},{10,9... | collective-permute-start | bytes 1376264 | tf_op jit(solution)/shard_map/ppermute | solution.py:24
  56.9 0.7 copy-done.9
  57.6 6.1 %weight_pass.2 = bf16[3584,512]{1,0:T(8,128)(2,1)} custom-call(bf16[80,4608]{1,0:T(8,128)(2,1)S(1)} %get-tuple-element.114.refs_0_, bf16[48,4096]{1,0:T(8,128)(2,1)} %get-tuple-element.115.refs_1_, bf16[128,4096]{1,0:T(8,128)(2,1)} %collective-permute-done.2.refs_0_.refs_2_, bf16[80,4608]{1,0:T(8,128)(2,1)S(1)} %collective-permute-done.3.refs_1_.refs_3_, ...), custom_call_target="tpu_custom_call" | custom-call | flops 1879048192 | bytes 11010048 | tf_op jit(solution)/shard_map/weight_pass/pallas_call | solution.py:213
  63.7 0.1 collective-permute-start.15
  63.8 0.7 collective-permute-start.13
  64.4 0.0 collective-permute-done.9
  64.4 0.9 %add_convert_fusion = bf16[64,3584]{1,0:T(8,128)(2,1)} fusion(bf16[64,3584]{1,0:T(8,128)(2,1)S(1)} %collective-permute-done.9, bf16[64,3584]{1,0:T(8,128)(2,1)S(1)} %get-tuple-element.124), kind=kLoop, calls=%fused_computation | loop fusion | flops 917504 | bytes 1376256 | tf_op jit(solution)/shard_map/convert_element_type | solution.py:48
  65.3 0.0 collective-permute-done.11.far_ref
  65.3 0.1 join.1
  65.4 0.7 collective-permute-start.12
  66.1 0.2 copy-done.11
  66.3 4.7 %collective-permute-start.10 = (bf16[64,3584]{1,0:T(8,128)(2,1)S(1)}, bf16[64,3584]{1,0:T(8,128)(2,1)S(1)}, u32[]{:S(2)}, u32[]{:S(2)}) collective-permute-start(bf16[64,3584]{1,0:T(8,128)(2,1)S(1)} %copy-done.11), channel_id=1, source_target_pairs={{0,7},{1,0},{2,1},{3,2},{4,3},{5,4},{6,5},{7,6},{8,15},{9,8},{10,9... | collective-permute-start | bytes 1376264 | tf_op jit(solution)/shard_map/ppermute | solution.py:24
  71.1 2.1 %collective-permute-done.13.hidden_back_ref = bf16[256,512]{1,0:T(8,128)(2,1)} collective-permute-done((bf16[256,512]{1,0:T(8,128)(2,1)}, bf16[256,512]{1,0:T(8,128)(2,1)}, u32[]{:S(2)}, u32[]{:S(2)}) %collective-permute-start.13) | collective-permute-done | bytes 262176 | tf_op jit(solution)/shard_map/ppermute | solution.py:24
  73.2 0.9 %add_convert_fusion.1 = bf16[256,256]{1,0:T(8,128)(2,1)S(1)} fusion(bf16[128,256]{1,0:T(8,128)(2,1)S(1)} %slice.66, bf16[128,256]{1,0:T(8,128)(2,1)S(1)} %slice.65, bf16[256,512]{1,0:T(8,128)(2,1)} %collective-permute-done.13.hidden_back_ref), kind=kLoop, calls=%fused_computation.1 | loop fusion | flops 458752 | bytes 393216 | tf_op jit(solution)/shard_map/convert_element_type | solution.py:48
  74.2 0.1 collective-permute-start.14
  74.3 0.0 collective-permute-done.15.refs_10_
  74.3 7.3 %weight_pass.3 = (bf16[3584,256]{1,0:T(8,128)(2,1)}, bf16[3584,256]{1,0:T(8,128)(2,1)}) custom-call(bf16[80,4608]{1,0:T(8,128)(2,1)S(1)} %get-tuple-element.114.refs_0_, bf16[48,4096]{1,0:T(8,128)(2,1)} %get-tuple-element.115.refs_1_, bf16[128,4096]{1,0:T(8,128)(2,1)} %collective-permute-done.2.refs_0_.refs_2_, ...), custom_call_target="tpu_custom_call" | custom-call | flops 1879048192 | bytes 11010048 | tf_op jit(solution)/shard_map/weight_pass/pallas_call | solution.py:213
  81.6 0.0 collective-permute-done.14.hidden_got_ref
  81.6 0.9 %collective-permute-done.10.head_ref = bf16[64,3584]{1,0:T(8,128)(2,1)S(1)} collective-permute-done((bf16[64,3584]{1,0:T(8,128)(2,1)S(1)}, bf16[64,3584]{1,0:T(8,128)(2,1)S(1)}, u32[]{:S(2)}, u32[]{:S(2)}) %collective-permute-start.10) | collective-permute-done | bytes 458784 | tf_op jit(solution)/shard_map/ppermute | solution.py:24
  82.5 2.3 %final.1 = (bf16[128,3584]{1,0:T(8,128)(2,1)}, bf16[4,128,256]{2,1,0:T(8,128)(2,1)}) custom-call(bf16[128,3584]{1,0:T(8,128)(2,1)S(1)} %get-tuple-element.116.near_ref, bf16[48,3584]{1,0:T(8,128)(2,1)S(1)} %copy-done.10, bf16[64,3584]{1,0:T(8,128)(2,1)S(1)} %collective-permute-done.6.low_near_ref, bf16[64,3584]{1,0:T(8,128)(2,1)S(1)} %collective-permute-done.10.head_ref, ...), custom_call_target="tpu_custom_call" | custom-call | flops 999999995904 | bytes 1000000000 | tf_op jit(solution)/shard_map/final/pallas_call | solution.py:285
  (26 shorter events, 0.1 us)
Async XLA Ops:
  0.6 14.8 %collective-permute-start = (bf16[3584,256]{1,0:T(8,128)(2,1)}, bf16[3584,256]{1,0:T(8,128)(2,1)S(1)}, u32[]{:S(2)}, u32[]{:S(2)}) collective-permute-start(bf16[3584,256]{1,0:T(8,128)(2,1)} %bitcast.20), channel_id=1, source_target_pairs={{0,8},{8,0},{16,24},{24,16},{1,9},{9,1},{17,25},{25,17},{2,10},{10... | collective-permute-start | bytes 5505032 | tf_op jit(solution)/shard_map/ppermute | solution.py:36
  1.1 14.3 %collective-permute-start.1 = (bf16[3584,256]{1,0:T(8,128)(2,1)}, bf16[3584,256]{1,0:T(8,128)(2,1)}, u32[]{:S(2)}, u32[]{:S(2)}) collective-permute-start(bf16[3584,256]{1,0:T(8,128)(2,1)} %bitcast.24), channel_id=1, source_target_pairs={{0,8},{8,0},{16,24},{24,16},{1,9},{9,1},{17,25},{25,17},{2,10},{10... | collective-permute-start | bytes 5505032 | tf_op jit(solution)/shard_map/ppermute | solution.py:36
  3.7 27.2 %collective-permute-start.2 = (bf16[128,4096]{1,0:T(8,128)(2,1)}, bf16[128,4096]{1,0:T(8,128)(2,1)}, u32[]{:S(2)}, u32[]{:S(2)}) collective-permute-start(bf16[128,4096]{1,0:T(8,128)(2,1)} %get-tuple-element.117), channel_id=1, source_target_pairs={{0,16},{8,24},{16,0},{24,8},{1,17},{9,25},{17,1},{25,9},{2,18},{10... | collective-permute-start | bytes 3145736 | tf_op jit(solution)/shard_map/ppermute | solution.py:30
  6.7 22.1 %collective-permute-start.3 = (bf16[80,4608]{1,0:T(8,128)(2,1)S(1)}, bf16[80,4608]{1,0:T(8,128)(2,1)S(1)}, u32[]{:S(2)}, u32[]{:S(2)}) collective-permute-start(bf16[80,4608]{1,0:T(8,128)(2,1)S(1)} %get-tuple-element.114.refs_0_), channel_id=1, source_target_pairs={{0,1},{1,2},{2,3},{3,4},{4,5},{5,6},{6,7},{7,0},{8,9},{9,10},{10,1... | collective-permute-start | bytes 2211848 | tf_op jit(solution)/shard_map/ppermute | solution.py:24
  8.2 28.0 %collective-permute-start.4 = (bf16[48,4096]{1,0:T(8,128)(2,1)}, bf16[48,4096]{1,0:T(8,128)(2,1)}, u32[]{:S(2)}, u32[]{:S(2)}) collective-permute-start(bf16[48,4096]{1,0:T(8,128)(2,1)} %get-tuple-element.115.refs_1_), channel_id=1, source_target_pairs={{0,1},{1,2},{2,3},{3,4},{4,5},{5,6},{6,7},{7,0},{8,9},{9,10},{10,1... | collective-permute-start | bytes 1179656 | tf_op jit(solution)/shard_map/ppermute | solution.py:24
  15.4 1.5 %copy-start = (bf16[1,3584,256]{2,1,0:T(8,128)(2,1)S(1)}, bf16[1,3584,256]{2,1,0:T(8,128)(2,1)}, u32[]{:S(2)}) copy-start(bf16[1,3584,256]{2,1,0:T(8,128)(2,1)} %param.28) | copy-start | bytes 5505028
  16.9 1.5 %copy-start.2 = (bf16[1,3584,256]{2,1,0:T(8,128)(2,1)S(1)}, bf16[1,3584,256]{2,1,0:T(8,128)(2,1)}, u32[]{:S(2)}) copy-start(bf16[1,3584,256]{2,1,0:T(8,128)(2,1)} %param.29) | copy-start | bytes 5505028
  18.4 0.9 %copy-start.6 = (f32[512,1]{1,0:T(8,128)S(1)}, f32[512,1]{1,0:T(8,128)}, u32[]{:S(2)}) copy-start(f32[512,1]{1,0:T(8,128)} %copy.14.refs_2_.refs_3_) | copy-start | bytes 6148
  19.4 16.8 %copy-start.3 = (bf16[1,3584,256]{2,1,0:T(8,128)(2,1)S(1)}, bf16[1,3584,256]{2,1,0:T(8,128)(2,1)}, u32[]{:S(2)}) copy-start(bf16[1,3584,256]{2,1,0:T(8,128)(2,1)} %param.29) | copy-start | bytes 5505028
  24.4 11.8 %copy-start.1 = (bf16[1,3584,256]{2,1,0:T(8,128)(2,1)S(1)}, bf16[1,3584,256]{2,1,0:T(8,128)(2,1)}, u32[]{:S(2)}) copy-start(bf16[1,3584,256]{2,1,0:T(8,128)(2,1)} %param.28) | copy-start | bytes 5505028
  28.8 16.3 %collective-permute-start.8 = (bf16[80,4096]{1,0:T(8,128)(2,1)S(1)}, bf16[80,4096]{1,0:T(8,128)(2,1)S(1)}, u32[]{:S(2)}, u32[]{:S(2)}) collective-permute-start(bf16[80,4096]{1,0:T(8,128)(2,1)S(1)} %slice.63), channel_id=1, source_target_pairs={{0,16},{8,24},{16,0},{24,8},{1,17},{9,25},{17,1},{25,9},{2,18},{10... | collective-permute-start | bytes 1966088 | tf_op jit(solution)/shard_map/ppermute | solution.py:30
  32.0 13.1 %collective-permute-start.7 = (bf16[48,4096]{1,0:T(8,128)(2,1)S(1)}, bf16[48,4096]{1,0:T(8,128)(2,1)S(1)}, u32[]{:S(2)}, u32[]{:S(2)}) collective-permute-start(bf16[48,4096]{1,0:T(8,128)(2,1)S(1)} %slice.64), channel_id=1, source_target_pairs={{0,1},{1,2},{2,3},{3,4},{4,5},{5,6},{6,7},{7,0},{8,9},{9,10},{10,1... | collective-permute-start | bytes 1179656 | tf_op jit(solution)/shard_map/ppermute | solution.py:24
  42.4 8.2 %copy-start.7 = (bf16[256,512]{1,0:T(8,128)(2,1)}, bf16[256,512]{1,0:T(8,128)(2,1)S(1)}, u32[]{:S(2)}) copy-start(bf16[256,512]{1,0:T(8,128)(2,1)S(1)} %get-tuple-element.125.refs_7_.hidden_far_ref) | copy-start | bytes 786436
  42.4 15.2 %collective-permute-start.6 = (bf16[64,3584]{1,0:T(8,128)(2,1)S(1)}, bf16[64,3584]{1,0:T(8,128)(2,1)S(1)}, u32[]{:S(2)}, u32[]{:S(2)}) collective-permute-start(bf16[64,3584]{1,0:T(8,128)(2,1)S(1)} %get-tuple-element.123), channel_id=1, source_target_pairs={{0,7},{1,0},{2,1},{3,2},{4,3},{5,4},{6,5},{7,6},{8,15},{9,8},{10,9... | collective-permute-start | bytes 1376264 | tf_op jit(solution)/shard_map/ppermute | solution.py:24
  44.2 12.7 %collective-permute-start.5 = (bf16[48,3584]{1,0:T(8,128)(2,1)S(1)}, bf16[48,3584]{1,0:T(8,128)(2,1)S(1)}, u32[]{:S(2)}, u32[]{:S(2)}) collective-permute-start(bf16[48,3584]{1,0:T(8,128)(2,1)S(1)} %get-tuple-element.122), channel_id=1, source_target_pairs={{0,16},{8,24},{16,0},{24,8},{1,17},{9,25},{17,1},{25,9},{2,18},{10... | collective-permute-start | bytes 1032200 | tf_op jit(solution)/shard_map/ppermute | solution.py:30
  45.1 12.5 %copy-start.4 = (bf16[48,4096]{1,0:T(8,128)(2,1)}, bf16[48,4096]{1,0:T(8,128)(2,1)S(1)}, u32[]{:S(2)}) copy-start(bf16[48,4096]{1,0:T(8,128)(2,1)S(1)} %collective-permute-done.7.refs_1_.refs_6_) | copy-start | bytes 1179652
  50.6 13.8 %collective-permute-start.9 = (bf16[64,3584]{1,0:T(8,128)(2,1)S(1)}, bf16[64,3584]{1,0:T(8,128)(2,1)S(1)}, u32[]{:S(2)}, u32[]{:S(2)}) collective-permute-start(bf16[64,3584]{1,0:T(8,128)(2,1)S(1)} %get-tuple-element.128), channel_id=1, source_target_pairs={{0,16},{8,24},{16,0},{24,8},{1,17},{9,25},{17,1},{25,9},{2,18},{10... | collective-permute-start | bytes 1376264 | tf_op jit(solution)/shard_map/ppermute | solution.py:30
  51.9 13.4 %collective-permute-start.11 = (bf16[64,3584]{1,0:T(8,128)(2,1)S(1)}, bf16[64,3584]{1,0:T(8,128)(2,1)S(1)}, u32[]{:S(2)}, u32[]{:S(2)}) collective-permute-start(bf16[64,3584]{1,0:T(8,128)(2,1)S(1)} %get-tuple-element.137), channel_id=1, source_target_pairs={{0,7},{1,0},{2,1},{3,2},{4,3},{5,4},{6,5},{7,6},{8,15},{9,8},{10,9... | collective-permute-start | bytes 1376264 | tf_op jit(solution)/shard_map/ppermute | solution.py:24
  56.9 0.7 copy-start.9
  63.7 10.6 %collective-permute-start.15 = (bf16[3584,512]{1,0:T(8,128)(2,1)}, bf16[3584,512]{1,0:T(8,128)(2,1)}, u32[]{:S(2)}, u32[]{:S(2)}) collective-permute-start(bf16[3584,512]{1,0:T(8,128)(2,1)} %weight_pass.2), channel_id=1, source_target_pairs={{0,8},{8,0},{16,24},{24,16},{1,9},{9,1},{17,25},{25,17},{2,10},{10... | collective-permute-start | bytes 11010056 | tf_op jit(solution)/shard_map/ppermute | solution.py:36
  63.8 9.5 %collective-permute-start.13 = (bf16[256,512]{1,0:T(8,128)(2,1)}, bf16[256,512]{1,0:T(8,128)(2,1)}, u32[]{:S(2)}, u32[]{:S(2)}) collective-permute-start(bf16[256,512]{1,0:T(8,128)(2,1)} %get-tuple-element.140), channel_id=1, source_target_pairs={{0,7},{1,0},{2,1},{3,2},{4,3},{5,4},{6,5},{7,6},{8,15},{9,8},{10,9... | collective-permute-start | bytes 786440 | tf_op jit(solution)/shard_map/ppermute | solution.py:24
  65.3 1.0 %copy-start.11 = (bf16[64,3584]{1,0:T(8,128)(2,1)S(1)}, bf16[64,3584]{1,0:T(8,128)(2,1)}, u32[]{:S(2)}) copy-start(bf16[64,3584]{1,0:T(8,128)(2,1)} %add_convert_fusion) | copy-start | bytes 1376260
  65.3 5.8 %copy-start.8 = (bf16[256,512]{1,0:T(8,128)(2,1)S(1)}, bf16[256,512]{1,0:T(8,128)(2,1)}, u32[]{:S(2)}) copy-start(bf16[256,512]{1,0:T(8,128)(2,1)} %copy-done.7) | copy-start | bytes 786436
  65.3 9.0 %copy-start.5 = (bf16[48,4096]{1,0:T(8,128)(2,1)S(1)}, bf16[48,4096]{1,0:T(8,128)(2,1)}, u32[]{:S(2)}) copy-start(bf16[48,4096]{1,0:T(8,128)(2,1)} %copy-done.4) | copy-start | bytes 1179652
  65.4 17.1 %collective-permute-start.12 = (bf16[80,3584]{1,0:T(8,128)(2,1)S(1)}, bf16[80,3584]{1,0:T(8,128)(2,1)S(1)}, u32[]{:S(2)}, u32[]{:S(2)}) collective-permute-start(bf16[80,3584]{1,0:T(8,128)(2,1)S(1)} %join.1), channel_id=1, source_target_pairs={{0,16},{8,24},{16,0},{24,8},{1,17},{9,25},{17,1},{25,9},{2,18},{10... | collective-permute-start | bytes 1720328 | tf_op jit(solution)/shard_map/ppermute | solution.py:30
  66.3 16.2 %collective-permute-start.10 = (bf16[64,3584]{1,0:T(8,128)(2,1)S(1)}, bf16[64,3584]{1,0:T(8,128)(2,1)S(1)}, u32[]{:S(2)}, u32[]{:S(2)}) collective-permute-start(bf16[64,3584]{1,0:T(8,128)(2,1)S(1)} %copy-done.11), channel_id=1, source_target_pairs={{0,7},{1,0},{2,1},{3,2},{4,3},{5,4},{6,5},{7,6},{8,15},{9,8},{10,9... | collective-permute-start | bytes 1376264 | tf_op jit(solution)/shard_map/ppermute | solution.py:24
  74.2 7.4 %collective-permute-start.14 = (bf16[256,256]{1,0:T(8,128)(2,1)S(1)}, bf16[256,256]{1,0:T(8,128)(2,1)S(1)}, u32[]{:S(2)}, u32[]{:S(2)}) collective-permute-start(bf16[256,256]{1,0:T(8,128)(2,1)S(1)} %add_convert_fusion.1), channel_id=1, source_target_pairs={{0,8},{8,0},{16,24},{24,16},{1,9},{9,1},{17,25},{25,17},{2,10},{10... | collective-permute-start | bytes 393224 | tf_op jit(solution)/shard_map/ppermute | solution.py:36
  74.3 8.2 %copy-start.10 = (bf16[48,3584]{1,0:T(8,128)(2,1)S(1)}, bf16[48,3584]{1,0:T(8,128)(2,1)}, u32[]{:S(2)}) copy-start(bf16[48,3584]{1,0:T(8,128)(2,1)} %copy-done.9) | copy-start | bytes 1032196

commit v5 on v4

--- a/solution.py
+++ b/solution.py
@@ -65,27 +65,24 @@
     return jnp.concatenate([ref[:, columns] for ref in refs], axis=0)
 
 
-def pack_body(tile_ref, grads_ref, top_ref, low_ref, far_ref):
+def pack_body(tile_ref, grads_ref, top_ref, low_ref, sent_ref):
     rank = lax.axis_index("dp")
     side, core = rank // 2, rank % 2
     width = tile_ref.shape[1]
     quarter = grads_ref.shape[1] // 4
     head, both = top_ref.shape[0], 2 * quarter
-    top, low = slice(0, head), slice(head, tile_ref.shape[0])
     parts = [
         grads_ref[:, pl.ds(pl.multiple_of((2 * which + first) * quarter, quarter), quarter)]
         for which in (1 - side, side)
         for first in (core, 1 - core)
     ]
     sent, kept = jnp.concatenate(parts[:2], axis=1), jnp.concatenate(parts[2:], axis=1)
-    tile = tile_ref[...]
-    far_ref[:, :width] = tile
-    far_ref[:, width:] = sent
-    top_ref[:, :width] = tile[top]
-    top_ref[:, width : width + both] = sent[top]
-    top_ref[:, width + both :] = kept[top]
-    low_ref[:, :width] = tile[low]
-    low_ref[:, width:] = kept[low]
+    sent_ref[...] = sent
+    top_ref[:, :width] = tile_ref[:head, :]
+    top_ref[:, width : width + both] = sent[:head]
+    top_ref[:, width + both :] = kept[:head]
+    low_ref[:, :width] = tile_ref[head:, :]
+    low_ref[:, width:] = kept[head:]
 
 
 def pack(tile, grads, head):
@@ -96,7 +93,7 @@
         out_shape=[
             jax.ShapeDtypeStruct((head, width + whole), tile.dtype),
             jax.ShapeDtypeStruct((rows - head, width + whole // 2), tile.dtype),
-            jax.ShapeDtypeStruct((rows, width + whole // 2), tile.dtype),
+            jax.ShapeDtypeStruct((rows, whole // 2), tile.dtype),
         ],
         compiler_params=pltpu.CompilerParams(vmem_limit_bytes=LIMIT),
         cost_estimate=work(0, 4 * rows * (width + whole)),
@@ -107,11 +104,15 @@
     )
 
 
-def block_body(grad_starts, scale_start, step, carried, *refs):
-    pieces, refs = refs[: len(grad_starts)], refs[len(grad_starts) :]
+def block_body(piece_count, sources, extra, scale_start, step, carried, handed, *refs):
+    held, refs = refs[: piece_count + extra], refs[piece_count + extra :]
+    pieces = held[:piece_count]
     scale_ref, *panels = refs[:5]
     carry_refs, refs = refs[5 : 5 + carried], refs[5 + carried :]
     hidden_ref, own_ref, other_ref, *part_refs = refs
+    for index, panel_index in enumerate(handed):
+        part_refs[index][...] = panels[panel_index][...]
+    part_refs = part_refs[len(handed) :]
     width, quarter = panels[0].shape
     rows = own_ref.shape[0]
     kept = hidden_ref.shape[0] - rows
@@ -129,8 +130,8 @@
         hidden_ref[kept:, columns] = b16(factor * activation * up_val)
         received = jnp.concatenate(
             [
-                piece[:, pl.ds(start + which * quarter, quarter)]
-                for piece, start in zip(pieces, grad_starts)
+                held[index][:, pl.ds(start + which * quarter, quarter)]
+                for index, start in sources
             ]
         )
         act_grad = factor * f32(received)
@@ -150,7 +151,9 @@
             first += part_ref.shape[0]
 
 
-def block_pass(pieces, grad_starts, scales, scale_start, panels, part_rows, carry=()):
+def block_pass(
+    pieces, sources, scales, scale_start, panels, part_rows, extra=(), carry=(), handed=()
+):
     rows = sum(piece.shape[0] for piece in pieces)
     width, quarter = panels[0].shape
 
@@ -158,24 +161,38 @@
         return jax.ShapeDtypeStruct((count, 2 * quarter), jnp.bfloat16)
 
     hidden, own, other, *parts = pl.pallas_call(
-        functools.partial(block_body, grad_starts, scale_start, column_step(width), len(carry)),
+        functools.partial(
+            block_body,
+            len(pieces),
+            sources,
+            len(extra),
+            scale_start,
+            column_step(width),
+            len(carry),
+            handed,
+        ),
         out_shape=[wide(rows + len(carry) * rows), wide(rows), wide(rows)]
+        + [jax.ShapeDtypeStruct((width, quarter), jnp.bfloat16)] * len(handed)
         + [jax.ShapeDtypeStruct((count, width), jnp.bfloat16) for count in part_rows],
         compiler_params=pltpu.CompilerParams(vmem_limit_bytes=LIMIT),
         cost_estimate=work(16 * rows * width * quarter, 4 * rows * width),
         name="block_pass",
-    )(*pieces, scales, *panels, *carry)
+    )(*pieces, *extra, scales, *panels, *carry)
     return hidden, own, other, parts
 
 
 def weight_body(piece_count, grad_count, step, *refs):
     pieces, refs = refs[:piece_count], refs[piece_count:]
     grad_refs, refs = refs[:grad_count], refs[grad_count:]
-    *outs, held_ref, out_sems = refs
+    *outs, held_ref, got_held_ref, out_sems, got_sems = refs
     got_ref, outs = (None, outs) if len(outs) == 1 else (outs[0], outs[1:])
     width, columns = outs[0].shape
     chunks = width // step
     grads = joined(grad_refs, slice(None))
+
+    def fetch(chunk):
+        rows = pl.ds(chunk * step, step)
+        return pltpu.make_async_copy(got_ref.at[rows, :], got_held_ref.at[rows, :], got_sems.at[chunk])
 
     def store(chunk):
         slot = chunk % 2
@@ -188,11 +205,15 @@
             for index, out_ref in enumerate(outs)
         ]
 
+    if got_ref is not None:
+        for chunk in range(chunks):
+            fetch(chunk).start()
     for chunk in range(chunks):
         slot = chunk % 2
         total = contract(joined(pieces, pl.ds(chunk * step, step)), grads, 0, 0)
         if got_ref is not None:
-            total = (total + f32(got_ref[pl.ds(chunk * step, step), :])) * (1.0 / TILE)
+            fetch(chunk).wait()
+            total = (total + f32(got_held_ref[pl.ds(chunk * step, step), :])) * (1.0 / TILE)
         if chunk >= 2:
             for copy in store(chunk - 2):
                 copy.wait()
@@ -212,36 +233,37 @@
     here, there = pl.BlockSpec(memory_space=pltpu.VMEM), pl.BlockSpec(memory_space=pl.ANY)
     return pl.pallas_call(
         functools.partial(weight_body, len(pieces), len(grads), step),
-        in_specs=[here] * (len(pieces) + len(grads) + (got is not None)),
+        in_specs=[here] * (len(pieces) + len(grads)) + ([] if got is None else [there]),
         out_specs=[there] * len(widths),
         out_shape=[jax.ShapeDtypeStruct((width, columns), jnp.bfloat16) for columns in widths],
         scratch_shapes=[
             pltpu.VMEM((2, step, both), jnp.bfloat16),
+            pltpu.VMEM((step if got is None else width, both), jnp.bfloat16),
             pltpu.SemaphoreType.DMA((2, 2)),
+            pltpu.SemaphoreType.DMA((width // step,)),
         ],
         compiler_params=pltpu.CompilerParams(vmem_limit_bytes=LIMIT),
         cost_estimate=work(2 * rows * width * both, 2 * width * (rows + 2 * both)),
         name="weight_pass",
     )(
-        *(
-            pltpu.with_memory_space_constraint(part, pltpu.VMEM)
-            for part in (*pieces, *grads, *([] if got is None else [got]))
-        )
+        *(pltpu.with_memory_space_constraint(part, pltpu.VMEM) for part in (*pieces, *grads)),
+        *([] if got is None else [got]),
     )
 
 
 def join_body(home_ref, far_ref, out_ref):
     kept = out_ref.shape[0] - far_ref.shape[0]
-    out_ref[:kept, :] = home_ref[:kept, :]
+    if kept:
+        out_ref[:kept, :] = home_ref[:kept, :]
     out_ref[kept:, :] = b16(f32(home_ref[kept:, :]) + f32(far_ref[...]))
 
 
-def join(home, far):
+def join(home, far, cost):
     return pl.pallas_call(
         join_body,
         out_shape=jax.ShapeDtypeStruct(home.shape, home.dtype),
         compiler_params=pltpu.CompilerParams(vmem_limit_bytes=LIMIT),
-        cost_estimate=LONG,
+        cost_estimate=cost,
         name="join",
     )(home, far)
 
@@ -323,34 +345,44 @@
 
     width = tile.shape[1]
     sent_at, kept_at = width, width + 2 * quarter
-    near_top, near_low, far_message = pack(tile, tile_grad, out_head)
-    x_top, x_low, y_tile = shifted(near_top, 1), shifted(near_low, 1), across(far_message)
+    y_tile = across(tile)
+    near_top, near_low, near_sent = pack(tile, tile_grad, out_head)
+    x_top, x_low, y_grads = shifted(near_top, 1), shifted(near_low, 1), across(near_sent)
     panels = (w_gate[0], w_up[0], within(w_gate[0]), within(w_up[0]))
     hid_hn, own_hn, other_hn, (part_hn,) = block_pass(
-        (near_top, near_low), (kept_at, sent_at), scales, 0, panels, (row_count,)
-    )
-    x_top = after(x_top, hid_hn)
+        (near_top, near_low), ((0, kept_at), (1, sent_at)), scales, 0, panels, (row_count,)
+    )
+    x_top, y_grads = after((x_top, y_grads), hid_hn)
     x_sent = x_top[:, :kept_at]
     xy_top = across(x_sent)
     y_tile = after(y_tile, x_sent)
-    y_sent = y_tile[out_head:]
+    y_sent = jnp.concatenate([y_tile[out_head:], y_grads[out_head:]], axis=1)
     xy_low = shifted(y_sent, 1)
     x_low = after(x_low, y_sent)
 
     lower = row_count - head
-    hid_mid, own_mid, other_mid, (first_hf, rest_hf, head_pn, lower_pn) = block_pass(
+    hid_mid, own_mid, other_mid, mid_parts = block_pass(
         (y_tile, x_top, x_low),
-        (sent_at, kept_at, sent_at),
+        ((3, 0), (1, kept_at), (2, sent_at)),
         scales,
         row_count,
         panels,
         (first, row_count - first, head, lower),
-    )
+        extra=(y_grads,),
+        handed=(2, 3),
+    )
+    *handed, first_hf, rest_hf, head_pn, lower_pn = mid_parts
     first_home = across(first_hf)
     low_near = shifted(lower_pn, -1)
     xy_low, xy_top = after((xy_low, xy_top), hid_mid)
     hid_past, own_pf, other_pf, (head_pf, lower_pf) = block_pass(
-        (xy_top, xy_low), (sent_at, sent_at), scales, 3 * row_count, panels, (head, lower), (hid_mid,)
+        (xy_top, xy_low),
+        ((0, sent_at), (1, sent_at)),
+        scales,
+        3 * row_count,
+        (*panels[:2], *handed),
+        (head, lower),
+        carry=(hid_mid,),
     )
     head_past = across(head_pf)
     low_far = shifted(lower_pf, -1)
@@ -359,20 +391,20 @@
     (sent,) = weight_pass(width, pieces, after((other_hn, other_mid, other_pf), first_home, low_near))
     got = within(sent)
     hid_back = shifted(after(hid_past, sent), -1)
-    head_sum = b16(f32(head_pn) + f32(after(head_past, sent)))
+    head_sum = join(head_pn, after(head_past, sent), work(0, 0))
     head_back = shifted(head_sum, -1)
-    low_sum = join(rest_hf, after(low_far, head_sum))
-    hid_back = after(hid_back, low_sum)
+    low_sum = join(rest_hf, after(low_far, head_sum), LONG)
     low_home = across(low_sum)
+    got = after(got, low_sum)
+    grad_gate, grad_up = weight_pass(width, pieces, (own_hn, own_mid, own_pf), got)
+    hid_back = after(hid_back, grad_gate)
     hid_other = jnp.concatenate([hid_hn[:, quarter:], hid_mid[:row_count, quarter:]])
     hid_other = b16(f32(hid_other) + f32(hid_back[:, quarter:]))
     hid_got = within(hid_other)
-    got = after(got, hid_other, low_sum)
-    grad_gate, grad_up = weight_pass(width, pieces, (own_hn, own_mid, own_pf), got)
     d_tokens, hidden = final(
         part_hn,
         *(first_home, low_near, head_back, low_home),
-        *(hid_hn, hid_mid, hid_back, after(hid_got, grad_gate)),
+        *(hid_hn, hid_mid, hid_back, hid_got),
     )
     return (d_tokens[None], hidden, grad_gate[None], grad_up[None])
 

time: 85.3 us -> 82.6 us (0.968)
  Pallas kernels: 34.9 us -> 30.1 us
  waiting for transfers between devices: 11.3 us -> 14.5 us
  local copies, waits for them, and re-layouts: 8.36 us -> 5.49 us
  starting transfers between devices: 24.2 us -> 26.9 us
    ppermute x5 -> x6, waiting for transfers between devices: 1.8 us -> 5.06 us  [across(): return lax.ppermute(value, 'dp', pairs)]
    pallas_call x2, Pallas kernels: 13.4 us -> 10.3 us  [weight_pass(): pl.pallas_call(functools.partial(weight_body, len(pieces), len(grads), st...]
    ppermute x5 -> x6, starting transfers between devices: 6.14 us -> 8.86 us  [across(): return lax.ppermute(value, 'dp', pairs)]
    pallas_call x1, Pallas kernels: 2.5 us -> 1.32 us  [pack(): pl.pallas_call(pack_body, out_shape=[jax.ShapeDtypeStruct((head, width +...]
    unnamed x24, local copies, waits for them, and re-layouts: 4.94 us -> 3.77 us
    slice x1 -> x2, local copies, waits for them, and re-layouts: 1.02 us -> 0.03 us  [per_device(): y_sent = jnp.concatenate([y_tile[out_head:], y_grads[out_head:]], axis=1)]
    convert_element_type x2 -> x1, other arithmetic: 1.81 us -> 0.94 us  [b16(): return value.astype(jnp.bfloat16)]
  transfers between devices with their start and end apart: 16 -> 17, of which waited for: 5 -> 3; matrix products, arithmetic and copies ran while one was open for 7% -> 4% of each run, Pallas kernels for 39% -> 34%
where the time goes in v5:
time: 82.6 us; the launch traced here: 82.3 us
  Pallas kernels  30.1 us (36%)
  starting transfers between devices  26.9 us (33%)
  waiting for transfers between devices  14.5 us (18%)
  local copies, waits for them, and re-layouts  5.49 us (7%)
  between operations  3.48 us (4%)
  other arithmetic  1.82 us (2%)
    ppermute x7, starting transfers between devices, shifted(): return lax.ppermute(value, 'expert', pairs)  17.3 us
    pallas_call x3, Pallas kernels, block_pass(): pl.pallas_call(functools.partial(block_body, len(pieces), sources, len(ex...  16 us
    pallas_call x2, Pallas kernels, weight_pass(): pl.pallas_call(functools.partial(weight_body, len(pieces), len(grads), st...  10.3 us
    ppermute x7, waiting for transfers between devices, shifted(): return lax.ppermute(value, 'expert', pairs)  9.42 us
    ppermute x6, starting transfers between devices, across(): return lax.ppermute(value, 'dp', pairs)  8.86 us
    ppermute x6, waiting for transfers between devices, across(): return lax.ppermute(value, 'dp', pairs)  5.06 us
    unnamed x24, local copies, waits for them, and re-layouts  3.77 us
    pallas_call x1, Pallas kernels, final(): pl.pallas_call(final_body, out_shape=[jax.ShapeDtypeStruct(near.shape, ne...  2.25 us
  transfers between devices with their start and end apart: 17, of which 3 were waited for; matrix products, arithmetic and copies ran while one was open for 4% of the time, Pallas kernels for 34%

profile of v5, /device:TPU:0, one launch (start us, length us, event | category | flops | bytes accessed | tf_op | source)
XLA Modules:
  0.0 82.3 jit_solution(14785280389864104287)
XLA Ops:
  0.6 0.5 collective-permute-start
  1.1 0.1 collective-permute-start.1
  1.2 2.9 %collective-permute-start.2 = (bf16[128,3584]{1,0:T(8,128)(2,1)}, bf16[128,3584]{1,0:T(8,128)(2,1)S(1)}, u32[]{:S(2)}, u32[]{:S(2)}) collective-permute-start(bf16[128,3584]{1,0:T(8,128)(2,1)} %bitcast.28), channel_id=1, source_target_pairs={{0,16},{8,24},{16,0},{24,8},{1,17},{9,25},{17,1},{25,9},{2,18},{10... | collective-permute-start | bytes 2752520 | tf_op jit(solution)/shard_map/ppermute | solution.py:30
  4.2 1.3 %pack.1 = (bf16[80,4608]{1,0:T(8,128)(2,1)S(1)}, bf16[48,4096]{1,0:T(8,128)(2,1)S(1)}, bf16[128,512]{1,0:T(8,128)(2,1)S(1)}) custom-call(bf16[128,3584]{1,0:T(8,128)(2,1)} %bitcast.29, bf16[128,1024]{1,0:T(8,128)(2,1)} %bitcast.30), custom_call_target="tpu_custom_call" | custom-call | bytes 2359296 | tf_op jit(solution)/shard_map/pack/pallas_call | solution.py:91
  5.5 1.5 %collective-permute-start.3 = (bf16[80,4608]{1,0:T(8,128)(2,1)S(1)}, bf16[80,4608]{1,0:T(8,128)(2,1)S(1)}, u32[]{:S(2)}, u32[]{:S(2)}) collective-permute-start(bf16[80,4608]{1,0:T(8,128)(2,1)S(1)} %get-tuple-element.116.refs_0_), channel_id=1, source_target_pairs={{0,1},{1,2},{2,3},{3,4},{4,5},{5,6},{6,7},{7,0},{8,9},{9,10},{10,1... | collective-permute-start | bytes 2211848 | tf_op jit(solution)/shard_map/ppermute | solution.py:24
  7.0 0.5 collective-permute-start.4
  7.5 1.5 %fusion.4 = (s32[1,1]{1,0:T(1,128)}, s32[1,1]{1,0:T(1,128)}, s32[1,1]{1,0:T(1,128)}, s32[1,1]{1,0:T(1,128)}) fusion(s32[4,8]{1,0:T(4,128)} %param.27, s32[]{:T(128)S(6)} %select_n.62, s32[]{:T(128)S(6)} %select_n.63, s32[]{:T(128)S(6)} %select_n.67, s32[]{:T(128)S(6)} %select_n.70), kind=kLoop, calls=%fused_computation.11 | loop fusion | bytes 48 | tf_op jit(solution)/shard_map/dynamic_slice | solution.py:333
  11.7 0.8 %fusion = (f32[128,1]{0,1:T(1,128)S(1)}, f32[128,1]{0,1:T(1,128)S(1)}, f32[128,1]{0,1:T(1,128)S(1)}, f32[128,1]{0,1:T(1,128)S(1)}) fusion(pred[]{:T(512)} %bitcast.3, f32[4,1024]{1,0:T(4,128)} %param.26, s32[]{:T(128)S(6)} %select_n.62, s32[]{:T(128)S(6)} %select_n.64, s32[]{:T(128)S(6)} %select_n.67, pred[]{:T(512)} %bitcast.5, s32[]{:T(128)S(6)} %select_n.71, ...), kind=kLoop, calls=%fused_computation.7 | loop fusion | flops 512 | bytes 4116 | tf_op jit(solution)/shard_map/reshape | solution.py:336
  12.5 0.1 copy.14.refs_2_.refs_4_
  12.7 0.0 collective-permute-done.refs_5_.refs_7_
  12.7 1.6 %collective-permute-start.5 = (bf16[48,4096]{1,0:T(8,128)(2,1)S(1)}, bf16[48,4096]{1,0:T(8,128)(2,1)S(1)}, u32[]{:S(2)}, u32[]{:S(2)}) collective-permute-start(bf16[48,4096]{1,0:T(8,128)(2,1)S(1)} %get-tuple-element.117.refs_1_), channel_id=1, source_target_pairs={{0,1},{1,2},{2,3},{3,4},{4,5},{5,6},{6,7},{7,0},{8,9},{9,10},{10,1... | collective-permute-start | bytes 1179656 | tf_op jit(solution)/shard_map/ppermute | solution.py:24
  14.3 1.5 %copy-done = bf16[1,3584,256]{2,1,0:T(8,128)(2,1)S(1)} copy-done((bf16[1,3584,256]{2,1,0:T(8,128)(2,1)S(1)}, bf16[1,3584,256]{2,1,0:T(8,128)(2,1)}, u32[]{:S(2)}) %copy-start) | copy-done | bytes 1835032
  15.8 1.5 %copy-done.2 = bf16[1,3584,256]{2,1,0:T(8,128)(2,1)S(1)} copy-done((bf16[1,3584,256]{2,1,0:T(8,128)(2,1)S(1)}, bf16[1,3584,256]{2,1,0:T(8,128)(2,1)}, u32[]{:S(2)}) %copy-start.2) | copy-done | bytes 1835032
  17.3 5.4 %block_pass.3 = (bf16[128,512]{1,0:T(8,128)(2,1)S(1)}, bf16[128,512]{1,0:T(8,128)(2,1)S(1)}, bf16[128,512]{1,0:T(8,128)(2,1)S(1)}, bf16[128,3584]{1,0:T(8,128)(2,1)S(1)}) custom-call(bf16[80,4608]{1,0:T(8,128)(2,1)S(1)} %get-tuple-element.116.refs_0_, bf16[48,4096]{1,0:T(8,128)(2,1)S(1)} %get-tuple-element.117.refs_1_, f32[512,1]{1,0:T(8,128)S(1)} %copy.14.refs_2_.refs_4_, ...), custom_call_target="tpu_custom_call" | custom-call | flops 1879048192 | bytes 1835008 | tf_op jit(solution)/shard_map/block_pass/pallas_call | solution.py:163
  22.7 0.0 copy-start.1
  22.7 5.0 %collective-permute-done.4.refs_3_ = bf16[128,512]{1,0:T(8,128)(2,1)S(1)} collective-permute-done((bf16[128,512]{1,0:T(8,128)(2,1)S(1)}, bf16[128,512]{1,0:T(8,128)(2,1)S(1)}, u32[]{:S(2)}, u32[]{:S(2)}) %collective-permute-start.4) | collective-permute-done | bytes 131104 | tf_op jit(solution)/shard_map/ppermute | solution.py:30
  27.8 1.8 %collective-permute-start.9 = (bf16[80,4096]{1,0:T(8,128)(2,1)S(1)}, bf16[80,4096]{1,0:T(8,128)(2,1)S(1)}, u32[]{:S(2)}, u32[]{:S(2)}) collective-permute-start(bf16[80,4096]{1,0:T(8,128)(2,1)S(1)} %slice.66), channel_id=1, source_target_pairs={{0,16},{8,24},{16,0},{24,8},{1,17},{9,25},{17,1},{25,9},{2,18},{10... | collective-permute-start | bytes 1966088 | tf_op jit(solution)/shard_map/ppermute | solution.py:30
  29.7 1.5 %collective-permute-start.8 = (bf16[48,4096]{1,0:T(8,128)(2,1)S(1)}, bf16[48,4096]{1,0:T(8,128)(2,1)S(1)}, u32[]{:S(2)}, u32[]{:S(2)}) collective-permute-start(bf16[48,4096]{1,0:T(8,128)(2,1)S(1)} %pad_maximum_fusion), channel_id=1, source_target_pairs={{0,1},{1,2},{2,3},{3,4},{4,5},{5,6},{6,7},{7,0},{8,9},{9,10},{10,1... | collective-permute-start | bytes 1179656 | tf_op jit(solution)/shard_map/ppermute | solution.py:24
  31.3 4.4 %collective-permute-done.5.refs_2_.refs_4_ = bf16[48,4096]{1,0:T(8,128)(2,1)S(1)} collective-permute-done((bf16[48,4096]{1,0:T(8,128)(2,1)S(1)}, bf16[48,4096]{1,0:T(8,128)(2,1)S(1)}, u32[]{:S(2)}, u32[]{:S(2)}) %collective-permute-start.5) | collective-permute-done | bytes 393248 | tf_op jit(solution)/shard_map/ppermute | solution.py:24
  35.7 6.6 %block_pass.4 = (bf16[256,512]{1,0:T(8,128)(2,1)S(1)}, bf16[256,512]{1,0:T(8,128)(2,1)S(1)}, bf16[256,512]{1,0:T(8,128)(2,1)S(1)}, bf16[3584,256]{1,0:T(8,128)(2...) custom-call(bf16[128,3584]{1,0:T(8,128)(2,1)S(1)} %collective-permut, ...), custom_call_target="tpu_custom_call" | custom-call | flops 3758096384 | bytes 3670016 | tf_op jit(solution)/shard_map/block_pass/pallas_call | solution.py:163
  42.4 0.0 copy-start.8
  42.4 1.8 %collective-permute-start.7 = (bf16[64,3584]{1,0:T(8,128)(2,1)S(1)}, bf16[64,3584]{1,0:T(8,128)(2,1)S(1)}, u32[]{:S(2)}, u32[]{:S(2)}) collective-permute-start(bf16[64,3584]{1,0:T(8,128)(2,1)S(1)} %get-tuple-element.126), channel_id=1, source_target_pairs={{0,7},{1,0},{2,1},{3,2},{4,3},{5,4},{6,5},{7,6},{8,15},{9,8},{10,9... | collective-permute-start | bytes 1376264 | tf_op jit(solution)/shard_map/ppermute | solution.py:24
  44.2 0.5 collective-permute-start.6
  44.7 3.9 %block_pass.5 = (bf16[256,512]{1,0:T(8,128)(2,1)}, bf16[128,512]{1,0:T(8,128)(2,1)S(1)}, bf16[128,512]{1,0:T(8,128)(2,1)S(1)}, bf16[64,3584]{1,0:T(8,128)(2,1)S(1)}, bf16[64,3584]{1,0:T(8,128)(2,1)S(1)}) custom-call(bf16[80,4096]{1,0:T(8,128)(2,1)S(1)} %collective-permute-done.9.refs_0_.refs_5_, bf16[48,4096]{1,0:T(8,128)(2,1)S(1)} %collective-permute-done.8.refs_1_.refs_6_, ...), custom_call_target="tpu_custom_call" | custom-call | flops 1879048192 | bytes 1835008 | tf_op jit(solution)/shard_map/block_pass/pallas_call | solution.py:163
  48.6 1.5 %collective-permute-start.10 = (bf16[64,3584]{1,0:T(8,128)(2,1)S(1)}, bf16[64,3584]{1,0:T(8,128)(2,1)S(1)}, u32[]{:S(2)}, u32[]{:S(2)}) collective-permute-start(bf16[64,3584]{1,0:T(8,128)(2,1)S(1)} %get-tuple-element.133), channel_id=1, source_target_pairs={{0,16},{8,24},{16,0},{24,8},{1,17},{9,25},{17,1},{25,9},{2,18},{10... | collective-permute-start | bytes 1376264 | tf_op jit(solution)/shard_map/ppermute | solution.py:30
  50.1 5.6 %collective-permute-start.12 = (bf16[64,3584]{1,0:T(8,128)(2,1)S(1)}, bf16[64,3584]{1,0:T(8,128)(2,1)S(1)}, u32[]{:S(2)}, u32[]{:S(2)}) collective-permute-start(bf16[64,3584]{1,0:T(8,128)(2,1)S(1)} %get-tuple-element.142), channel_id=1, source_target_pairs={{0,7},{1,0},{2,1},{3,2},{4,3},{5,4},{6,5},{7,6},{8,15},{9,8},{10,9... | collective-permute-start | bytes 1376264 | tf_op jit(solution)/shard_map/ppermute | solution.py:24
  55.7 0.0 collective-permute-done.6.first_ref
  55.7 0.7 copy-done.10
  56.5 4.7 %weight_pass.2 = bf16[3584,512]{1,0:T(8,128)(2,1)} custom-call(bf16[80,4608]{1,0:T(8,128)(2,1)S(1)} %get-tuple-element.116.refs_0_, bf16[48,4096]{1,0:T(8,128)(2,1)S(1)} %get-tuple-element.117.refs_1_, bf16[128,3584]{1,0:T(8,128)(2,1)S(1)} %collective-permute-done.2.refs_0_.refs_2_, bf16[80,4608]{1,0:T(8,128)(2,1)S(1)} %collective-permute-done.3.refs_1_.refs_3_, ...), custom_call_target="tpu_custom_call" | custom-call | flops 1879048192 | bytes 11010048 | tf_op jit(solution)/shard_map/weight_pass/pallas_call | solution.py:234
  61.2 0.1 collective-permute-start.15
  61.2 2.0 %collective-permute-start.14 = (bf16[256,512]{1,0:T(8,128)(2,1)}, bf16[256,512]{1,0:T(8,128)(2,1)}, u32[]{:S(2)}, u32[]{:S(2)}) collective-permute-start(bf16[256,512]{1,0:T(8,128)(2,1)} %get-tuple-element.145), channel_id=1, source_target_pairs={{0,7},{1,0},{2,1},{3,2},{4,3},{5,4},{6,5},{7,6},{8,15},{9,8},{10,9... | collective-permute-start | bytes 786440 | tf_op jit(solution)/shard_map/ppermute | solution.py:24
  63.3 0.0 collective-permute-done.10.far_ref
  63.3 0.1 join.2
  63.4 0.0 collective-permute-done.12.far_ref
  63.4 0.0 copy-start.9
  63.4 0.0 copy-start.5
  63.4 0.0 copy-start.7
  63.4 0.1 join.3
  63.5 1.6 %collective-permute-start.13 = (bf16[80,3584]{1,0:T(8,128)(2,1)S(1)}, bf16[80,3584]{1,0:T(8,128)(2,1)S(1)}, u32[]{:S(2)}, u32[]{:S(2)}) collective-permute-start(bf16[80,3584]{1,0:T(8,128)(2,1)S(1)} %join.3), channel_id=1, source_target_pairs={{0,16},{8,24},{16,0},{24,8},{1,17},{9,25},{17,1},{25,9},{2,18},{10... | collective-permute-start | bytes 1720328 | tf_op jit(solution)/shard_map/ppermute | solution.py:30
  65.2 3.2 %collective-permute-start.11 = (bf16[64,3584]{1,0:T(8,128)(2,1)S(1)}, bf16[64,3584]{1,0:T(8,128)(2,1)S(1)}, u32[]{:S(2)}, u32[]{:S(2)}) collective-permute-start(bf16[64,3584]{1,0:T(8,128)(2,1)S(1)} %join.2), channel_id=1, source_target_pairs={{0,7},{1,0},{2,1},{3,2},{4,3},{5,4},{6,5},{7,6},{8,15},{9,8},{10,9... | collective-permute-start | bytes 1376264 | tf_op jit(solution)/shard_map/ppermute | solution.py:24
  68.3 0.0 collective-permute-done.15.refs_10_
  68.3 5.7 %weight_pass.3 = (bf16[3584,256]{1,0:T(8,128)(2,1)}, bf16[3584,256]{1,0:T(8,128)(2,1)}) custom-call(bf16[80,4608]{1,0:T(8,128)(2,1)S(1)} %get-tuple-element.116.refs_0_, bf16[48,4096]{1,0:T(8,128)(2,1)S(1)} %get-tuple-element.117.refs_1_, bf16[128,3584]{1,0:T(8,128)(2,1)S(1)} %collective-permute-done.2.refs_0_.refs_2_, ...), custom_call_target="tpu_custom_call" | custom-call | flops 1879048192 | bytes 11010048 | tf_op jit(solution)/shard_map/weight_pass/pallas_call | solution.py:234
  74.0 0.9 %add_convert_fusion = bf16[256,256]{1,0:T(8,128)(2,1)S(1)} fusion(bf16[128,256]{1,0:T(8,128)(2,1)S(1)} %slice.70, bf16[128,256]{1,0:T(8,128)(2,1)S(1)} %slice.69, bf16[256,512]{1,0:T(8,128)(2,1)} %collective-permute-done.14.hidden_back_ref), kind=kLoop, calls=%fused_computation.1 | loop fusion | flops 458752 | bytes 393216 | tf_op jit(solution)/shard_map/convert_element_type | solution.py:48
  74.9 0.1 collective-permute-start.16
  75.0 5.0 %collective-permute-done.11.head_ref = bf16[64,3584]{1,0:T(8,128)(2,1)S(1)} collective-permute-done((bf16[64,3584]{1,0:T(8,128)(2,1)S(1)}, bf16[64,3584]{1,0:T(8,128)(2,1)S(1)}, u32[]{:S(2)}, u32[]{:S(2)}) %collective-permute-start.11) | collective-permute-done | bytes 458784 | tf_op jit(solution)/shard_map/ppermute | solution.py:24
  80.0 0.0 collective-permute-done.13.low_ref
  80.0 0.0 collective-permute-done.16.hidden_got_ref
  80.0 2.3 %final.1 = (bf16[128,3584]{1,0:T(8,128)(2,1)}, bf16[4,128,256]{2,1,0:T(8,128)(2,1)}) custom-call(bf16[128,3584]{1,0:T(8,128)(2,1)S(1)} %get-tuple-element.118.near_ref, bf16[48,3584]{1,0:T(8,128)(2,1)S(1)} %copy-done.11, bf16[64,3584]{1,0:T(8,128)(2,1)S(1)} %collective-permute-done.7.low_near_ref, bf16[64,3584]{1,0:T(8,128)(2,1)S(1)} %collective-permute-done.11.head_ref, ...), custom_call_target="tpu_custom_call" | custom-call | flops 999999995904 | bytes 1000000000 | tf_op jit(solution)/shard_map/final/pallas_call | solution.py:307
  (30 shorter events, 0.2 us)
Async XLA Ops:
  0.6 12.0 %collective-permute-start = (bf16[3584,256]{1,0:T(8,128)(2,1)}, bf16[3584,256]{1,0:T(8,128)(2,1)}, u32[]{:S(2)}, u32[]{:S(2)}) collective-permute-start(bf16[3584,256]{1,0:T(8,128)(2,1)} %bitcast.20), channel_id=1, source_target_pairs={{0,8},{8,0},{16,24},{24,16},{1,9},{9,1},{17,25},{25,17},{2,10},{10... | collective-permute-start | bytes 5505032 | tf_op jit(solution)/shard_map/ppermute | solution.py:36
  1.1 13.1 %collective-permute-start.1 = (bf16[3584,256]{1,0:T(8,128)(2,1)}, bf16[3584,256]{1,0:T(8,128)(2,1)}, u32[]{:S(2)}, u32[]{:S(2)}) collective-permute-start(bf16[3584,256]{1,0:T(8,128)(2,1)} %bitcast.24), channel_id=1, source_target_pairs={{0,8},{8,0},{16,24},{24,16},{1,9},{9,1},{17,25},{25,17},{2,10},{10... | collective-permute-start | bytes 5505032 | tf_op jit(solution)/shard_map/ppermute | solution.py:36
  1.2 28.4 %collective-permute-start.2 = (bf16[128,3584]{1,0:T(8,128)(2,1)}, bf16[128,3584]{1,0:T(8,128)(2,1)S(1)}, u32[]{:S(2)}, u32[]{:S(2)}) collective-permute-start(bf16[128,3584]{1,0:T(8,128)(2,1)} %bitcast.28), channel_id=1, source_target_pairs={{0,16},{8,24},{16,0},{24,8},{1,17},{9,25},{17,1},{25,9},{2,18},{10... | collective-permute-start | bytes 2752520 | tf_op jit(solution)/shard_map/ppermute | solution.py:30
  5.5 22.3 %collective-permute-start.3 = (bf16[80,4608]{1,0:T(8,128)(2,1)S(1)}, bf16[80,4608]{1,0:T(8,128)(2,1)S(1)}, u32[]{:S(2)}, u32[]{:S(2)}) collective-permute-start(bf16[80,4608]{1,0:T(8,128)(2,1)S(1)} %get-tuple-element.116.refs_0_), channel_id=1, source_target_pairs={{0,1},{1,2},{2,3},{3,4},{4,5},{5,6},{6,7},{7,0},{8,9},{9,10},{10,1... | collective-permute-start | bytes 2211848 | tf_op jit(solution)/shard_map/ppermute | solution.py:24
  7.0 20.7 %collective-permute-start.4 = (bf16[128,512]{1,0:T(8,128)(2,1)S(1)}, bf16[128,512]{1,0:T(8,128)(2,1)S(1)}, u32[]{:S(2)}, u32[]{:S(2)}) collective-permute-start(bf16[128,512]{1,0:T(8,128)(2,1)S(1)} %get-tuple-element.119), channel_id=1, source_target_pairs={{0,16},{8,24},{16,0},{24,8},{1,17},{9,25},{17,1},{25,9},{2,18},{10... | collective-permute-start | bytes 393224 | tf_op jit(solution)/shard_map/ppermute | solution.py:30
  12.7 23.0 %collective-permute-start.5 = (bf16[48,4096]{1,0:T(8,128)(2,1)S(1)}, bf16[48,4096]{1,0:T(8,128)(2,1)S(1)}, u32[]{:S(2)}, u32[]{:S(2)}) collective-permute-start(bf16[48,4096]{1,0:T(8,128)(2,1)S(1)} %get-tuple-element.117.refs_1_), channel_id=1, source_target_pairs={{0,1},{1,2},{2,3},{3,4},{4,5},{5,6},{6,7},{7,0},{8,9},{9,10},{10,1... | collective-permute-start | bytes 1179656 | tf_op jit(solution)/shard_map/ppermute | solution.py:24
  14.3 1.5 %copy-start = (bf16[1,3584,256]{2,1,0:T(8,128)(2,1)S(1)}, bf16[1,3584,256]{2,1,0:T(8,128)(2,1)}, u32[]{:S(2)}) copy-start(bf16[1,3584,256]{2,1,0:T(8,128)(2,1)} %param.28) | copy-start | bytes 5505028
  15.8 1.5 %copy-start.2 = (bf16[1,3584,256]{2,1,0:T(8,128)(2,1)S(1)}, bf16[1,3584,256]{2,1,0:T(8,128)(2,1)}, u32[]{:S(2)}) copy-start(bf16[1,3584,256]{2,1,0:T(8,128)(2,1)} %param.29) | copy-start | bytes 5505028
  17.3 18.4 %copy-start.3 = (bf16[1,3584,256]{2,1,0:T(8,128)(2,1)S(1)}, bf16[1,3584,256]{2,1,0:T(8,128)(2,1)}, u32[]{:S(2)}) copy-start(bf16[1,3584,256]{2,1,0:T(8,128)(2,1)} %param.29) | copy-start | bytes 5505028
  22.7 13.0 %copy-start.1 = (bf16[1,3584,256]{2,1,0:T(8,128)(2,1)S(1)}, bf16[1,3584,256]{2,1,0:T(8,128)(2,1)}, u32[]{:S(2)}) copy-start(bf16[1,3584,256]{2,1,0:T(8,128)(2,1)} %param.28) | copy-start | bytes 5505028
  27.8 16.9 %collective-permute-start.9 = (bf16[80,4096]{1,0:T(8,128)(2,1)S(1)}, bf16[80,4096]{1,0:T(8,128)(2,1)S(1)}, u32[]{:S(2)}, u32[]{:S(2)}) collective-permute-start(bf16[80,4096]{1,0:T(8,128)(2,1)S(1)} %slice.66), channel_id=1, source_target_pairs={{0,16},{8,24},{16,0},{24,8},{1,17},{9,25},{17,1},{25,9},{2,18},{10... | collective-permute-start | bytes 1966088 | tf_op jit(solution)/shard_map/ppermute | solution.py:30
  29.7 15.0 %collective-permute-start.8 = (bf16[48,4096]{1,0:T(8,128)(2,1)S(1)}, bf16[48,4096]{1,0:T(8,128)(2,1)S(1)}, u32[]{:S(2)}, u32[]{:S(2)}) collective-permute-start(bf16[48,4096]{1,0:T(8,128)(2,1)S(1)} %pad_maximum_fusion), channel_id=1, source_target_pairs={{0,1},{1,2},{2,3},{3,4},{4,5},{5,6},{6,7},{7,0},{8,9},{9,10},{10,1... | collective-permute-start | bytes 1179656 | tf_op jit(solution)/shard_map/ppermute | solution.py:24
  35.7 20.7 %copy-start.6 = (bf16[48,4096]{1,0:T(8,128)(2,1)}, bf16[48,4096]{1,0:T(8,128)(2,1)S(1)}, u32[]{:S(2)}) copy-start(bf16[48,4096]{1,0:T(8,128)(2,1)S(1)} %collective-permute-done.5.refs_2_.refs_4_) | copy-start | bytes 1179652
  42.4 6.2 %copy-start.8 = (bf16[256,512]{1,0:T(8,128)(2,1)}, bf16[256,512]{1,0:T(8,128)(2,1)S(1)}, u32[]{:S(2)}) copy-start(bf16[256,512]{1,0:T(8,128)(2,1)S(1)} %get-tuple-element.128.refs_7_.hidden_far_ref) | copy-start | bytes 786436
  42.4 14.1 %collective-permute-start.7 = (bf16[64,3584]{1,0:T(8,128)(2,1)S(1)}, bf16[64,3584]{1,0:T(8,128)(2,1)S(1)}, u32[]{:S(2)}, u32[]{:S(2)}) collective-permute-start(bf16[64,3584]{1,0:T(8,128)(2,1)S(1)} %get-tuple-element.126), channel_id=1, source_target_pairs={{0,7},{1,0},{2,1},{3,2},{4,3},{5,4},{6,5},{7,6},{8,15},{9,8},{10,9... | collective-permute-start | bytes 1376264 | tf_op jit(solution)/shard_map/ppermute | solution.py:24
  44.2 11.5 %collective-permute-start.6 = (bf16[48,3584]{1,0:T(8,128)(2,1)S(1)}, bf16[48,3584]{1,0:T(8,128)(2,1)S(1)}, u32[]{:S(2)}, u32[]{:S(2)}) collective-permute-start(bf16[48,3584]{1,0:T(8,128)(2,1)S(1)} %get-tuple-element.125), channel_id=1, source_target_pairs={{0,16},{8,24},{16,0},{24,8},{1,17},{9,25},{17,1},{25,9},{2,18},{10... | collective-permute-start | bytes 1032200 | tf_op jit(solution)/shard_map/ppermute | solution.py:30
  44.7 11.8 %copy-start.4 = (bf16[48,4096]{1,0:T(8,128)(2,1)}, bf16[48,4096]{1,0:T(8,128)(2,1)S(1)}, u32[]{:S(2)}) copy-start(bf16[48,4096]{1,0:T(8,128)(2,1)S(1)} %collective-permute-done.8.refs_1_.refs_6_) | copy-start | bytes 1179652
  48.6 14.7 %collective-permute-start.10 = (bf16[64,3584]{1,0:T(8,128)(2,1)S(1)}, bf16[64,3584]{1,0:T(8,128)(2,1)S(1)}, u32[]{:S(2)}, u32[]{:S(2)}) collective-permute-start(bf16[64,3584]{1,0:T(8,128)(2,1)S(1)} %get-tuple-element.133), channel_id=1, source_target_pairs={{0,16},{8,24},{16,0},{24,8},{1,17},{9,25},{17,1},{25,9},{2,18},{10... | collective-permute-start | bytes 1376264 | tf_op jit(solution)/shard_map/ppermute | solution.py:30
  50.1 13.3 %collective-permute-start.12 = (bf16[64,3584]{1,0:T(8,128)(2,1)S(1)}, bf16[64,3584]{1,0:T(8,128)(2,1)S(1)}, u32[]{:S(2)}, u32[]{:S(2)}) collective-permute-start(bf16[64,3584]{1,0:T(8,128)(2,1)S(1)} %get-tuple-element.142), channel_id=1, source_target_pairs={{0,7},{1,0},{2,1},{3,2},{4,3},{5,4},{6,5},{7,6},{8,15},{9,8},{10,9... | collective-permute-start | bytes 1376264 | tf_op jit(solution)/shard_map/ppermute | solution.py:24
  55.7 0.7 copy-start.10
  61.2 7.2 %collective-permute-start.15 = (bf16[3584,512]{1,0:T(8,128)(2,1)}, bf16[3584,512]{1,0:T(8,128)(2,1)}, u32[]{:S(2)}, u32[]{:S(2)}) collective-permute-start(bf16[3584,512]{1,0:T(8,128)(2,1)} %weight_pass.2), channel_id=1, source_target_pairs={{0,8},{8,0},{16,24},{24,16},{1,9},{9,1},{17,25},{25,17},{2,10},{10... | collective-permute-start | bytes 11010056 | tf_op jit(solution)/shard_map/ppermute | solution.py:36
  61.2 12.8 %collective-permute-start.14 = (bf16[256,512]{1,0:T(8,128)(2,1)}, bf16[256,512]{1,0:T(8,128)(2,1)}, u32[]{:S(2)}, u32[]{:S(2)}) collective-permute-start(bf16[256,512]{1,0:T(8,128)(2,1)} %get-tuple-element.145), channel_id=1, source_target_pairs={{0,7},{1,0},{2,1},{3,2},{4,3},{5,4},{6,5},{7,6},{8,15},{9,8},{10,9... | collective-permute-start | bytes 786440 | tf_op jit(solution)/shard_map/ppermute | solution.py:24
  63.4 1.7 %copy-start.9 = (bf16[256,512]{1,0:T(8,128)(2,1)S(1)}, bf16[256,512]{1,0:T(8,128)(2,1)}, u32[]{:S(2)}) copy-start(bf16[256,512]{1,0:T(8,128)(2,1)} %copy-done.8) | copy-start | bytes 786436
  63.4 4.9 %copy-start.5 = (bf16[48,4096]{1,0:T(8,128)(2,1)S(1)}, bf16[48,4096]{1,0:T(8,128)(2,1)}, u32[]{:S(2)}) copy-start(bf16[48,4096]{1,0:T(8,128)(2,1)} %copy-done.4) | copy-start | bytes 1179652
  63.4 4.9 %copy-start.7 = (bf16[48,4096]{1,0:T(8,128)(2,1)S(1)}, bf16[48,4096]{1,0:T(8,128)(2,1)}, u32[]{:S(2)}) copy-start(bf16[48,4096]{1,0:T(8,128)(2,1)} %copy-done.6) | copy-start | bytes 1179652
  63.5 16.4 %collective-permute-start.13 = (bf16[80,3584]{1,0:T(8,128)(2,1)S(1)}, bf16[80,3584]{1,0:T(8,128)(2,1)S(1)}, u32[]{:S(2)}, u32[]{:S(2)}) collective-permute-start(bf16[80,3584]{1,0:T(8,128)(2,1)S(1)} %join.3), channel_id=1, source_target_pairs={{0,16},{8,24},{16,0},{24,8},{1,17},{9,25},{17,1},{25,9},{2,18},{10... | collective-permute-start | bytes 1720328 | tf_op jit(solution)/shard_map/ppermute | solution.py:30
  65.2 14.8 %collective-permute-start.11 = (bf16[64,3584]{1,0:T(8,128)(2,1)S(1)}, bf16[64,3584]{1,0:T(8,128)(2,1)S(1)}, u32[]{:S(2)}, u32[]{:S(2)}) collective-permute-start(bf16[64,3584]{1,0:T(8,128)(2,1)S(1)} %join.2), channel_id=1, source_target_pairs={{0,7},{1,0},{2,1},{3,2},{4,3},{5,4},{6,5},{7,6},{8,15},{9,8},{10,9... | collective-permute-start | bytes 1376264 | tf_op jit(solution)/shard_map/ppermute | solution.py:24
  68.3 11.7 %copy-start.11 = (bf16[48,3584]{1,0:T(8,128)(2,1)S(1)}, bf16[48,3584]{1,0:T(8,128)(2,1)}, u32[]{:S(2)}) copy-start(bf16[48,3584]{1,0:T(8,128)(2,1)} %copy-done.10) | copy-start | bytes 1032196
  74.9 5.0 %collective-permute-start.16 = (bf16[256,256]{1,0:T(8,128)(2,1)S(1)}, bf16[256,256]{1,0:T(8,128)(2,1)S(1)}, u32[]{:S(2)}, u32[]{:S(2)}) collective-permute-start(bf16[256,256]{1,0:T(8,128)(2,1)S(1)} %add_convert_fusion), channel_id=1, source_target_pairs={{0,8},{8,0},{16,24},{24,16},{1,9},{9,1},{17,25},{25,17},{2,10},{10... | collective-permute-start | bytes 393224 | tf_op jit(solution)/shard_map/ppermute | solution.py:36

commit v6 on v5

--- a/solution.py
+++ b/solution.py
@@ -70,7 +70,7 @@
     side, core = rank // 2, rank % 2
     width = tile_ref.shape[1]
     quarter = grads_ref.shape[1] // 4
-    head, both = top_ref.shape[0], 2 * quarter
+    head = top_ref.shape[0]
     parts = [
         grads_ref[:, pl.ds(pl.multiple_of((2 * which + first) * quarter, quarter), quarter)]
         for which in (1 - side, side)
@@ -79,8 +79,7 @@
     sent, kept = jnp.concatenate(parts[:2], axis=1), jnp.concatenate(parts[2:], axis=1)
     sent_ref[...] = sent
     top_ref[:, :width] = tile_ref[:head, :]
-    top_ref[:, width : width + both] = sent[:head]
-    top_ref[:, width + both :] = kept[:head]
+    top_ref[:, width:] = kept[:head]
     low_ref[:, :width] = tile_ref[head:, :]
     low_ref[:, width:] = kept[head:]
 
@@ -91,7 +90,7 @@
     return pl.pallas_call(
         pack_body,
         out_shape=[
-            jax.ShapeDtypeStruct((head, width + whole), tile.dtype),
+            jax.ShapeDtypeStruct((head, width + whole // 2), tile.dtype),
             jax.ShapeDtypeStruct((rows - head, width + whole // 2), tile.dtype),
             jax.ShapeDtypeStruct((rows, whole // 2), tile.dtype),
         ],
@@ -274,12 +273,7 @@
     low_near_ref,
     head_ref,
     low_ref,
-    hidden_near_ref,
-    hidden_far_ref,
-    hidden_back_ref,
-    hidden_got_ref,
     tokens_ref,
-    hidden_ref,
 ):
     rows = tokens_ref.shape[0]
     first, head = first_ref.shape[0], head_ref.shape[0]
@@ -293,27 +287,37 @@
     tokens_ref[head:, :] = b16(
         f32(near_ref[head:, :]) + f32(low_near_ref[...]) + f32(low_ref[rest:, :])
     )
-    rank = lax.axis_index("dp")
-    quarter = hidden_ref.shape[2]
-    for block, home_ref in enumerate((hidden_near_ref, hidden_far_ref)):
-        back = hidden_back_ref[pl.ds(block * rows, rows), :quarter]
-        hidden_ref[(2 * block) ^ rank] = b16(f32(home_ref[:rows, :quarter]) + f32(back))
-        hidden_ref[(2 * block + 1) ^ rank] = hidden_got_ref[pl.ds(block * rows, rows), :]
 
 
 def final(near, *others):
-    rows = near.shape[0]
-    quarter = others[-1].shape[1]
     return pl.pallas_call(
         final_body,
-        out_shape=[
-            jax.ShapeDtypeStruct(near.shape, near.dtype),
-            jax.ShapeDtypeStruct((4, rows, quarter), near.dtype),
-        ],
+        out_shape=jax.ShapeDtypeStruct(near.shape, near.dtype),
         compiler_params=pltpu.CompilerParams(vmem_limit_bytes=LIMIT),
         cost_estimate=LONG,
         name="final",
-    )(*(pltpu.with_memory_space_constraint(part, pltpu.VMEM) for part in (near, *others)))
+    )(near, *others)
+
+
+def hidden_body(near_ref, far_ref, back_ref, got_ref, out_ref):
+    rank = lax.axis_index("dp")
+    _, rows, quarter = out_ref.shape
+    for block, home_ref in enumerate((near_ref, far_ref)):
+        part = pl.ds(block * rows, rows)
+        home, back = home_ref[:rows, :quarter], back_ref[part, :quarter]
+        out_ref[(2 * block) ^ rank] = b16(f32(home) + f32(back))
+        out_ref[(2 * block + 1) ^ rank] = got_ref[part, :]
+
+
+def hidden_pass(near, far, back, got):
+    rows, both = near.shape
+    return pl.pallas_call(
+        hidden_body,
+        out_shape=jax.ShapeDtypeStruct((4, rows, both // 2), near.dtype),
+        compiler_params=pltpu.CompilerParams(vmem_limit_bytes=LIMIT),
+        cost_estimate=work(0, 0),
+        name="hidden_pass",
+    )(near, far, back, got)
 
 
 def per_device(tokens, cotangent, gate_weights, tile_expert, w_gate, w_up):
@@ -344,26 +348,26 @@
     )
 
     width = tile.shape[1]
-    sent_at, kept_at = width, width + 2 * quarter
     y_tile = across(tile)
     near_top, near_low, near_sent = pack(tile, tile_grad, out_head)
     x_top, x_low, y_grads = shifted(near_top, 1), shifted(near_low, 1), across(near_sent)
     panels = (w_gate[0], w_up[0], within(w_gate[0]), within(w_up[0]))
     hid_hn, own_hn, other_hn, (part_hn,) = block_pass(
-        (near_top, near_low), ((0, kept_at), (1, sent_at)), scales, 0, panels, (row_count,)
+        (near_top, near_low), ((0, width), (1, width)), scales, 0, panels, (row_count,)
     )
     x_top, y_grads = after((x_top, y_grads), hid_hn)
-    x_sent = x_top[:, :kept_at]
+    x_sent = x_top[:, :width]
     xy_top = across(x_sent)
     y_tile = after(y_tile, x_sent)
-    y_sent = jnp.concatenate([y_tile[out_head:], y_grads[out_head:]], axis=1)
+    y_sent = y_tile[out_head:]
     xy_low = shifted(y_sent, 1)
+    xy_grads = shifted(y_grads, 1)
     x_low = after(x_low, y_sent)
 
     lower = row_count - head
     hid_mid, own_mid, other_mid, mid_parts = block_pass(
         (y_tile, x_top, x_low),
-        ((3, 0), (1, kept_at), (2, sent_at)),
+        ((3, 0), (1, width), (2, width)),
         scales,
         row_count,
         panels,
@@ -374,14 +378,15 @@
     *handed, first_hf, rest_hf, head_pn, lower_pn = mid_parts
     first_home = across(first_hf)
     low_near = shifted(lower_pn, -1)
-    xy_low, xy_top = after((xy_low, xy_top), hid_mid)
+    xy_low, xy_top, xy_grads = after((xy_low, xy_top, xy_grads), hid_mid)
     hid_past, own_pf, other_pf, (head_pf, lower_pf) = block_pass(
         (xy_top, xy_low),
-        ((0, sent_at), (1, sent_at)),
+        ((2, 0),),
         scales,
         3 * row_count,
         (*panels[:2], *handed),
         (head, lower),
+        extra=(xy_grads,),
         carry=(hid_mid,),
     )
     head_past = across(head_pf)
@@ -401,11 +406,8 @@
     hid_other = jnp.concatenate([hid_hn[:, quarter:], hid_mid[:row_count, quarter:]])
     hid_other = b16(f32(hid_other) + f32(hid_back[:, quarter:]))
     hid_got = within(hid_other)
-    d_tokens, hidden = final(
-        part_hn,
-        *(first_home, low_near, head_back, low_home),
-        *(hid_hn, hid_mid, hid_back, hid_got),
-    )
+    hidden = hidden_pass(hid_hn, hid_mid, hid_back, hid_got)
+    d_tokens = final(part_hn, first_home, low_near, after(head_back, hidden), low_home)
     return (d_tokens[None], hidden, grad_gate[None], grad_up[None])
 
 

time: 82.6 us -> 80.9 us (0.979)
  waiting for transfers between devices: 14.5 us -> 12.8 us
    ppermute x7 -> x8, waiting for transfers between devices: 9.42 us -> 6.32 us  [shifted(): return lax.ppermute(value, 'expert', pairs)]
    ppermute x6, starting transfers between devices: 8.86 us -> 6.85 us  [across(): return lax.ppermute(value, 'dp', pairs)]
    ppermute x7 -> x8, starting transfers between devices: 17.3 us -> 19.3 us  [shifted(): return lax.ppermute(value, 'expert', pairs)]
    ppermute x4, waiting for transfers between devices: 0.01 us -> 1.34 us  [within(): return lax.ppermute(value, 'dp', pairs)]
    pallas_call x1 -> x2, Pallas kernels: 2.25 us -> 2.94 us  [the longest x1 1.69 us: hidden_pass(): pl.pallas_call(hidden_body, out_shape=jax.ShapeDtypeStruct((4, rows, both...]
  transfers between devices with their start and end apart: 17 -> 18, of which waited for: 3 -> 7; matrix products, arithmetic and copies ran while one was open for 4% -> 4% of each run, Pallas kernels for 34% -> 37%
where the time goes in v6:
time: 80.9 us; the launch traced here: 80.5 us
  Pallas kernels  30.7 us (38%)
  starting transfers between devices  26.9 us (33%)
  waiting for transfers between devices  12.8 us (16%)
  local copies, waits for them, and re-layouts  4.94 us (6%)
  between operations  3.36 us (4%)
  other arithmetic  1.79 us (2%)
    ppermute x8, starting transfers between devices, shifted(): return lax.ppermute(value, 'expert', pairs)  19.3 us
    pallas_call x3, Pallas kernels, block_pass(): pl.pallas_call(functools.partial(block_body, len(pieces), sources, len(ex...  15.9 us
    pallas_call x2, Pallas kernels, weight_pass(): pl.pallas_call(functools.partial(weight_body, len(pieces), len(grads), st...  10.3 us
    ppermute x6, starting transfers between devices, across(): return lax.ppermute(value, 'dp', pairs)  6.85 us
    ppermute x8, waiting for transfers between devices, shifted(): return lax.ppermute(value, 'expert', pairs)  6.32 us
    ppermute x6, waiting for transfers between devices, across(): return lax.ppermute(value, 'dp', pairs)  5.17 us
    unnamed x24, local copies, waits for them, and re-layouts  3.27 us
    pallas_call x1, Pallas kernels, hidden_pass(): pl.pallas_call(hidden_body, out_shape=jax.ShapeDtypeStruct((4, rows, both...  1.69 us
  transfers between devices with their start and end apart: 18, of which 7 were waited for; matrix products, arithmetic and copies ran while one was open for 4% of the time, Pallas kernels for 37%

profile of v6, /device:TPU:0, one launch (start us, length us, event | category | flops | bytes accessed | tf_op | source)
XLA Modules:
  0.0 80.5 jit_solution(13810315536030425748)
XLA Ops:
  0.6 0.5 collective-permute-start
  1.1 0.1 collective-permute-start.1
  1.2 2.9 %collective-permute-start.2 = (bf16[128,3584]{1,0:T(8,128)(2,1)}, bf16[128,3584]{1,0:T(8,128)(2,1)S(1)}, u32[]{:S(2)}, u32[]{:S(2)}) collective-permute-start(bf16[128,3584]{1,0:T(8,128)(2,1)} %bitcast.28), channel_id=1, source_target_pairs={{0,16},{8,24},{16,0},{24,8},{1,17},{9,25},{17,1},{25,9},{2,18},{10... | collective-permute-start | bytes 2752520 | tf_op jit(solution)/shard_map/ppermute | solution.py:30
  4.2 1.3 %pack.1 = (bf16[80,4096]{1,0:T(8,128)(2,1)S(1)}, bf16[48,4096]{1,0:T(8,128)(2,1)S(1)}, bf16[128,512]{1,0:T(8,128)(2,1)S(1)}) custom-call(bf16[128,3584]{1,0:T(8,128)(2,1)} %bitcast.29, bf16[128,1024]{1,0:T(8,128)(2,1)} %bitcast.30), custom_call_target="tpu_custom_call" | custom-call | bytes 2359296 | tf_op jit(solution)/shard_map/pack/pallas_call | solution.py:90
  5.5 1.5 %collective-permute-start.3 = (bf16[80,4096]{1,0:T(8,128)(2,1)S(1)}, bf16[80,4096]{1,0:T(8,128)(2,1)S(1)}, u32[]{:S(2)}, u32[]{:S(2)}) collective-permute-start(bf16[80,4096]{1,0:T(8,128)(2,1)S(1)} %get-tuple-element.116.refs_0_), channel_id=1, source_target_pairs={{0,1},{1,2},{2,3},{3,4},{4,5},{5,6},{6,7},{7,0},{8,9},{9,10},{10,1... | collective-permute-start | bytes 1966088 | tf_op jit(solution)/shard_map/ppermute | solution.py:24
  7.0 0.5 collective-permute-start.4
  7.5 1.5 %fusion.4 = (s32[1,1]{1,0:T(1,128)}, s32[1,1]{1,0:T(1,128)}, s32[1,1]{1,0:T(1,128)}, s32[1,1]{1,0:T(1,128)}) fusion(s32[4,8]{1,0:T(4,128)} %param.27, s32[]{:T(128)S(6)} %select_n.62, s32[]{:T(128)S(6)} %select_n.63, s32[]{:T(128)S(6)} %select_n.67, s32[]{:T(128)S(6)} %select_n.70), kind=kLoop, calls=%fused_computation.10 | loop fusion | bytes 48 | tf_op jit(solution)/shard_map/dynamic_slice | solution.py:337
  11.6 0.8 %fusion = (f32[128,1]{0,1:T(1,128)S(1)}, f32[128,1]{0,1:T(1,128)S(1)}, f32[128,1]{0,1:T(1,128)S(1)}, f32[128,1]{0,1:T(1,128)S(1)}) fusion(pred[]{:T(512)} %bitcast.3, f32[4,1024]{1,0:T(4,128)} %param.26, s32[]{:T(128)S(6)} %select_n.62, s32[]{:T(128)S(6)} %select_n.64, s32[]{:T(128)S(6)} %select_n.67, pred[]{:T(512)} %bitcast.5, s32[]{:T(128)S(6)} %select_n.71, ...), kind=kLoop, calls=%fused_computation.6 | loop fusion | flops 512 | bytes 4116 | tf_op jit(solution)/shard_map/reshape | solution.py:340
  12.4 0.1 copy.14.refs_2_.refs_4_.refs_3_
  12.6 0.0 collective-permute-done.refs_5_.refs_7_
  12.6 1.6 %collective-permute-start.5 = (bf16[48,4096]{1,0:T(8,128)(2,1)S(1)}, bf16[48,4096]{1,0:T(8,128)(2,1)S(1)}, u32[]{:S(2)}, u32[]{:S(2)}) collective-permute-start(bf16[48,4096]{1,0:T(8,128)(2,1)S(1)} %get-tuple-element.117.refs_1_), channel_id=1, source_target_pairs={{0,1},{1,2},{2,3},{3,4},{4,5},{5,6},{6,7},{7,0},{8,9},{9,10},{10,1... | collective-permute-start | bytes 1179656 | tf_op jit(solution)/shard_map/ppermute | solution.py:24
  14.2 0.0 collective-permute-done.1.refs_6_.refs_8_
  14.2 1.5 %copy-done = bf16[1,3584,256]{2,1,0:T(8,128)(2,1)S(1)} copy-done((bf16[1,3584,256]{2,1,0:T(8,128)(2,1)S(1)}, bf16[1,3584,256]{2,1,0:T(8,128)(2,1)}, u32[]{:S(2)}) %copy-start) | copy-done | bytes 1835032
  15.7 1.5 %copy-done.2 = bf16[1,3584,256]{2,1,0:T(8,128)(2,1)S(1)} copy-done((bf16[1,3584,256]{2,1,0:T(8,128)(2,1)S(1)}, bf16[1,3584,256]{2,1,0:T(8,128)(2,1)}, u32[]{:S(2)}) %copy-start.2) | copy-done | bytes 1835032
  17.2 5.4 %block_pass.3 = (bf16[128,512]{1,0:T(8,128)(2,1)S(1)}, bf16[128,512]{1,0:T(8,128)(2,1)S(1)}, bf16[128,512]{1,0:T(8,128)(2,1)S(1)}, bf16[128,3584]{1,0:T(8,128)(2,1)S(1)}) custom-call(bf16[80,4096]{1,0:T(8,128)(2,1)S(1)} %get-tuple-element.116.refs_0_, bf16[48,4096]{1,0:T(8,128)(2,1)S(1)} %get-tuple-element.117.refs_1_, ...), custom_call_target="tpu_custom_call" | custom-call | flops 1879048192 | bytes 1835008 | tf_op jit(solution)/shard_map/block_pass/pallas_call | solution.py:162
  22.6 0.0 copy-start.1
  22.6 5.2 %collective-permute-done.4.refs_3_ = bf16[128,512]{1,0:T(8,128)(2,1)S(1)} collective-permute-done((bf16[128,512]{1,0:T(8,128)(2,1)S(1)}, bf16[128,512]{1,0:T(8,128)(2,1)S(1)}, u32[]{:S(2)}, u32[]{:S(2)}) %collective-permute-start.4) | collective-permute-done | bytes 131104 | tf_op jit(solution)/shard_map/ppermute | solution.py:30
  27.8 1.8 %collective-permute-start.9 = (bf16[80,3584]{1,0:T(8,128)(2,1)S(1)}, bf16[80,3584]{1,0:T(8,128)(2,1)S(1)}, u32[]{:S(2)}, u32[]{:S(2)}) collective-permute-start(bf16[80,3584]{1,0:T(8,128)(2,1)S(1)} %slice.63), channel_id=1, source_target_pairs={{0,16},{8,24},{16,0},{24,8},{1,17},{9,25},{17,1},{25,9},{2,18},{10... | collective-permute-start | bytes 1720328 | tf_op jit(solution)/shard_map/ppermute | solution.py:30
  29.6 1.5 %collective-permute-start.10 = (bf16[128,512]{1,0:T(8,128)(2,1)S(1)}, bf16[128,512]{1,0:T(8,128)(2,1)S(1)}, u32[]{:S(2)}, u32[]{:S(2)}) collective-permute-start(bf16[128,512]{1,0:T(8,128)(2,1)S(1)} %collective-permute-done.4.refs_3_), channel_id=1, source_target_pairs={{0,1},{1,2},{2,3},{3,4},{4,5},{5,6},{6,7},{7,0},{8,9},{9,10},{10,1... | collective-permute-start | bytes 393224 | tf_op jit(solution)/shard_map/ppermute | solution.py:24
  31.2 1.6 %collective-permute-start.8 = (bf16[48,3584]{1,0:T(8,128)(2,1)S(1)}, bf16[48,3584]{1,0:T(8,128)(2,1)S(1)}, u32[]{:S(2)}, u32[]{:S(2)}) collective-permute-start(bf16[48,3584]{1,0:T(8,128)(2,1)S(1)} %slice.64), channel_id=1, source_target_pairs={{0,1},{1,2},{2,3},{3,4},{4,5},{5,6},{6,7},{7,0},{8,9},{9,10},{10,1... | collective-permute-start | bytes 1032200 | tf_op jit(solution)/shard_map/ppermute | solution.py:24
  32.8 0.4 collective-permute-done.5.refs_2_.refs_4_
  33.2 6.7 %block_pass.4 = (bf16[256,512]{1,0:T(8,128)(2,1)S(1)}, bf16[256,512]{1,0:T(8,128)(2,1)S(1)}, bf16[256,512]{1,0:T(8,128)(2,1)S(1)}, bf16[3584,256]{1,0:T(8,128)(2...) custom-call(bf16[128,3584]{1,0:T(8,128)(2,1)S(1)} %collective-permut, ...), custom_call_target="tpu_custom_call" | custom-call | flops 3758096384 | bytes 3670016 | tf_op jit(solution)/shard_map/block_pass/pallas_call | solution.py:162
  39.9 2.8 %collective-permute-start.7 = (bf16[64,3584]{1,0:T(8,128)(2,1)S(1)}, bf16[64,3584]{1,0:T(8,128)(2,1)S(1)}, u32[]{:S(2)}, u32[]{:S(2)}) collective-permute-start(bf16[64,3584]{1,0:T(8,128)(2,1)S(1)} %get-tuple-element.126), channel_id=1, source_target_pairs={{0,7},{1,0},{2,1},{3,2},{4,3},{5,4},{6,5},{7,6},{8,15},{9,8},{10,9... | collective-permute-start | bytes 1376264 | tf_op jit(solution)/shard_map/ppermute | solution.py:24
  42.7 0.5 collective-permute-start.6
  43.2 1.1 %collective-permute-done.8.refs_1_.refs_6_ = bf16[48,3584]{1,0:T(8,128)(2,1)S(1)} collective-permute-done((bf16[48,3584]{1,0:T(8,128)(2,1)S(1)}, bf16[48,3584]{1,0:T(8,128)(2,1)S(1)}, u32[]{:S(2)}, u32[]{:S(2)}) %collective-permute-start.8) | collective-permute-done | bytes 344096 | tf_op jit(solution)/shard_map/ppermute | solution.py:24
  44.3 0.0 collective-permute-done.9.refs_0_.refs_5_
  44.3 3.9 %block_pass.5 = (bf16[256,512]{1,0:T(8,128)(2,1)}, bf16[128,512]{1,0:T(8,128)(2,1)S(1)}, bf16[128,512]{1,0:T(8,128)(2,1)S(1)}, bf16[64,3584]{1,0:T(8,128)(2,1)S(1)}, bf16[64,3584]{1,0:T(8,128)(2,1)S(1)}) custom-call(bf16[80,3584]{1,0:T(8,128)(2,1)S(1)} %collective-permute-done.9.refs_0_.refs_5_, bf16[48,3584]{1,0:T(8,128)(2,1)S(1)} %collective-permute-done.8.refs_1_.refs_6_, ...), custom_call_target="tpu_custom_call" | custom-call | flops 1879048192 | bytes 1835008 | tf_op jit(solution)/shard_map/block_pass/pallas_call | solution.py:162
  48.2 0.5 collective-permute-start.11
  48.7 5.3 %collective-permute-start.15 = (bf16[64,3584]{1,0:T(8,128)(2,1)S(1)}, bf16[64,3584]{1,0:T(8,128)(2,1)S(1)}, u32[]{:S(2)}, u32[]{:S(2)}) collective-permute-start(bf16[64,3584]{1,0:T(8,128)(2,1)S(1)} %get-tuple-element.148), channel_id=1, source_target_pairs={{0,7},{1,0},{2,1},{3,2},{4,3},{5,4},{6,5},{7,6},{8,15},{9,8},{10,9... | collective-permute-start | bytes 1376264 | tf_op jit(solution)/shard_map/ppermute | solution.py:24
  54.0 0.1 collective-permute-done.7.low_near_ref
  54.1 4.7 %weight_pass.2 = bf16[3584,512]{1,0:T(8,128)(2,1)} custom-call(bf16[80,4096]{1,0:T(8,128)(2,1)S(1)} %get-tuple-element.116.refs_0_, bf16[48,4096]{1,0:T(8,128)(2,1)S(1)} %get-tuple-element.117.refs_1_, bf16[128,3584]{1,0:T(8,128)(2,1)S(1)} %collective-permute-done.2.refs_0_.refs_2_, bf16[80,4096]{1,0:T(8,128)(2,1)S(1)} %collective-permute-done.3.refs_1_.refs_3_, ...), custom_call_target="tpu_custom_call" | custom-call | flops 1879048192 | bytes 11010048 | tf_op jit(solution)/shard_map/weight_pass/pallas_call | solution.py:233
  58.8 0.1 collective-permute-start.14
  58.9 2.8 %collective-permute-start.13 = (bf16[256,512]{1,0:T(8,128)(2,1)}, bf16[256,512]{1,0:T(8,128)(2,1)}, u32[]{:S(2)}, u32[]{:S(2)}) collective-permute-start(bf16[256,512]{1,0:T(8,128)(2,1)} %get-tuple-element.143), channel_id=1, source_target_pairs={{0,7},{1,0},{2,1},{3,2},{4,3},{5,4},{6,5},{7,6},{8,15},{9,8},{10,9... | collective-permute-start | bytes 786440 | tf_op jit(solution)/shard_map/ppermute | solution.py:24
  61.7 0.0 collective-permute-done.11.far_ref
  61.7 0.1 join.2
  61.8 2.1 %collective-permute-done.15.far_ref = bf16[64,3584]{1,0:T(8,128)(2,1)S(1)} collective-permute-done((bf16[64,3584]{1,0:T(8,128)(2,1)S(1)}, bf16[64,3584]{1,0:T(8,128)(2,1)S(1)}, u32[]{:S(2)}, u32[]{:S(2)}) %collective-permute-start.15) | collective-permute-done | bytes 458784 | tf_op jit(solution)/shard_map/ppermute | solution.py:24
  63.9 0.1 join.3
  64.1 0.6 collective-permute-start.17
  64.6 0.2 copy-done.11
  64.9 2.1 %collective-permute-start.12 = (bf16[64,3584]{1,0:T(8,128)(2,1)S(1)}, bf16[64,3584]{1,0:T(8,128)(2,1)S(1)}, u32[]{:S(2)}, u32[]{:S(2)}) collective-permute-start(bf16[64,3584]{1,0:T(8,128)(2,1)S(1)} %join.2), channel_id=1, source_target_pairs={{0,7},{1,0},{2,1},{3,2},{4,3},{5,4},{6,5},{7,6},{8,15},{9,8},{10,9... | collective-permute-start | bytes 1376264 | tf_op jit(solution)/shard_map/ppermute | solution.py:24
  67.0 0.0 collective-permute-done.14.refs_10_
  67.0 5.6 %weight_pass.3 = (bf16[3584,256]{1,0:T(8,128)(2,1)}, bf16[3584,256]{1,0:T(8,128)(2,1)}) custom-call(bf16[80,4096]{1,0:T(8,128)(2,1)S(1)} %get-tuple-element.116.refs_0_, bf16[48,4096]{1,0:T(8,128)(2,1)S(1)} %get-tuple-element.117.refs_1_, bf16[128,3584]{1,0:T(8,128)(2,1)S(1)} %collective-permute-done.2.refs_0_.refs_2_, ...), custom_call_target="tpu_custom_call" | custom-call | flops 1879048192 | bytes 11010048 | tf_op jit(solution)/shard_map/weight_pass/pallas_call | solution.py:233
  72.7 0.9 %add_convert_fusion = bf16[256,256]{1,0:T(8,128)(2,1)S(1)} fusion(bf16[128,256]{1,0:T(8,128)(2,1)S(1)} %slice.66, bf16[128,256]{1,0:T(8,128)(2,1)S(1)} %slice.65, bf16[256,512]{1,0:T(8,128)(2,1)} %collective-permute-done.13.back_ref), kind=kLoop, calls=%fused_computation | loop fusion | flops 458752 | bytes 393216 | tf_op jit(solution)/shard_map/convert_element_type | solution.py:48
  73.6 0.1 collective-permute-start.16
  73.7 1.3 %collective-permute-done.16.got_ref = bf16[256,256]{1,0:T(8,128)(2,1)S(1)} collective-permute-done((bf16[256,256]{1,0:T(8,128)(2,1)S(1)}, bf16[256,256]{1,0:T(8,128)(2,1)S(1)}, u32[]{:S(2)}, u32[]{:S(2)}) %collective-permute-start.16) | collective-permute-done | bytes 131104 | tf_op jit(solution)/shard_map/ppermute | solution.py:36
  75.0 1.7 %hidden_pass.1 = bf16[4,128,256]{2,1,0:T(8,128)(2,1)} custom-call(bf16[128,512]{1,0:T(8,128)(2,1)S(1)} %get-tuple-element.120.near_ref, bf16[256,512]{1,0:T(8,128)(2,1)S(1)} %copy-done.11, bf16[256,512]{1,0:T(8,128)(2,1)} %collective-permute-done.13.back_ref, bf16[256,256]{1,0:T(8,128)(2,1)S(1)} %collective-permute-done.16.got_ref), custom_call_target="tpu_custom_call" | custom-call | tf_op jit(solution)/shard_map/hidden_pass/pallas_call | solution.py:314
  76.7 2.6 %collective-permute-done.12.head_ref = bf16[64,3584]{1,0:T(8,128)(2,1)S(1)} collective-permute-done((bf16[64,3584]{1,0:T(8,128)(2,1)S(1)}, bf16[64,3584]{1,0:T(8,128)(2,1)S(1)}, u32[]{:S(2)}, u32[]{:S(2)}) %collective-permute-start.12) | collective-permute-done | bytes 458784 | tf_op jit(solution)/shard_map/ppermute | solution.py:24
  79.3 1.3 %final.1 = bf16[128,3584]{1,0:T(8,128)(2,1)} custom-call(bf16[128,3584]{1,0:T(8,128)(2,1)S(1)} %get-tuple-element.118.near_ref, bf16[48,3584]{1,0:T(8,128)(2,1)S(1)} %collective-permute-done.6.first_ref, bf16[64,3584]{1,0:T(8,128)(2,1)S(1)} %collective-permute-done.7.low_near_ref, bf16[64,3584]{1,0:T(8,128)(2,1)S(1)} %collective-permute-done.12.head_ref, ...), custom_call_target="tpu_custom_call" | custom-call | flops 999999995904 | bytes 1000000000 | tf_op jit(solution)/shard_map/final/pallas_call | solution.py:293
  (31 shorter events, 0.1 us)
Async XLA Ops:
  0.6 11.9 %collective-permute-start = (bf16[3584,256]{1,0:T(8,128)(2,1)}, bf16[3584,256]{1,0:T(8,128)(2,1)}, u32[]{:S(2)}, u32[]{:S(2)}) collective-permute-start(bf16[3584,256]{1,0:T(8,128)(2,1)} %bitcast.20), channel_id=1, source_target_pairs={{0,8},{8,0},{16,24},{24,16},{1,9},{9,1},{17,25},{25,17},{2,10},{10... | collective-permute-start | bytes 5505032 | tf_op jit(solution)/shard_map/ppermute | solution.py:36
  1.1 13.0 %collective-permute-start.1 = (bf16[3584,256]{1,0:T(8,128)(2,1)}, bf16[3584,256]{1,0:T(8,128)(2,1)}, u32[]{:S(2)}, u32[]{:S(2)}) collective-permute-start(bf16[3584,256]{1,0:T(8,128)(2,1)} %bitcast.24), channel_id=1, source_target_pairs={{0,8},{8,0},{16,24},{24,16},{1,9},{9,1},{17,25},{25,17},{2,10},{10... | collective-permute-start | bytes 5505032 | tf_op jit(solution)/shard_map/ppermute | solution.py:36
  1.2 29.9 %collective-permute-start.2 = (bf16[128,3584]{1,0:T(8,128)(2,1)}, bf16[128,3584]{1,0:T(8,128)(2,1)S(1)}, u32[]{:S(2)}, u32[]{:S(2)}) collective-permute-start(bf16[128,3584]{1,0:T(8,128)(2,1)} %bitcast.28), channel_id=1, source_target_pairs={{0,16},{8,24},{16,0},{24,8},{1,17},{9,25},{17,1},{25,9},{2,18},{10... | collective-permute-start | bytes 2752520 | tf_op jit(solution)/shard_map/ppermute | solution.py:30
  5.5 22.3 %collective-permute-start.3 = (bf16[80,4096]{1,0:T(8,128)(2,1)S(1)}, bf16[80,4096]{1,0:T(8,128)(2,1)S(1)}, u32[]{:S(2)}, u32[]{:S(2)}) collective-permute-start(bf16[80,4096]{1,0:T(8,128)(2,1)S(1)} %get-tuple-element.116.refs_0_), channel_id=1, source_target_pairs={{0,1},{1,2},{2,3},{3,4},{4,5},{5,6},{6,7},{7,0},{8,9},{9,10},{10,1... | collective-permute-start | bytes 1966088 | tf_op jit(solution)/shard_map/ppermute | solution.py:24
  7.0 20.8 %collective-permute-start.4 = (bf16[128,512]{1,0:T(8,128)(2,1)S(1)}, bf16[128,512]{1,0:T(8,128)(2,1)S(1)}, u32[]{:S(2)}, u32[]{:S(2)}) collective-permute-start(bf16[128,512]{1,0:T(8,128)(2,1)S(1)} %get-tuple-element.119), channel_id=1, source_target_pairs={{0,16},{8,24},{16,0},{24,8},{1,17},{9,25},{17,1},{25,9},{2,18},{10... | collective-permute-start | bytes 393224 | tf_op jit(solution)/shard_map/ppermute | solution.py:30
  12.6 20.6 %collective-permute-start.5 = (bf16[48,4096]{1,0:T(8,128)(2,1)S(1)}, bf16[48,4096]{1,0:T(8,128)(2,1)S(1)}, u32[]{:S(2)}, u32[]{:S(2)}) collective-permute-start(bf16[48,4096]{1,0:T(8,128)(2,1)S(1)} %get-tuple-element.117.refs_1_), channel_id=1, source_target_pairs={{0,1},{1,2},{2,3},{3,4},{4,5},{5,6},{6,7},{7,0},{8,9},{9,10},{10,1... | collective-permute-start | bytes 1179656 | tf_op jit(solution)/shard_map/ppermute | solution.py:24
  14.2 1.5 %copy-start = (bf16[1,3584,256]{2,1,0:T(8,128)(2,1)S(1)}, bf16[1,3584,256]{2,1,0:T(8,128)(2,1)}, u32[]{:S(2)}) copy-start(bf16[1,3584,256]{2,1,0:T(8,128)(2,1)} %param.28) | copy-start | bytes 5505028
  15.7 1.5 %copy-start.2 = (bf16[1,3584,256]{2,1,0:T(8,128)(2,1)S(1)}, bf16[1,3584,256]{2,1,0:T(8,128)(2,1)}, u32[]{:S(2)}) copy-start(bf16[1,3584,256]{2,1,0:T(8,128)(2,1)} %param.29) | copy-start | bytes 5505028
  17.2 16.0 %copy-start.3 = (bf16[1,3584,256]{2,1,0:T(8,128)(2,1)S(1)}, bf16[1,3584,256]{2,1,0:T(8,128)(2,1)}, u32[]{:S(2)}) copy-start(bf16[1,3584,256]{2,1,0:T(8,128)(2,1)} %param.29) | copy-start | bytes 5505028
  22.6 10.6 %copy-start.1 = (bf16[1,3584,256]{2,1,0:T(8,128)(2,1)S(1)}, bf16[1,3584,256]{2,1,0:T(8,128)(2,1)}, u32[]{:S(2)}) copy-start(bf16[1,3584,256]{2,1,0:T(8,128)(2,1)} %param.28) | copy-start | bytes 5505028
  27.8 16.4 %collective-permute-start.9 = (bf16[80,3584]{1,0:T(8,128)(2,1)S(1)}, bf16[80,3584]{1,0:T(8,128)(2,1)S(1)}, u32[]{:S(2)}, u32[]{:S(2)}) collective-permute-start(bf16[80,3584]{1,0:T(8,128)(2,1)S(1)} %slice.63), channel_id=1, source_target_pairs={{0,16},{8,24},{16,0},{24,8},{1,17},{9,25},{17,1},{25,9},{2,18},{10... | collective-permute-start | bytes 1720328 | tf_op jit(solution)/shard_map/ppermute | solution.py:30
  29.6 13.6 %collective-permute-start.10 = (bf16[128,512]{1,0:T(8,128)(2,1)S(1)}, bf16[128,512]{1,0:T(8,128)(2,1)S(1)}, u32[]{:S(2)}, u32[]{:S(2)}) collective-permute-start(bf16[128,512]{1,0:T(8,128)(2,1)S(1)} %collective-permute-done.4.refs_3_), channel_id=1, source_target_pairs={{0,1},{1,2},{2,3},{3,4},{4,5},{5,6},{6,7},{7,0},{8,9},{9,10},{10,1... | collective-permute-start | bytes 393224 | tf_op jit(solution)/shard_map/ppermute | solution.py:24
  31.2 13.1 %collective-permute-start.8 = (bf16[48,3584]{1,0:T(8,128)(2,1)S(1)}, bf16[48,3584]{1,0:T(8,128)(2,1)S(1)}, u32[]{:S(2)}, u32[]{:S(2)}) collective-permute-start(bf16[48,3584]{1,0:T(8,128)(2,1)S(1)} %slice.64), channel_id=1, source_target_pairs={{0,1},{1,2},{2,3},{3,4},{4,5},{5,6},{6,7},{7,0},{8,9},{9,10},{10,1... | collective-permute-start | bytes 1032200 | tf_op jit(solution)/shard_map/ppermute | solution.py:24
  33.2 20.9 %copy-start.8 = (bf16[48,4096]{1,0:T(8,128)(2,1)}, bf16[48,4096]{1,0:T(8,128)(2,1)S(1)}, u32[]{:S(2)}) copy-start(bf16[48,4096]{1,0:T(8,128)(2,1)S(1)} %collective-permute-done.5.refs_2_.refs_4_) | copy-start | bytes 1179652
  39.9 8.3 %copy-start.10 = (bf16[256,512]{1,0:T(8,128)(2,1)}, bf16[256,512]{1,0:T(8,128)(2,1)S(1)}, u32[]{:S(2)}) copy-start(bf16[256,512]{1,0:T(8,128)(2,1)S(1)} %get-tuple-element.128.refs_8_.far_ref) | copy-start | bytes 786436
  39.9 14.2 %collective-permute-start.7 = (bf16[64,3584]{1,0:T(8,128)(2,1)S(1)}, bf16[64,3584]{1,0:T(8,128)(2,1)S(1)}, u32[]{:S(2)}, u32[]{:S(2)}) collective-permute-start(bf16[64,3584]{1,0:T(8,128)(2,1)S(1)} %get-tuple-element.126), channel_id=1, source_target_pairs={{0,7},{1,0},{2,1},{3,2},{4,3},{5,4},{6,5},{7,6},{8,15},{9,8},{10,9... | collective-permute-start | bytes 1376264 | tf_op jit(solution)/shard_map/ppermute | solution.py:24
  42.7 11.3 %collective-permute-start.6 = (bf16[48,3584]{1,0:T(8,128)(2,1)S(1)}, bf16[48,3584]{1,0:T(8,128)(2,1)S(1)}, u32[]{:S(2)}, u32[]{:S(2)}) collective-permute-start(bf16[48,3584]{1,0:T(8,128)(2,1)S(1)} %get-tuple-element.125), channel_id=1, source_target_pairs={{0,16},{8,24},{16,0},{24,8},{1,17},{9,25},{17,1},{25,9},{2,18},{10... | collective-permute-start | bytes 1032200 | tf_op jit(solution)/shard_map/ppermute | solution.py:30
  44.3 9.8 %copy-start.6 = (bf16[48,3584]{1,0:T(8,128)(2,1)}, bf16[48,3584]{1,0:T(8,128)(2,1)S(1)}, u32[]{:S(2)}) copy-start(bf16[48,3584]{1,0:T(8,128)(2,1)S(1)} %collective-permute-done.8.refs_1_.refs_6_) | copy-start | bytes 1032196
  44.3 9.8 %copy-start.4 = (bf16[80,3584]{1,0:T(8,128)(2,1)}, bf16[80,3584]{1,0:T(8,128)(2,1)S(1)}, u32[]{:S(2)}) copy-start(bf16[80,3584]{1,0:T(8,128)(2,1)S(1)} %collective-permute-done.9.refs_0_.refs_5_) | copy-start | bytes 1720324
  48.2 13.5 %collective-permute-start.11 = (bf16[64,3584]{1,0:T(8,128)(2,1)S(1)}, bf16[64,3584]{1,0:T(8,128)(2,1)S(1)}, u32[]{:S(2)}, u32[]{:S(2)}) collective-permute-start(bf16[64,3584]{1,0:T(8,128)(2,1)S(1)} %get-tuple-element.134), channel_id=1, source_target_pairs={{0,16},{8,24},{16,0},{24,8},{1,17},{9,25},{17,1},{25,9},{2,18},{10... | collective-permute-start | bytes 1376264 | tf_op jit(solution)/shard_map/ppermute | solution.py:30
  48.7 15.3 %collective-permute-start.15 = (bf16[64,3584]{1,0:T(8,128)(2,1)S(1)}, bf16[64,3584]{1,0:T(8,128)(2,1)S(1)}, u32[]{:S(2)}, u32[]{:S(2)}) collective-permute-start(bf16[64,3584]{1,0:T(8,128)(2,1)S(1)} %get-tuple-element.148), channel_id=1, source_target_pairs={{0,7},{1,0},{2,1},{3,2},{4,3},{5,4},{6,5},{7,6},{8,15},{9,8},{10,9... | collective-permute-start | bytes 1376264 | tf_op jit(solution)/shard_map/ppermute | solution.py:24
  58.8 8.2 %collective-permute-start.14 = (bf16[3584,512]{1,0:T(8,128)(2,1)}, bf16[3584,512]{1,0:T(8,128)(2,1)}, u32[]{:S(2)}, u32[]{:S(2)}) collective-permute-start(bf16[3584,512]{1,0:T(8,128)(2,1)} %weight_pass.2), channel_id=1, source_target_pairs={{0,8},{8,0},{16,24},{24,16},{1,9},{9,1},{17,25},{25,17},{2,10},{10... | collective-permute-start | bytes 11010056 | tf_op jit(solution)/shard_map/ppermute | solution.py:36
  58.9 13.8 %collective-permute-start.13 = (bf16[256,512]{1,0:T(8,128)(2,1)}, bf16[256,512]{1,0:T(8,128)(2,1)}, u32[]{:S(2)}, u32[]{:S(2)}) collective-permute-start(bf16[256,512]{1,0:T(8,128)(2,1)} %get-tuple-element.143), channel_id=1, source_target_pairs={{0,7},{1,0},{2,1},{3,2},{4,3},{5,4},{6,5},{7,6},{8,15},{9,8},{10,9... | collective-permute-start | bytes 786440 | tf_op jit(solution)/shard_map/ppermute | solution.py:24
  63.9 1.0 %copy-start.11 = (bf16[256,512]{1,0:T(8,128)(2,1)S(1)}, bf16[256,512]{1,0:T(8,128)(2,1)}, u32[]{:S(2)}) copy-start(bf16[256,512]{1,0:T(8,128)(2,1)} %copy-done.10) | copy-start | bytes 786436
  63.9 3.1 %copy-start.5 = (bf16[80,3584]{1,0:T(8,128)(2,1)S(1)}, bf16[80,3584]{1,0:T(8,128)(2,1)}, u32[]{:S(2)}) copy-start(bf16[80,3584]{1,0:T(8,128)(2,1)} %copy-done.4) | copy-start | bytes 1720324
  63.9 3.1 %copy-start.7 = (bf16[48,3584]{1,0:T(8,128)(2,1)S(1)}, bf16[48,3584]{1,0:T(8,128)(2,1)}, u32[]{:S(2)}) copy-start(bf16[48,3584]{1,0:T(8,128)(2,1)} %copy-done.6) | copy-start | bytes 1032196
  63.9 3.1 %copy-start.9 = (bf16[48,4096]{1,0:T(8,128)(2,1)S(1)}, bf16[48,4096]{1,0:T(8,128)(2,1)}, u32[]{:S(2)}) copy-start(bf16[48,4096]{1,0:T(8,128)(2,1)} %copy-done.8) | copy-start | bytes 1179652
  64.1 15.2 %collective-permute-start.17 = (bf16[80,3584]{1,0:T(8,128)(2,1)S(1)}, bf16[80,3584]{1,0:T(8,128)(2,1)S(1)}, u32[]{:S(2)}, u32[]{:S(2)}) collective-permute-start(bf16[80,3584]{1,0:T(8,128)(2,1)S(1)} %join.3), channel_id=1, source_target_pairs={{0,16},{8,24},{16,0},{24,8},{1,17},{9,25},{17,1},{25,9},{2,18},{10... | collective-permute-start | bytes 1720328 | tf_op jit(solution)/shard_map/ppermute | solution.py:30
  64.9 14.4 %collective-permute-start.12 = (bf16[64,3584]{1,0:T(8,128)(2,1)S(1)}, bf16[64,3584]{1,0:T(8,128)(2,1)S(1)}, u32[]{:S(2)}, u32[]{:S(2)}) collective-permute-start(bf16[64,3584]{1,0:T(8,128)(2,1)S(1)} %join.2), channel_id=1, source_target_pairs={{0,7},{1,0},{2,1},{3,2},{4,3},{5,4},{6,5},{7,6},{8,15},{9,8},{10,9... | collective-permute-start | bytes 1376264 | tf_op jit(solution)/shard_map/ppermute | solution.py:24
  73.6 1.4 %collective-permute-start.16 = (bf16[256,256]{1,0:T(8,128)(2,1)S(1)}, bf16[256,256]{1,0:T(8,128)(2,1)S(1)}, u32[]{:S(2)}, u32[]{:S(2)}) collective-permute-start(bf16[256,256]{1,0:T(8,128)(2,1)S(1)} %add_convert_fusion), channel_id=1, source_target_pairs={{0,8},{8,0},{16,24},{24,16},{1,9},{9,1},{17,25},{25,17},{2,10},{10... | collective-permute-start | bytes 393224 | tf_op jit(solution)/shard_map/ppermute | solution.py:36

commit v7 on v6

--- a/solution.py
+++ b/solution.py
@@ -9,9 +9,9 @@
 
 TILE = 128
 OUT_SHARE = 80
-BACK_SHARE = (48, 64)
+BACK_SHARE = (48, 80)
 LIMIT = 20 * 2**20
-LONG = pl.CostEstimate(flops=10**12, bytes_accessed=10**9, transcendentals=0)
+LONG = pl.CostEstimate(flops=4 * 10**10, bytes_accessed=10**8, transcendentals=0)
 
 
 def work(flops, moved):
@@ -267,24 +267,33 @@
     )(home, far)
 
 
-def final_body(
-    near_ref,
-    first_ref,
-    low_near_ref,
-    head_ref,
-    low_ref,
-    tokens_ref,
-):
-    rows = tokens_ref.shape[0]
-    first, head = first_ref.shape[0], head_ref.shape[0]
-    rest = head - first
-    tokens_ref[:first, :] = b16(
-        f32(near_ref[:first, :]) + f32(first_ref[...]) + f32(head_ref[:first, :])
-    )
-    tokens_ref[first:head, :] = b16(
-        f32(near_ref[first:head, :]) + f32(low_ref[:rest, :]) + f32(head_ref[first:, :])
-    )
-    tokens_ref[head:, :] = b16(
+def hidden_sum_body(near_ref, far_ref, back_ref, out_ref):
+    rows, quarter = near_ref.shape[0], out_ref.shape[1]
+    for block, home_ref in enumerate((near_ref, far_ref)):
+        part = pl.ds(block * rows, rows)
+        out_ref[part, :] = b16(f32(home_ref[:rows, quarter:]) + f32(back_ref[part, quarter:]))
+
+
+def hidden_sum(near, far, back):
+    rows, both = back.shape
+    return pl.pallas_call(
+        hidden_sum_body,
+        out_shape=jax.ShapeDtypeStruct((rows, both // 2), back.dtype),
+        compiler_params=pltpu.CompilerParams(vmem_limit_bytes=LIMIT),
+        cost_estimate=LONG,
+        name="hidden_sum",
+    )(near, far, back)
+
+
+def final_body(near_ref, home_ref, low_near_ref, first_ref, middle_ref, low_ref, out_ref):
+    first = first_ref.shape[0]
+    rest = middle_ref.shape[0]
+    head = first + rest
+    out_ref[:first, :] = b16(f32(near_ref[:first, :]) + f32(home_ref[...]) + f32(first_ref[...]))
+    out_ref[first:head, :] = b16(
+        f32(near_ref[first:head, :]) + f32(low_ref[:rest, :]) + f32(middle_ref[...])
+    )
+    out_ref[head:, :] = b16(
         f32(near_ref[head:, :]) + f32(low_near_ref[...]) + f32(low_ref[rest:, :])
     )
 
@@ -371,43 +380,45 @@
         scales,
         row_count,
         panels,
-        (first, row_count - first, head, lower),
+        (first, row_count - first, first, head - first, lower),
         extra=(y_grads,),
         handed=(2, 3),
     )
-    *handed, first_hf, rest_hf, head_pn, lower_pn = mid_parts
+    *handed, first_hf, rest_hf, first_pn, middle_pn, lower_pn = mid_parts
     first_home = across(first_hf)
     low_near = shifted(lower_pn, -1)
     xy_low, xy_top, xy_grads = after((xy_low, xy_top, xy_grads), hid_mid)
-    hid_past, own_pf, other_pf, (head_pf, lower_pf) = block_pass(
+    hid_past, own_pf, other_pf, (first_pf, middle_pf, lower_pf) = block_pass(
         (xy_top, xy_low),
         ((2, 0),),
         scales,
         3 * row_count,
         (*panels[:2], *handed),
-        (head, lower),
+        (first, head - first, lower),
         extra=(xy_grads,),
         carry=(hid_mid,),
     )
-    head_past = across(head_pf)
+    first_past, middle_past = across(first_pf), across(middle_pf)
     low_far = shifted(lower_pf, -1)
 
     pieces = (near_top, near_low, y_tile, x_top, x_low, xy_top, xy_low)
     (sent,) = weight_pass(width, pieces, after((other_hn, other_mid, other_pf), first_home, low_near))
     got = within(sent)
-    hid_back = shifted(after(hid_past, sent), -1)
-    head_sum = join(head_pn, after(head_past, sent), work(0, 0))
-    head_back = shifted(head_sum, -1)
-    low_sum = join(rest_hf, after(low_far, head_sum), LONG)
+    hid_back = shifted(hid_past, -1)
+    low_sum = join(rest_hf, after(low_far, sent), work(0, 0))
     low_home = across(low_sum)
-    got = after(got, low_sum)
-    grad_gate, grad_up = weight_pass(width, pieces, (own_hn, own_mid, own_pf), got)
-    hid_back = after(hid_back, grad_gate)
-    hid_other = jnp.concatenate([hid_hn[:, quarter:], hid_mid[:row_count, quarter:]])
-    hid_other = b16(f32(hid_other) + f32(hid_back[:, quarter:]))
+    first_sum = join(first_pn, after(first_past, low_sum), work(0, 0))
+    first_back = shifted(first_sum, -1)
+    middle_sum = join(middle_pn, after(middle_past, first_sum), work(0, 0))
+    middle_back = shifted(middle_sum, -1)
+    hid_other = hidden_sum(hid_hn, hid_mid, after(hid_back, middle_sum))
     hid_got = within(hid_other)
+    grad_gate, grad_up = weight_pass(
+        width, pieces, (own_hn, own_mid, own_pf), after(got, hid_other)
+    )
+    hid_got = after(hid_got, grad_gate)
     hidden = hidden_pass(hid_hn, hid_mid, hid_back, hid_got)
-    d_tokens = final(part_hn, first_home, low_near, after(head_back, hidden), low_home)
+    d_tokens = final(part_hn, first_home, low_near, after(first_back, hidden), middle_back, low_home)
     return (d_tokens[None], hidden, grad_gate[None], grad_up[None])
 
 

time: 80.9 us -> 78.6 us (0.972)
  Pallas kernels: 30.7 us -> 27.6 us
  starting transfers between devices: 26.9 us -> 28.8 us
  other arithmetic: 1.79 us -> 0.85 us
    ppermute x6 -> x7, starting transfers between devices: 6.85 us -> 10.1 us  [across(): return lax.ppermute(value, 'dp', pairs)]
    pallas_call x2, Pallas kernels: 10.3 us -> 8.81 us  [weight_pass(): pl.pallas_call(functools.partial(weight_body, len(pieces), len(grads), st...]
    ppermute x8 -> x9, waiting for transfers between devices: 6.32 us -> 7.82 us  [shifted(): return lax.ppermute(value, 'expert', pairs)]
    ppermute x4, waiting for transfers between devices: 1.34 us -> 0.01 us  [within(): return lax.ppermute(value, 'dp', pairs)]
    ppermute x8 -> x9, starting transfers between devices: 19.3 us -> 18 us  [shifted(): return lax.ppermute(value, 'expert', pairs)]
    pallas_call x1, Pallas kernels: 1.69 us -> 0.74 us  [hidden_pass(): pl.pallas_call(hidden_body, out_shape=jax.ShapeDtypeStruct((4, rows, both...]
    convert_element_type x1 -> x0, other arithmetic: 0.94 us -> none  [b16(): return value.astype(jnp.bfloat16)]
    unnamed x24 -> x8, local copies, waits for them, and re-layouts: 3.27 us -> 3.01 us
  transfers between devices with their start and end apart: 18 -> 20, of which waited for: 7 -> 5; matrix products, arithmetic and copies ran while one was open for 4% -> 3% of each run, Pallas kernels for 37% -> 34%
where the time goes in v7:
time: 78.6 us; the launch traced here: 78.3 us
  starting transfers between devices  28.8 us (37%)
  Pallas kernels  27.6 us (35%)
  waiting for transfers between devices  13 us (17%)
  local copies, waits for them, and re-layouts  4.64 us (6%)
  between operations  3.3 us (4%)
  other arithmetic  0.85 us (1%)
    ppermute x9, starting transfers between devices, shifted(): return lax.ppermute(value, 'expert', pairs)  18 us
    pallas_call x3, Pallas kernels, block_pass(): pl.pallas_call(functools.partial(block_body, len(pieces), sources, len(ex...  15.2 us
    ppermute x7, starting transfers between devices, across(): return lax.ppermute(value, 'dp', pairs)  10.1 us
    pallas_call x2, Pallas kernels, weight_pass(): pl.pallas_call(functools.partial(weight_body, len(pieces), len(grads), st...  8.81 us
    ppermute x9, waiting for transfers between devices, shifted(): return lax.ppermute(value, 'expert', pairs)  7.82 us
    ppermute x7, waiting for transfers between devices, across(): return lax.ppermute(value, 'dp', pairs)  5.2 us
    unnamed x8, local copies, waits for them, and re-layouts  3.01 us
  transfers between devices with their start and end apart: 20, of which 5 were waited for; matrix products, arithmetic and copies ran while one was open for 3% of the time, Pallas kernels for 34%

profile of v7, /device:TPU:0, one launch (start us, length us, event | category | flops | bytes accessed | tf_op | source)
XLA Modules:
  0.0 78.3 jit_solution(16656248700652550545)
XLA Ops:
  0.6 0.5 collective-permute-start
  1.1 0.1 collective-permute-start.1
  1.2 2.9 %collective-permute-start.2 = (bf16[128,3584]{1,0:T(8,128)(2,1)}, bf16[128,3584]{1,0:T(8,128)(2,1)S(1)}, u32[]{:S(2)}, u32[]{:S(2)}) collective-permute-start(bf16[128,3584]{1,0:T(8,128)(2,1)} %bitcast.28), channel_id=1, source_target_pairs={{0,16},{8,24},{16,0},{24,8},{1,17},{9,25},{17,1},{25,9},{2,18},{10... | collective-permute-start | bytes 2752520 | tf_op jit(solution)/shard_map/ppermute | solution.py:30
  4.2 1.3 %pack.1 = (bf16[80,4096]{1,0:T(8,128)(2,1)S(1)}, bf16[48,4096]{1,0:T(8,128)(2,1)S(1)}, bf16[128,512]{1,0:T(8,128)(2,1)S(1)}) custom-call(bf16[128,3584]{1,0:T(8,128)(2,1)} %bitcast.29, bf16[128,1024]{1,0:T(8,128)(2,1)} %bitcast.30), custom_call_target="tpu_custom_call" | custom-call | bytes 2359296 | tf_op jit(solution)/shard_map/pack/pallas_call | solution.py:90
  5.5 1.5 %collective-permute-start.3 = (bf16[80,4096]{1,0:T(8,128)(2,1)S(1)}, bf16[80,4096]{1,0:T(8,128)(2,1)S(1)}, u32[]{:S(2)}, u32[]{:S(2)}) collective-permute-start(bf16[80,4096]{1,0:T(8,128)(2,1)S(1)} %get-tuple-element.119.refs_0_), channel_id=1, source_target_pairs={{0,1},{1,2},{2,3},{3,4},{4,5},{5,6},{6,7},{7,0},{8,9},{9,10},{10,1... | collective-permute-start | bytes 1966088 | tf_op jit(solution)/shard_map/ppermute | solution.py:24
  7.1 1.5 %collective-permute-start.5 = (bf16[48,4096]{1,0:T(8,128)(2,1)S(1)}, bf16[48,4096]{1,0:T(8,128)(2,1)S(1)}, u32[]{:S(2)}, u32[]{:S(2)}) collective-permute-start(bf16[48,4096]{1,0:T(8,128)(2,1)S(1)} %get-tuple-element.120.refs_1_), channel_id=1, source_target_pairs={{0,1},{1,2},{2,3},{3,4},{4,5},{5,6},{6,7},{7,0},{8,9},{9,10},{10,1... | collective-permute-start | bytes 1179656 | tf_op jit(solution)/shard_map/ppermute | solution.py:24
  8.6 1.4 %fusion.4 = (s32[1,1]{1,0:T(1,128)}, s32[1,1]{1,0:T(1,128)}, s32[1,1]{1,0:T(1,128)}, s32[1,1]{1,0:T(1,128)}) fusion(s32[4,8]{1,0:T(4,128)} %param.27, s32[]{:T(128)S(6)} %select_n.62, s32[]{:T(128)S(6)} %select_n.63, s32[]{:T(128)S(6)} %select_n.67, s32[]{:T(128)S(6)} %select_n.70), kind=kLoop, calls=%fused_computation.9 | loop fusion | bytes 48 | tf_op jit(solution)/shard_map/dynamic_slice | solution.py:346
  12.6 0.8 %fusion = (f32[128,1]{0,1:T(1,128)S(1)}, f32[128,1]{0,1:T(1,128)S(1)}, f32[128,1]{0,1:T(1,128)S(1)}, f32[128,1]{0,1:T(1,128)S(1)}) fusion(pred[]{:T(512)} %bitcast.3, f32[4,1024]{1,0:T(4,128)} %param.26, s32[]{:T(128)S(6)} %select_n.62, s32[]{:T(128)S(6)} %select_n.64, s32[]{:T(128)S(6)} %select_n.67, pred[]{:T(512)} %bitcast.5, s32[]{:T(128)S(6)} %select_n.71, ...), kind=kLoop, calls=%fused_computation.5 | loop fusion | flops 512 | bytes 4116 | tf_op jit(solution)/shard_map/reshape | solution.py:349
  13.4 0.1 copy.14.refs_2_.refs_4_.refs_3_
  13.6 0.6 collective-permute-start.4
  14.2 1.5 %copy-done = bf16[1,3584,256]{2,1,0:T(8,128)(2,1)S(1)} copy-done((bf16[1,3584,256]{2,1,0:T(8,128)(2,1)S(1)}, bf16[1,3584,256]{2,1,0:T(8,128)(2,1)}, u32[]{:S(2)}) %copy-start) | copy-done | bytes 1835032
  15.7 1.5 %copy-done.2 = bf16[1,3584,256]{2,1,0:T(8,128)(2,1)S(1)} copy-done((bf16[1,3584,256]{2,1,0:T(8,128)(2,1)S(1)}, bf16[1,3584,256]{2,1,0:T(8,128)(2,1)}, u32[]{:S(2)}) %copy-start.2) | copy-done | bytes 1835032
  17.2 5.4 %block_pass.3 = (bf16[128,512]{1,0:T(8,128)(2,1)S(1)}, bf16[128,512]{1,0:T(8,128)(2,1)S(1)}, bf16[128,512]{1,0:T(8,128)(2,1)S(1)}, bf16[128,3584]{1,0:T(8,128)(2,1)S(1)}) custom-call(bf16[80,4096]{1,0:T(8,128)(2,1)S(1)} %get-tuple-element.119.refs_0_, bf16[48,4096]{1,0:T(8,128)(2,1)S(1)} %get-tuple-element.120.refs_1_, ...), custom_call_target="tpu_custom_call" | custom-call | flops 1879048192 | bytes 1835008 | tf_op jit(solution)/shard_map/block_pass/pallas_call | solution.py:162
  22.6 0.0 copy-start.1
  22.6 5.2 %collective-permute-done.4.refs_3_ = bf16[128,512]{1,0:T(8,128)(2,1)S(1)} collective-permute-done((bf16[128,512]{1,0:T(8,128)(2,1)S(1)}, bf16[128,512]{1,0:T(8,128)(2,1)S(1)}, u32[]{:S(2)}, u32[]{:S(2)}) %collective-permute-start.4) | collective-permute-done | bytes 131104 | tf_op jit(solution)/shard_map/ppermute | solution.py:30
  27.8 0.0 collective-permute-done.3.refs_1_.refs_3_
  27.8 1.8 %collective-permute-start.9 = (bf16[80,3584]{1,0:T(8,128)(2,1)S(1)}, bf16[80,3584]{1,0:T(8,128)(2,1)S(1)}, u32[]{:S(2)}, u32[]{:S(2)}) collective-permute-start(bf16[80,3584]{1,0:T(8,128)(2,1)S(1)} %slice.54), channel_id=1, source_target_pairs={{0,16},{8,24},{16,0},{24,8},{1,17},{9,25},{17,1},{25,9},{2,18},{10... | collective-permute-start | bytes 1720328 | tf_op jit(solution)/shard_map/ppermute | solution.py:30
  29.6 0.0 collective-permute-done.2.refs_0_.refs_2_
  29.7 1.5 %collective-permute-start.8 = (bf16[48,3584]{1,0:T(8,128)(2,1)S(1)}, bf16[48,3584]{1,0:T(8,128)(2,1)S(1)}, u32[]{:S(2)}, u32[]{:S(2)}) collective-permute-start(bf16[48,3584]{1,0:T(8,128)(2,1)S(1)} %slice.55), channel_id=1, source_target_pairs={{0,1},{1,2},{2,3},{3,4},{4,5},{5,6},{6,7},{7,0},{8,9},{9,10},{10,1... | collective-permute-start | bytes 1032200 | tf_op jit(solution)/shard_map/ppermute | solution.py:24
  31.2 2.0 %collective-permute-done.5.refs_2_.refs_4_ = bf16[48,4096]{1,0:T(8,128)(2,1)S(1)} collective-permute-done((bf16[48,4096]{1,0:T(8,128)(2,1)S(1)}, bf16[48,4096]{1,0:T(8,128)(2,1)S(1)}, u32[]{:S(2)}, u32[]{:S(2)}) %collective-permute-start.5) | collective-permute-done | bytes 393248 | tf_op jit(solution)/shard_map/ppermute | solution.py:24
  33.2 0.0 collective-permute-start.10
  33.2 6.5 %block_pass.4 = (bf16[256,512]{1,0:T(8,128)(2,1)S(1)}, bf16[256,512]{1,0:T(8,128)(2,1)S(1)}, bf16[256,512]{1,0:T(8,128)(2,1)S(1)}, bf16[3584,256]{1,0:T(8,128)(2...) custom-call(bf16[128,3584]{1,0:T(8,128)(2,1)S(1)} %collective-permut, ...), custom_call_target="tpu_custom_call" | custom-call | flops 3758096384 | bytes 3670016 | tf_op jit(solution)/shard_map/block_pass/pallas_call | solution.py:162
  39.8 0.6 collective-permute-start.6
  40.3 4.7 %collective-permute-start.7 = (bf16[48,3584]{1,0:T(8,128)(2,1)S(1)}, bf16[48,3584]{1,0:T(8,128)(2,1)S(1)}, u32[]{:S(2)}, u32[]{:S(2)}) collective-permute-start(bf16[48,3584]{1,0:T(8,128)(2,1)S(1)} %get-tuple-element.129), channel_id=1, source_target_pairs={{0,7},{1,0},{2,1},{3,2},{4,3},{5,4},{6,5},{7,6},{8,15},{9,8},{10,9... | collective-permute-start | bytes 1032200 | tf_op jit(solution)/shard_map/ppermute | solution.py:24
  45.1 3.2 %block_pass.5 = (bf16[256,512]{1,0:T(8,128)(2,1)S(1)}, bf16[128,512]{1,0:T(8,128)(2,1)S(1)}, bf16[128,512]{1,0:T(8,128)(2,1)S(1)}, bf16[48,3584]{1,0:T(8,128)(2,...) custom-call(bf16[80,3584]{1,0:T(8,128)(2,1)S(1)} %collective-permute-done.9.refs_0_.refs_5_, ...), custom_call_target="tpu_custom_call" | custom-call | flops 1879048192 | bytes 1835008 | tf_op jit(solution)/shard_map/block_pass/pallas_call | solution.py:162
  48.3 2.6 %collective-permute-start.12 = (bf16[48,3584]{1,0:T(8,128)(2,1)S(1)}, bf16[48,3584]{1,0:T(8,128)(2,1)S(1)}, u32[]{:S(2)}, u32[]{:S(2)}) collective-permute-start(bf16[48,3584]{1,0:T(8,128)(2,1)S(1)} %get-tuple-element.139), channel_id=1, source_target_pairs={{0,7},{1,0},{2,1},{3,2},{4,3},{5,4},{6,5},{7,6},{8,15},{9,8},{10,9... | collective-permute-start | bytes 1032200 | tf_op jit(solution)/shard_map/ppermute | solution.py:24
  50.9 2.3 %collective-permute-start.11 = (bf16[48,3584]{1,0:T(8,128)(2,1)S(1)}, bf16[48,3584]{1,0:T(8,128)(2,1)S(1)}, u32[]{:S(2)}, u32[]{:S(2)}) collective-permute-start(bf16[48,3584]{1,0:T(8,128)(2,1)S(1)} %get-tuple-element.137), channel_id=1, source_target_pairs={{0,16},{8,24},{16,0},{24,8},{1,17},{9,25},{17,1},{25,9},{2,18},{10... | collective-permute-start | bytes 1032200 | tf_op jit(solution)/shard_map/ppermute | solution.py:30
  53.2 0.7 collective-permute-start.14
  53.9 0.5 collective-permute-start.15
  54.4 0.0 collective-permute-done.7.low_near_ref
  54.4 3.9 %weight_pass.2 = bf16[3584,512]{1,0:T(8,128)(2,1)S(1)} custom-call(bf16[80,4096]{1,0:T(8,128)(2,1)S(1)} %get-tuple-element.119.refs_0_, bf16[48,4096]{1,0:T(8,128)(2,1)S(1)} %get-tuple-element.120.refs_1_, bf16[128,3584]{1,0:T(8,128)(2,1)S(1)} %collective-permute-done.2.refs_0_.refs_2_, bf16[80,4096]{1,0:T(8,128)(2,1)S(1)} %collective-permute-done.3.refs_1_.refs_3_, ...), custom_call_target="tpu_custom_call" | custom-call | flops 1879048192 | bytes 11010048 | tf_op jit(solution)/shard_map/weight_pass/pallas_call | solution.py:233
  58.3 0.1 collective-permute-start.17
  58.4 2.5 %collective-permute-done.12.far_ref = bf16[48,3584]{1,0:T(8,128)(2,1)S(1)} collective-permute-done((bf16[48,3584]{1,0:T(8,128)(2,1)S(1)}, bf16[48,3584]{1,0:T(8,128)(2,1)S(1)}, u32[]{:S(2)}, u32[]{:S(2)}) %collective-permute-start.12) | collective-permute-done | bytes 344096 | tf_op jit(solution)/shard_map/ppermute | solution.py:24
  60.9 0.1 join.3
  61.0 1.4 %collective-permute-start.19 = (bf16[80,3584]{1,0:T(8,128)(2,1)S(1)}, bf16[80,3584]{1,0:T(8,128)(2,1)S(1)}, u32[]{:S(2)}, u32[]{:S(2)}) collective-permute-start(bf16[80,3584]{1,0:T(8,128)(2,1)S(1)} %join.3), channel_id=1, source_target_pairs={{0,16},{8,24},{16,0},{24,8},{1,17},{9,25},{17,1},{25,9},{2,18},{10... | collective-permute-start | bytes 1720328 | tf_op jit(solution)/shard_map/ppermute | solution.py:30
  62.5 0.1 join.4
  62.6 5.2 %collective-permute-start.13 = (bf16[48,3584]{1,0:T(8,128)(2,1)S(1)}, bf16[48,3584]{1,0:T(8,128)(2,1)S(1)}, u32[]{:S(2)}, u32[]{:S(2)}) collective-permute-start(bf16[48,3584]{1,0:T(8,128)(2,1)S(1)} %join.4), channel_id=1, source_target_pairs={{0,7},{1,0},{2,1},{3,2},{4,3},{5,4},{6,5},{7,6},{8,15},{9,8},{10,9... | collective-permute-start | bytes 1032200 | tf_op jit(solution)/shard_map/ppermute | solution.py:24
  67.8 0.0 collective-permute-done.15.far_ref
  67.8 0.1 join.5
  67.8 0.1 collective-permute-start.18
  67.9 0.0 collective-permute-done.14.back_ref
  68.0 0.1 collective-permute-start.16
  68.0 0.0 collective-permute-done.17.refs_10_
  68.1 4.9 %weight_pass.3 = (bf16[3584,256]{1,0:T(8,128)(2,1)}, bf16[3584,256]{1,0:T(8,128)(2,1)}) custom-call(bf16[80,4096]{1,0:T(8,128)(2,1)S(1)} %get-tuple-element.119.refs_0_, bf16[48,4096]{1,0:T(8,128)(2,1)S(1)} %get-tuple-element.120.refs_1_, bf16[128,3584]{1,0:T(8,128)(2,1)S(1)} %collective-permute-done.2.refs_0_.refs_2_, ...), custom_call_target="tpu_custom_call" | custom-call | flops 1879048192 | bytes 11010048 | tf_op jit(solution)/shard_map/weight_pass/pallas_call | solution.py:233
  73.0 0.7 hidden_pass.1
  73.7 0.8 %collective-permute-done.13.first_ref = bf16[48,3584]{1,0:T(8,128)(2,1)S(1)} collective-permute-done((bf16[48,3584]{1,0:T(8,128)(2,1)S(1)}, bf16[48,3584]{1,0:T(8,128)(2,1)S(1)}, u32[]{:S(2)}, u32[]{:S(2)}) %collective-permute-start.13) | collective-permute-done | bytes 344096 | tf_op jit(solution)/shard_map/ppermute | solution.py:24
  74.5 2.5 %collective-permute-done.18.middle_ref = bf16[32,3584]{1,0:T(8,128)(2,1)S(1)} collective-permute-done((bf16[32,3584]{1,0:T(8,128)(2,1)S(1)}, bf16[32,3584]{1,0:T(8,128)(2,1)S(1)}, u32[]{:S(2)}, u32[]{:S(2)}) %collective-permute-start.18) | collective-permute-done | bytes 229408 | tf_op jit(solution)/shard_map/ppermute | solution.py:24
  77.0 1.3 %final.1 = bf16[128,3584]{1,0:T(8,128)(2,1)} custom-call(bf16[128,3584]{1,0:T(8,128)(2,1)S(1)} %get-tuple-element.121.near_ref, bf16[48,3584]{1,0:T(8,128)(2,1)S(1)} %collective-permute-done.6.home_ref, bf16[48,3584]{1,0:T(8,128)(2,1)S(1)} %collective-permute-done.7.low_near_ref, bf16[48,3584]{1,0:T(8,128)(2,1)S(1)} %collective-permute-done.13.first_ref, ...), custom_call_target="tpu_custom_call" | custom-call | flops 40000000000 | bytes 100000000 | tf_op jit(solution)/shard_map/final/pallas_call | solution.py:302
  (18 shorter events, 0.1 us)
Async XLA Ops:
  0.6 12.9 %collective-permute-start = (bf16[3584,256]{1,0:T(8,128)(2,1)}, bf16[3584,256]{1,0:T(8,128)(2,1)}, u32[]{:S(2)}, u32[]{:S(2)}) collective-permute-start(bf16[3584,256]{1,0:T(8,128)(2,1)} %bitcast.20), channel_id=1, source_target_pairs={{0,8},{8,0},{16,24},{24,16},{1,9},{9,1},{17,25},{25,17},{2,10},{10... | collective-permute-start | bytes 5505032 | tf_op jit(solution)/shard_map/ppermute | solution.py:36
  1.1 13.0 %collective-permute-start.1 = (bf16[3584,256]{1,0:T(8,128)(2,1)}, bf16[3584,256]{1,0:T(8,128)(2,1)}, u32[]{:S(2)}, u32[]{:S(2)}) collective-permute-start(bf16[3584,256]{1,0:T(8,128)(2,1)} %bitcast.24), channel_id=1, source_target_pairs={{0,8},{8,0},{16,24},{24,16},{1,9},{9,1},{17,25},{25,17},{2,10},{10... | collective-permute-start | bytes 5505032 | tf_op jit(solution)/shard_map/ppermute | solution.py:36
  1.2 28.4 %collective-permute-start.2 = (bf16[128,3584]{1,0:T(8,128)(2,1)}, bf16[128,3584]{1,0:T(8,128)(2,1)S(1)}, u32[]{:S(2)}, u32[]{:S(2)}) collective-permute-start(bf16[128,3584]{1,0:T(8,128)(2,1)} %bitcast.28), channel_id=1, source_target_pairs={{0,16},{8,24},{16,0},{24,8},{1,17},{9,25},{17,1},{25,9},{2,18},{10... | collective-permute-start | bytes 2752520 | tf_op jit(solution)/shard_map/ppermute | solution.py:30
  5.5 22.3 %collective-permute-start.3 = (bf16[80,4096]{1,0:T(8,128)(2,1)S(1)}, bf16[80,4096]{1,0:T(8,128)(2,1)S(1)}, u32[]{:S(2)}, u32[]{:S(2)}) collective-permute-start(bf16[80,4096]{1,0:T(8,128)(2,1)S(1)} %get-tuple-element.119.refs_0_), channel_id=1, source_target_pairs={{0,1},{1,2},{2,3},{3,4},{4,5},{5,6},{6,7},{7,0},{8,9},{9,10},{10,1... | collective-permute-start | bytes 1966088 | tf_op jit(solution)/shard_map/ppermute | solution.py:24
  7.1 26.2 %collective-permute-start.5 = (bf16[48,4096]{1,0:T(8,128)(2,1)S(1)}, bf16[48,4096]{1,0:T(8,128)(2,1)S(1)}, u32[]{:S(2)}, u32[]{:S(2)}) collective-permute-start(bf16[48,4096]{1,0:T(8,128)(2,1)S(1)} %get-tuple-element.120.refs_1_), channel_id=1, source_target_pairs={{0,1},{1,2},{2,3},{3,4},{4,5},{5,6},{6,7},{7,0},{8,9},{9,10},{10,1... | collective-permute-start | bytes 1179656 | tf_op jit(solution)/shard_map/ppermute | solution.py:24
  13.6 14.2 %collective-permute-start.4 = (bf16[128,512]{1,0:T(8,128)(2,1)S(1)}, bf16[128,512]{1,0:T(8,128)(2,1)S(1)}, u32[]{:S(2)}, u32[]{:S(2)}) collective-permute-start(bf16[128,512]{1,0:T(8,128)(2,1)S(1)} %get-tuple-element.122), channel_id=1, source_target_pairs={{0,16},{8,24},{16,0},{24,8},{1,17},{9,25},{17,1},{25,9},{2,18},{10... | collective-permute-start | bytes 393224 | tf_op jit(solution)/shard_map/ppermute | solution.py:30
  14.2 1.5 %copy-start = (bf16[1,3584,256]{2,1,0:T(8,128)(2,1)S(1)}, bf16[1,3584,256]{2,1,0:T(8,128)(2,1)}, u32[]{:S(2)}) copy-start(bf16[1,3584,256]{2,1,0:T(8,128)(2,1)} %param.28) | copy-start | bytes 5505028
  15.7 1.5 %copy-start.2 = (bf16[1,3584,256]{2,1,0:T(8,128)(2,1)S(1)}, bf16[1,3584,256]{2,1,0:T(8,128)(2,1)}, u32[]{:S(2)}) copy-start(bf16[1,3584,256]{2,1,0:T(8,128)(2,1)} %param.29) | copy-start | bytes 5505028
  17.2 16.1 %copy-start.3 = (bf16[1,3584,256]{2,1,0:T(8,128)(2,1)S(1)}, bf16[1,3584,256]{2,1,0:T(8,128)(2,1)}, u32[]{:S(2)}) copy-start(bf16[1,3584,256]{2,1,0:T(8,128)(2,1)} %param.29) | copy-start | bytes 5505028
  22.6 10.7 %copy-start.1 = (bf16[1,3584,256]{2,1,0:T(8,128)(2,1)S(1)}, bf16[1,3584,256]{2,1,0:T(8,128)(2,1)}, u32[]{:S(2)}) copy-start(bf16[1,3584,256]{2,1,0:T(8,128)(2,1)} %param.28) | copy-start | bytes 5505028
  27.8 17.2 %collective-permute-start.9 = (bf16[80,3584]{1,0:T(8,128)(2,1)S(1)}, bf16[80,3584]{1,0:T(8,128)(2,1)S(1)}, u32[]{:S(2)}, u32[]{:S(2)}) collective-permute-start(bf16[80,3584]{1,0:T(8,128)(2,1)S(1)} %slice.54), channel_id=1, source_target_pairs={{0,16},{8,24},{16,0},{24,8},{1,17},{9,25},{17,1},{25,9},{2,18},{10... | collective-permute-start | bytes 1720328 | tf_op jit(solution)/shard_map/ppermute | solution.py:30
  29.7 15.4 %collective-permute-start.8 = (bf16[48,3584]{1,0:T(8,128)(2,1)S(1)}, bf16[48,3584]{1,0:T(8,128)(2,1)S(1)}, u32[]{:S(2)}, u32[]{:S(2)}) collective-permute-start(bf16[48,3584]{1,0:T(8,128)(2,1)S(1)} %slice.55), channel_id=1, source_target_pairs={{0,1},{1,2},{2,3},{3,4},{4,5},{5,6},{6,7},{7,0},{8,9},{9,10},{10,1... | collective-permute-start | bytes 1032200 | tf_op jit(solution)/shard_map/ppermute | solution.py:24
  33.2 11.8 %collective-permute-start.10 = (bf16[128,512]{1,0:T(8,128)(2,1)S(1)}, bf16[128,512]{1,0:T(8,128)(2,1)S(1)}, u32[]{:S(2)}, u32[]{:S(2)}) collective-permute-start(bf16[128,512]{1,0:T(8,128)(2,1)S(1)} %collective-permute-done.4.refs_3_), channel_id=1, source_target_pairs={{0,1},{1,2},{2,3},{3,4},{4,5},{5,6},{6,7},{7,0},{8,9},{9,10},{10,1... | collective-permute-start | bytes 393224 | tf_op jit(solution)/shard_map/ppermute | solution.py:24
  39.8 14.2 %collective-permute-start.6 = (bf16[48,3584]{1,0:T(8,128)(2,1)S(1)}, bf16[48,3584]{1,0:T(8,128)(2,1)S(1)}, u32[]{:S(2)}, u32[]{:S(2)}) collective-permute-start(bf16[48,3584]{1,0:T(8,128)(2,1)S(1)} %get-tuple-element.128), channel_id=1, source_target_pairs={{0,16},{8,24},{16,0},{24,8},{1,17},{9,25},{17,1},{25,9},{2,18},{10... | collective-permute-start | bytes 1032200 | tf_op jit(solution)/shard_map/ppermute | solution.py:30
  40.3 14.1 %collective-permute-start.7 = (bf16[48,3584]{1,0:T(8,128)(2,1)S(1)}, bf16[48,3584]{1,0:T(8,128)(2,1)S(1)}, u32[]{:S(2)}, u32[]{:S(2)}) collective-permute-start(bf16[48,3584]{1,0:T(8,128)(2,1)S(1)} %get-tuple-element.129), channel_id=1, source_target_pairs={{0,7},{1,0},{2,1},{3,2},{4,3},{5,4},{6,5},{7,6},{8,15},{9,8},{10,9... | collective-permute-start | bytes 1032200 | tf_op jit(solution)/shard_map/ppermute | solution.py:24
  48.3 12.6 %collective-permute-start.12 = (bf16[48,3584]{1,0:T(8,128)(2,1)S(1)}, bf16[48,3584]{1,0:T(8,128)(2,1)S(1)}, u32[]{:S(2)}, u32[]{:S(2)}) collective-permute-start(bf16[48,3584]{1,0:T(8,128)(2,1)S(1)} %get-tuple-element.139), channel_id=1, source_target_pairs={{0,7},{1,0},{2,1},{3,2},{4,3},{5,4},{6,5},{7,6},{8,15},{9,8},{10,9... | collective-permute-start | bytes 1032200 | tf_op jit(solution)/shard_map/ppermute | solution.py:24
  50.9 11.6 %collective-permute-start.11 = (bf16[48,3584]{1,0:T(8,128)(2,1)S(1)}, bf16[48,3584]{1,0:T(8,128)(2,1)S(1)}, u32[]{:S(2)}, u32[]{:S(2)}) collective-permute-start(bf16[48,3584]{1,0:T(8,128)(2,1)S(1)} %get-tuple-element.137), channel_id=1, source_target_pairs={{0,16},{8,24},{16,0},{24,8},{1,17},{9,25},{17,1},{25,9},{2,18},{10... | collective-permute-start | bytes 1032200 | tf_op jit(solution)/shard_map/ppermute | solution.py:30
  53.2 14.7 %collective-permute-start.14 = (bf16[256,512]{1,0:T(8,128)(2,1)S(1)}, bf16[256,512]{1,0:T(8,128)(2,1)S(1)}, u32[]{:S(2)}, u32[]{:S(2)}) collective-permute-start(bf16[256,512]{1,0:T(8,128)(2,1)S(1)} %get-tuple-element.148), channel_id=1, source_target_pairs={{0,7},{1,0},{2,1},{3,2},{4,3},{5,4},{6,5},{7,6},{8,15},{9,8},{10,9... | collective-permute-start | bytes 786440 | tf_op jit(solution)/shard_map/ppermute | solution.py:24
  53.9 13.9 %collective-permute-start.15 = (bf16[32,3584]{1,0:T(8,128)(2,1)S(1)}, bf16[32,3584]{1,0:T(8,128)(2,1)S(1)}, u32[]{:S(2)}, u32[]{:S(2)}) collective-permute-start(bf16[32,3584]{1,0:T(8,128)(2,1)S(1)} %get-tuple-element.150), channel_id=1, source_target_pairs={{0,16},{8,24},{16,0},{24,8},{1,17},{9,25},{17,1},{25,9},{2,18},{10... | collective-permute-start | bytes 688136 | tf_op jit(solution)/shard_map/ppermute | solution.py:30
  58.3 9.7 %collective-permute-start.17 = (bf16[3584,512]{1,0:T(8,128)(2,1)S(1)}, bf16[3584,512]{1,0:T(8,128)(2,1)S(1)}, u32[]{:S(2)}, u32[]{:S(2)}) collective-permute-start(bf16[3584,512]{1,0:T(8,128)(2,1)S(1)} %weight_pass.2), channel_id=1, source_target_pairs={{0,8},{8,0},{16,24},{24,16},{1,9},{9,1},{17,25},{25,17},{2,10},{10... | collective-permute-start | bytes 11010056 | tf_op jit(solution)/shard_map/ppermute | solution.py:36
  61.0 16.0 %collective-permute-start.19 = (bf16[80,3584]{1,0:T(8,128)(2,1)S(1)}, bf16[80,3584]{1,0:T(8,128)(2,1)S(1)}, u32[]{:S(2)}, u32[]{:S(2)}) collective-permute-start(bf16[80,3584]{1,0:T(8,128)(2,1)S(1)} %join.3), channel_id=1, source_target_pairs={{0,16},{8,24},{16,0},{24,8},{1,17},{9,25},{17,1},{25,9},{2,18},{10... | collective-permute-start | bytes 1720328 | tf_op jit(solution)/shard_map/ppermute | solution.py:30
  62.6 12.0 %collective-permute-start.13 = (bf16[48,3584]{1,0:T(8,128)(2,1)S(1)}, bf16[48,3584]{1,0:T(8,128)(2,1)S(1)}, u32[]{:S(2)}, u32[]{:S(2)}) collective-permute-start(bf16[48,3584]{1,0:T(8,128)(2,1)S(1)} %join.4), channel_id=1, source_target_pairs={{0,7},{1,0},{2,1},{3,2},{4,3},{5,4},{6,5},{7,6},{8,15},{9,8},{10,9... | collective-permute-start | bytes 1032200 | tf_op jit(solution)/shard_map/ppermute | solution.py:24
  67.8 9.2 %collective-permute-start.18 = (bf16[32,3584]{1,0:T(8,128)(2,1)S(1)}, bf16[32,3584]{1,0:T(8,128)(2,1)S(1)}, u32[]{:S(2)}, u32[]{:S(2)}) collective-permute-start(bf16[32,3584]{1,0:T(8,128)(2,1)S(1)} %join.5), channel_id=1, source_target_pairs={{0,7},{1,0},{2,1},{3,2},{4,3},{5,4},{6,5},{7,6},{8,15},{9,8},{10,9... | collective-permute-start | bytes 688136 | tf_op jit(solution)/shard_map/ppermute | solution.py:24
  68.0 5.0 %collective-permute-start.16 = (bf16[256,256]{1,0:T(8,128)(2,1)S(1)}, bf16[256,256]{1,0:T(8,128)(2,1)S(1)}, u32[]{:S(2)}, u32[]{:S(2)}) collective-permute-start(bf16[256,256]{1,0:T(8,128)(2,1)S(1)} %hidden_sum.1), channel_id=1, source_target_pairs={{0,8},{8,0},{16,24},{24,16},{1,9},{9,1},{17,25},{25,17},{2,10},{10... | collective-permute-start | bytes 393224 | tf_op jit(solution)/shard_map/ppermute | solution.py:36

commit v8 on v7

--- a/solution.py
+++ b/solution.py
@@ -11,7 +11,7 @@
 OUT_SHARE = 80
 BACK_SHARE = (48, 80)
 LIMIT = 20 * 2**20
-LONG = pl.CostEstimate(flops=4 * 10**10, bytes_accessed=10**8, transcendentals=0)
+LONG = pl.CostEstimate(flops=8 * 10**10, bytes_accessed=2 * 10**8, transcendentals=0)
 
 
 def work(flops, moved):
@@ -402,10 +402,11 @@
     low_far = shifted(lower_pf, -1)
 
     pieces = (near_top, near_low, y_tile, x_top, x_low, xy_top, xy_low)
-    (sent,) = weight_pass(width, pieces, after((other_hn, other_mid, other_pf), first_home, low_near))
+    (sent,) = weight_pass(width, pieces, after((other_hn, other_mid, other_pf), first_home))
     got = within(sent)
     hid_back = shifted(hid_past, -1)
-    low_sum = join(rest_hf, after(low_far, sent), work(0, 0))
+    low_near, low_far = after((low_near, low_far), sent)
+    low_sum = join(rest_hf, low_far, work(0, 0))
     low_home = across(low_sum)
     first_sum = join(first_pn, after(first_past, low_sum), work(0, 0))
     first_back = shifted(first_sum, -1)

time: 78.6 us -> 78.5 us (level)
  transfers between devices with their start and end apart: 20 -> 20, of which waited for: 5 -> 4; matrix products, arithmetic and copies ran while one was open for 3% -> 3% of each run, Pallas kernels for 34% -> 34%
where the time goes in v8:
time: 78.5 us; the launch traced here: 78.2 us
  starting transfers between devices  29.3 us (37%)
  Pallas kernels  27.6 us (35%)
  waiting for transfers between devices  12.4 us (16%)
  local copies, waits for them, and re-layouts  4.64 us (6%)
  between operations  3.31 us (4%)
  other arithmetic  0.85 us (1%)
    ppermute x9, starting transfers between devices, shifted(): return lax.ppermute(value, 'expert', pairs)  18.5 us
    pallas_call x3, Pallas kernels, block_pass(): pl.pallas_call(functools.partial(block_body, len(pieces), sources, len(ex...  15.2 us
    ppermute x7, starting transfers between devices, across(): return lax.ppermute(value, 'dp', pairs)  10.1 us
    pallas_call x2, Pallas kernels, weight_pass(): pl.pallas_call(functools.partial(weight_body, len(pieces), len(grads), st...  8.8 us
    ppermute x9, waiting for transfers between devices, shifted(): return lax.ppermute(value, 'expert', pairs)  7.22 us
    ppermute x7, waiting for transfers between devices, across(): return lax.ppermute(value, 'dp', pairs)  5.2 us
    unnamed x8, local copies, waits for them, and re-layouts  3.01 us
  transfers between devices with their start and end apart: 20, of which 4 were waited for; matrix products, arithmetic and copies ran while one was open for 3% of the time, Pallas kernels for 34%

profile of v8, /device:TPU:0, one launch (start us, length us, event | category | flops | bytes accessed | tf_op | source)
XLA Modules:
  0.0 78.2 jit_solution(6957184239153770067)
XLA Ops:
  0.6 0.5 collective-permute-start
  1.1 0.1 collective-permute-start.1
  1.2 2.9 %collective-permute-start.2 = (bf16[128,3584]{1,0:T(8,128)(2,1)}, bf16[128,3584]{1,0:T(8,128)(2,1)S(1)}, u32[]{:S(2)}, u32[]{:S(2)}) collective-permute-start(bf16[128,3584]{1,0:T(8,128)(2,1)} %bitcast.28), channel_id=1, source_target_pairs={{0,16},{8,24},{16,0},{24,8},{1,17},{9,25},{17,1},{25,9},{2,18},{10... | collective-permute-start | bytes 2752520 | tf_op jit(solution)/shard_map/ppermute | solution.py:30
  4.2 1.3 %pack.1 = (bf16[80,4096]{1,0:T(8,128)(2,1)S(1)}, bf16[48,4096]{1,0:T(8,128)(2,1)S(1)}, bf16[128,512]{1,0:T(8,128)(2,1)S(1)}) custom-call(bf16[128,3584]{1,0:T(8,128)(2,1)} %bitcast.29, bf16[128,1024]{1,0:T(8,128)(2,1)} %bitcast.30), custom_call_target="tpu_custom_call" | custom-call | bytes 2359296 | tf_op jit(solution)/shard_map/pack/pallas_call | solution.py:90
  5.5 1.5 %collective-permute-start.3 = (bf16[80,4096]{1,0:T(8,128)(2,1)S(1)}, bf16[80,4096]{1,0:T(8,128)(2,1)S(1)}, u32[]{:S(2)}, u32[]{:S(2)}) collective-permute-start(bf16[80,4096]{1,0:T(8,128)(2,1)S(1)} %get-tuple-element.120.refs_0_), channel_id=1, source_target_pairs={{0,1},{1,2},{2,3},{3,4},{4,5},{5,6},{6,7},{7,0},{8,9},{9,10},{10,1... | collective-permute-start | bytes 1966088 | tf_op jit(solution)/shard_map/ppermute | solution.py:24
  7.1 1.5 %collective-permute-start.5 = (bf16[48,4096]{1,0:T(8,128)(2,1)S(1)}, bf16[48,4096]{1,0:T(8,128)(2,1)S(1)}, u32[]{:S(2)}, u32[]{:S(2)}) collective-permute-start(bf16[48,4096]{1,0:T(8,128)(2,1)S(1)} %get-tuple-element.121.refs_1_), channel_id=1, source_target_pairs={{0,1},{1,2},{2,3},{3,4},{4,5},{5,6},{6,7},{7,0},{8,9},{9,10},{10,1... | collective-permute-start | bytes 1179656 | tf_op jit(solution)/shard_map/ppermute | solution.py:24
  8.6 1.4 %fusion.4 = (s32[1,1]{1,0:T(1,128)}, s32[1,1]{1,0:T(1,128)}, s32[1,1]{1,0:T(1,128)}, s32[1,1]{1,0:T(1,128)}) fusion(s32[4,8]{1,0:T(4,128)} %param.27, s32[]{:T(128)S(6)} %select_n.62, s32[]{:T(128)S(6)} %select_n.63, s32[]{:T(128)S(6)} %select_n.67, s32[]{:T(128)S(6)} %select_n.70), kind=kLoop, calls=%fused_computation.9 | loop fusion | bytes 48 | tf_op jit(solution)/shard_map/dynamic_slice | solution.py:346
  12.6 0.8 %fusion = (f32[128,1]{0,1:T(1,128)S(1)}, f32[128,1]{0,1:T(1,128)S(1)}, f32[128,1]{0,1:T(1,128)S(1)}, f32[128,1]{0,1:T(1,128)S(1)}) fusion(pred[]{:T(512)} %bitcast.3, f32[4,1024]{1,0:T(4,128)} %param.26, s32[]{:T(128)S(6)} %select_n.62, s32[]{:T(128)S(6)} %select_n.64, s32[]{:T(128)S(6)} %select_n.67, pred[]{:T(512)} %bitcast.5, s32[]{:T(128)S(6)} %select_n.71, ...), kind=kLoop, calls=%fused_computation.5 | loop fusion | flops 512 | bytes 4116 | tf_op jit(solution)/shard_map/reshape | solution.py:349
  13.4 0.1 copy.14.refs_2_.refs_4_.refs_3_
  13.6 0.0 collective-permute-done.refs_5_.refs_7_
  13.6 0.6 collective-permute-start.4
  14.1 0.0 collective-permute-done.1.refs_6_.refs_8_
  14.2 1.5 %copy-done = bf16[1,3584,256]{2,1,0:T(8,128)(2,1)S(1)} copy-done((bf16[1,3584,256]{2,1,0:T(8,128)(2,1)S(1)}, bf16[1,3584,256]{2,1,0:T(8,128)(2,1)}, u32[]{:S(2)}) %copy-start) | copy-done | bytes 1835032
  15.7 1.5 %copy-done.2 = bf16[1,3584,256]{2,1,0:T(8,128)(2,1)S(1)} copy-done((bf16[1,3584,256]{2,1,0:T(8,128)(2,1)S(1)}, bf16[1,3584,256]{2,1,0:T(8,128)(2,1)}, u32[]{:S(2)}) %copy-start.2) | copy-done | bytes 1835032
  17.2 5.4 %block_pass.3 = (bf16[128,512]{1,0:T(8,128)(2,1)S(1)}, bf16[128,512]{1,0:T(8,128)(2,1)S(1)}, bf16[128,512]{1,0:T(8,128)(2,1)S(1)}, bf16[128,3584]{1,0:T(8,128)(2,1)S(1)}) custom-call(bf16[80,4096]{1,0:T(8,128)(2,1)S(1)} %get-tuple-element.120.refs_0_, bf16[48,4096]{1,0:T(8,128)(2,1)S(1)} %get-tuple-element.121.refs_1_, ...), custom_call_target="tpu_custom_call" | custom-call | flops 1879048192 | bytes 1835008 | tf_op jit(solution)/shard_map/block_pass/pallas_call | solution.py:162
  22.6 0.0 copy-start.1
  22.6 5.2 %collective-permute-done.4.refs_3_ = bf16[128,512]{1,0:T(8,128)(2,1)S(1)} collective-permute-done((bf16[128,512]{1,0:T(8,128)(2,1)S(1)}, bf16[128,512]{1,0:T(8,128)(2,1)S(1)}, u32[]{:S(2)}, u32[]{:S(2)}) %collective-permute-start.4) | collective-permute-done | bytes 131104 | tf_op jit(solution)/shard_map/ppermute | solution.py:30
  27.8 0.0 collective-permute-done.3.refs_1_.refs_3_
  27.8 1.8 %collective-permute-start.9 = (bf16[80,3584]{1,0:T(8,128)(2,1)S(1)}, bf16[80,3584]{1,0:T(8,128)(2,1)S(1)}, u32[]{:S(2)}, u32[]{:S(2)}) collective-permute-start(bf16[80,3584]{1,0:T(8,128)(2,1)S(1)} %slice.54), channel_id=1, source_target_pairs={{0,16},{8,24},{16,0},{24,8},{1,17},{9,25},{17,1},{25,9},{2,18},{10... | collective-permute-start | bytes 1720328 | tf_op jit(solution)/shard_map/ppermute | solution.py:30
  29.6 0.0 collective-permute-done.2.refs_0_.refs_2_
  29.7 1.5 %collective-permute-start.8 = (bf16[48,3584]{1,0:T(8,128)(2,1)S(1)}, bf16[48,3584]{1,0:T(8,128)(2,1)S(1)}, u32[]{:S(2)}, u32[]{:S(2)}) collective-permute-start(bf16[48,3584]{1,0:T(8,128)(2,1)S(1)} %slice.55), channel_id=1, source_target_pairs={{0,1},{1,2},{2,3},{3,4},{4,5},{5,6},{6,7},{7,0},{8,9},{9,10},{10,1... | collective-permute-start | bytes 1032200 | tf_op jit(solution)/shard_map/ppermute | solution.py:24
  31.2 2.0 %collective-permute-done.5.refs_2_.refs_4_ = bf16[48,4096]{1,0:T(8,128)(2,1)S(1)} collective-permute-done((bf16[48,4096]{1,0:T(8,128)(2,1)S(1)}, bf16[48,4096]{1,0:T(8,128)(2,1)S(1)}, u32[]{:S(2)}, u32[]{:S(2)}) %collective-permute-start.5) | collective-permute-done | bytes 393248 | tf_op jit(solution)/shard_map/ppermute | solution.py:24
  33.2 0.0 collective-permute-start.10
  33.2 6.5 %block_pass.4 = (bf16[256,512]{1,0:T(8,128)(2,1)S(1)}, bf16[256,512]{1,0:T(8,128)(2,1)S(1)}, bf16[256,512]{1,0:T(8,128)(2,1)S(1)}, bf16[3584,256]{1,0:T(8,128)(2...) custom-call(bf16[128,3584]{1,0:T(8,128)(2,1)S(1)} %collective-permut, ...), custom_call_target="tpu_custom_call" | custom-call | flops 3758096384 | bytes 3670016 | tf_op jit(solution)/shard_map/block_pass/pallas_call | solution.py:162
  39.8 0.6 collective-permute-start.6
  40.3 4.7 %collective-permute-start.7 = (bf16[48,3584]{1,0:T(8,128)(2,1)S(1)}, bf16[48,3584]{1,0:T(8,128)(2,1)S(1)}, u32[]{:S(2)}, u32[]{:S(2)}) collective-permute-start(bf16[48,3584]{1,0:T(8,128)(2,1)S(1)} %get-tuple-element.130), channel_id=1, source_target_pairs={{0,7},{1,0},{2,1},{3,2},{4,3},{5,4},{6,5},{7,6},{8,15},{9,8},{10,9... | collective-permute-start | bytes 1032200 | tf_op jit(solution)/shard_map/ppermute | solution.py:24
  45.1 0.0 collective-permute-done.9.refs_0_.refs_5_
  45.1 3.2 %block_pass.5 = (bf16[256,512]{1,0:T(8,128)(2,1)S(1)}, bf16[128,512]{1,0:T(8,128)(2,1)S(1)}, bf16[128,512]{1,0:T(8,128)(2,1)S(1)}, bf16[48,3584]{1,0:T(8,128)(2,...) custom-call(bf16[80,3584]{1,0:T(8,128)(2,1)S(1)} %collective-permute-done.9.refs_0_.refs_5_, ...), custom_call_target="tpu_custom_call" | custom-call | flops 1879048192 | bytes 1835008 | tf_op jit(solution)/shard_map/block_pass/pallas_call | solution.py:162
  48.3 2.6 %collective-permute-start.11 = (bf16[48,3584]{1,0:T(8,128)(2,1)S(1)}, bf16[48,3584]{1,0:T(8,128)(2,1)S(1)}, u32[]{:S(2)}, u32[]{:S(2)}) collective-permute-start(bf16[48,3584]{1,0:T(8,128)(2,1)S(1)} %get-tuple-element.137), channel_id=1, source_target_pairs={{0,7},{1,0},{2,1},{3,2},{4,3},{5,4},{6,5},{7,6},{8,15},{9,8},{10,9... | collective-permute-start | bytes 1032200 | tf_op jit(solution)/shard_map/ppermute | solution.py:24
  50.9 2.3 %collective-permute-start.12 = (bf16[48,3584]{1,0:T(8,128)(2,1)S(1)}, bf16[48,3584]{1,0:T(8,128)(2,1)S(1)}, u32[]{:S(2)}, u32[]{:S(2)}) collective-permute-start(bf16[48,3584]{1,0:T(8,128)(2,1)S(1)} %get-tuple-element.146), channel_id=1, source_target_pairs={{0,16},{8,24},{16,0},{24,8},{1,17},{9,25},{17,1},{25,9},{2,18},{10... | collective-permute-start | bytes 1032200 | tf_op jit(solution)/shard_map/ppermute | solution.py:30
  53.2 0.7 collective-permute-start.14
  53.9 0.5 collective-permute-start.15
  54.4 3.9 %weight_pass.2 = bf16[3584,512]{1,0:T(8,128)(2,1)S(1)} custom-call(bf16[80,4096]{1,0:T(8,128)(2,1)S(1)} %get-tuple-element.120.refs_0_, bf16[48,4096]{1,0:T(8,128)(2,1)S(1)} %get-tuple-element.121.refs_1_, bf16[128,3584]{1,0:T(8,128)(2,1)S(1)} %collective-permute-done.2.refs_0_.refs_2_, bf16[80,4096]{1,0:T(8,128)(2,1)S(1)} %collective-permute-done.3.refs_1_.refs_3_, ...), custom_call_target="tpu_custom_call" | custom-call | flops 1879048192 | bytes 11010048 | tf_op jit(solution)/shard_map/weight_pass/pallas_call | solution.py:233
  58.3 0.0 collective-permute-done.7.low_near_ref
  58.3 0.1 collective-permute-start.17
  58.4 2.5 %collective-permute-done.11.far_ref = bf16[48,3584]{1,0:T(8,128)(2,1)S(1)} collective-permute-done((bf16[48,3584]{1,0:T(8,128)(2,1)S(1)}, bf16[48,3584]{1,0:T(8,128)(2,1)S(1)}, u32[]{:S(2)}, u32[]{:S(2)}) %collective-permute-start.11) | collective-permute-done | bytes 344096 | tf_op jit(solution)/shard_map/ppermute | solution.py:24
  60.9 0.1 join.3
  61.0 1.4 %collective-permute-start.19 = (bf16[80,3584]{1,0:T(8,128)(2,1)S(1)}, bf16[80,3584]{1,0:T(8,128)(2,1)S(1)}, u32[]{:S(2)}, u32[]{:S(2)}) collective-permute-start(bf16[80,3584]{1,0:T(8,128)(2,1)S(1)} %join.3), channel_id=1, source_target_pairs={{0,16},{8,24},{16,0},{24,8},{1,17},{9,25},{17,1},{25,9},{2,18},{10... | collective-permute-start | bytes 1720328 | tf_op jit(solution)/shard_map/ppermute | solution.py:30
  62.5 0.1 join.4
  62.6 5.2 %collective-permute-start.13 = (bf16[48,3584]{1,0:T(8,128)(2,1)S(1)}, bf16[48,3584]{1,0:T(8,128)(2,1)S(1)}, u32[]{:S(2)}, u32[]{:S(2)}) collective-permute-start(bf16[48,3584]{1,0:T(8,128)(2,1)S(1)} %join.4), channel_id=1, source_target_pairs={{0,7},{1,0},{2,1},{3,2},{4,3},{5,4},{6,5},{7,6},{8,15},{9,8},{10,9... | collective-permute-start | bytes 1032200 | tf_op jit(solution)/shard_map/ppermute | solution.py:24
  67.8 0.0 collective-permute-done.15.far_ref
  67.8 0.1 join.5
  67.8 0.6 collective-permute-start.18
  68.5 0.1 collective-permute-start.16
  68.6 4.9 %weight_pass.3 = (bf16[3584,256]{1,0:T(8,128)(2,1)}, bf16[3584,256]{1,0:T(8,128)(2,1)}) custom-call(bf16[80,4096]{1,0:T(8,128)(2,1)S(1)} %get-tuple-element.120.refs_0_, bf16[48,4096]{1,0:T(8,128)(2,1)S(1)} %get-tuple-element.121.refs_1_, bf16[128,3584]{1,0:T(8,128)(2,1)S(1)} %collective-permute-done.2.refs_0_.refs_2_, ...), custom_call_target="tpu_custom_call" | custom-call | flops 1879048192 | bytes 11010048 | tf_op jit(solution)/shard_map/weight_pass/pallas_call | solution.py:233
  73.5 0.7 hidden_pass.1
  74.2 2.7 %collective-permute-done.18.middle_ref = bf16[32,3584]{1,0:T(8,128)(2,1)S(1)} collective-permute-done((bf16[32,3584]{1,0:T(8,128)(2,1)S(1)}, bf16[32,3584]{1,0:T(8,128)(2,1)S(1)}, u32[]{:S(2)}, u32[]{:S(2)}) %collective-permute-start.18) | collective-permute-done | bytes 229408 | tf_op jit(solution)/shard_map/ppermute | solution.py:24
  76.9 1.3 %final.1 = bf16[128,3584]{1,0:T(8,128)(2,1)} custom-call(bf16[128,3584]{1,0:T(8,128)(2,1)S(1)} %get-tuple-element.122.near_ref, bf16[48,3584]{1,0:T(8,128)(2,1)S(1)} %collective-permute-done.6.home_ref, bf16[48,3584]{1,0:T(8,128)(2,1)S(1)} %collective-permute-done.7.low_near_ref, bf16[48,3584]{1,0:T(8,128)(2,1)S(1)} %collective-permute-done.13.first_ref, ...), custom_call_target="tpu_custom_call" | custom-call | flops 80000000000 | bytes 200000000 | tf_op jit(solution)/shard_map/final/pallas_call | solution.py:302
  (18 shorter events, 0.1 us)
Async XLA Ops:
  0.6 12.9 %collective-permute-start = (bf16[3584,256]{1,0:T(8,128)(2,1)}, bf16[3584,256]{1,0:T(8,128)(2,1)}, u32[]{:S(2)}, u32[]{:S(2)}) collective-permute-start(bf16[3584,256]{1,0:T(8,128)(2,1)} %bitcast.20), channel_id=1, source_target_pairs={{0,8},{8,0},{16,24},{24,16},{1,9},{9,1},{17,25},{25,17},{2,10},{10... | collective-permute-start | bytes 5505032 | tf_op jit(solution)/shard_map/ppermute | solution.py:36
  1.1 13.0 %collective-permute-start.1 = (bf16[3584,256]{1,0:T(8,128)(2,1)}, bf16[3584,256]{1,0:T(8,128)(2,1)}, u32[]{:S(2)}, u32[]{:S(2)}) collective-permute-start(bf16[3584,256]{1,0:T(8,128)(2,1)} %bitcast.24), channel_id=1, source_target_pairs={{0,8},{8,0},{16,24},{24,16},{1,9},{9,1},{17,25},{25,17},{2,10},{10... | collective-permute-start | bytes 5505032 | tf_op jit(solution)/shard_map/ppermute | solution.py:36
  1.2 28.4 %collective-permute-start.2 = (bf16[128,3584]{1,0:T(8,128)(2,1)}, bf16[128,3584]{1,0:T(8,128)(2,1)S(1)}, u32[]{:S(2)}, u32[]{:S(2)}) collective-permute-start(bf16[128,3584]{1,0:T(8,128)(2,1)} %bitcast.28), channel_id=1, source_target_pairs={{0,16},{8,24},{16,0},{24,8},{1,17},{9,25},{17,1},{25,9},{2,18},{10... | collective-permute-start | bytes 2752520 | tf_op jit(solution)/shard_map/ppermute | solution.py:30
  5.5 22.3 %collective-permute-start.3 = (bf16[80,4096]{1,0:T(8,128)(2,1)S(1)}, bf16[80,4096]{1,0:T(8,128)(2,1)S(1)}, u32[]{:S(2)}, u32[]{:S(2)}) collective-permute-start(bf16[80,4096]{1,0:T(8,128)(2,1)S(1)} %get-tuple-element.120.refs_0_), channel_id=1, source_target_pairs={{0,1},{1,2},{2,3},{3,4},{4,5},{5,6},{6,7},{7,0},{8,9},{9,10},{10,1... | collective-permute-start | bytes 1966088 | tf_op jit(solution)/shard_map/ppermute | solution.py:24
  7.1 26.2 %collective-permute-start.5 = (bf16[48,4096]{1,0:T(8,128)(2,1)S(1)}, bf16[48,4096]{1,0:T(8,128)(2,1)S(1)}, u32[]{:S(2)}, u32[]{:S(2)}) collective-permute-start(bf16[48,4096]{1,0:T(8,128)(2,1)S(1)} %get-tuple-element.121.refs_1_), channel_id=1, source_target_pairs={{0,1},{1,2},{2,3},{3,4},{4,5},{5,6},{6,7},{7,0},{8,9},{9,10},{10,1... | collective-permute-start | bytes 1179656 | tf_op jit(solution)/shard_map/ppermute | solution.py:24
  13.6 14.2 %collective-permute-start.4 = (bf16[128,512]{1,0:T(8,128)(2,1)S(1)}, bf16[128,512]{1,0:T(8,128)(2,1)S(1)}, u32[]{:S(2)}, u32[]{:S(2)}) collective-permute-start(bf16[128,512]{1,0:T(8,128)(2,1)S(1)} %get-tuple-element.123), channel_id=1, source_target_pairs={{0,16},{8,24},{16,0},{24,8},{1,17},{9,25},{17,1},{25,9},{2,18},{10... | collective-permute-start | bytes 393224 | tf_op jit(solution)/shard_map/ppermute | solution.py:30
  14.2 1.5 %copy-start = (bf16[1,3584,256]{2,1,0:T(8,128)(2,1)S(1)}, bf16[1,3584,256]{2,1,0:T(8,128)(2,1)}, u32[]{:S(2)}) copy-start(bf16[1,3584,256]{2,1,0:T(8,128)(2,1)} %param.28) | copy-start | bytes 5505028
  15.7 1.5 %copy-start.2 = (bf16[1,3584,256]{2,1,0:T(8,128)(2,1)S(1)}, bf16[1,3584,256]{2,1,0:T(8,128)(2,1)}, u32[]{:S(2)}) copy-start(bf16[1,3584,256]{2,1,0:T(8,128)(2,1)} %param.29) | copy-start | bytes 5505028
  17.2 16.1 %copy-start.3 = (bf16[1,3584,256]{2,1,0:T(8,128)(2,1)S(1)}, bf16[1,3584,256]{2,1,0:T(8,128)(2,1)}, u32[]{:S(2)}) copy-start(bf16[1,3584,256]{2,1,0:T(8,128)(2,1)} %param.29) | copy-start | bytes 5505028
  22.6 10.7 %copy-start.1 = (bf16[1,3584,256]{2,1,0:T(8,128)(2,1)S(1)}, bf16[1,3584,256]{2,1,0:T(8,128)(2,1)}, u32[]{:S(2)}) copy-start(bf16[1,3584,256]{2,1,0:T(8,128)(2,1)} %param.28) | copy-start | bytes 5505028
  27.8 17.2 %collective-permute-start.9 = (bf16[80,3584]{1,0:T(8,128)(2,1)S(1)}, bf16[80,3584]{1,0:T(8,128)(2,1)S(1)}, u32[]{:S(2)}, u32[]{:S(2)}) collective-permute-start(bf16[80,3584]{1,0:T(8,128)(2,1)S(1)} %slice.54), channel_id=1, source_target_pairs={{0,16},{8,24},{16,0},{24,8},{1,17},{9,25},{17,1},{25,9},{2,18},{10... | collective-permute-start | bytes 1720328 | tf_op jit(solution)/shard_map/ppermute | solution.py:30
  29.7 15.4 %collective-permute-start.8 = (bf16[48,3584]{1,0:T(8,128)(2,1)S(1)}, bf16[48,3584]{1,0:T(8,128)(2,1)S(1)}, u32[]{:S(2)}, u32[]{:S(2)}) collective-permute-start(bf16[48,3584]{1,0:T(8,128)(2,1)S(1)} %slice.55), channel_id=1, source_target_pairs={{0,1},{1,2},{2,3},{3,4},{4,5},{5,6},{6,7},{7,0},{8,9},{9,10},{10,1... | collective-permute-start | bytes 1032200 | tf_op jit(solution)/shard_map/ppermute | solution.py:24
  33.2 11.8 %collective-permute-start.10 = (bf16[128,512]{1,0:T(8,128)(2,1)S(1)}, bf16[128,512]{1,0:T(8,128)(2,1)S(1)}, u32[]{:S(2)}, u32[]{:S(2)}) collective-permute-start(bf16[128,512]{1,0:T(8,128)(2,1)S(1)} %collective-permute-done.4.refs_3_), channel_id=1, source_target_pairs={{0,1},{1,2},{2,3},{3,4},{4,5},{5,6},{6,7},{7,0},{8,9},{9,10},{10,1... | collective-permute-start | bytes 393224 | tf_op jit(solution)/shard_map/ppermute | solution.py:24
  39.8 14.2 %collective-permute-start.6 = (bf16[48,3584]{1,0:T(8,128)(2,1)S(1)}, bf16[48,3584]{1,0:T(8,128)(2,1)S(1)}, u32[]{:S(2)}, u32[]{:S(2)}) collective-permute-start(bf16[48,3584]{1,0:T(8,128)(2,1)S(1)} %get-tuple-element.129), channel_id=1, source_target_pairs={{0,16},{8,24},{16,0},{24,8},{1,17},{9,25},{17,1},{25,9},{2,18},{10... | collective-permute-start | bytes 1032200 | tf_op jit(solution)/shard_map/ppermute | solution.py:30
  40.3 18.0 %collective-permute-start.7 = (bf16[48,3584]{1,0:T(8,128)(2,1)S(1)}, bf16[48,3584]{1,0:T(8,128)(2,1)S(1)}, u32[]{:S(2)}, u32[]{:S(2)}) collective-permute-start(bf16[48,3584]{1,0:T(8,128)(2,1)S(1)} %get-tuple-element.130), channel_id=1, source_target_pairs={{0,7},{1,0},{2,1},{3,2},{4,3},{5,4},{6,5},{7,6},{8,15},{9,8},{10,9... | collective-permute-start | bytes 1032200 | tf_op jit(solution)/shard_map/ppermute | solution.py:24
  48.3 12.6 %collective-permute-start.11 = (bf16[48,3584]{1,0:T(8,128)(2,1)S(1)}, bf16[48,3584]{1,0:T(8,128)(2,1)S(1)}, u32[]{:S(2)}, u32[]{:S(2)}) collective-permute-start(bf16[48,3584]{1,0:T(8,128)(2,1)S(1)} %get-tuple-element.137), channel_id=1, source_target_pairs={{0,7},{1,0},{2,1},{3,2},{4,3},{5,4},{6,5},{7,6},{8,15},{9,8},{10,9... | collective-permute-start | bytes 1032200 | tf_op jit(solution)/shard_map/ppermute | solution.py:24
  50.9 11.6 %collective-permute-start.12 = (bf16[48,3584]{1,0:T(8,128)(2,1)S(1)}, bf16[48,3584]{1,0:T(8,128)(2,1)S(1)}, u32[]{:S(2)}, u32[]{:S(2)}) collective-permute-start(bf16[48,3584]{1,0:T(8,128)(2,1)S(1)} %get-tuple-element.146), channel_id=1, source_target_pairs={{0,16},{8,24},{16,0},{24,8},{1,17},{9,25},{17,1},{25,9},{2,18},{10... | collective-permute-start | bytes 1032200 | tf_op jit(solution)/shard_map/ppermute | solution.py:30
  53.2 15.2 %collective-permute-start.14 = (bf16[256,512]{1,0:T(8,128)(2,1)S(1)}, bf16[256,512]{1,0:T(8,128)(2,1)S(1)}, u32[]{:S(2)}, u32[]{:S(2)}) collective-permute-start(bf16[256,512]{1,0:T(8,128)(2,1)S(1)} %get-tuple-element.150), channel_id=1, source_target_pairs={{0,7},{1,0},{2,1},{3,2},{4,3},{5,4},{6,5},{7,6},{8,15},{9,8},{10,9... | collective-permute-start | bytes 786440 | tf_op jit(solution)/shard_map/ppermute | solution.py:24
  53.9 13.9 %collective-permute-start.15 = (bf16[32,3584]{1,0:T(8,128)(2,1)S(1)}, bf16[32,3584]{1,0:T(8,128)(2,1)S(1)}, u32[]{:S(2)}, u32[]{:S(2)}) collective-permute-start(bf16[32,3584]{1,0:T(8,128)(2,1)S(1)} %get-tuple-element.152), channel_id=1, source_target_pairs={{0,16},{8,24},{16,0},{24,8},{1,17},{9,25},{17,1},{25,9},{2,18},{10... | collective-permute-start | bytes 688136 | tf_op jit(solution)/shard_map/ppermute | solution.py:30
  58.3 10.2 %collective-permute-start.17 = (bf16[3584,512]{1,0:T(8,128)(2,1)S(1)}, bf16[3584,512]{1,0:T(8,128)(2,1)S(1)}, u32[]{:S(2)}, u32[]{:S(2)}) collective-permute-start(bf16[3584,512]{1,0:T(8,128)(2,1)S(1)} %weight_pass.2), channel_id=1, source_target_pairs={{0,8},{8,0},{16,24},{24,16},{1,9},{9,1},{17,25},{25,17},{2,10},{10... | collective-permute-start | bytes 11010056 | tf_op jit(solution)/shard_map/ppermute | solution.py:36
  61.0 15.9 %collective-permute-start.19 = (bf16[80,3584]{1,0:T(8,128)(2,1)S(1)}, bf16[80,3584]{1,0:T(8,128)(2,1)S(1)}, u32[]{:S(2)}, u32[]{:S(2)}) collective-permute-start(bf16[80,3584]{1,0:T(8,128)(2,1)S(1)} %join.3), channel_id=1, source_target_pairs={{0,16},{8,24},{16,0},{24,8},{1,17},{9,25},{17,1},{25,9},{2,18},{10... | collective-permute-start | bytes 1720328 | tf_op jit(solution)/shard_map/ppermute | solution.py:30
  62.6 11.7 %collective-permute-start.13 = (bf16[48,3584]{1,0:T(8,128)(2,1)S(1)}, bf16[48,3584]{1,0:T(8,128)(2,1)S(1)}, u32[]{:S(2)}, u32[]{:S(2)}) collective-permute-start(bf16[48,3584]{1,0:T(8,128)(2,1)S(1)} %join.4), channel_id=1, source_target_pairs={{0,7},{1,0},{2,1},{3,2},{4,3},{5,4},{6,5},{7,6},{8,15},{9,8},{10,9... | collective-permute-start | bytes 1032200 | tf_op jit(solution)/shard_map/ppermute | solution.py:24
  67.8 9.1 %collective-permute-start.18 = (bf16[32,3584]{1,0:T(8,128)(2,1)S(1)}, bf16[32,3584]{1,0:T(8,128)(2,1)S(1)}, u32[]{:S(2)}, u32[]{:S(2)}) collective-permute-start(bf16[32,3584]{1,0:T(8,128)(2,1)S(1)} %join.5), channel_id=1, source_target_pairs={{0,7},{1,0},{2,1},{3,2},{4,3},{5,4},{6,5},{7,6},{8,15},{9,8},{10,9... | collective-permute-start | bytes 688136 | tf_op jit(solution)/shard_map/ppermute | solution.py:24
  68.5 5.0 %collective-permute-start.16 = (bf16[256,256]{1,0:T(8,128)(2,1)S(1)}, bf16[256,256]{1,0:T(8,128)(2,1)S(1)}, u32[]{:S(2)}, u32[]{:S(2)}) collective-permute-start(bf16[256,256]{1,0:T(8,128)(2,1)S(1)} %hidden_sum.1), channel_id=1, source_target_pairs={{0,8},{8,0},{16,24},{24,16},{1,9},{9,1},{17,25},{25,17},{2,10},{10... | collective-permute-start | bytes 393224 | tf_op jit(solution)/shard_map/ppermute | solution.py:36

commit v9 on v8

--- a/solution.py
+++ b/solution.py
@@ -371,7 +371,7 @@
     y_sent = y_tile[out_head:]
     xy_low = shifted(y_sent, 1)
     xy_grads = shifted(y_grads, 1)
-    x_low = after(x_low, y_sent)
+    x_low = after(x_low, y_sent, y_grads)
 
     lower = row_count - head
     hid_mid, own_mid, other_mid, mid_parts = block_pass(

time: 78.5 us -> 78.5 us (level)
  starting transfers between devices: 29.3 us -> 31.2 us
  waiting for transfers between devices: 12.4 us -> 10.6 us
    ppermute x9, starting transfers between devices: 18.5 us -> 21.2 us  [shifted(): return lax.ppermute(value, 'expert', pairs)]
    ppermute x9, waiting for transfers between devices: 7.22 us -> 5.35 us  [shifted(): return lax.ppermute(value, 'expert', pairs)]
    ppermute x7, starting transfers between devices: 10.1 us -> 9.25 us  [across(): return lax.ppermute(value, 'dp', pairs)]
  transfers between devices with their start and end apart: 20 -> 20, of which waited for: 4 -> 5; matrix products, arithmetic and copies ran while one was open for 3% -> 3% of each run, Pallas kernels for 34% -> 34%
where the time goes in v9:
time: 78.5 us; the launch traced here: 78.2 us
  starting transfers between devices  31.2 us (40%)
  Pallas kernels  27.6 us (35%)
  waiting for transfers between devices  10.6 us (14%)
  local copies, waits for them, and re-layouts  4.64 us (6%)
  between operations  3.3 us (4%)
  other arithmetic  0.85 us (1%)
    ppermute x9, starting transfers between devices, shifted(): return lax.ppermute(value, 'expert', pairs)  21.2 us
    pallas_call x3, Pallas kernels, block_pass(): pl.pallas_call(functools.partial(block_body, len(pieces), sources, len(ex...  15.2 us
    ppermute x7, starting transfers between devices, across(): return lax.ppermute(value, 'dp', pairs)  9.25 us
    pallas_call x2, Pallas kernels, weight_pass(): pl.pallas_call(functools.partial(weight_body, len(pieces), len(grads), st...  8.8 us
    ppermute x9, waiting for transfers between devices, shifted(): return lax.ppermute(value, 'expert', pairs)  5.35 us
    ppermute x7, waiting for transfers between devices, across(): return lax.ppermute(value, 'dp', pairs)  5.23 us
    unnamed x8, local copies, waits for them, and re-layouts  3.01 us
  transfers between devices with their start and end apart: 20, of which 5 were waited for; matrix products, arithmetic and copies ran while one was open for 3% of the time, Pallas kernels for 34%

profile of v9, /device:TPU:0, one launch (start us, length us, event | category | flops | bytes accessed | tf_op | source)
XLA Modules:
  0.0 78.2 jit_solution(13620967890476283052)
XLA Ops:
  0.6 0.5 collective-permute-start
  1.1 0.1 collective-permute-start.1
  1.2 2.9 %collective-permute-start.2 = (bf16[128,3584]{1,0:T(8,128)(2,1)}, bf16[128,3584]{1,0:T(8,128)(2,1)S(1)}, u32[]{:S(2)}, u32[]{:S(2)}) collective-permute-start(bf16[128,3584]{1,0:T(8,128)(2,1)} %bitcast.28), channel_id=1, source_target_pairs={{0,16},{8,24},{16,0},{24,8},{1,17},{9,25},{17,1},{25,9},{2,18},{10... | collective-permute-start | bytes 2752520 | tf_op jit(solution)/shard_map/ppermute | solution.py:30
  4.2 1.3 %pack.1 = (bf16[80,4096]{1,0:T(8,128)(2,1)S(1)}, bf16[48,4096]{1,0:T(8,128)(2,1)S(1)}, bf16[128,512]{1,0:T(8,128)(2,1)S(1)}) custom-call(bf16[128,3584]{1,0:T(8,128)(2,1)} %bitcast.29, bf16[128,1024]{1,0:T(8,128)(2,1)} %bitcast.30), custom_call_target="tpu_custom_call" | custom-call | bytes 2359296 | tf_op jit(solution)/shard_map/pack/pallas_call | solution.py:90
  5.5 1.5 %collective-permute-start.3 = (bf16[80,4096]{1,0:T(8,128)(2,1)S(1)}, bf16[80,4096]{1,0:T(8,128)(2,1)S(1)}, u32[]{:S(2)}, u32[]{:S(2)}) collective-permute-start(bf16[80,4096]{1,0:T(8,128)(2,1)S(1)} %get-tuple-element.120.refs_0_), channel_id=1, source_target_pairs={{0,1},{1,2},{2,3},{3,4},{4,5},{5,6},{6,7},{7,0},{8,9},{9,10},{10,1... | collective-permute-start | bytes 1966088 | tf_op jit(solution)/shard_map/ppermute | solution.py:24
  7.1 1.5 %collective-permute-start.5 = (bf16[48,4096]{1,0:T(8,128)(2,1)S(1)}, bf16[48,4096]{1,0:T(8,128)(2,1)S(1)}, u32[]{:S(2)}, u32[]{:S(2)}) collective-permute-start(bf16[48,4096]{1,0:T(8,128)(2,1)S(1)} %get-tuple-element.121.refs_1_), channel_id=1, source_target_pairs={{0,1},{1,2},{2,3},{3,4},{4,5},{5,6},{6,7},{7,0},{8,9},{9,10},{10,1... | collective-permute-start | bytes 1179656 | tf_op jit(solution)/shard_map/ppermute | solution.py:24
  8.6 1.4 %fusion.4 = (s32[1,1]{1,0:T(1,128)}, s32[1,1]{1,0:T(1,128)}, s32[1,1]{1,0:T(1,128)}, s32[1,1]{1,0:T(1,128)}) fusion(s32[4,8]{1,0:T(4,128)} %param.27, s32[]{:T(128)S(6)} %select_n.62, s32[]{:T(128)S(6)} %select_n.63, s32[]{:T(128)S(6)} %select_n.67, s32[]{:T(128)S(6)} %select_n.70), kind=kLoop, calls=%fused_computation.9 | loop fusion | bytes 48 | tf_op jit(solution)/shard_map/dynamic_slice | solution.py:346
  12.6 0.8 %fusion = (f32[128,1]{0,1:T(1,128)S(1)}, f32[128,1]{0,1:T(1,128)S(1)}, f32[128,1]{0,1:T(1,128)S(1)}, f32[128,1]{0,1:T(1,128)S(1)}) fusion(pred[]{:T(512)} %bitcast.3, f32[4,1024]{1,0:T(4,128)} %param.26, s32[]{:T(128)S(6)} %select_n.62, s32[]{:T(128)S(6)} %select_n.64, s32[]{:T(128)S(6)} %select_n.67, pred[]{:T(512)} %bitcast.5, s32[]{:T(128)S(6)} %select_n.71, ...), kind=kLoop, calls=%fused_computation.5 | loop fusion | flops 512 | bytes 4116 | tf_op jit(solution)/shard_map/reshape | solution.py:349
  13.4 0.1 copy.14.refs_2_.refs_4_.refs_3_
  13.6 0.0 collective-permute-done.refs_5_.refs_7_
  13.6 0.6 collective-permute-start.4
  14.1 0.0 collective-permute-done.1.refs_6_.refs_8_
  14.2 1.5 %copy-done = bf16[1,3584,256]{2,1,0:T(8,128)(2,1)S(1)} copy-done((bf16[1,3584,256]{2,1,0:T(8,128)(2,1)S(1)}, bf16[1,3584,256]{2,1,0:T(8,128)(2,1)}, u32[]{:S(2)}) %copy-start) | copy-done | bytes 1835032
  15.7 1.5 %copy-done.2 = bf16[1,3584,256]{2,1,0:T(8,128)(2,1)S(1)} copy-done((bf16[1,3584,256]{2,1,0:T(8,128)(2,1)S(1)}, bf16[1,3584,256]{2,1,0:T(8,128)(2,1)}, u32[]{:S(2)}) %copy-start.2) | copy-done | bytes 1835032
  17.2 5.4 %block_pass.3 = (bf16[128,512]{1,0:T(8,128)(2,1)S(1)}, bf16[128,512]{1,0:T(8,128)(2,1)S(1)}, bf16[128,512]{1,0:T(8,128)(2,1)S(1)}, bf16[128,3584]{1,0:T(8,128)(2,1)S(1)}) custom-call(bf16[80,4096]{1,0:T(8,128)(2,1)S(1)} %get-tuple-element.120.refs_0_, bf16[48,4096]{1,0:T(8,128)(2,1)S(1)} %get-tuple-element.121.refs_1_, ...), custom_call_target="tpu_custom_call" | custom-call | flops 1879048192 | bytes 1835008 | tf_op jit(solution)/shard_map/block_pass/pallas_call | solution.py:162
  22.6 0.0 copy-start.1
  22.6 5.2 %collective-permute-done.4.refs_3_ = bf16[128,512]{1,0:T(8,128)(2,1)S(1)} collective-permute-done((bf16[128,512]{1,0:T(8,128)(2,1)S(1)}, bf16[128,512]{1,0:T(8,128)(2,1)S(1)}, u32[]{:S(2)}, u32[]{:S(2)}) %collective-permute-start.4) | collective-permute-done | bytes 131104 | tf_op jit(solution)/shard_map/ppermute | solution.py:30
  27.8 0.0 collective-permute-done.3.refs_1_.refs_3_
  27.8 1.8 %collective-permute-start.9 = (bf16[80,3584]{1,0:T(8,128)(2,1)S(1)}, bf16[80,3584]{1,0:T(8,128)(2,1)S(1)}, u32[]{:S(2)}, u32[]{:S(2)}) collective-permute-start(bf16[80,3584]{1,0:T(8,128)(2,1)S(1)} %slice.54), channel_id=1, source_target_pairs={{0,16},{8,24},{16,0},{24,8},{1,17},{9,25},{17,1},{25,9},{2,18},{10... | collective-permute-start | bytes 1720328 | tf_op jit(solution)/shard_map/ppermute | solution.py:30
  29.7 1.5 %collective-permute-start.8 = (bf16[48,3584]{1,0:T(8,128)(2,1)S(1)}, bf16[48,3584]{1,0:T(8,128)(2,1)S(1)}, u32[]{:S(2)}, u32[]{:S(2)}) collective-permute-start(bf16[48,3584]{1,0:T(8,128)(2,1)S(1)} %slice.55), channel_id=1, source_target_pairs={{0,1},{1,2},{2,3},{3,4},{4,5},{5,6},{6,7},{7,0},{8,9},{9,10},{10,1... | collective-permute-start | bytes 1032200 | tf_op jit(solution)/shard_map/ppermute | solution.py:24
  31.2 1.5 %collective-permute-start.10 = (bf16[128,512]{1,0:T(8,128)(2,1)S(1)}, bf16[128,512]{1,0:T(8,128)(2,1)S(1)}, u32[]{:S(2)}, u32[]{:S(2)}) collective-permute-start(bf16[128,512]{1,0:T(8,128)(2,1)S(1)} %collective-permute-done.4.refs_3_), channel_id=1, source_target_pairs={{0,1},{1,2},{2,3},{3,4},{4,5},{5,6},{6,7},{7,0},{8,9},{9,10},{10,1... | collective-permute-start | bytes 393224 | tf_op jit(solution)/shard_map/ppermute | solution.py:24
  32.8 0.5 collective-permute-done.5.refs_2_.refs_4_
  33.2 6.5 %block_pass.4 = (bf16[256,512]{1,0:T(8,128)(2,1)S(1)}, bf16[256,512]{1,0:T(8,128)(2,1)S(1)}, bf16[256,512]{1,0:T(8,128)(2,1)S(1)}, bf16[3584,256]{1,0:T(8,128)(2...) custom-call(bf16[128,3584]{1,0:T(8,128)(2,1)S(1)} %collective-permut, ...), custom_call_target="tpu_custom_call" | custom-call | flops 3758096384 | bytes 3670016 | tf_op jit(solution)/shard_map/block_pass/pallas_call | solution.py:162
  39.7 0.6 collective-permute-start.6
  40.3 2.7 %collective-permute-start.7 = (bf16[48,3584]{1,0:T(8,128)(2,1)S(1)}, bf16[48,3584]{1,0:T(8,128)(2,1)S(1)}, u32[]{:S(2)}, u32[]{:S(2)}) collective-permute-start(bf16[48,3584]{1,0:T(8,128)(2,1)S(1)} %get-tuple-element.130), channel_id=1, source_target_pairs={{0,7},{1,0},{2,1},{3,2},{4,3},{5,4},{6,5},{7,6},{8,15},{9,8},{10,9... | collective-permute-start | bytes 1032200 | tf_op jit(solution)/shard_map/ppermute | solution.py:24
  43.0 1.3 %collective-permute-done.10.refs_2_ = bf16[128,512]{1,0:T(8,128)(2,1)S(1)} collective-permute-done((bf16[128,512]{1,0:T(8,128)(2,1)S(1)}, bf16[128,512]{1,0:T(8,128)(2,1)S(1)}, u32[]{:S(2)}, u32[]{:S(2)}) %collective-permute-start.10) | collective-permute-done | bytes 131104 | tf_op jit(solution)/shard_map/ppermute | solution.py:24
  44.4 0.0 collective-permute-done.8.refs_1_.refs_6_
  44.4 3.2 %block_pass.5 = (bf16[256,512]{1,0:T(8,128)(2,1)S(1)}, bf16[128,512]{1,0:T(8,128)(2,1)S(1)}, bf16[128,512]{1,0:T(8,128)(2,1)S(1)}, bf16[48,3584]{1,0:T(8,128)(2,...) custom-call(bf16[80,3584]{1,0:T(8,128)(2,1)S(1)} %collective-permute-done.9.refs_0_.refs_5_, ...), custom_call_target="tpu_custom_call" | custom-call | flops 1879048192 | bytes 1835008 | tf_op jit(solution)/shard_map/block_pass/pallas_call | solution.py:162
  47.6 4.3 %collective-permute-start.11 = (bf16[48,3584]{1,0:T(8,128)(2,1)S(1)}, bf16[48,3584]{1,0:T(8,128)(2,1)S(1)}, u32[]{:S(2)}, u32[]{:S(2)}) collective-permute-start(bf16[48,3584]{1,0:T(8,128)(2,1)S(1)} %get-tuple-element.137), channel_id=1, source_target_pairs={{0,7},{1,0},{2,1},{3,2},{4,3},{5,4},{6,5},{7,6},{8,15},{9,8},{10,9... | collective-permute-start | bytes 1032200 | tf_op jit(solution)/shard_map/ppermute | solution.py:24
  51.9 1.5 %collective-permute-start.12 = (bf16[48,3584]{1,0:T(8,128)(2,1)S(1)}, bf16[48,3584]{1,0:T(8,128)(2,1)S(1)}, u32[]{:S(2)}, u32[]{:S(2)}) collective-permute-start(bf16[48,3584]{1,0:T(8,128)(2,1)S(1)} %get-tuple-element.146), channel_id=1, source_target_pairs={{0,16},{8,24},{16,0},{24,8},{1,17},{9,25},{17,1},{25,9},{2,18},{10... | collective-permute-start | bytes 1032200 | tf_op jit(solution)/shard_map/ppermute | solution.py:30
  53.4 0.5 collective-permute-start.14
  53.9 0.0 collective-permute-done.6.home_ref
  53.9 0.5 collective-permute-start.15
  54.4 3.9 %weight_pass.2 = bf16[3584,512]{1,0:T(8,128)(2,1)S(1)} custom-call(bf16[80,4096]{1,0:T(8,128)(2,1)S(1)} %get-tuple-element.120.refs_0_, bf16[48,4096]{1,0:T(8,128)(2,1)S(1)} %get-tuple-element.121.refs_1_, bf16[128,3584]{1,0:T(8,128)(2,1)S(1)} %collective-permute-done.2.refs_0_.refs_2_, bf16[80,4096]{1,0:T(8,128)(2,1)S(1)} %collective-permute-done.3.refs_1_.refs_3_, ...), custom_call_target="tpu_custom_call" | custom-call | flops 1879048192 | bytes 11010048 | tf_op jit(solution)/shard_map/weight_pass/pallas_call | solution.py:233
  58.3 0.1 collective-permute-start.17
  58.4 0.7 collective-permute-done.11.far_ref
  59.1 0.1 join.3
  59.2 1.3 %collective-permute-start.19 = (bf16[80,3584]{1,0:T(8,128)(2,1)S(1)}, bf16[80,3584]{1,0:T(8,128)(2,1)S(1)}, u32[]{:S(2)}, u32[]{:S(2)}) collective-permute-start(bf16[80,3584]{1,0:T(8,128)(2,1)S(1)} %join.3), channel_id=1, source_target_pairs={{0,16},{8,24},{16,0},{24,8},{1,17},{9,25},{17,1},{25,9},{2,18},{10... | collective-permute-start | bytes 1720328 | tf_op jit(solution)/shard_map/ppermute | solution.py:30
  60.5 0.0 collective-permute-done.12.far_ref
  60.5 0.1 join.4
  60.6 5.2 %collective-permute-start.13 = (bf16[48,3584]{1,0:T(8,128)(2,1)S(1)}, bf16[48,3584]{1,0:T(8,128)(2,1)S(1)}, u32[]{:S(2)}, u32[]{:S(2)}) collective-permute-start(bf16[48,3584]{1,0:T(8,128)(2,1)S(1)} %join.4), channel_id=1, source_target_pairs={{0,7},{1,0},{2,1},{3,2},{4,3},{5,4},{6,5},{7,6},{8,15},{9,8},{10,9... | collective-permute-start | bytes 1032200 | tf_op jit(solution)/shard_map/ppermute | solution.py:24
  65.8 0.1 join.5
  65.9 2.3 %collective-permute-start.18 = (bf16[32,3584]{1,0:T(8,128)(2,1)S(1)}, bf16[32,3584]{1,0:T(8,128)(2,1)S(1)}, u32[]{:S(2)}, u32[]{:S(2)}) collective-permute-start(bf16[32,3584]{1,0:T(8,128)(2,1)S(1)} %join.5), channel_id=1, source_target_pairs={{0,7},{1,0},{2,1},{3,2},{4,3},{5,4},{6,5},{7,6},{8,15},{9,8},{10,9... | collective-permute-start | bytes 688136 | tf_op jit(solution)/shard_map/ppermute | solution.py:24
  68.3 0.1 collective-permute-start.16
  68.3 4.9 %weight_pass.3 = (bf16[3584,256]{1,0:T(8,128)(2,1)}, bf16[3584,256]{1,0:T(8,128)(2,1)}) custom-call(bf16[80,4096]{1,0:T(8,128)(2,1)S(1)} %get-tuple-element.120.refs_0_, bf16[48,4096]{1,0:T(8,128)(2,1)S(1)} %get-tuple-element.121.refs_1_, bf16[128,3584]{1,0:T(8,128)(2,1)S(1)} %collective-permute-done.2.refs_0_.refs_2_, ...), custom_call_target="tpu_custom_call" | custom-call | flops 1879048192 | bytes 11010048 | tf_op jit(solution)/shard_map/weight_pass/pallas_call | solution.py:233
  73.3 0.7 hidden_pass.1
  74.0 2.9 %collective-permute-done.18.middle_ref = bf16[32,3584]{1,0:T(8,128)(2,1)S(1)} collective-permute-done((bf16[32,3584]{1,0:T(8,128)(2,1)S(1)}, bf16[32,3584]{1,0:T(8,128)(2,1)S(1)}, u32[]{:S(2)}, u32[]{:S(2)}) %collective-permute-start.18) | collective-permute-done | bytes 229408 | tf_op jit(solution)/shard_map/ppermute | solution.py:24
  76.9 1.3 %final.1 = bf16[128,3584]{1,0:T(8,128)(2,1)} custom-call(bf16[128,3584]{1,0:T(8,128)(2,1)S(1)} %get-tuple-element.122.near_ref, bf16[48,3584]{1,0:T(8,128)(2,1)S(1)} %collective-permute-done.6.home_ref, bf16[48,3584]{1,0:T(8,128)(2,1)S(1)} %collective-permute-done.7.low_near_ref, bf16[48,3584]{1,0:T(8,128)(2,1)S(1)} %collective-permute-done.13.first_ref, ...), custom_call_target="tpu_custom_call" | custom-call | flops 80000000000 | bytes 200000000 | tf_op jit(solution)/shard_map/final/pallas_call | solution.py:302
  (18 shorter events, 0.1 us)
Async XLA Ops:
  0.6 12.9 %collective-permute-start = (bf16[3584,256]{1,0:T(8,128)(2,1)}, bf16[3584,256]{1,0:T(8,128)(2,1)}, u32[]{:S(2)}, u32[]{:S(2)}) collective-permute-start(bf16[3584,256]{1,0:T(8,128)(2,1)} %bitcast.20), channel_id=1, source_target_pairs={{0,8},{8,0},{16,24},{24,16},{1,9},{9,1},{17,25},{25,17},{2,10},{10... | collective-permute-start | bytes 5505032 | tf_op jit(solution)/shard_map/ppermute | solution.py:36
  1.1 13.0 %collective-permute-start.1 = (bf16[3584,256]{1,0:T(8,128)(2,1)}, bf16[3584,256]{1,0:T(8,128)(2,1)}, u32[]{:S(2)}, u32[]{:S(2)}) collective-permute-start(bf16[3584,256]{1,0:T(8,128)(2,1)} %bitcast.24), channel_id=1, source_target_pairs={{0,8},{8,0},{16,24},{24,16},{1,9},{9,1},{17,25},{25,17},{2,10},{10... | collective-permute-start | bytes 5505032 | tf_op jit(solution)/shard_map/ppermute | solution.py:36
  1.2 28.4 %collective-permute-start.2 = (bf16[128,3584]{1,0:T(8,128)(2,1)}, bf16[128,3584]{1,0:T(8,128)(2,1)S(1)}, u32[]{:S(2)}, u32[]{:S(2)}) collective-permute-start(bf16[128,3584]{1,0:T(8,128)(2,1)} %bitcast.28), channel_id=1, source_target_pairs={{0,16},{8,24},{16,0},{24,8},{1,17},{9,25},{17,1},{25,9},{2,18},{10... | collective-permute-start | bytes 2752520 | tf_op jit(solution)/shard_map/ppermute | solution.py:30
  5.5 22.3 %collective-permute-start.3 = (bf16[80,4096]{1,0:T(8,128)(2,1)S(1)}, bf16[80,4096]{1,0:T(8,128)(2,1)S(1)}, u32[]{:S(2)}, u32[]{:S(2)}) collective-permute-start(bf16[80,4096]{1,0:T(8,128)(2,1)S(1)} %get-tuple-element.120.refs_0_), channel_id=1, source_target_pairs={{0,1},{1,2},{2,3},{3,4},{4,5},{5,6},{6,7},{7,0},{8,9},{9,10},{10,1... | collective-permute-start | bytes 1966088 | tf_op jit(solution)/shard_map/ppermute | solution.py:24
  7.1 26.2 %collective-permute-start.5 = (bf16[48,4096]{1,0:T(8,128)(2,1)S(1)}, bf16[48,4096]{1,0:T(8,128)(2,1)S(1)}, u32[]{:S(2)}, u32[]{:S(2)}) collective-permute-start(bf16[48,4096]{1,0:T(8,128)(2,1)S(1)} %get-tuple-element.121.refs_1_), channel_id=1, source_target_pairs={{0,1},{1,2},{2,3},{3,4},{4,5},{5,6},{6,7},{7,0},{8,9},{9,10},{10,1... | collective-permute-start | bytes 1179656 | tf_op jit(solution)/shard_map/ppermute | solution.py:24
  13.6 14.2 %collective-permute-start.4 = (bf16[128,512]{1,0:T(8,128)(2,1)S(1)}, bf16[128,512]{1,0:T(8,128)(2,1)S(1)}, u32[]{:S(2)}, u32[]{:S(2)}) collective-permute-start(bf16[128,512]{1,0:T(8,128)(2,1)S(1)} %get-tuple-element.123), channel_id=1, source_target_pairs={{0,16},{8,24},{16,0},{24,8},{1,17},{9,25},{17,1},{25,9},{2,18},{10... | collective-permute-start | bytes 393224 | tf_op jit(solution)/shard_map/ppermute | solution.py:30
  14.2 1.5 %copy-start = (bf16[1,3584,256]{2,1,0:T(8,128)(2,1)S(1)}, bf16[1,3584,256]{2,1,0:T(8,128)(2,1)}, u32[]{:S(2)}) copy-start(bf16[1,3584,256]{2,1,0:T(8,128)(2,1)} %param.28) | copy-start | bytes 5505028
  15.7 1.5 %copy-start.2 = (bf16[1,3584,256]{2,1,0:T(8,128)(2,1)S(1)}, bf16[1,3584,256]{2,1,0:T(8,128)(2,1)}, u32[]{:S(2)}) copy-start(bf16[1,3584,256]{2,1,0:T(8,128)(2,1)} %param.29) | copy-start | bytes 5505028
  17.2 16.1 %copy-start.3 = (bf16[1,3584,256]{2,1,0:T(8,128)(2,1)S(1)}, bf16[1,3584,256]{2,1,0:T(8,128)(2,1)}, u32[]{:S(2)}) copy-start(bf16[1,3584,256]{2,1,0:T(8,128)(2,1)} %param.29) | copy-start | bytes 5505028
  22.6 10.6 %copy-start.1 = (bf16[1,3584,256]{2,1,0:T(8,128)(2,1)S(1)}, bf16[1,3584,256]{2,1,0:T(8,128)(2,1)}, u32[]{:S(2)}) copy-start(bf16[1,3584,256]{2,1,0:T(8,128)(2,1)} %param.28) | copy-start | bytes 5505028
  27.8 16.5 %collective-permute-start.9 = (bf16[80,3584]{1,0:T(8,128)(2,1)S(1)}, bf16[80,3584]{1,0:T(8,128)(2,1)S(1)}, u32[]{:S(2)}, u32[]{:S(2)}) collective-permute-start(bf16[80,3584]{1,0:T(8,128)(2,1)S(1)} %slice.54), channel_id=1, source_target_pairs={{0,16},{8,24},{16,0},{24,8},{1,17},{9,25},{17,1},{25,9},{2,18},{10... | collective-permute-start | bytes 1720328 | tf_op jit(solution)/shard_map/ppermute | solution.py:30
  29.7 14.7 %collective-permute-start.8 = (bf16[48,3584]{1,0:T(8,128)(2,1)S(1)}, bf16[48,3584]{1,0:T(8,128)(2,1)S(1)}, u32[]{:S(2)}, u32[]{:S(2)}) collective-permute-start(bf16[48,3584]{1,0:T(8,128)(2,1)S(1)} %slice.55), channel_id=1, source_target_pairs={{0,1},{1,2},{2,3},{3,4},{4,5},{5,6},{6,7},{7,0},{8,9},{9,10},{10,1... | collective-permute-start | bytes 1032200 | tf_op jit(solution)/shard_map/ppermute | solution.py:24
  31.2 13.1 %collective-permute-start.10 = (bf16[128,512]{1,0:T(8,128)(2,1)S(1)}, bf16[128,512]{1,0:T(8,128)(2,1)S(1)}, u32[]{:S(2)}, u32[]{:S(2)}) collective-permute-start(bf16[128,512]{1,0:T(8,128)(2,1)S(1)} %collective-permute-done.4.refs_3_), channel_id=1, source_target_pairs={{0,1},{1,2},{2,3},{3,4},{4,5},{5,6},{6,7},{7,0},{8,9},{9,10},{10,1... | collective-permute-start | bytes 393224 | tf_op jit(solution)/shard_map/ppermute | solution.py:24
  39.7 14.2 %collective-permute-start.6 = (bf16[48,3584]{1,0:T(8,128)(2,1)S(1)}, bf16[48,3584]{1,0:T(8,128)(2,1)S(1)}, u32[]{:S(2)}, u32[]{:S(2)}) collective-permute-start(bf16[48,3584]{1,0:T(8,128)(2,1)S(1)} %get-tuple-element.129), channel_id=1, source_target_pairs={{0,16},{8,24},{16,0},{24,8},{1,17},{9,25},{17,1},{25,9},{2,18},{10... | collective-permute-start | bytes 1032200 | tf_op jit(solution)/shard_map/ppermute | solution.py:30
  40.3 18.0 %collective-permute-start.7 = (bf16[48,3584]{1,0:T(8,128)(2,1)S(1)}, bf16[48,3584]{1,0:T(8,128)(2,1)S(1)}, u32[]{:S(2)}, u32[]{:S(2)}) collective-permute-start(bf16[48,3584]{1,0:T(8,128)(2,1)S(1)} %get-tuple-element.130), channel_id=1, source_target_pairs={{0,7},{1,0},{2,1},{3,2},{4,3},{5,4},{6,5},{7,6},{8,15},{9,8},{10,9... | collective-permute-start | bytes 1032200 | tf_op jit(solution)/shard_map/ppermute | solution.py:24
  47.6 11.5 %collective-permute-start.11 = (bf16[48,3584]{1,0:T(8,128)(2,1)S(1)}, bf16[48,3584]{1,0:T(8,128)(2,1)S(1)}, u32[]{:S(2)}, u32[]{:S(2)}) collective-permute-start(bf16[48,3584]{1,0:T(8,128)(2,1)S(1)} %get-tuple-element.137), channel_id=1, source_target_pairs={{0,7},{1,0},{2,1},{3,2},{4,3},{5,4},{6,5},{7,6},{8,15},{9,8},{10,9... | collective-permute-start | bytes 1032200 | tf_op jit(solution)/shard_map/ppermute | solution.py:24
  51.9 8.7 %collective-permute-start.12 = (bf16[48,3584]{1,0:T(8,128)(2,1)S(1)}, bf16[48,3584]{1,0:T(8,128)(2,1)S(1)}, u32[]{:S(2)}, u32[]{:S(2)}) collective-permute-start(bf16[48,3584]{1,0:T(8,128)(2,1)S(1)} %get-tuple-element.146), channel_id=1, source_target_pairs={{0,16},{8,24},{16,0},{24,8},{1,17},{9,25},{17,1},{25,9},{2,18},{10... | collective-permute-start | bytes 1032200 | tf_op jit(solution)/shard_map/ppermute | solution.py:30
  53.4 14.8 %collective-permute-start.14 = (bf16[256,512]{1,0:T(8,128)(2,1)S(1)}, bf16[256,512]{1,0:T(8,128)(2,1)S(1)}, u32[]{:S(2)}, u32[]{:S(2)}) collective-permute-start(bf16[256,512]{1,0:T(8,128)(2,1)S(1)} %get-tuple-element.150), channel_id=1, source_target_pairs={{0,7},{1,0},{2,1},{3,2},{4,3},{5,4},{6,5},{7,6},{8,15},{9,8},{10,9... | collective-permute-start | bytes 786440 | tf_op jit(solution)/shard_map/ppermute | solution.py:24
  53.9 11.9 %collective-permute-start.15 = (bf16[32,3584]{1,0:T(8,128)(2,1)S(1)}, bf16[32,3584]{1,0:T(8,128)(2,1)S(1)}, u32[]{:S(2)}, u32[]{:S(2)}) collective-permute-start(bf16[32,3584]{1,0:T(8,128)(2,1)S(1)} %get-tuple-element.152), channel_id=1, source_target_pairs={{0,16},{8,24},{16,0},{24,8},{1,17},{9,25},{17,1},{25,9},{2,18},{10... | collective-permute-start | bytes 688136 | tf_op jit(solution)/shard_map/ppermute | solution.py:30
  58.3 10.0 %collective-permute-start.17 = (bf16[3584,512]{1,0:T(8,128)(2,1)S(1)}, bf16[3584,512]{1,0:T(8,128)(2,1)S(1)}, u32[]{:S(2)}, u32[]{:S(2)}) collective-permute-start(bf16[3584,512]{1,0:T(8,128)(2,1)S(1)} %weight_pass.2), channel_id=1, source_target_pairs={{0,8},{8,0},{16,24},{24,16},{1,9},{9,1},{17,25},{25,17},{2,10},{10... | collective-permute-start | bytes 11010056 | tf_op jit(solution)/shard_map/ppermute | solution.py:36
  59.2 17.7 %collective-permute-start.19 = (bf16[80,3584]{1,0:T(8,128)(2,1)S(1)}, bf16[80,3584]{1,0:T(8,128)(2,1)S(1)}, u32[]{:S(2)}, u32[]{:S(2)}) collective-permute-start(bf16[80,3584]{1,0:T(8,128)(2,1)S(1)} %join.3), channel_id=1, source_target_pairs={{0,16},{8,24},{16,0},{24,8},{1,17},{9,25},{17,1},{25,9},{2,18},{10... | collective-permute-start | bytes 1720328 | tf_op jit(solution)/shard_map/ppermute | solution.py:30
  60.6 13.4 %collective-permute-start.13 = (bf16[48,3584]{1,0:T(8,128)(2,1)S(1)}, bf16[48,3584]{1,0:T(8,128)(2,1)S(1)}, u32[]{:S(2)}, u32[]{:S(2)}) collective-permute-start(bf16[48,3584]{1,0:T(8,128)(2,1)S(1)} %join.4), channel_id=1, source_target_pairs={{0,7},{1,0},{2,1},{3,2},{4,3},{5,4},{6,5},{7,6},{8,15},{9,8},{10,9... | collective-permute-start | bytes 1032200 | tf_op jit(solution)/shard_map/ppermute | solution.py:24
  65.9 11.0 %collective-permute-start.18 = (bf16[32,3584]{1,0:T(8,128)(2,1)S(1)}, bf16[32,3584]{1,0:T(8,128)(2,1)S(1)}, u32[]{:S(2)}, u32[]{:S(2)}) collective-permute-start(bf16[32,3584]{1,0:T(8,128)(2,1)S(1)} %join.5), channel_id=1, source_target_pairs={{0,7},{1,0},{2,1},{3,2},{4,3},{5,4},{6,5},{7,6},{8,15},{9,8},{10,9... | collective-permute-start | bytes 688136 | tf_op jit(solution)/shard_map/ppermute | solution.py:24
  68.3 5.0 %collective-permute-start.16 = (bf16[256,256]{1,0:T(8,128)(2,1)S(1)}, bf16[256,256]{1,0:T(8,128)(2,1)S(1)}, u32[]{:S(2)}, u32[]{:S(2)}) collective-permute-start(bf16[256,256]{1,0:T(8,128)(2,1)S(1)} %hidden_sum.1), channel_id=1, source_target_pairs={{0,8},{8,0},{16,24},{24,16},{1,9},{9,1},{17,25},{25,17},{2,10},{10... | collective-permute-start | bytes 393224 | tf_op jit(solution)/shard_map/ppermute | solution.py:36

commit v10 on v9

--- a/solution.py
+++ b/solution.py
@@ -174,7 +174,7 @@
         + [jax.ShapeDtypeStruct((width, quarter), jnp.bfloat16)] * len(handed)
         + [jax.ShapeDtypeStruct((count, width), jnp.bfloat16) for count in part_rows],
         compiler_params=pltpu.CompilerParams(vmem_limit_bytes=LIMIT),
-        cost_estimate=work(16 * rows * width * quarter, 4 * rows * width),
+        cost_estimate=work(24 * rows * width * quarter, 4 * rows * width),
         name="block_pass",
     )(*pieces, *extra, scales, *panels, *carry)
     return hidden, own, other, parts

time: 78.5 us -> 78.5 us (level)
    unnamed x8 -> x4, local copies, waits for them, and re-layouts: 3.01 us -> 3 us
  transfers between devices with their start and end apart: 20 -> 20, of which waited for: 5 -> 5; matrix products, arithmetic and copies ran while one was open for 3% -> 3% of each run, Pallas kernels for 34% -> 33%
where the time goes in v10:
time: 78.5 us; the launch traced here: 78.2 us
  starting transfers between devices  31.2 us (40%)
  Pallas kernels  27.4 us (35%)
  waiting for transfers between devices  10.6 us (14%)
  local copies, waits for them, and re-layouts  4.71 us (6%)
  between operations  3.42 us (4%)
  other arithmetic  0.85 us (1%)
    ppermute x9, starting transfers between devices, shifted(): return lax.ppermute(value, 'expert', pairs)  21.2 us
    pallas_call x3, Pallas kernels, block_pass(): pl.pallas_call(functools.partial(block_body, len(pieces), sources, len(ex...  15 us
    ppermute x7, starting transfers between devices, across(): return lax.ppermute(value, 'dp', pairs)  9.23 us
    pallas_call x2, Pallas kernels, weight_pass(): pl.pallas_call(functools.partial(weight_body, len(pieces), len(grads), st...  8.8 us
    ppermute x9, waiting for transfers between devices, shifted(): return lax.ppermute(value, 'expert', pairs)  5.37 us
    ppermute x7, waiting for transfers between devices, across(): return lax.ppermute(value, 'dp', pairs)  5.19 us
    unnamed x4, local copies, waits for them, and re-layouts  3 us
  transfers between devices with their start and end apart: 20, of which 5 were waited for; matrix products, arithmetic and copies ran while one was open for 3% of the time, Pallas kernels for 33%

profile of v10, /device:TPU:0, one launch (start us, length us, event | category | flops | bytes accessed | tf_op | source)
XLA Modules:
  0.0 78.2 jit_solution(1796485101491214718)
XLA Ops:
  0.6 0.5 collective-permute-start
  1.1 0.1 collective-permute-start.1
  1.2 2.9 %collective-permute-start.2 = (bf16[128,3584]{1,0:T(8,128)(2,1)}, bf16[128,3584]{1,0:T(8,128)(2,1)S(1)}, u32[]{:S(2)}, u32[]{:S(2)}) collective-permute-start(bf16[128,3584]{1,0:T(8,128)(2,1)} %bitcast.28), channel_id=1, source_target_pairs={{0,16},{8,24},{16,0},{24,8},{1,17},{9,25},{17,1},{25,9},{2,18},{10... | collective-permute-start | bytes 2752520 | tf_op jit(solution)/shard_map/ppermute | solution.py:30
  4.2 1.3 %pack.1 = (bf16[80,4096]{1,0:T(8,128)(2,1)S(1)}, bf16[48,4096]{1,0:T(8,128)(2,1)S(1)}, bf16[128,512]{1,0:T(8,128)(2,1)S(1)}) custom-call(bf16[128,3584]{1,0:T(8,128)(2,1)} %bitcast.29, bf16[128,1024]{1,0:T(8,128)(2,1)} %bitcast.30), custom_call_target="tpu_custom_call" | custom-call | bytes 2359296 | tf_op jit(solution)/shard_map/pack/pallas_call | solution.py:90
  5.5 1.5 %collective-permute-start.3 = (bf16[80,4096]{1,0:T(8,128)(2,1)S(1)}, bf16[80,4096]{1,0:T(8,128)(2,1)S(1)}, u32[]{:S(2)}, u32[]{:S(2)}) collective-permute-start(bf16[80,4096]{1,0:T(8,128)(2,1)S(1)} %get-tuple-element.120.refs_0_), channel_id=1, source_target_pairs={{0,1},{1,2},{2,3},{3,4},{4,5},{5,6},{6,7},{7,0},{8,9},{9,10},{10,1... | collective-permute-start | bytes 1966088 | tf_op jit(solution)/shard_map/ppermute | solution.py:24
  7.1 1.5 %collective-permute-start.5 = (bf16[48,4096]{1,0:T(8,128)(2,1)S(1)}, bf16[48,4096]{1,0:T(8,128)(2,1)S(1)}, u32[]{:S(2)}, u32[]{:S(2)}) collective-permute-start(bf16[48,4096]{1,0:T(8,128)(2,1)S(1)} %get-tuple-element.121.refs_1_), channel_id=1, source_target_pairs={{0,1},{1,2},{2,3},{3,4},{4,5},{5,6},{6,7},{7,0},{8,9},{9,10},{10,1... | collective-permute-start | bytes 1179656 | tf_op jit(solution)/shard_map/ppermute | solution.py:24
  8.6 1.5 %fusion.4 = (s32[1,1]{1,0:T(1,128)}, s32[1,1]{1,0:T(1,128)}, s32[1,1]{1,0:T(1,128)}, s32[1,1]{1,0:T(1,128)}) fusion(s32[4,8]{1,0:T(4,128)} %param.27, s32[]{:T(128)S(6)} %select_n.62, s32[]{:T(128)S(6)} %select_n.63, s32[]{:T(128)S(6)} %select_n.67, s32[]{:T(128)S(6)} %select_n.70), kind=kLoop, calls=%fused_computation.9 | loop fusion | bytes 48 | tf_op jit(solution)/shard_map/dynamic_slice | solution.py:346
  12.8 0.8 %fusion = (f32[128,1]{0,1:T(1,128)S(1)}, f32[128,1]{0,1:T(1,128)S(1)}, f32[128,1]{0,1:T(1,128)S(1)}, f32[128,1]{0,1:T(1,128)S(1)}) fusion(pred[]{:T(512)} %bitcast.3, f32[4,1024]{1,0:T(4,128)} %param.26, s32[]{:T(128)S(6)} %select_n.62, s32[]{:T(128)S(6)} %select_n.64, s32[]{:T(128)S(6)} %select_n.67, pred[]{:T(512)} %bitcast.5, s32[]{:T(128)S(6)} %select_n.71, ...), kind=kLoop, calls=%fused_computation.5 | loop fusion | flops 512 | bytes 4116 | tf_op jit(solution)/shard_map/reshape | solution.py:349
  13.6 0.1 copy.14.refs_2_.refs_4_.refs_3_
  13.8 0.0 collective-permute-done.refs_5_.refs_7_
  13.8 0.6 collective-permute-start.4
  14.4 0.0 collective-permute-done.1.refs_6_.refs_8_
  14.4 1.5 %copy-done = bf16[1,3584,256]{2,1,0:T(8,128)(2,1)S(1)} copy-done((bf16[1,3584,256]{2,1,0:T(8,128)(2,1)S(1)}, bf16[1,3584,256]{2,1,0:T(8,128)(2,1)}, u32[]{:S(2)}) %copy-start) | copy-done | bytes 1835032
  15.9 1.5 %copy-done.1 = bf16[1,3584,256]{2,1,0:T(8,128)(2,1)S(1)} copy-done((bf16[1,3584,256]{2,1,0:T(8,128)(2,1)S(1)}, bf16[1,3584,256]{2,1,0:T(8,128)(2,1)}, u32[]{:S(2)}) %copy-start.1) | copy-done | bytes 1835032
  17.4 5.3 %block_pass.3 = (bf16[128,512]{1,0:T(8,128)(2,1)S(1)}, bf16[128,512]{1,0:T(8,128)(2,1)S(1)}, bf16[128,512]{1,0:T(8,128)(2,1)S(1)}, bf16[128,3584]{1,0:T(8,128)(2,1)S(1)}) custom-call(bf16[80,4096]{1,0:T(8,128)(2,1)S(1)} %get-tuple-element.120.refs_0_, bf16[48,4096]{1,0:T(8,128)(2,1)S(1)} %get-tuple-element.121.refs_1_, ...), custom_call_target="tpu_custom_call" | custom-call | flops 2818572288 | bytes 1835008 | tf_op jit(solution)/shard_map/block_pass/pallas_call | solution.py:162
  22.6 5.1 %collective-permute-done.4.refs_3_ = bf16[128,512]{1,0:T(8,128)(2,1)S(1)} collective-permute-done((bf16[128,512]{1,0:T(8,128)(2,1)S(1)}, bf16[128,512]{1,0:T(8,128)(2,1)S(1)}, u32[]{:S(2)}, u32[]{:S(2)}) %collective-permute-start.4) | collective-permute-done | bytes 131104 | tf_op jit(solution)/shard_map/ppermute | solution.py:30
  27.8 0.0 collective-permute-done.3.refs_1_.refs_3_
  27.8 1.8 %collective-permute-start.9 = (bf16[80,3584]{1,0:T(8,128)(2,1)S(1)}, bf16[80,3584]{1,0:T(8,128)(2,1)S(1)}, u32[]{:S(2)}, u32[]{:S(2)}) collective-permute-start(bf16[80,3584]{1,0:T(8,128)(2,1)S(1)} %slice.54), channel_id=1, source_target_pairs={{0,16},{8,24},{16,0},{24,8},{1,17},{9,25},{17,1},{25,9},{2,18},{10... | collective-permute-start | bytes 1720328 | tf_op jit(solution)/shard_map/ppermute | solution.py:30
  29.7 1.5 %collective-permute-start.8 = (bf16[48,3584]{1,0:T(8,128)(2,1)S(1)}, bf16[48,3584]{1,0:T(8,128)(2,1)S(1)}, u32[]{:S(2)}, u32[]{:S(2)}) collective-permute-start(bf16[48,3584]{1,0:T(8,128)(2,1)S(1)} %slice.55), channel_id=1, source_target_pairs={{0,1},{1,2},{2,3},{3,4},{4,5},{5,6},{6,7},{7,0},{8,9},{9,10},{10,1... | collective-permute-start | bytes 1032200 | tf_op jit(solution)/shard_map/ppermute | solution.py:24
  31.2 1.5 %collective-permute-start.10 = (bf16[128,512]{1,0:T(8,128)(2,1)S(1)}, bf16[128,512]{1,0:T(8,128)(2,1)S(1)}, u32[]{:S(2)}, u32[]{:S(2)}) collective-permute-start(bf16[128,512]{1,0:T(8,128)(2,1)S(1)} %collective-permute-done.4.refs_3_), channel_id=1, source_target_pairs={{0,1},{1,2},{2,3},{3,4},{4,5},{5,6},{6,7},{7,0},{8,9},{9,10},{10,1... | collective-permute-start | bytes 393224 | tf_op jit(solution)/shard_map/ppermute | solution.py:24
  32.8 0.5 collective-permute-done.5.refs_2_.refs_4_
  33.2 6.5 %block_pass.4 = (bf16[256,512]{1,0:T(8,128)(2,1)S(1)}, bf16[256,512]{1,0:T(8,128)(2,1)S(1)}, bf16[256,512]{1,0:T(8,128)(2,1)S(1)}, bf16[3584,256]{1,0:T(8,128)(2...) custom-call(bf16[128,3584]{1,0:T(8,128)(2,1)S(1)} %collective-permut, ...), custom_call_target="tpu_custom_call" | custom-call | flops 5637144576 | bytes 3670016 | tf_op jit(solution)/shard_map/block_pass/pallas_call | solution.py:162
  39.7 0.6 collective-permute-start.6
  40.3 2.7 %collective-permute-start.7 = (bf16[48,3584]{1,0:T(8,128)(2,1)S(1)}, bf16[48,3584]{1,0:T(8,128)(2,1)S(1)}, u32[]{:S(2)}, u32[]{:S(2)}) collective-permute-start(bf16[48,3584]{1,0:T(8,128)(2,1)S(1)} %get-tuple-element.130), channel_id=1, source_target_pairs={{0,7},{1,0},{2,1},{3,2},{4,3},{5,4},{6,5},{7,6},{8,15},{9,8},{10,9... | collective-permute-start | bytes 1032200 | tf_op jit(solution)/shard_map/ppermute | solution.py:24
  43.0 1.3 %collective-permute-done.10.refs_2_ = bf16[128,512]{1,0:T(8,128)(2,1)S(1)} collective-permute-done((bf16[128,512]{1,0:T(8,128)(2,1)S(1)}, bf16[128,512]{1,0:T(8,128)(2,1)S(1)}, u32[]{:S(2)}, u32[]{:S(2)}) %collective-permute-start.10) | collective-permute-done | bytes 131104 | tf_op jit(solution)/shard_map/ppermute | solution.py:24
  44.4 0.0 collective-permute-done.8.refs_1_.refs_6_
  44.4 3.2 %block_pass.5 = (bf16[256,512]{1,0:T(8,128)(2,1)S(1)}, bf16[128,512]{1,0:T(8,128)(2,1)S(1)}, bf16[128,512]{1,0:T(8,128)(2,1)S(1)}, bf16[48,3584]{1,0:T(8,128)(2,...) custom-call(bf16[80,3584]{1,0:T(8,128)(2,1)S(1)} %collective-permute-done.9.refs_0_.refs_5_, ...), custom_call_target="tpu_custom_call" | custom-call | flops 2818572288 | bytes 1835008 | tf_op jit(solution)/shard_map/block_pass/pallas_call | solution.py:162
  47.6 4.3 %collective-permute-start.11 = (bf16[48,3584]{1,0:T(8,128)(2,1)S(1)}, bf16[48,3584]{1,0:T(8,128)(2,1)S(1)}, u32[]{:S(2)}, u32[]{:S(2)}) collective-permute-start(bf16[48,3584]{1,0:T(8,128)(2,1)S(1)} %get-tuple-element.137), channel_id=1, source_target_pairs={{0,7},{1,0},{2,1},{3,2},{4,3},{5,4},{6,5},{7,6},{8,15},{9,8},{10,9... | collective-permute-start | bytes 1032200 | tf_op jit(solution)/shard_map/ppermute | solution.py:24
  51.9 1.5 %collective-permute-start.12 = (bf16[48,3584]{1,0:T(8,128)(2,1)S(1)}, bf16[48,3584]{1,0:T(8,128)(2,1)S(1)}, u32[]{:S(2)}, u32[]{:S(2)}) collective-permute-start(bf16[48,3584]{1,0:T(8,128)(2,1)S(1)} %get-tuple-element.146), channel_id=1, source_target_pairs={{0,16},{8,24},{16,0},{24,8},{1,17},{9,25},{17,1},{25,9},{2,18},{10... | collective-permute-start | bytes 1032200 | tf_op jit(solution)/shard_map/ppermute | solution.py:30
  53.4 0.5 collective-permute-start.14
  53.9 0.0 collective-permute-done.6.home_ref
  53.9 0.5 collective-permute-start.15
  54.4 3.9 %weight_pass.2 = bf16[3584,512]{1,0:T(8,128)(2,1)S(1)} custom-call(bf16[80,4096]{1,0:T(8,128)(2,1)S(1)} %get-tuple-element.120.refs_0_, bf16[48,4096]{1,0:T(8,128)(2,1)S(1)} %get-tuple-element.121.refs_1_, bf16[128,3584]{1,0:T(8,128)(2,1)S(1)} %collective-permute-done.2.refs_0_.refs_2_, bf16[80,4096]{1,0:T(8,128)(2,1)S(1)} %collective-permute-done.3.refs_1_.refs_3_, ...), custom_call_target="tpu_custom_call" | custom-call | flops 1879048192 | bytes 11010048 | tf_op jit(solution)/shard_map/weight_pass/pallas_call | solution.py:233
  58.3 0.1 collective-permute-start.17
  58.4 0.7 collective-permute-done.11.far_ref
  59.1 0.1 join.3
  59.2 1.3 %collective-permute-start.19 = (bf16[80,3584]{1,0:T(8,128)(2,1)S(1)}, bf16[80,3584]{1,0:T(8,128)(2,1)S(1)}, u32[]{:S(2)}, u32[]{:S(2)}) collective-permute-start(bf16[80,3584]{1,0:T(8,128)(2,1)S(1)} %join.3), channel_id=1, source_target_pairs={{0,16},{8,24},{16,0},{24,8},{1,17},{9,25},{17,1},{25,9},{2,18},{10... | collective-permute-start | bytes 1720328 | tf_op jit(solution)/shard_map/ppermute | solution.py:30
  60.5 0.0 collective-permute-done.12.far_ref
  60.5 0.1 join.4
  60.6 5.2 %collective-permute-start.13 = (bf16[48,3584]{1,0:T(8,128)(2,1)S(1)}, bf16[48,3584]{1,0:T(8,128)(2,1)S(1)}, u32[]{:S(2)}, u32[]{:S(2)}) collective-permute-start(bf16[48,3584]{1,0:T(8,128)(2,1)S(1)} %join.4), channel_id=1, source_target_pairs={{0,7},{1,0},{2,1},{3,2},{4,3},{5,4},{6,5},{7,6},{8,15},{9,8},{10,9... | collective-permute-start | bytes 1032200 | tf_op jit(solution)/shard_map/ppermute | solution.py:24
  65.8 0.0 collective-permute-done.15.far_ref
  65.8 0.1 join.5
  65.9 2.3 %collective-permute-start.18 = (bf16[32,3584]{1,0:T(8,128)(2,1)S(1)}, bf16[32,3584]{1,0:T(8,128)(2,1)S(1)}, u32[]{:S(2)}, u32[]{:S(2)}) collective-permute-start(bf16[32,3584]{1,0:T(8,128)(2,1)S(1)} %join.5), channel_id=1, source_target_pairs={{0,7},{1,0},{2,1},{3,2},{4,3},{5,4},{6,5},{7,6},{8,15},{9,8},{10,9... | collective-permute-start | bytes 688136 | tf_op jit(solution)/shard_map/ppermute | solution.py:24
  68.3 0.1 collective-permute-start.16
  68.3 4.9 %weight_pass.3 = (bf16[3584,256]{1,0:T(8,128)(2,1)}, bf16[3584,256]{1,0:T(8,128)(2,1)}) custom-call(bf16[80,4096]{1,0:T(8,128)(2,1)S(1)} %get-tuple-element.120.refs_0_, bf16[48,4096]{1,0:T(8,128)(2,1)S(1)} %get-tuple-element.121.refs_1_, bf16[128,3584]{1,0:T(8,128)(2,1)S(1)} %collective-permute-done.2.refs_0_.refs_2_, ...), custom_call_target="tpu_custom_call" | custom-call | flops 1879048192 | bytes 11010048 | tf_op jit(solution)/shard_map/weight_pass/pallas_call | solution.py:233
  73.3 0.7 hidden_pass.1
  74.0 2.9 %collective-permute-done.18.middle_ref = bf16[32,3584]{1,0:T(8,128)(2,1)S(1)} collective-permute-done((bf16[32,3584]{1,0:T(8,128)(2,1)S(1)}, bf16[32,3584]{1,0:T(8,128)(2,1)S(1)}, u32[]{:S(2)}, u32[]{:S(2)}) %collective-permute-start.18) | collective-permute-done | bytes 229408 | tf_op jit(solution)/shard_map/ppermute | solution.py:24
  76.9 1.3 %final.1 = bf16[128,3584]{1,0:T(8,128)(2,1)} custom-call(bf16[128,3584]{1,0:T(8,128)(2,1)S(1)} %get-tuple-element.122.near_ref, bf16[48,3584]{1,0:T(8,128)(2,1)S(1)} %collective-permute-done.6.home_ref, bf16[48,3584]{1,0:T(8,128)(2,1)S(1)} %collective-permute-done.7.low_near_ref, bf16[48,3584]{1,0:T(8,128)(2,1)S(1)} %collective-permute-done.13.first_ref, ...), custom_call_target="tpu_custom_call" | custom-call | flops 80000000000 | bytes 200000000 | tf_op jit(solution)/shard_map/final/pallas_call | solution.py:302
  (14 shorter events, 0.1 us)
Async XLA Ops:
  0.6 13.1 %collective-permute-start = (bf16[3584,256]{1,0:T(8,128)(2,1)}, bf16[3584,256]{1,0:T(8,128)(2,1)}, u32[]{:S(2)}, u32[]{:S(2)}) collective-permute-start(bf16[3584,256]{1,0:T(8,128)(2,1)} %bitcast.20), channel_id=1, source_target_pairs={{0,8},{8,0},{16,24},{24,16},{1,9},{9,1},{17,25},{25,17},{2,10},{10... | collective-permute-start | bytes 5505032 | tf_op jit(solution)/shard_map/ppermute | solution.py:36
  1.1 13.2 %collective-permute-start.1 = (bf16[3584,256]{1,0:T(8,128)(2,1)}, bf16[3584,256]{1,0:T(8,128)(2,1)}, u32[]{:S(2)}, u32[]{:S(2)}) collective-permute-start(bf16[3584,256]{1,0:T(8,128)(2,1)} %bitcast.24), channel_id=1, source_target_pairs={{0,8},{8,0},{16,24},{24,16},{1,9},{9,1},{17,25},{25,17},{2,10},{10... | collective-permute-start | bytes 5505032 | tf_op jit(solution)/shard_map/ppermute | solution.py:36
  1.2 28.4 %collective-permute-start.2 = (bf16[128,3584]{1,0:T(8,128)(2,1)}, bf16[128,3584]{1,0:T(8,128)(2,1)S(1)}, u32[]{:S(2)}, u32[]{:S(2)}) collective-permute-start(bf16[128,3584]{1,0:T(8,128)(2,1)} %bitcast.28), channel_id=1, source_target_pairs={{0,16},{8,24},{16,0},{24,8},{1,17},{9,25},{17,1},{25,9},{2,18},{10... | collective-permute-start | bytes 2752520 | tf_op jit(solution)/shard_map/ppermute | solution.py:30
  5.5 22.3 %collective-permute-start.3 = (bf16[80,4096]{1,0:T(8,128)(2,1)S(1)}, bf16[80,4096]{1,0:T(8,128)(2,1)S(1)}, u32[]{:S(2)}, u32[]{:S(2)}) collective-permute-start(bf16[80,4096]{1,0:T(8,128)(2,1)S(1)} %get-tuple-element.120.refs_0_), channel_id=1, source_target_pairs={{0,1},{1,2},{2,3},{3,4},{4,5},{5,6},{6,7},{7,0},{8,9},{9,10},{10,1... | collective-permute-start | bytes 1966088 | tf_op jit(solution)/shard_map/ppermute | solution.py:24
  7.1 26.2 %collective-permute-start.5 = (bf16[48,4096]{1,0:T(8,128)(2,1)S(1)}, bf16[48,4096]{1,0:T(8,128)(2,1)S(1)}, u32[]{:S(2)}, u32[]{:S(2)}) collective-permute-start(bf16[48,4096]{1,0:T(8,128)(2,1)S(1)} %get-tuple-element.121.refs_1_), channel_id=1, source_target_pairs={{0,1},{1,2},{2,3},{3,4},{4,5},{5,6},{6,7},{7,0},{8,9},{9,10},{10,1... | collective-permute-start | bytes 1179656 | tf_op jit(solution)/shard_map/ppermute | solution.py:24
  13.8 14.0 %collective-permute-start.4 = (bf16[128,512]{1,0:T(8,128)(2,1)S(1)}, bf16[128,512]{1,0:T(8,128)(2,1)S(1)}, u32[]{:S(2)}, u32[]{:S(2)}) collective-permute-start(bf16[128,512]{1,0:T(8,128)(2,1)S(1)} %get-tuple-element.123), channel_id=1, source_target_pairs={{0,16},{8,24},{16,0},{24,8},{1,17},{9,25},{17,1},{25,9},{2,18},{10... | collective-permute-start | bytes 393224 | tf_op jit(solution)/shard_map/ppermute | solution.py:30
  14.4 1.5 %copy-start = (bf16[1,3584,256]{2,1,0:T(8,128)(2,1)S(1)}, bf16[1,3584,256]{2,1,0:T(8,128)(2,1)}, u32[]{:S(2)}) copy-start(bf16[1,3584,256]{2,1,0:T(8,128)(2,1)} %param.28) | copy-start | bytes 5505028
  15.9 1.5 %copy-start.1 = (bf16[1,3584,256]{2,1,0:T(8,128)(2,1)S(1)}, bf16[1,3584,256]{2,1,0:T(8,128)(2,1)}, u32[]{:S(2)}) copy-start(bf16[1,3584,256]{2,1,0:T(8,128)(2,1)} %param.29) | copy-start | bytes 5505028
  27.8 16.5 %collective-permute-start.9 = (bf16[80,3584]{1,0:T(8,128)(2,1)S(1)}, bf16[80,3584]{1,0:T(8,128)(2,1)S(1)}, u32[]{:S(2)}, u32[]{:S(2)}) collective-permute-start(bf16[80,3584]{1,0:T(8,128)(2,1)S(1)} %slice.54), channel_id=1, source_target_pairs={{0,16},{8,24},{16,0},{24,8},{1,17},{9,25},{17,1},{25,9},{2,18},{10... | collective-permute-start | bytes 1720328 | tf_op jit(solution)/shard_map/ppermute | solution.py:30
  29.7 14.7 %collective-permute-start.8 = (bf16[48,3584]{1,0:T(8,128)(2,1)S(1)}, bf16[48,3584]{1,0:T(8,128)(2,1)S(1)}, u32[]{:S(2)}, u32[]{:S(2)}) collective-permute-start(bf16[48,3584]{1,0:T(8,128)(2,1)S(1)} %slice.55), channel_id=1, source_target_pairs={{0,1},{1,2},{2,3},{3,4},{4,5},{5,6},{6,7},{7,0},{8,9},{9,10},{10,1... | collective-permute-start | bytes 1032200 | tf_op jit(solution)/shard_map/ppermute | solution.py:24
  31.2 13.1 %collective-permute-start.10 = (bf16[128,512]{1,0:T(8,128)(2,1)S(1)}, bf16[128,512]{1,0:T(8,128)(2,1)S(1)}, u32[]{:S(2)}, u32[]{:S(2)}) collective-permute-start(bf16[128,512]{1,0:T(8,128)(2,1)S(1)} %collective-permute-done.4.refs_3_), channel_id=1, source_target_pairs={{0,1},{1,2},{2,3},{3,4},{4,5},{5,6},{6,7},{7,0},{8,9},{9,10},{10,1... | collective-permute-start | bytes 393224 | tf_op jit(solution)/shard_map/ppermute | solution.py:24
  39.7 14.2 %collective-permute-start.6 = (bf16[48,3584]{1,0:T(8,128)(2,1)S(1)}, bf16[48,3584]{1,0:T(8,128)(2,1)S(1)}, u32[]{:S(2)}, u32[]{:S(2)}) collective-permute-start(bf16[48,3584]{1,0:T(8,128)(2,1)S(1)} %get-tuple-element.129), channel_id=1, source_target_pairs={{0,16},{8,24},{16,0},{24,8},{1,17},{9,25},{17,1},{25,9},{2,18},{10... | collective-permute-start | bytes 1032200 | tf_op jit(solution)/shard_map/ppermute | solution.py:30
  40.3 18.0 %collective-permute-start.7 = (bf16[48,3584]{1,0:T(8,128)(2,1)S(1)}, bf16[48,3584]{1,0:T(8,128)(2,1)S(1)}, u32[]{:S(2)}, u32[]{:S(2)}) collective-permute-start(bf16[48,3584]{1,0:T(8,128)(2,1)S(1)} %get-tuple-element.130), channel_id=1, source_target_pairs={{0,7},{1,0},{2,1},{3,2},{4,3},{5,4},{6,5},{7,6},{8,15},{9,8},{10,9... | collective-permute-start | bytes 1032200 | tf_op jit(solution)/shard_map/ppermute | solution.py:24
  47.6 11.5 %collective-permute-start.11 = (bf16[48,3584]{1,0:T(8,128)(2,1)S(1)}, bf16[48,3584]{1,0:T(8,128)(2,1)S(1)}, u32[]{:S(2)}, u32[]{:S(2)}) collective-permute-start(bf16[48,3584]{1,0:T(8,128)(2,1)S(1)} %get-tuple-element.137), channel_id=1, source_target_pairs={{0,7},{1,0},{2,1},{3,2},{4,3},{5,4},{6,5},{7,6},{8,15},{9,8},{10,9... | collective-permute-start | bytes 1032200 | tf_op jit(solution)/shard_map/ppermute | solution.py:24
  51.9 8.7 %collective-permute-start.12 = (bf16[48,3584]{1,0:T(8,128)(2,1)S(1)}, bf16[48,3584]{1,0:T(8,128)(2,1)S(1)}, u32[]{:S(2)}, u32[]{:S(2)}) collective-permute-start(bf16[48,3584]{1,0:T(8,128)(2,1)S(1)} %get-tuple-element.146), channel_id=1, source_target_pairs={{0,16},{8,24},{16,0},{24,8},{1,17},{9,25},{17,1},{25,9},{2,18},{10... | collective-permute-start | bytes 1032200 | tf_op jit(solution)/shard_map/ppermute | solution.py:30
  53.4 14.8 %collective-permute-start.14 = (bf16[256,512]{1,0:T(8,128)(2,1)S(1)}, bf16[256,512]{1,0:T(8,128)(2,1)S(1)}, u32[]{:S(2)}, u32[]{:S(2)}) collective-permute-start(bf16[256,512]{1,0:T(8,128)(2,1)S(1)} %get-tuple-element.150), channel_id=1, source_target_pairs={{0,7},{1,0},{2,1},{3,2},{4,3},{5,4},{6,5},{7,6},{8,15},{9,8},{10,9... | collective-permute-start | bytes 786440 | tf_op jit(solution)/shard_map/ppermute | solution.py:24
  53.9 11.9 %collective-permute-start.15 = (bf16[32,3584]{1,0:T(8,128)(2,1)S(1)}, bf16[32,3584]{1,0:T(8,128)(2,1)S(1)}, u32[]{:S(2)}, u32[]{:S(2)}) collective-permute-start(bf16[32,3584]{1,0:T(8,128)(2,1)S(1)} %get-tuple-element.152), channel_id=1, source_target_pairs={{0,16},{8,24},{16,0},{24,8},{1,17},{9,25},{17,1},{25,9},{2,18},{10... | collective-permute-start | bytes 688136 | tf_op jit(solution)/shard_map/ppermute | solution.py:30
  58.3 10.0 %collective-permute-start.17 = (bf16[3584,512]{1,0:T(8,128)(2,1)S(1)}, bf16[3584,512]{1,0:T(8,128)(2,1)S(1)}, u32[]{:S(2)}, u32[]{:S(2)}) collective-permute-start(bf16[3584,512]{1,0:T(8,128)(2,1)S(1)} %weight_pass.2), channel_id=1, source_target_pairs={{0,8},{8,0},{16,24},{24,16},{1,9},{9,1},{17,25},{25,17},{2,10},{10... | collective-permute-start | bytes 11010056 | tf_op jit(solution)/shard_map/ppermute | solution.py:36
  59.2 17.7 %collective-permute-start.19 = (bf16[80,3584]{1,0:T(8,128)(2,1)S(1)}, bf16[80,3584]{1,0:T(8,128)(2,1)S(1)}, u32[]{:S(2)}, u32[]{:S(2)}) collective-permute-start(bf16[80,3584]{1,0:T(8,128)(2,1)S(1)} %join.3), channel_id=1, source_target_pairs={{0,16},{8,24},{16,0},{24,8},{1,17},{9,25},{17,1},{25,9},{2,18},{10... | collective-permute-start | bytes 1720328 | tf_op jit(solution)/shard_map/ppermute | solution.py:30
  60.6 13.4 %collective-permute-start.13 = (bf16[48,3584]{1,0:T(8,128)(2,1)S(1)}, bf16[48,3584]{1,0:T(8,128)(2,1)S(1)}, u32[]{:S(2)}, u32[]{:S(2)}) collective-permute-start(bf16[48,3584]{1,0:T(8,128)(2,1)S(1)} %join.4), channel_id=1, source_target_pairs={{0,7},{1,0},{2,1},{3,2},{4,3},{5,4},{6,5},{7,6},{8,15},{9,8},{10,9... | collective-permute-start | bytes 1032200 | tf_op jit(solution)/shard_map/ppermute | solution.py:24
  65.9 11.0 %collective-permute-start.18 = (bf16[32,3584]{1,0:T(8,128)(2,1)S(1)}, bf16[32,3584]{1,0:T(8,128)(2,1)S(1)}, u32[]{:S(2)}, u32[]{:S(2)}) collective-permute-start(bf16[32,3584]{1,0:T(8,128)(2,1)S(1)} %join.5), channel_id=1, source_target_pairs={{0,7},{1,0},{2,1},{3,2},{4,3},{5,4},{6,5},{7,6},{8,15},{9,8},{10,9... | collective-permute-start | bytes 688136 | tf_op jit(solution)/shard_map/ppermute | solution.py:24
  68.3 5.0 %collective-permute-start.16 = (bf16[256,256]{1,0:T(8,128)(2,1)S(1)}, bf16[256,256]{1,0:T(8,128)(2,1)S(1)}, u32[]{:S(2)}, u32[]{:S(2)}) collective-permute-start(bf16[256,256]{1,0:T(8,128)(2,1)S(1)} %hidden_sum.1), channel_id=1, source_target_pairs={{0,8},{8,0},{16,24},{24,16},{1,9},{9,1},{17,25},{25,17},{2,10},{10... | collective-permute-start | bytes 393224 | tf_op jit(solution)/shard_map/ppermute | solution.py:36
